TPU v7x, 512 devices: a whole 4x4x16 slice. The times are simulated.
512 devices in a mesh: seq: 32 (over y, x, core), head: 16 (over z).
Axes of the slice: x: 4, y: 4, z: 16, core: 2. Of those that a mesh axis runs over, the one named last changes fastest.
Arguments:
- queries: bfloat16 [32768, 2048], P('seq', 'head'), may hold values from -72 to 72
- encodings: bfloat16 [224, 128, 896], P('seq'), may hold values from -6 to 6
- key_weight: bfloat16 [896, 2048], P(None, 'head'), may hold values from -0.1875 to 0.1875
- value_weight: bfloat16 [896, 2048], P(None, 'head'), may hold values from -0.1875 to 0.1875
- reads: int32 [512, 2], replicated, may hold values from 0 to 223, as said below
- out_grad: bfloat16 [32768, 2048], P('seq', 'head'), may hold values from -6 to 6
Outputs:
- attended: bfloat16 [32768, 2048], P('seq', 'head')
- query_grad: bfloat16 [32768, 2048], P('seq', 'head')
- encoding_grad: float32 [224, 128, 896], P('seq', 'head')
- key_weight_grad: float32 [896, 2048], P('seq', 'head')
- value_weight_grad: float32 [896, 2048], P('seq', 'head')
Inputs may be any that keep to these rules, and one draw needn't show every extreme that they name: reads[c, k] is held by seq shard reads[c, k] // 7. Of the 32 reads of the segments of one seq shard, at most 2 fall on the encodings of one holder shard; in every draw one holder shard is read exactly 2 times by every seq shard.
All inputs are finite; a program needn't handle non-finite values.
Results may differ from a plain program's by a relative error of at most 0.012.
The roundings to bfloat16 on the way count: a program that leaves them out, or rounds other values in their place, can miss the bound.
Values may be sent and summed in bfloat16 or wider, within the bound.
No kernel may reach another device: no remote copies, remote signals or barrier semaphores. Data moves between devices by JAX's collectives and lax.ppermute only.
A program may use at most 128 MiB of HBM per device.

v0:
```python
import math

import jax
import jax.numpy as jnp
from jax import lax
from jax.sharding import PartitionSpec as P

SEGMENT = 64
NEIGH = 2


def read_tables(reads, seq_count, block_count, read_count):
    pair_ids = reads.reshape(seq_count, read_count)
    holders = pair_ids // block_count
    in_shard = pair_ids % block_count
    order = jnp.arange(read_count)
    earlier = order[None, :] < order[:, None]
    same_holder = holders[:, :, None] == holders[:, None, :]
    slot_rank = jnp.sum(same_holder & earlier[None], axis=2)
    return (holders, in_shard, slot_rank)


def on_device(queries, encodings, key_weight, value_weight, reads, out_grad):
    seq_count = lax.axis_size("seq")
    my_index = lax.axis_index("seq")
    block_count = encodings.shape[0]
    block_len = encodings.shape[1]
    enc_width = encodings.shape[2]
    head_dim = key_weight.shape[1]
    segments = queries.shape[0] // SEGMENT
    read_count = NEIGH * segments
    capacity = max(2, 2 * NEIGH * segments // seq_count)
    slot_count = seq_count * capacity
    score_scale = 1.0 / math.sqrt(head_dim)
    holders, in_shard, slot_rank = read_tables(reads, seq_count, block_count, read_count)
    is_mine = holders == my_index
    slot_hit = is_mine[:, :, None] & (slot_rank[:, :, None] == jnp.arange(capacity)[None, None, :])
    block_hit = in_shard[:, :, None] == jnp.arange(block_count)[None, None, :]
    selector = jnp.einsum(
        "sjr,sjl->srl", slot_hit.astype(jnp.float32), block_hit.astype(jnp.float32)
    ).reshape(slot_count, block_count)
    my_holders = lax.dynamic_index_in_dim(holders, my_index, 0, keepdims=False)
    my_ranks = lax.dynamic_index_in_dim(slot_rank, my_index, 0, keepdims=False)
    my_slots = my_holders * capacity + my_ranks
    flat_enc = encodings.reshape(block_count * block_len, enc_width)
    key_rows = jnp.dot(flat_enc, key_weight, preferred_element_type=jnp.float32).astype(
        jnp.bfloat16
    )
    value_rows = jnp.dot(flat_enc, value_weight, preferred_element_type=jnp.float32).astype(
        jnp.bfloat16
    )
    kv_owned = jnp.concatenate(
        [
            key_rows.reshape(block_count, block_len, head_dim),
            value_rows.reshape(block_count, block_len, head_dim),
        ],
        axis=2,
    )
    kv_owned = kv_owned.reshape(block_count, block_len * 2 * head_dim)
    kv_slots = jnp.dot(
        selector.astype(jnp.bfloat16), kv_owned, preferred_element_type=jnp.float32
    ).astype(jnp.bfloat16)
    kv_slots = kv_slots.reshape(slot_count, block_len, 2 * head_dim)
    query_segs = queries.reshape(segments, SEGMENT, head_dim)
    grad_segs = out_grad.reshape(segments, SEGMENT, head_dim)
    incoming = lax.all_to_all(kv_slots, "seq", split_axis=0, concat_axis=0, tiled=True)
    picked = incoming[my_slots].reshape(segments, NEIGH * block_len, 2 * head_dim)
    seg_keys = picked[:, :, :head_dim]
    seg_values = picked[:, :, head_dim:]
    scores = (
        jnp.einsum("cqd,ckd->cqk", query_segs, seg_keys, preferred_element_type=jnp.float32)
        * score_scale
    )
    probs = jax.nn.softmax(scores, axis=-1)
    probs_bf = probs.astype(jnp.bfloat16)
    attended = jnp.einsum(
        "cqk,ckd->cqd", probs_bf, seg_values, preferred_element_type=jnp.float32
    ).astype(jnp.bfloat16)
    value_part = jnp.einsum("cqk,cqd->ckd", probs_bf, grad_segs, preferred_element_type=jnp.float32)
    prob_grad = jnp.einsum(
        "cqd,ckd->cqk", grad_segs, seg_values, preferred_element_type=jnp.float32
    )
    delta_sum = jnp.sum(probs * prob_grad, axis=-1, keepdims=True)
    score_grad = (probs * (prob_grad - delta_sum) * score_scale).astype(jnp.bfloat16)
    query_grad = jnp.einsum(
        "cqk,ckd->cqd", score_grad, seg_keys, preferred_element_type=jnp.float32
    ).astype(jnp.bfloat16)
    key_part = jnp.einsum(
        "cqk,cqd->ckd", score_grad, query_segs, preferred_element_type=jnp.float32
    )
    pair_grads = jnp.concatenate([key_part, value_part], axis=2).reshape(
        read_count, block_len, 2 * head_dim
    )
    outgoing = (
        jnp.zeros((slot_count, block_len, 2 * head_dim), jnp.float32).at[my_slots].set(pair_grads)
    )
    returned = lax.all_to_all(outgoing, "seq", split_axis=0, concat_axis=0, tiled=True)
    slot_grads = returned.reshape(slot_count, block_len * 2 * head_dim)
    block_grads = jnp.dot(selector.T, slot_grads, precision=lax.Precision.HIGHEST)
    block_grads = block_grads.reshape(block_count * block_len, 2 * head_dim)
    key_grad_rows = block_grads[:, :head_dim].astype(jnp.bfloat16)
    value_grad_rows = block_grads[:, head_dim:].astype(jnp.bfloat16)
    key_term = jnp.einsum("nw,nd->wd", flat_enc, key_grad_rows, preferred_element_type=jnp.float32)
    value_term = jnp.einsum(
        "nw,nd->wd", flat_enc, value_grad_rows, preferred_element_type=jnp.float32
    )
    key_weight_grad, value_weight_grad = (
        lax.psum_scatter(key_term, "seq", scatter_dimension=0, tiled=True),
        lax.psum_scatter(value_term, "seq", scatter_dimension=0, tiled=True),
    )
    enc_term = jnp.einsum(
        "nd,wd->nw", key_grad_rows, key_weight, preferred_element_type=jnp.float32
    ) + jnp.einsum("nd,wd->nw", value_grad_rows, value_weight, preferred_element_type=jnp.float32)
    encoding_grad = lax.psum_scatter(
        enc_term.reshape(block_count, block_len, enc_width), "head", scatter_dimension=1, tiled=True
    )
    return (
        attended.reshape(segments * SEGMENT, head_dim),
        query_grad.reshape(segments * SEGMENT, head_dim),
        encoding_grad,
        key_weight_grad,
        value_weight_grad,
    )


def solution(mesh):
    in_specs = (
        P("seq", "head"),
        P("seq", None, None),
        P(None, "head"),
        P(None, "head"),
        P(),
        P("seq", "head"),
    )
    out_specs = (
        P("seq", "head"),
        P("seq", "head"),
        P("seq", "head", None),
        P("seq", "head"),
        P("seq", "head"),
    )
    return jax.shard_map(
        on_device, mesh=mesh, in_specs=in_specs, out_specs=out_specs, check_vma=False
    )
```

profile of v0, /device:TPU:1, one launch (start us, length us, event | category | flops | bytes accessed | tf_op | source)
XLA Modules:
  0.0 387.3 jit_solution(13494664901466757000)
XLA Ops:
  8.0 0.8 broadcast_divide_fusion.1
  8.9 0.7 sign_compare_fusion
  10.6 1.5 convolution_convert_fusion.4
  13.1 0.8 convert_reduce_fusion
  14.0 1.2 convolution_convert_fusion
  15.2 3.1 copy.36
  18.3 11.3 %all-to-all-start = ((bf16[64,128,256]{2,1,0:T(8,128)(2,1)}), bf16[64,128,256]{2,1,0:T(8,128)(2,1)}, u32[]{:S(2)}, u32[]{:S(2)}) async-start(bf16[64,128,256]{2,1,0:T(8,128)(2,1)} %bitcast.61), calls=%async_computation | async-start | bytes 8388608 | tf_op jit(solution)/shard_map/all_to_all | solution.py:66
  29.7 50.3 %all-to-all-done = bf16[64,128,256]{2,1,0:T(8,128)(2,1)} async-done(((bf16[64,128,256]{2,1,0:T(8,128)(2,1)}), bf16[64,128,256]{2,1,0:T(8,128)(2,1)}, u32[]{:S(2)}, u32[]{:S(2)}) %all-to-all-start) | async-done | bytes 4194336 | tf_op jit(solution)/shard_map/all_to_all | solution.py:66
  80.0 4.2 %gather_fusion = bf16[32,128,256]{2,1,0:T(8,128)(2,1)} fusion(bf16[64,128,256]{2,1,0:T(8,128)(2,1)} %all-to-all-done, s32[1024]{0:T(1024)S(1)} %pad_clamp_fusion), kind=kCustom, calls=%fused_computation | custom fusion | bytes 4194432 | tf_op jit(solution)/shard_map/gather | solution.py:67
  84.2 1.9 fusion.7
  86.1 1.2 fusion.39
  87.3 1.5 convolution_bitcast_fusion
  88.8 3.4 fusion.20
  92.2 9.3 %fusion.9 = f32[16,256,128]{1,2,0:T(8,128)} fusion(bf16[16,64,128]{2,1,0:T(8,128)(2,1)} %bitcast.75, f32[16,64,256]{2,1,0:T(8,128)} %convolution_bitcast_fusion, f32[16,64,256]{2,1,0:T(8,128)} %get-tuple-element.34, f32[16,64]{1,0:T(8,128)S(1)} %get-tuple-element.33), kind=kOutput, calls=%fused_computation.23 | convolution fusion | flops 68945152 | bytes 4460544 | tf_op jit(solution)/shard_map/cqk,cqd->ckd/dot_general | solution.py:88
  101.5 4.5 %pad_maximum_fusion = f32[16,256,256]{1,2,0:T(8,128)} fusion(f32[16,256,128]{1,2,0:T(8,128)} %fusion.20, f32[16,256,128]{1,2,0:T(8,128)} %fusion.9), kind=kLoop, calls=%fused_computation.6 | loop fusion | flops 1048576 | bytes 8388608 | tf_op jit(solution)/shard_map/concatenate | solution.py:91
  106.1 5.3 %copy.28 = f32[16,256,256]{2,1,0:T(8,128)} copy(f32[16,256,256]{1,2,0:T(8,128)} %pad_maximum_fusion) | data formatting | bytes 8388608 | tf_op jit(solution)/shard_map/concatenate | solution.py:91
  111.4 4.2 %broadcast_in_dim.2 = f32[64,128,256]{2,1,0:T(8,128)} broadcast(f32[]{:T(128)} %constant.46.clone.1), dimensions={} | broadcast | bytes 8388612 | tf_op jit(solution)/shard_map/broadcast_in_dim | solution.py:95
  115.6 8.3 %scatter_fusion = f32[64,128,256]{2,1,0:T(8,128)} fusion(f32[64,128,256]{2,1,0:T(8,128)} %broadcast_in_dim.2, s32[32]{0:T(128)S(1)} %fusion.33, f32[32,128,256]{2,1,0:T(8,128)} %bitcast.62), kind=kCustom, calls=%fused_computation.1 | custom fusion | bytes 12583040 | tf_op jit(solution)/shard_map/scatter | solution.py:95
  124.0 103.2 %all_to_all.10 = f32[64,128,256]{2,1,0:T(8,128)S(1)} all-to-all(f32[64,128,256]{2,1,0:T(8,128)} %scatter_fusion), channel_id=1, replica_groups=mesh['seq'=32,'head'=16] {'seq'}, dimensions={0} | all-to-all | bytes 16777216 | tf_op jit(solution)/shard_map/all_to_all | solution.py:97
  227.1 4.7 %copy.37 = f32[8,8,128,256]{3,1,2,0:T(8,128)S(1)} copy(f32[8,8,128,256]{3,2,1,0:T(8,128)S(1)} %bitcast.60) | data formatting | bytes 16777216
  231.9 4.8 %convolution_convert_fusion.1 = bf16[7,32768]{1,0:T(8,128)(2,1)} fusion(f32[64,7]{1,0:T(8,128)S(1)} %bitcast.76, f32[64,32768]{1,0:T(8,128)S(1)} %bitcast.59), kind=kOutput, calls=%fused_computation.5 | convolution fusion | flops 176390144 | bytes 8849152 | tf_op jit(solution)/shard_map/dot_general | solution.py:99
  236.7 1.7 reshape.178
  238.5 1.2 convolution_bitcast_fusion.2
  239.7 1.2 convolution_bitcast_fusion.1
  242.2 2.3 convolution_add_fusion
  244.5 1.3 dynamic-slice
  246.4 3.8 convolution_convert_fusion.3
  250.2 8.6 %convolution_convert_fusion.2 = bf16[16,64,128]{2,1,0:T(8,128)(2,1)} fusion(f32[16,64,256]{2,1,0:T(8,128)} %convolution_bitcast_fusion, bf16[16,256,256]{2,1,0:T(8,128)(2,1)} %bitcast.67, f32[16,64,256]{2,1,0:T(8,128)} %get-tuple-element.34, f32[16,64]{1,0:T(8,128)S(1)} %get-tuple-element.33), kind=kOutput, calls=%fused_computation.19 | convolution fusion | flops 69076224 | bytes 5521408 | tf_op jit(solution)/shard_map/cqk,ckd->cqd/dot_general | solution.py:85
  258.8 117.7 %all-reduce.5.cloned.1.call-done = (f32[896,128]{0,1:T(8,128)}, f32[896,128]{0,1:T(8,128)}) async-done(((f32[896,128]{0,1:T(8,128)}, f32[896,128]{0,1:T(8,128)}), (f32[896,128]{0,1:T(8,128)}, f32[896,128]{0,1:T(8,128)})) %all-reduce.5.cloned.1.call-update) | async-done | bytes 917520
  376.5 1.0 constant_dynamic-slice_fusion.1
  377.4 0.7 copy.29
  378.1 1.0 constant_dynamic-slice_fusion
  (31 shorter events, 4.1 us)
Async XLA Ops:
  8.0 2.6 copy-start
  8.0 4.1 %copy-start.2 = (bf16[896,128]{1,0:T(8,128)(2,1)S(1)}, bf16[896,128]{1,0:T(8,128)(2,1)}, u32[]{:S(2)}) copy-start(bf16[896,128]{1,0:T(8,128)(2,1)} %param.8) | copy-start | bytes 688132
  18.3 61.7 %all-to-all-start = ((bf16[64,128,256]{2,1,0:T(8,128)(2,1)}), bf16[64,128,256]{2,1,0:T(8,128)(2,1)}, u32[]{:S(2)}, u32[]{:S(2)}) async-start(bf16[64,128,256]{2,1,0:T(8,128)(2,1)} %bitcast.61), calls=%async_computation | async-start | bytes 8388608 | tf_op jit(solution)/shard_map/all_to_all | solution.py:66
  29.6 346.8 %all-reduce.5.cloned.1.call-start = ((), (), s32[]{:S(2)}) async-start(), calls=%async_computation.4 | async-start | bytes 1835008
  84.2 3.1 copy-start.1
  84.2 3.1 copy-start.4
  241.0 138.8 %reduce-scatter.4.cloned.1.call-start = ((), (), s32[]{:S(2)}) async-start(), calls=%async_computation.3 | async-start | bytes 3411968 | tf_op jit(solution)/shard_map/reduce_scatter | solution.py:114
  241.2 0.9 copy-start.3
Sparse Core Ops, SparseCore 0:
  241.1 135.3 all-reduce.4
Sparse Core Ops, SparseCore 1:
  244.9 67.7 reduce-scatter.3
where the time goes:
time: 388 us; the launch traced here: 387 us
  waiting for transfers between devices  168 us (43%)
  blocking collectives  103 us (27%)
  matrix products  42.1 us (11%)
  local copies, waits for them, and re-layouts  37.9 us (10%)
  between operations  16.3 us (4%)
  starting transfers between devices  11.6 us (3%)
  other arithmetic  8.15 us (2%)
    unnamed x3, waiting for transfers between devices  118 us
    all_to_all x1, blocking collectives, on_device(): lax.all_to_all(outgoing, 'seq', split_axis=0, concat_axis=0, tiled=True)  103 us
    all_to_all x1, waiting for transfers between devices, on_device(): lax.all_to_all(kv_slots, 'seq', split_axis=0, concat_axis=0, tiled=True)  50.3 us
    unnamed x18, local copies, waits for them, and re-layouts  13 us
    all_to_all x1, starting transfers between devices, on_device(): lax.all_to_all(kv_slots, 'seq', split_axis=0, concat_axis=0, tiled=True)  11.3 us
    dot_general x1, matrix products, on_device(): jnp.einsum('cqk,cqd->ckd', score_grad, query_segs, preferred_element_type...  9.29 us
    dot_general x1, matrix products, on_device(): jnp.einsum('cqk,ckd->cqd', score_grad, seg_keys, preferred_element_type=j...  8.61 us
    scatter x1, local copies, waits for them, and re-layouts, on_device(): jnp.zeros((slot_count, block_len, 2 * head_dim), jnp.float32).at[my_slots]  8.32 us
  transfers between devices with their start and end apart: 3, of which 2 were waited for; matrix products, arithmetic and copies ran while one was open for 5% of the time, Pallas kernels for 0%

commit v1 on v0

v1 whole, which is shorter than its diff:
```python
import math

import jax
import jax.numpy as jnp
from jax import lax
from jax.experimental import pallas as pl
from jax.experimental.pallas import tpu as pltpu
from jax.sharding import PartitionSpec as P

SEGMENT = 64
NEIGH = 2
CAP = 2
VMEM_LIMIT = 40 * 1024 * 1024
VMEM = pltpu.VMEM
SMEM = pltpu.SMEM


def params():
    return pltpu.CompilerParams(vmem_limit_bytes=VMEM_LIMIT)


def spec(space):
    return pl.BlockSpec(memory_space=space)


def nt_dot(a, b):
    return lax.dot_general(a, b, (((1,), (1,)), ((), ())), preferred_element_type=jnp.float32)


def tn_dot(a, b):
    return lax.dot_general(a, b, (((0,), (0,)), ((), ())), preferred_element_type=jnp.float32)


def nn_dot(a, b):
    return jnp.dot(a, b, preferred_element_type=jnp.float32)


def pack_kernel(block_count, seq_count, read_count, reads_ref, q_ref, g_ref, out_ref, slots_ref, used):
    head_dim = q_ref.shape[2]
    out_ref[...] = jnp.zeros_like(out_ref)

    def clear(h, _):
        used[h] = 0
        return 0

    lax.fori_loop(0, seq_count, clear, 0)

    def place(j, _):
        holder = lax.div(reads_ref[j], block_count)
        rank = used[holder]
        used[holder] = rank + 1
        slot = holder * CAP + rank
        slots_ref[j] = slot
        seg = lax.div(j, NEIGH)
        out_ref[slot, :, :head_dim] = q_ref[seg]
        out_ref[slot, :, head_dim:] = g_ref[seg]
        return 0

    lax.fori_loop(0, read_count, place, 0)


def pair_operands(x, kv_a, kv_b):
    head_dim = x.shape[1] // 2
    first = lax.broadcasted_iota(jnp.int32, (x.shape[0], head_dim), 0) < SEGMENT
    zero = jnp.zeros((x.shape[0], head_dim), x.dtype)
    q, g = x[:, :head_dim], x[:, head_dim:]
    q_diag = jnp.concatenate([jnp.where(first, q, zero), jnp.where(first, zero, q)], axis=1)
    g_diag = jnp.concatenate([jnp.where(first, g, zero), jnp.where(first, zero, g)], axis=1)
    keys = jnp.concatenate([kv_a[:, :head_dim], kv_b[:, :head_dim]], axis=1)
    values = jnp.concatenate([kv_a[:, head_dim:], kv_b[:, head_dim:]], axis=1)
    return q_diag, g_diag, keys, values, first


def stats_kernel(scale, blocks_ref, x_ref, kv_ref, out_ref):
    def step(s, _):
        kv_a = kv_ref[blocks_ref[CAP * s]]
        kv_b = kv_ref[blocks_ref[CAP * s + 1]]
        q_diag, g_diag, keys, values, _ = pair_operands(x_ref[s], kv_a, kv_b)
        scores = nt_dot(keys, q_diag) * scale
        top = jnp.max(scores, axis=0, keepdims=True)
        weight = jnp.exp(scores - top)
        total = jnp.sum(weight, axis=0, keepdims=True)
        prob_grad = nt_dot(values, g_diag)
        mean = jnp.sum(weight * prob_grad, axis=0, keepdims=True) / total
        both = jnp.concatenate([top + jnp.log(total), mean], axis=0)
        out_ref[CAP * s] = both
        out_ref[CAP * s + 1] = pltpu.roll(both, SEGMENT, 1)
        return 0

    lax.fori_loop(0, x_ref.shape[0], step, 0, unroll=2)


def merge_kernel(slots_ref, in_ref, out_ref):
    out_ref[...] = jnp.zeros_like(out_ref)
    for c in range(slots_ref.shape[0] // NEIGH):
        slot_a, slot_b = slots_ref[NEIGH * c], slots_ref[NEIGH * c + 1]
        one, two = in_ref[slot_a], in_ref[slot_b]
        lse_a, lse_b = one[0:1], two[0:1]
        top = jnp.maximum(lse_a, lse_b)
        lse = top + jnp.log(jnp.exp(lse_a - top) + jnp.exp(lse_b - top))
        delta = jnp.exp(lse_a - lse) * one[1:2] + jnp.exp(lse_b - lse) * two[1:2]
        both = jnp.concatenate([lse, delta], axis=0)
        out_ref[slot_a] = both
        out_ref[slot_b] = both


def grads_kernel(scale, blocks_ref, x_ref, kv_ref, stats_ref, enc_t_ref, out_ref, rows_ref, acc_k, acc_v):
    head_dim = kv_ref.shape[2] // 2
    pair = x_ref.shape[1]
    acc_k[...] = jnp.zeros_like(acc_k)
    acc_v[...] = jnp.zeros_like(acc_v)

    def step(s, _):
        block_a = blocks_ref[CAP * s]
        block_b = blocks_ref[CAP * s + 1]
        q_diag, g_diag, keys, values, first = pair_operands(x_ref[s], kv_ref[block_a], kv_ref[block_b])
        left = lax.broadcasted_iota(jnp.int32, (2, pair), 1) < SEGMENT
        both = jnp.where(left, stats_ref[CAP * s], pltpu.roll(stats_ref[CAP * s + 1], SEGMENT, 1))
        scores = nt_dot(keys, q_diag) * scale
        probs = jnp.exp(scores - both[0:1])
        prob_grad = nt_dot(values, g_diag)
        score_grad = (probs * (prob_grad - both[1:2]) * scale).astype(jnp.bfloat16)
        probs = probs.astype(jnp.bfloat16)
        attended = tn_dot(probs, values)
        query_grad = tn_dot(score_grad, keys)
        out_ref[s, :pair, :head_dim] = jnp.where(
            first, attended[:, :head_dim], attended[:, head_dim:]
        ).astype(jnp.bfloat16)
        out_ref[s, :pair, head_dim:] = jnp.where(
            first, query_grad[:, :head_dim], query_grad[:, head_dim:]
        ).astype(jnp.bfloat16)
        value_part = nn_dot(probs, g_diag)
        key_part = nn_dot(score_grad, q_diag)
        acc_k[block_a] += key_part[:, :head_dim]
        acc_v[block_a] += value_part[:, :head_dim]
        acc_k[block_b] += key_part[:, head_dim:]
        acc_v[block_b] += value_part[:, head_dim:]
        return 0

    lax.fori_loop(0, x_ref.shape[0], step, 0, unroll=2)
    rows_ref[:, :, :head_dim] = acc_k[...].astype(jnp.bfloat16)
    rows_ref[:, :, head_dim:] = acc_v[...].astype(jnp.bfloat16)
    rows = rows_ref[...].reshape(-1, 2 * head_dim)
    share = enc_t_ref.shape[0] // x_ref.shape[0]
    pad = out_ref.shape[1] - pair - share
    group = 4
    for s in range(0, x_ref.shape[0], group):
        term = nn_dot(enc_t_ref[s * share:(s + group) * share], rows).reshape(group, share, 2 * head_dim)
        if pad:
            term = jnp.concatenate([term, jnp.zeros((group, pad, 2 * head_dim), jnp.float32)], axis=1)
        out_ref[s:s + group, pair:] = term.astype(jnp.bfloat16)


def finish_kernel(slots_ref, in_ref, att_ref, qg_ref, kw_ref, vw_ref):
    head_dim = att_ref.shape[2]
    share = kw_ref.shape[0]
    pair = CAP * SEGMENT

    def step(c, _):
        slot_a, slot_b = slots_ref[NEIGH * c], slots_ref[NEIGH * c + 1]

        def part(slot):
            holder = lax.div(slot, CAP)
            row = pl.multiple_of((slot - holder * CAP) * SEGMENT, SEGMENT)
            return in_ref[holder, pl.ds(row, SEGMENT), :].astype(jnp.float32)

        total = (part(slot_a) + part(slot_b)).astype(jnp.bfloat16)
        att_ref[c] = total[:, :head_dim]
        qg_ref[c] = total[:, head_dim:]
        return 0

    lax.fori_loop(0, att_ref.shape[0], step, 0, unroll=2)
    total = in_ref[0, pair:, :].astype(jnp.float32)
    for s in range(1, in_ref.shape[0]):
        total = total + in_ref[s, pair:, :].astype(jnp.float32)
    kw_ref[...] = total[:share, :head_dim]
    vw_ref[...] = total[:share, head_dim:]


def project_kernel(rows_ref, weights_ref, out_ref):
    @pl.when(pl.program_id(0) == 0)
    def _():
        out_ref[...] = jnp.zeros_like(out_ref)

    out_ref[...] += nt_dot(rows_ref[0], weights_ref[0])


def on_device(queries, encodings, key_weight, value_weight, reads, out_grad):
    seq_count = lax.axis_size("seq")
    head_count = lax.axis_size("head")
    me = lax.axis_index("seq")
    block_count, block_len, enc_width = encodings.shape
    head_dim = key_weight.shape[1]
    segments = queries.shape[0] // SEGMENT
    read_count = NEIGH * segments
    slot_count = seq_count * CAP
    scale = 1.0 / math.sqrt(head_dim)
    bf16, f32 = jnp.bfloat16, jnp.float32

    tables = reads.reshape(seq_count, read_count)
    my_reads = lax.dynamic_index_in_dim(tables, me, 0, keepdims=False)
    packed, slots = pl.pallas_call(
        lambda *refs: pack_kernel(block_count, seq_count, read_count, *refs),
        out_shape=(
            jax.ShapeDtypeStruct((slot_count, SEGMENT, 2 * head_dim), bf16),
            jax.ShapeDtypeStruct((read_count,), jnp.int32),
        ),
        in_specs=[spec(SMEM), spec(VMEM), spec(VMEM)],
        out_specs=(spec(VMEM), spec(SMEM)),
        scratch_shapes=[pltpu.SMEM((seq_count,), jnp.int32)],
        compiler_params=params(),
        name="pack",
    )(
        my_reads,
        queries.reshape(segments, SEGMENT, head_dim),
        out_grad.reshape(segments, SEGMENT, head_dim),
    )
    arrived = lax.all_to_all(packed, "seq", split_axis=0, concat_axis=0, tiled=True)
    pairs = arrived.reshape(seq_count, CAP * SEGMENT, 2 * head_dim)

    weights = jnp.concatenate([key_weight, value_weight], axis=1)
    all_weights = lax.all_gather(weights, "head", axis=0, tiled=False)
    flat_enc = encodings.reshape(block_count * block_len, enc_width)
    kv = jnp.dot(flat_enc, weights, preferred_element_type=f32).astype(bf16)
    kv = kv.reshape(block_count, block_len, 2 * head_dim)
    enc_t = flat_enc.T

    mine = (tables // block_count) == me
    rank = jnp.cumsum(mine.astype(jnp.int32), axis=1)
    blocks = jnp.stack(
        [
            jnp.sum(jnp.where(mine & (rank == k + 1), tables % block_count, 0), axis=1)
            for k in range(CAP)
        ],
        axis=1,
    ).reshape(slot_count)

    stats = pl.pallas_call(
        lambda *refs: stats_kernel(scale, *refs),
        out_shape=jax.ShapeDtypeStruct((slot_count, 2, CAP * SEGMENT), f32),
        in_specs=[spec(SMEM), spec(VMEM), spec(VMEM)],
        out_specs=spec(VMEM),
        compiler_params=params(),
        name="stats",
    )(blocks, pairs, kv)
    stats = lax.all_to_all(stats, "seq", split_axis=0, concat_axis=0, tiled=True)
    merged = pl.pallas_call(
        merge_kernel,
        out_shape=jax.ShapeDtypeStruct(stats.shape, f32),
        in_specs=[spec(SMEM), spec(VMEM)],
        out_specs=spec(VMEM),
        compiler_params=params(),
        name="merge",
    )(slots, stats)
    merged = lax.all_to_all(merged, "seq", split_axis=0, concat_axis=0, tiled=True)

    share = enc_width // seq_count
    room = -(-share // 16) * 16
    back, grad_rows = pl.pallas_call(
        lambda *refs: grads_kernel(scale, *refs),
        out_shape=(
            jax.ShapeDtypeStruct((seq_count, CAP * SEGMENT + room, 2 * head_dim), bf16),
            jax.ShapeDtypeStruct((block_count, block_len, 2 * head_dim), bf16),
        ),
        in_specs=[spec(SMEM), spec(VMEM), spec(VMEM), spec(VMEM), spec(VMEM)],
        out_specs=(spec(VMEM), spec(VMEM)),
        scratch_shapes=[
            pltpu.VMEM((block_count, block_len, head_dim), f32),
            pltpu.VMEM((block_count, block_len, head_dim), f32),
        ],
        compiler_params=params(),
        name="grads",
    )(blocks, pairs, kv, merged, enc_t)

    row_share = block_len // head_count
    by_row = grad_rows.reshape(block_count, head_count, row_share, 2 * head_dim)
    by_row = by_row.transpose(1, 0, 2, 3).reshape(head_count, block_count * row_share, 2 * head_dim)
    row_parts = lax.all_to_all(by_row, "head", split_axis=0, concat_axis=0, tiled=True)
    encoding_grad = pl.pallas_call(
        project_kernel,
        grid=(head_count,),
        out_shape=jax.ShapeDtypeStruct((block_count * row_share, enc_width), f32),
        in_specs=[
            pl.BlockSpec((1, block_count * row_share, 2 * head_dim), lambda h: (h, 0, 0)),
            pl.BlockSpec((1, enc_width, 2 * head_dim), lambda h: (h, 0, 0)),
        ],
        out_specs=pl.BlockSpec((block_count * row_share, enc_width), lambda h: (0, 0)),
        compiler_params=params(),
        name="project",
    )(row_parts, all_weights)

    returned = lax.all_to_all(back, "seq", split_axis=0, concat_axis=0, tiled=True)
    attended, query_grad, key_weight_grad, value_weight_grad = pl.pallas_call(
        finish_kernel,
        out_shape=(
            jax.ShapeDtypeStruct((segments, SEGMENT, head_dim), bf16),
            jax.ShapeDtypeStruct((segments, SEGMENT, head_dim), bf16),
            jax.ShapeDtypeStruct((share, head_dim), f32),
            jax.ShapeDtypeStruct((share, head_dim), f32),
        ),
        in_specs=[spec(SMEM), spec(VMEM)],
        out_specs=(spec(VMEM),) * 4,
        compiler_params=params(),
        name="finish",
    )(slots, returned)
    return (
        attended.reshape(segments * SEGMENT, head_dim),
        query_grad.reshape(segments * SEGMENT, head_dim),
        encoding_grad.reshape(block_count, row_share, enc_width),
        key_weight_grad,
        value_weight_grad,
    )


def solution(mesh):
    in_specs = (
        P("seq", "head"),
        P("seq", None, None),
        P(None, "head"),
        P(None, "head"),
        P(),
        P("seq", "head"),
    )
    out_specs = (
        P("seq", "head"),
        P("seq", "head"),
        P("seq", "head", None),
        P("seq", "head"),
        P("seq", "head"),
    )
    return jax.shard_map(
        on_device, mesh=mesh, in_specs=in_specs, out_specs=out_specs, check_vma=False
    )
```

time: 388 us -> 193 us (0.50)
  the two profiles are of different devices: /device:TPU:1 before, /device:TPU:16 now
where the time goes in v1:
time: 193 us; the launch traced here: 192 us
  waiting for transfers between devices  83.4 us (43%)
  starting transfers between devices  34.7 us (18%)
  Pallas kernels  29.7 us (15%)
  local copies, waits for them, and re-layouts  16.9 us (9%)
  between operations  14.2 us (7%)
  blocking collectives  10.8 us (6%)
  matrix products  2.19 us (1%)
    all_to_all x1, waiting for transfers between devices, on_device(): lax.all_to_all(back, 'seq', split_axis=0, concat_axis=0, tiled=True)  32.7 us
    all_to_all x1, waiting for transfers between devices, on_device(): lax.all_to_all(by_row, 'head', split_axis=0, concat_axis=0, tiled=True)  25.3 us
    all_to_all x1, waiting for transfers between devices, on_device(): lax.all_to_all(packed, 'seq', split_axis=0, concat_axis=0, tiled=True)  23.5 us
    pallas_call x1, Pallas kernels, on_device(): pl.pallas_call(lambda *refs: grads_kernel(scale, *refs), out_shape=(jax.S...  13.2 us
    all_to_all x1, starting transfers between devices, on_device(): lax.all_to_all(by_row, 'head', split_axis=0, concat_axis=0, tiled=True)  13.1 us
    all_to_all x1, blocking collectives, on_device(): lax.all_to_all(stats, 'seq', split_axis=0, concat_axis=0, tiled=True)  10.8 us
    unnamed x20, local copies, waits for them, and re-layouts  10.1 us
    all_to_all x1, starting transfers between devices, on_device(): lax.all_to_all(packed, 'seq', split_axis=0, concat_axis=0, tiled=True)  9.61 us
  transfers between devices with their start and end apart: 5, of which 4 were waited for; matrix products, arithmetic and copies ran while one was open for 5% of the time, Pallas kernels for 13%

profile of v1, /device:TPU:16, one launch (start us, length us, event | category | flops | bytes accessed | tf_op | source)
XLA Modules:
  0.0 192.4 jit_solution(5669676107764876996)
XLA Ops:
  7.2 1.0 constant_dynamic-update-slice_fusion.1
  8.3 1.0 constant_dynamic-update-slice_fusion
  9.3 0.8 copy-done.6
  10.1 0.8 copy.29
  10.9 0.1 reshape.54
  11.1 2.1 %pack.1 = (bf16[64,64,256]{2,1,0:T(8,128)(2,1)S(1)}, s32[32]{0:T(128)S(1)}) custom-call(s32[32]{0:T(128)S(1)} %dynamic-slice_bitcast_fusion.refs_0_, bf16[16,64,128]{2,1,0:T(8,128)(2,1)S(1)} %bitcast.31, bf16[16,64,128]{2,1,0:T(8,128)(2,1)S(1)} %bitcast.32), custom_call_target="tpu_custom_call" | custom-call | tf_op jit(solution)/shard_map/pack/pallas_call | solution.py:202
  13.2 1.4 copy-done.3
  14.6 9.6 %all-to-all-start = ((bf16[64,64,256]{2,1,0:T(8,128)(2,1)}), bf16[64,64,256]{2,1,0:T(8,128)(2,1)S(1)}, u32[]{:S(2)}, u32[]{:S(2)}) async-start(bf16[64,64,256]{2,1,0:T(8,128)(2,1)} %copy-done.3), calls=%async_computation | async-start | bytes 4194304 | tf_op jit(solution)/shard_map/all_to_all | solution.py:218
  24.2 0.2 reduce_window_sum.11
  24.4 0.2 eq.38
  24.6 0.1 copy.30
  24.8 0.2 eq.41
  25.8 2.2 %fusion = bf16[896,256]{0,1:T(8,128)(2,1)S(1)} fusion(bf16[896,256]{1,0:T(8,128)(2,1)S(1)} %copy-done.7, bf16[896,896]{1,0:T(8,128)(2,1)} %bitcast.33), kind=kOutput, calls=%fused_computation.1 | convolution fusion | flops 411271168 | bytes 2523136 | tf_op jit(solution)/shard_map/dot_general | solution.py:224
  28.0 0.2 copy.33
  28.2 23.5 %all-to-all-done = bf16[64,64,256]{2,1,0:T(8,128)(2,1)S(1)} async-done(((bf16[64,64,256]{2,1,0:T(8,128)(2,1)}), bf16[64,64,256]{2,1,0:T(8,128)(2,1)S(1)}, u32[]{:S(2)}, u32[]{:S(2)}) %all-to-all-start) | async-done | bytes 2097184 | tf_op jit(solution)/shard_map/all_to_all | solution.py:218
  51.8 6.2 %stats.1 = f32[64,2,128]{2,1,0:T(2,128)S(1)} custom-call(s32[64]{0:T(128)S(1)} %reshape.57.refs_0_, bf16[32,128,256]{2,1,0:T(8,128)(2,1)S(1)} %bitcast.25, bf16[7,128,256]{2,1,0:T(8,128)(2,1)S(1)} %bitcast.29), custom_call_target="tpu_custom_call" | custom-call | tf_op jit(solution)/shard_map/stats/pallas_call | solution.py:238
  57.9 10.8 %all_to_all.25.in_ref = f32[64,2,128]{2,1,0:T(2,128)S(1)} all-to-all(f32[64,2,128]{2,1,0:T(2,128)S(1)} %stats.1), channel_id=1, replica_groups=mesh['seq'=32,'head'=16] {'seq'}, dimensions={0} | all-to-all | bytes 131072 | tf_op jit(solution)/shard_map/all_to_all | solution.py:246
  68.8 1.3 merge.1
  70.0 5.9 %all-to-all-start.2 = ((f32[64,2,128]{2,1,0:T(2,128)}), f32[64,2,128]{2,1,0:T(2,128)S(1)}, u32[]{:S(2)}, u32[]{:S(2)}) async-start(f32[64,2,128]{2,1,0:T(2,128)} %merge.1), calls=%async_computation.2 | async-start | bytes 131072 | tf_op jit(solution)/shard_map/all_to_all | solution.py:255
  75.9 3.6 %copy.34 = bf16[896,896]{0,1:T(8,128)(2,1)} copy(bf16[896,896]{1,0:T(8,128)(2,1)} %bitcast.34) | data formatting | bytes 3211264 | tf_op jit(solution)/shard_map/reshape | solution.py:223
  79.5 1.8 all-to-all-done.2.refs_3_
  81.4 1.4 copy-done.1
  82.8 13.2 %grads.1 = (bf16[32,160,256]{2,1,0:T(8,128)(2,1)S(1)}, bf16[7,128,256]{2,1,0:T(8,128)(2,1)S(1)}) custom-call(s32[64]{0:T(128)S(1)} %reshape.57.refs_0_, bf16[32,128,256]{2,1,0:T(8,128)(2,1)S(1)} %bitcast.26, bf16[7,128,256]{2,1,0:T(8,128)(2,1)S(1)} %bitcast.30, f32[64,2,128]{2,1,0:T(2,128)S(1)} %all-to-all-done.2.refs_3_, bf16[896,896]{1,0:T(8,128)(2,1)S(1)} %bitcast.28), custom_call_target="tpu_custom_call" | custom-call | tf_op jit(solution)/shard_map/grads/pallas_call | solution.py:259
  96.1 1.5 copy-done.2
  97.6 6.1 %all-to-all-start.3 = ((bf16[32,160,256]{2,1,0:T(8,128)(2,1)}), bf16[32,160,256]{2,1,0:T(8,128)(2,1)S(1)}, u32[]{:S(2)}, u32[]{:S(2)}) async-start(bf16[32,160,256]{2,1,0:T(8,128)(2,1)} %copy-done.2), calls=%async_computation.3 | async-start | bytes 5242880 | tf_op jit(solution)/shard_map/all_to_all | solution.py:292
  103.7 0.8 copy_bitcast_fusion
  104.5 32.7 %all-to-all-done.3.in_ref = bf16[32,160,256]{2,1,0:T(8,128)(2,1)S(1)} async-done(((bf16[32,160,256]{2,1,0:T(8,128)(2,1)}), bf16[32,160,256]{2,1,0:T(8,128)(2,1)S(1)}, u32[]{:S(2)}, u32[]{:S(2)}) %all-to-all-start.3) | async-done | bytes 2621472 | tf_op jit(solution)/shard_map/all_to_all | solution.py:292
  137.2 13.1 %all-to-all-start.4 = ((bf16[16,56,256]{2,1,0:T(8,128)(2,1)}), bf16[16,56,256]{2,1,0:T(8,128)(2,1)S(1)}, u32[]{:S(2)}, u32[]{:S(2)}) async-start(bf16[16,56,256]{2,1,0:T(8,128)(2,1)} %copy_bitcast_fusion), calls=%async_computation.4 | async-start | bytes 917504 | tf_op jit(solution)/shard_map/all_to_all | solution.py:278
  150.3 1.6 finish.1
  152.0 25.3 %all-to-all-done.4.rows_ref = bf16[16,56,256]{2,1,0:T(8,128)(2,1)S(1)} async-done(((bf16[16,56,256]{2,1,0:T(8,128)(2,1)}), bf16[16,56,256]{2,1,0:T(8,128)(2,1)S(1)}, u32[]{:S(2)}, u32[]{:S(2)}) %all-to-all-start.4) | async-done | bytes 458784 | tf_op jit(solution)/shard_map/all_to_all | solution.py:278
  177.2 3.1 %copy-done = bf16[14336,256]{1,0:T(8,128)(2,1)S(1)} copy-done((bf16[14336,256]{1,0:T(8,128)(2,1)S(1)}, bf16[14336,256]{1,0:T(8,128)(2,1)}, u32[]{:S(2)}) %copy-start) | copy-done | bytes 7340056
  180.3 5.3 %project.1 = f32[56,896]{1,0:T(8,128)} custom-call(bf16[16,56,256]{2,1,0:T(8,128)(2,1)S(1)} %all-to-all-done.4.rows_ref, bf16[16,896,256]{2,1,0:T(8,128)(2,1)S(1)} %bitcast.27), custom_call_target="tpu_custom_call" | custom-call | tf_op jit(solution)/shard_map/project/pallas_call | solution.py:279
  (28 shorter events, 0.9 us)
Async XLA Ops:
  7.2 3.9 %copy-start.4 = (bf16[1024,128]{1,0:T(8,128)(2,1)S(1)}, bf16[1024,128]{1,0:T(8,128)(2,1)}, u32[]{:S(2)}) copy-start(bf16[1024,128]{1,0:T(8,128)(2,1)} %param.6) | copy-start | bytes 786436
  7.2 3.9 %copy-start.5 = (bf16[1024,128]{1,0:T(8,128)(2,1)S(1)}, bf16[1024,128]{1,0:T(8,128)(2,1)}, u32[]{:S(2)}) copy-start(bf16[1024,128]{1,0:T(8,128)(2,1)} %param.11) | copy-start | bytes 786436
  7.2 170.1 %all-gather.3.cloned.1.call-start = ((), (), s32[]{:S(2)}) async-start(), calls=%async_computation.5 | async-start | bytes 7798784 | tf_op jit(solution)/shard_map/all_gather | solution.py:222
  9.3 0.8 copy-start.6
  13.2 1.4 copy-start.3
  14.6 10.5 %copy-start.8 = (s32[512,2]{0,1:T(2,128)S(1)}, s32[512,2]{0,1:T(2,128)}, u32[]{:S(2)}) copy-start(s32[512,2]{0,1:T(2,128)} %param.10) | copy-start | bytes 12292
  14.6 11.2 %copy-start.7 = (bf16[896,256]{1,0:T(8,128)(2,1)S(1)}, bf16[896,256]{1,0:T(8,128)(2,1)}, u32[]{:S(2)}) copy-start(bf16[896,256]{1,0:T(8,128)(2,1)} %copy-done.6) | copy-start | bytes 1376260
  14.6 37.2 %all-to-all-start = ((bf16[64,64,256]{2,1,0:T(8,128)(2,1)}), bf16[64,64,256]{2,1,0:T(8,128)(2,1)S(1)}, u32[]{:S(2)}, u32[]{:S(2)}) async-start(bf16[64,64,256]{2,1,0:T(8,128)(2,1)} %copy-done.3), calls=%async_computation | async-start | bytes 4194304 | tf_op jit(solution)/shard_map/all_to_all | solution.py:218
  70.0 11.3 %all-to-all-start.2 = ((f32[64,2,128]{2,1,0:T(2,128)}), f32[64,2,128]{2,1,0:T(2,128)S(1)}, u32[]{:S(2)}, u32[]{:S(2)}) async-start(f32[64,2,128]{2,1,0:T(2,128)} %merge.1), calls=%async_computation.2 | async-start | bytes 131072 | tf_op jit(solution)/shard_map/all_to_all | solution.py:255
  81.4 1.5 copy-start.1
  96.1 1.5 copy-start.2
  97.6 39.6 %all-to-all-start.3 = ((bf16[32,160,256]{2,1,0:T(8,128)(2,1)}), bf16[32,160,256]{2,1,0:T(8,128)(2,1)S(1)}, u32[]{:S(2)}, u32[]{:S(2)}) async-start(bf16[32,160,256]{2,1,0:T(8,128)(2,1)} %copy-done.2), calls=%async_computation.3 | async-start | bytes 5242880 | tf_op jit(solution)/shard_map/all_to_all | solution.py:292
  137.2 40.0 %all-to-all-start.4 = ((bf16[16,56,256]{2,1,0:T(8,128)(2,1)}), bf16[16,56,256]{2,1,0:T(8,128)(2,1)S(1)}, u32[]{:S(2)}, u32[]{:S(2)}) async-start(bf16[16,56,256]{2,1,0:T(8,128)(2,1)} %copy_bitcast_fusion), calls=%async_computation.4 | async-start | bytes 917504 | tf_op jit(solution)/shard_map/all_to_all | solution.py:278
  177.2 3.1 %copy-start = (bf16[14336,256]{1,0:T(8,128)(2,1)S(1)}, bf16[14336,256]{1,0:T(8,128)(2,1)}, u32[]{:S(2)}) copy-start(bf16[14336,256]{1,0:T(8,128)(2,1)} %all-gather.3.cloned.1.call-done) | copy-start | bytes 22020100
Sparse Core Ops, SparseCore 0:
  10.2 99.6 all-gather.2

commit v2 on v1

v2 whole, which is shorter than its diff:
```python
import math

import jax
import jax.numpy as jnp
from jax import lax
from jax.experimental import pallas as pl
from jax.experimental.pallas import tpu as pltpu
from jax.sharding import PartitionSpec as P

SEGMENT = 64
NEIGH = 2
CAP = 2
STEPS_NEAR = (0, 1, -1, 2)
STEPS_FAR = (0, 4, -4, 8)
VMEM_LIMIT = 40 * 1024 * 1024
VMEM = pltpu.VMEM
SMEM = pltpu.SMEM


def params():
    return pltpu.CompilerParams(vmem_limit_bytes=VMEM_LIMIT)


def spec(space):
    return pl.BlockSpec(memory_space=space)


def nt_dot(a, b):
    return lax.dot_general(a, b, (((1,), (1,)), ((), ())), preferred_element_type=jnp.float32)


def tn_dot(a, b):
    return lax.dot_general(a, b, (((0,), (0,)), ((), ())), preferred_element_type=jnp.float32)


def nn_dot(a, b):
    return jnp.dot(a, b, preferred_element_type=jnp.float32)


def pack_kernel(block_count, reads_ref, q_ref, g_ref, out_ref, slots_ref, used, zeros, copied, cleared):
    seq_count = used.shape[0]
    read_count = slots_ref.shape[0]
    zeros[...] = jnp.zeros_like(zeros)

    def clear(h, _):
        used[h] = 0
        return 0

    lax.fori_loop(0, seq_count, clear, 0)

    def copies(j, slot):
        seg = lax.div(j, NEIGH)
        return (
            pltpu.make_async_copy(q_ref.at[seg], out_ref.at[slot, 0], copied.at[j, 0]),
            pltpu.make_async_copy(g_ref.at[seg], out_ref.at[slot, 1], copied.at[j, 1]),
        )

    def place(j, _):
        holder = lax.div(reads_ref[j], block_count)
        rank = used[holder]
        used[holder] = rank + 1
        slot = holder * CAP + rank
        slots_ref[j] = slot
        for copy in copies(j, slot):
            copy.start()
        return 0

    lax.fori_loop(0, read_count, place, 0)

    def blank(slot):
        return pltpu.make_async_copy(zeros, out_ref.at[slot], cleared.at[slot])

    def wipe(slot, finish):
        holder = lax.div(slot, CAP)

        @pl.when(slot - holder * CAP >= used[holder])
        def _():
            if finish:
                blank(slot).wait()
            else:
                blank(slot).start()

    def wipe_start(slot, _):
        wipe(slot, False)
        return 0

    def wipe_wait(slot, _):
        wipe(slot, True)
        return 0

    def arrive(j, _):
        for copy in copies(j, slots_ref[j]):
            copy.wait()
        return 0

    lax.fori_loop(0, CAP * seq_count, wipe_start, 0)
    lax.fori_loop(0, read_count, arrive, 0)
    lax.fori_loop(0, CAP * seq_count, wipe_wait, 0)


def pair_operands(x_ref, s, kv_a, kv_b):
    head_dim = x_ref.shape[3]

    def diagonal(i):
        one, two = x_ref[CAP * s, i], x_ref[CAP * s + 1, i]
        zero = jnp.zeros_like(one)
        return jnp.concatenate(
            [jnp.concatenate([one, zero], axis=1), jnp.concatenate([zero, two], axis=1)], axis=0
        )

    keys = jnp.concatenate([kv_a[:, :head_dim], kv_b[:, :head_dim]], axis=1)
    values = jnp.concatenate([kv_a[:, head_dim:], kv_b[:, head_dim:]], axis=1)
    return diagonal(0), diagonal(1), keys, values


def stats_kernel(scale, unroll, blocks_ref, x_ref, kv_ref, out_ref):
    def step(s, _):
        kv_a = kv_ref[blocks_ref[CAP * s]]
        kv_b = kv_ref[blocks_ref[CAP * s + 1]]
        q_diag, g_diag, keys, values = pair_operands(x_ref, s, kv_a, kv_b)
        scores = nt_dot(keys, q_diag) * scale
        top = jnp.max(scores, axis=0, keepdims=True)
        weight = jnp.exp(scores - top)
        total = jnp.sum(weight, axis=0, keepdims=True)
        prob_grad = nt_dot(values, g_diag)
        mean = jnp.sum(weight * prob_grad, axis=0, keepdims=True) / total
        both = jnp.concatenate([top + jnp.log(total), mean], axis=0)
        out_ref[CAP * s] = both
        out_ref[CAP * s + 1] = pltpu.roll(both, SEGMENT, 1)
        return 0

    lax.fori_loop(0, x_ref.shape[0] // CAP, step, 0, unroll=unroll)


def merge_kernel(slots_ref, in_ref, out_ref):
    out_ref[...] = jnp.zeros_like(out_ref)
    for c in range(slots_ref.shape[0] // NEIGH):
        slot_a, slot_b = slots_ref[NEIGH * c], slots_ref[NEIGH * c + 1]
        one, two = in_ref[slot_a], in_ref[slot_b]
        lse_a, lse_b = one[0:1], two[0:1]
        top = jnp.maximum(lse_a, lse_b)
        lse = top + jnp.log(jnp.exp(lse_a - top) + jnp.exp(lse_b - top))
        delta = jnp.exp(lse_a - lse) * one[1:2] + jnp.exp(lse_b - lse) * two[1:2]
        both = jnp.concatenate([lse, delta], axis=0)
        out_ref[slot_a] = both
        out_ref[slot_b] = both


def grads_kernel(
    scale, unroll, me_ref, blocks_ref, x_ref, kv_ref, stats_ref, enc_t_ref, *refs
):
    near = len(STEPS_NEAR)
    out_ref = refs[0]
    rows_refs = refs[1:1 + near]
    stage, rows_all, acc_k, acc_v, sems = refs[1 + near:]
    head_dim = kv_ref.shape[2] // 2
    seq_count = x_ref.shape[0] // CAP
    pair = CAP * SEGMENT
    parts = 2 * pair
    acc_k[...] = jnp.zeros_like(acc_k)
    acc_v[...] = jnp.zeros_like(acc_v)

    def leave(s):
        return pltpu.make_async_copy(stage.at[s], out_ref.at[s], sems.at[s])

    def step(s, _):
        block_a = blocks_ref[CAP * s]
        block_b = blocks_ref[CAP * s + 1]
        q_diag, g_diag, keys, values = pair_operands(x_ref, s, kv_ref[block_a], kv_ref[block_b])
        left = lax.broadcasted_iota(jnp.int32, (2, pair), 1) < SEGMENT
        both = jnp.where(left, stats_ref[CAP * s], pltpu.roll(stats_ref[CAP * s + 1], SEGMENT, 1))
        scores = nt_dot(keys, q_diag) * scale
        probs = jnp.exp(scores - both[0:1])
        prob_grad = nt_dot(values, g_diag)
        score_grad = (probs * (prob_grad - both[1:2]) * scale).astype(jnp.bfloat16)
        probs = probs.astype(jnp.bfloat16)
        attended = tn_dot(probs, values).astype(jnp.bfloat16)
        query_grad = tn_dot(score_grad, keys).astype(jnp.bfloat16)
        stage[s, :SEGMENT] = attended[:SEGMENT, :head_dim]
        stage[s, SEGMENT:pair] = query_grad[:SEGMENT, :head_dim]
        stage[s, pair:pair + SEGMENT] = attended[SEGMENT:, head_dim:]
        stage[s, pair + SEGMENT:parts] = query_grad[SEGMENT:, head_dim:]
        value_part = nn_dot(probs, g_diag)
        key_part = nn_dot(score_grad, q_diag)
        acc_k[block_a] += key_part[:, :head_dim]
        acc_v[block_a] += value_part[:, :head_dim]
        acc_k[block_b] += key_part[:, head_dim:]
        acc_v[block_b] += value_part[:, head_dim:]
        return 0

    lax.fori_loop(0, seq_count, step, 0, unroll=unroll)
    head_count = near * len(STEPS_FAR)
    block_count, block_len, _ = acc_k.shape
    row_share = block_len // head_count
    z = me_ref[0]
    for i, a in enumerate(STEPS_NEAR):
        for j, b in enumerate(STEPS_FAR):
            dest = lax.rem(z + (a + b + head_count), head_count)
            at = pl.ds(pl.multiple_of(dest * row_share, row_share), row_share)
            rows = jnp.concatenate([acc_k[:, at, :], acc_v[:, at, :]], axis=2)
            rows_refs[i][j] = rows.reshape(block_count * row_share, 2 * head_dim).astype(jnp.bfloat16)
    rows_all[:, :head_dim] = acc_k[...].reshape(-1, head_dim).astype(jnp.bfloat16)
    rows_all[:, head_dim:] = acc_v[...].reshape(-1, head_dim).astype(jnp.bfloat16)
    room = (stage.shape[1] - parts) // 2
    group = 8

    def weigh(i, _):
        at = pl.multiple_of(i * (group * room), group * room)
        term = nn_dot(enc_t_ref[pl.ds(at, group * room)], rows_all[...]).astype(jnp.bfloat16)
        term = term.reshape(group, room, 2 * head_dim)
        for g in range(group):
            stage[i * group + g, parts:parts + room] = term[g, :, :head_dim]
            stage[i * group + g, parts + room:] = term[g, :, head_dim:]
            leave(i * group + g).start()
        return 0

    lax.fori_loop(0, seq_count // group, weigh, 0)

    def left_all(s, _):
        leave(s).wait()
        return 0

    lax.fori_loop(0, seq_count, left_all, 0)


def finish_kernel(slots_ref, in_ref, att_ref, qg_ref, kw_ref, vw_ref):
    share = kw_ref.shape[0]
    parts = 2 * CAP * SEGMENT
    room = (in_ref.shape[1] - parts) // 2

    def step(c, _):
        slot_a, slot_b = slots_ref[NEIGH * c], slots_ref[NEIGH * c + 1]

        def part(slot):
            holder = lax.div(slot, CAP)
            row = pl.multiple_of((slot - holder * CAP) * 2 * SEGMENT, 2 * SEGMENT)
            return in_ref[holder, pl.ds(row, 2 * SEGMENT), :].astype(jnp.float32)

        total = (part(slot_a) + part(slot_b)).astype(jnp.bfloat16)
        att_ref[c] = total[:SEGMENT]
        qg_ref[c] = total[SEGMENT:]
        return 0

    lax.fori_loop(0, att_ref.shape[0], step, 0, unroll=2)
    total = in_ref[0, parts:, :].astype(jnp.float32)
    for s in range(1, in_ref.shape[0]):
        total = total + in_ref[s, parts:, :].astype(jnp.float32)
    kw_ref[...] = total[:share]
    vw_ref[...] = total[room:room + share]


def project_kernel(*refs):
    near = len(STEPS_NEAR)
    rows_refs, weight_refs, own_ref, far_refs = refs[:near], refs[near:2 * near], refs[2 * near], refs[2 * near + 1:]
    far, rows, width = rows_refs[0].shape
    half = far // 2
    for i in range(0, far, half):
        total = jnp.zeros((half * rows, own_ref.shape[1]), jnp.float32)
        for rows_ref, weight_ref in zip(rows_refs, weight_refs):
            total = total + nt_dot(rows_ref[i:i + half].reshape(half * rows, width), weight_ref[...])
        for j in range(half):
            part = total[j * rows:(j + 1) * rows]
            if i + j == 0:
                own_ref[...] = part
            else:
                far_refs[i + j - 1][...] = part.astype(jnp.bfloat16)


def shifted(x, step, count):
    return lax.ppermute(x, "head", [(z, (z + step) % count) for z in range(count)])


def on_device(queries, encodings, key_weight, value_weight, reads, out_grad):
    seq_count = lax.axis_size("seq")
    head_count = lax.axis_size("head")
    me = lax.axis_index("seq")
    block_count, block_len, enc_width = encodings.shape
    head_dim = key_weight.shape[1]
    segments = queries.shape[0] // SEGMENT
    read_count = NEIGH * segments
    slot_count = seq_count * CAP
    scale = 1.0 / math.sqrt(head_dim)
    bf16, f32 = jnp.bfloat16, jnp.float32

    tables = reads.reshape(seq_count, read_count)
    my_reads = lax.dynamic_index_in_dim(tables, me, 0, keepdims=False)
    packed, slots = pl.pallas_call(
        lambda *refs: pack_kernel(block_count, *refs),
        out_shape=(
            jax.ShapeDtypeStruct((slot_count, 2, SEGMENT, head_dim), bf16),
            jax.ShapeDtypeStruct((read_count,), jnp.int32),
        ),
        in_specs=[spec(SMEM), spec(pl.ANY), spec(pl.ANY)],
        out_specs=(spec(pl.ANY), spec(SMEM)),
        scratch_shapes=[
            pltpu.SMEM((seq_count,), jnp.int32),
            pltpu.VMEM((2, SEGMENT, head_dim), bf16),
            pltpu.SemaphoreType.DMA((read_count, 2)),
            pltpu.SemaphoreType.DMA((slot_count,)),
        ],
        compiler_params=params(),
        name="pack",
    )(
        my_reads,
        queries.reshape(segments, SEGMENT, head_dim),
        out_grad.reshape(segments, SEGMENT, head_dim),
    )
    arrived = lax.all_to_all(packed, "seq", split_axis=0, concat_axis=0, tiled=True)

    weights = jnp.concatenate([key_weight, value_weight], axis=1)
    near_weights = [weights if a == 0 else shifted(weights, a, head_count) for a in STEPS_NEAR]
    flat_enc = encodings.reshape(block_count * block_len, enc_width)
    kv = jnp.dot(flat_enc, weights, preferred_element_type=f32).astype(bf16)
    kv = kv.reshape(block_count, block_len, 2 * head_dim)
    share = enc_width // seq_count
    room = -(-share // 16) * 16
    enc_t = jnp.pad(flat_enc.T.reshape(seq_count, share, -1), ((0, 0), (0, room - share), (0, 0)))
    enc_t = enc_t.reshape(seq_count * room, block_count * block_len)

    mine = (tables // block_count) == me
    rank = jnp.cumsum(mine.astype(jnp.int32), axis=1)
    blocks = jnp.stack(
        [
            jnp.sum(jnp.where(mine & (rank == k + 1), tables % block_count, 0), axis=1)
            for k in range(CAP)
        ],
        axis=1,
    ).reshape(slot_count)
    kv, enc_t, blocks, *near_weights = lax.optimization_barrier((kv, enc_t, blocks, *near_weights))

    stats = pl.pallas_call(
        lambda *refs: stats_kernel(scale, 2, *refs),
        out_shape=jax.ShapeDtypeStruct((slot_count, 2, CAP * SEGMENT), f32),
        in_specs=[spec(SMEM), spec(VMEM), spec(VMEM)],
        out_specs=spec(VMEM),
        compiler_params=params(),
        name="stats",
    )(blocks, arrived, kv)
    stats = lax.all_to_all(stats, "seq", split_axis=0, concat_axis=0, tiled=True)
    merged = pl.pallas_call(
        merge_kernel,
        out_shape=jax.ShapeDtypeStruct(stats.shape, f32),
        in_specs=[spec(SMEM), spec(VMEM)],
        out_specs=spec(VMEM),
        compiler_params=params(),
        name="merge",
    )(slots, stats)
    merged = lax.all_to_all(merged, "seq", split_axis=0, concat_axis=0, tiled=True)

    row_share = block_len // head_count
    rows = block_count * row_share
    near, far = len(STEPS_NEAR), len(STEPS_FAR)
    back_shape = (seq_count, 2 * CAP * SEGMENT + 2 * room, head_dim)
    back, *near_rows = pl.pallas_call(
        lambda *refs: grads_kernel(scale, 2, *refs),
        out_shape=(
            jax.ShapeDtypeStruct(back_shape, bf16),
            *[jax.ShapeDtypeStruct((far, rows, 2 * head_dim), bf16)] * near,
        ),
        in_specs=[spec(SMEM), spec(SMEM), spec(VMEM), spec(VMEM), spec(VMEM), spec(VMEM)],
        out_specs=(spec(pl.ANY), *[spec(VMEM)] * near),
        scratch_shapes=[
            pltpu.VMEM(back_shape, bf16),
            pltpu.VMEM((block_count * block_len, 2 * head_dim), bf16),
            pltpu.VMEM((block_count, block_len, head_dim), f32),
            pltpu.VMEM((block_count, block_len, head_dim), f32),
            pltpu.SemaphoreType.DMA((seq_count,)),
        ],
        compiler_params=params(),
        name="grads",
    )(lax.axis_index("head").astype(jnp.int32).reshape(1), blocks, arrived, kv, merged, enc_t)

    returned = lax.all_to_all(back, "seq", split_axis=0, concat_axis=0, tiled=True)
    near_rows = [r if a == 0 else shifted(r, a, head_count) for a, r in zip(STEPS_NEAR, near_rows)]
    own, *far_sums = pl.pallas_call(
        project_kernel,
        out_shape=(
            jax.ShapeDtypeStruct((rows, enc_width), f32),
            *[jax.ShapeDtypeStruct((rows, enc_width), bf16)] * (far - 1),
        ),
        in_specs=[spec(VMEM)] * (2 * near),
        out_specs=(spec(VMEM),) * far,
        compiler_params=params(),
        name="project",
    )(*near_rows, *near_weights)
    encoding_grad = own
    for b, part in zip(STEPS_FAR[1:], far_sums):
        encoding_grad = encoding_grad + shifted(part, b, head_count).astype(f32)

    attended, query_grad, key_weight_grad, value_weight_grad = pl.pallas_call(
        finish_kernel,
        out_shape=(
            jax.ShapeDtypeStruct((segments, SEGMENT, head_dim), bf16),
            jax.ShapeDtypeStruct((segments, SEGMENT, head_dim), bf16),
            jax.ShapeDtypeStruct((share, head_dim), f32),
            jax.ShapeDtypeStruct((share, head_dim), f32),
        ),
        in_specs=[spec(SMEM), spec(VMEM)],
        out_specs=(spec(VMEM),) * 4,
        compiler_params=params(),
        name="finish",
    )(slots, returned)
    return (
        attended.reshape(segments * SEGMENT, head_dim),
        query_grad.reshape(segments * SEGMENT, head_dim),
        encoding_grad.reshape(block_count, row_share, enc_width),
        key_weight_grad,
        value_weight_grad,
    )


def solution(mesh):
    in_specs = (
        P("seq", "head"),
        P("seq", None, None),
        P(None, "head"),
        P(None, "head"),
        P(),
        P("seq", "head"),
    )
    out_specs = (
        P("seq", "head"),
        P("seq", "head"),
        P("seq", "head", None),
        P("seq", "head"),
        P("seq", "head"),
    )
    return jax.shard_map(
        on_device, mesh=mesh, in_specs=in_specs, out_specs=out_specs, check_vma=False
    )
```

time: 193 us -> 177 us (0.917)
  the two profiles are of different devices: /device:TPU:16 before, /device:TPU:34 now
where the time goes in v2:
time: 177 us; the launch traced here: 176 us
  starting transfers between devices  63 us (36%)
  Pallas kernels  36.2 us (20%)
  waiting for transfers between devices  34.3 us (19%)
  local copies, waits for them, and re-layouts  23.7 us (13%)
  blocking collectives  13.5 us (8%)
  matrix products  2.96 us (2%)
    ppermute x9, starting transfers between devices, shifted(): lax.ppermute(x, 'head', [(z, (z + step) % count) for z in range(count)])  45.1 us
    ppermute x9, waiting for transfers between devices, shifted(): lax.ppermute(x, 'head', [(z, (z + step) % count) for z in range(count)])  27.9 us
    pallas_call x1, Pallas kernels, on_device(): pl.pallas_call(lambda *refs: grads_kernel(scale, 2, *refs), out_shape=(ja...  17.6 us
    all_to_all x1, blocking collectives, on_device(): lax.all_to_all(stats, 'seq', split_axis=0, concat_axis=0, tiled=True)  13.5 us
    unnamed x30, local copies, waits for them, and re-layouts  11.2 us
    pallas_call x1, Pallas kernels, on_device(): pl.pallas_call(lambda *refs: pack_kernel(block_count, *refs), out_shape=(...  7.91 us
    all_to_all x1, starting transfers between devices, on_device(): lax.all_to_all(packed, 'seq', split_axis=0, concat_axis=0, tiled=True)  7.75 us
    all_to_all x1, waiting for transfers between devices, on_device(): lax.all_to_all(merged, 'seq', split_axis=0, concat_axis=0, tiled=True)  6.39 us
  transfers between devices with their start and end apart: 12, of which 6 were waited for; matrix products, arithmetic and copies ran while one was open for 9% of the time, Pallas kernels for 1%

profile of v2, /device:TPU:34, one launch (start us, length us, event | category | flops | bytes accessed | tf_op | source)
XLA Modules:
  0.0 175.7 jit_solution(4547581677063526364)
XLA Ops:
  2.6 0.9 copy-done.4
  3.5 7.9 %pack.1 = (bf16[64,2,64,128]{3,2,1,0:T(8,128)(2,1)S(1)}, s32[32]{0:T(128)S(1)}) custom-call(s32[32]{0:T(128)S(1)} %dynamic-slice_bitcast_fusion.refs_0_, bf16[16,64,128]{2,1,0:T(8,128)(2,1)S(1)} %bitcast.22, bf16[16,64,128]{2,1,0:T(8,128)(2,1)S(1)} %bitcast.23), custom_call_target="tpu_custom_call" | custom-call | tf_op jit(solution)/shard_map/pack/pallas_call | solution.py:287
  11.5 1.3 copy-done.2
  12.8 7.8 %all-to-all-start = ((bf16[64,2,64,128]{3,2,1,0:T(8,128)(2,1)}), bf16[64,2,64,128]{3,2,1,0:T(8,128)(2,1)S(1)}, u32[]{:S(2)}, u32[]{:S(2)}) async-start(bf16[64,2,64,128]{3,2,1,0:T(8,128)(2,1)} %copy-done.2), calls=%async_computation | async-start | bytes 4194304 | tf_op jit(solution)/shard_map/all_to_all | solution.py:308
  20.7 5.2 %collective-permute-start.2 = (bf16[896,256]{1,0:T(8,128)(2,1)S(1)}, bf16[896,256]{1,0:T(8,128)(2,1)S(1)}, u32[]{:S(2)}, u32[]{:S(2)}) collective-permute-start(bf16[896,256]{1,0:T(8,128)(2,1)S(1)} %constant_dynamic-update-slice_fusion.refs_4_), channel_id=1, source_target_pairs={{0,2},{1,3},{2,4},{3,5},{4,6},{5,7},{6,8},{7,9},{8,10},{9,11},{10,... | collective-permute-start | bytes 1376264 | tf_op jit(solution)/shard_map/ppermute | solution.py:270
  25.9 2.0 %collective-permute-start.1 = (bf16[896,256]{1,0:T(8,128)(2,1)S(1)}, bf16[896,256]{1,0:T(8,128)(2,1)}, u32[]{:S(2)}, u32[]{:S(2)}) collective-permute-start(bf16[896,256]{1,0:T(8,128)(2,1)S(1)} %constant_dynamic-update-slice_fusion.refs_4_), channel_id=1, source_target_pairs={{0,15},{1,0},{2,1},{3,2},{4,3},{5,4},{6,5},{7,6},{8,7},{9,8},{10,9... | collective-permute-start | bytes 1376264 | tf_op jit(solution)/shard_map/ppermute | solution.py:270
  27.9 4.9 %collective-permute-start = (bf16[896,256]{1,0:T(8,128)(2,1)S(1)}, bf16[896,256]{1,0:T(8,128)(2,1)}, u32[]{:S(2)}, u32[]{:S(2)}) collective-permute-start(bf16[896,256]{1,0:T(8,128)(2,1)S(1)} %constant_dynamic-update-slice_fusion.refs_4_), channel_id=1, source_target_pairs={{0,1},{1,2},{2,3},{3,4},{4,5},{5,6},{6,7},{7,8},{8,9},{9,10},{10,1... | collective-permute-start | bytes 1376264 | tf_op jit(solution)/shard_map/ppermute | solution.py:270
  34.4 3.6 %copy.29 = bf16[896,896]{0,1:T(8,128)(2,1)} copy(bf16[896,896]{1,0:T(8,128)(2,1)} %bitcast.25) | data formatting | bytes 3211264 | tf_op jit(solution)/shard_map/reshape | solution.py:312
  38.0 3.0 %fusion = bf16[896,256]{0,1:T(8,128)(2,1)} fusion(bf16[896,256]{1,0:T(8,128)(2,1)S(1)} %constant_dynamic-update-slice_fusion.refs_4_, bf16[896,896]{1,0:T(8,128)(2,1)} %bitcast.26), kind=kOutput, calls=%fused_computation.1 | convolution fusion | flops 411271168 | bytes 2523136 | tf_op jit(solution)/shard_map/dot_general | solution.py:313
  41.0 1.2 copy.28
  42.2 3.5 %reshape.60 = bf16[32,28,896]{2,1,0:T(8,128)(2,1)} reshape(bf16[896,896]{1,0:T(8,128)(2,1)} %bitcast.24) | data formatting | bytes 3211264 | tf_op jit(solution)/shard_map/reshape | solution.py:317
  45.7 2.9 %pad.4 = bf16[32,32,896]{2,1,0:T(8,128)(2,1)} pad(bf16[32,28,896]{2,1,0:T(8,128)(2,1)} %reshape.60, bf16[]{:T(256)} %constant.41.clone.1), padding=0_0x0_4x0_0 | pad | bytes 3440642 | tf_op jit(solution)/shard_map/jit(_pad)/pad | solution.py:317
  48.7 4.1 %collective-permute-done.2.refs_7_ = bf16[896,256]{1,0:T(8,128)(2,1)S(1)} collective-permute-done((bf16[896,256]{1,0:T(8,128)(2,1)S(1)}, bf16[896,256]{1,0:T(8,128)(2,1)S(1)}, u32[]{:S(2)}, u32[]{:S(2)}) %collective-permute-start.2) | collective-permute-done | bytes 458784 | tf_op jit(solution)/shard_map/ppermute | solution.py:270
  52.8 3.6 %collective-permute-done.refs_5_ = bf16[896,256]{1,0:T(8,128)(2,1)} collective-permute-done((bf16[896,256]{1,0:T(8,128)(2,1)S(1)}, bf16[896,256]{1,0:T(8,128)(2,1)}, u32[]{:S(2)}, u32[]{:S(2)}) %collective-permute-start) | collective-permute-done | bytes 458784 | tf_op jit(solution)/shard_map/ppermute | solution.py:270
  56.4 6.1 %stats.1 = f32[64,2,128]{2,1,0:T(2,128)S(1)} custom-call(s32[64]{0:T(128)S(1)} %reshape.62.refs_0_.refs_1_, bf16[64,2,64,128]{3,2,1,0:T(8,128)(2,1)S(1)} %all-to-all-done.refs_1_.refs_2_, bf16[7,128,256]{2,1,0:T(8,128)(2,1)S(1)} %bitcast.20), custom_call_target="tpu_custom_call" | custom-call | tf_op jit(solution)/shard_map/stats/pallas_call | solution.py:331
  62.5 13.5 %all_to_all.20.in_ref = f32[64,2,128]{2,1,0:T(2,128)S(1)} all-to-all(f32[64,2,128]{2,1,0:T(2,128)S(1)} %stats.1), channel_id=1, replica_groups=mesh['seq'=32,'head'=16] {'seq'}, dimensions={0} | all-to-all | bytes 131072 | tf_op jit(solution)/shard_map/all_to_all | solution.py:339
  77.2 4.9 %all-to-all-start.2 = ((f32[64,2,128]{2,1,0:T(2,128)}), f32[64,2,128]{2,1,0:T(2,128)S(1)}, u32[]{:S(2)}, u32[]{:S(2)}) async-start(f32[64,2,128]{2,1,0:T(2,128)} %copy-done.5), calls=%async_computation.2 | async-start | bytes 131072 | tf_op jit(solution)/shard_map/all_to_all | solution.py:348
  82.2 6.4 %all-to-all-done.2.refs_4_ = f32[64,2,128]{2,1,0:T(2,128)S(1)} async-done(((f32[64,2,128]{2,1,0:T(2,128)}), f32[64,2,128]{2,1,0:T(2,128)S(1)}, u32[]{:S(2)}, u32[]{:S(2)}) %all-to-all-start.2) | async-done | bytes 65568 | tf_op jit(solution)/shard_map/all_to_all | solution.py:348
  88.6 1.5 copy-done
  90.1 17.6 %grads.1 = (bf16[32,320,128]{2,1,0:T(8,128)(2,1)S(1)}, bf16[4,56,256]{2,1,0:T(8,128)(2,1)S(1)}, bf16[4,56,256]{2,1,0:T(8,128)(2,1)S(1)}, bf16[4,56,256]{2,1,0:T(8,128)(2,1)S(1)}, bf16[4,56,256]{2,1,0:T(8,128)(2,1)S(1)}) custom-call(s32[1]{0:T(128)} %bitcast.3.refs_0_, s32[64]{0:T(128)S(1)} %reshape.62.refs_0_.refs_1_, ...), custom_call_target="tpu_custom_call" | custom-call | tf_op jit(solution)/shard_map/grads/pallas_call | solution.py:354
  107.7 1.5 copy-done.1
  111.8 5.2 %all-to-all-start.3 = ((bf16[32,320,128]{2,1,0:T(8,128)(2,1)}), bf16[32,320,128]{2,1,0:T(8,128)(2,1)S(1)}, u32[]{:S(2)}, u32[]{:S(2)}) async-start(bf16[32,320,128]{2,1,0:T(8,128)(2,1)} %copy-done.1), calls=%async_computation.3 | async-start | bytes 5242880 | tf_op jit(solution)/shard_map/all_to_all | solution.py:373
  117.0 4.3 %collective-permute-start.3 = (bf16[4,56,256]{2,1,0:T(8,128)(2,1)}, bf16[4,56,256]{2,1,0:T(8,128)(2,1)S(1)}, u32[]{:S(2)}, u32[]{:S(2)}) collective-permute-start(bf16[4,56,256]{2,1,0:T(8,128)(2,1)} %copy-done.10), channel_id=1, source_target_pairs={{0,1},{1,2},{2,3},{3,4},{4,5},{5,6},{6,7},{7,8},{8,9},{9,10},{10,1... | collective-permute-start | bytes 344072 | tf_op jit(solution)/shard_map/ppermute | solution.py:270
  121.2 6.0 %collective-permute-start.4 = (bf16[4,56,256]{2,1,0:T(8,128)(2,1)}, bf16[4,56,256]{2,1,0:T(8,128)(2,1)S(1)}, u32[]{:S(2)}, u32[]{:S(2)}) collective-permute-start(bf16[4,56,256]{2,1,0:T(8,128)(2,1)} %copy-done.9), channel_id=1, source_target_pairs={{0,15},{1,0},{2,1},{3,2},{4,3},{5,4},{6,5},{7,6},{8,7},{9,8},{10,9... | collective-permute-start | bytes 344072 | tf_op jit(solution)/shard_map/ppermute | solution.py:270
  127.2 2.5 %collective-permute-start.5 = (bf16[4,56,256]{2,1,0:T(8,128)(2,1)}, bf16[4,56,256]{2,1,0:T(8,128)(2,1)S(1)}, u32[]{:S(2)}, u32[]{:S(2)}) collective-permute-start(bf16[4,56,256]{2,1,0:T(8,128)(2,1)} %copy-done.8), channel_id=1, source_target_pairs={{0,2},{1,3},{2,4},{3,5},{4,6},{5,7},{6,8},{7,9},{8,10},{9,11},{10,... | collective-permute-start | bytes 344072 | tf_op jit(solution)/shard_map/ppermute | solution.py:270
  130.2 6.2 %collective-permute-done.5.refs_3_ = bf16[4,56,256]{2,1,0:T(8,128)(2,1)S(1)} collective-permute-done((bf16[4,56,256]{2,1,0:T(8,128)(2,1)}, bf16[4,56,256]{2,1,0:T(8,128)(2,1)S(1)}, u32[]{:S(2)}, u32[]{:S(2)}) %collective-permute-start.5) | collective-permute-done | bytes 114720 | tf_op jit(solution)/shard_map/ppermute | solution.py:270
  137.4 2.3 %project.1 = (f32[56,896]{1,0:T(8,128)S(1)}, bf16[56,896]{1,0:T(8,128)(2,1)S(1)}, bf16[56,896]{1,0:T(8,128)(2,1)S(1)}, bf16[56,896]{1,0:T(8,128)(2,1)S(1)}) custom-call(bf16[4,56,256]{2,1,0:T(8,128)(2,1)S(1)} %copy-done.7, bf16[4,56,256]{2,1,0:T(8,128)(2,1)S(1)} %collective-permute-done.3.refs_1_, bf16[4,56,256]{2,1,0:T(8,128)(2,1)S(1)} %collective-permute-done.4.refs_2_, ...), custom_call_target="tpu_custom_call" | custom-call | tf_op jit(solution)/shard_map/project/pallas_call | solution.py:375
  139.7 7.3 %collective-permute-start.6 = (bf16[56,896]{1,0:T(8,128)(2,1)S(1)}, bf16[56,896]{1,0:T(8,128)(2,1)S(1)}, u32[]{:S(2)}, u32[]{:S(2)}) collective-permute-start(bf16[56,896]{1,0:T(8,128)(2,1)S(1)} %get-tuple-element.44), channel_id=1, source_target_pairs={{0,4},{1,5},{2,6},{3,7},{4,8},{5,9},{6,10},{7,11},{8,12},{9,13},{1... | collective-permute-start | bytes 301064 | tf_op jit(solution)/shard_map/ppermute | solution.py:270
  147.1 2.4 %collective-permute-start.7 = (bf16[56,896]{1,0:T(8,128)(2,1)S(1)}, bf16[56,896]{1,0:T(8,128)(2,1)S(1)}, u32[]{:S(2)}, u32[]{:S(2)}) collective-permute-start(bf16[56,896]{1,0:T(8,128)(2,1)S(1)} %get-tuple-element.45), channel_id=1, source_target_pairs={{0,12},{1,13},{2,14},{3,15},{4,0},{5,1},{6,2},{7,3},{8,4},{9,5},{1... | collective-permute-start | bytes 301064 | tf_op jit(solution)/shard_map/ppermute | solution.py:270
  149.5 10.4 %collective-permute-start.8 = (bf16[56,896]{1,0:T(8,128)(2,1)S(1)}, bf16[56,896]{1,0:T(8,128)(2,1)S(1)}, u32[]{:S(2)}, u32[]{:S(2)}) collective-permute-start(bf16[56,896]{1,0:T(8,128)(2,1)S(1)} %get-tuple-element.46), channel_id=1, source_target_pairs={{0,8},{1,9},{2,10},{3,11},{4,12},{5,13},{6,14},{7,15},{8,0},{9,1},... | collective-permute-start | bytes 301064 | tf_op jit(solution)/shard_map/ppermute | solution.py:270
  159.9 13.5 %collective-permute-done.8 = bf16[56,896]{1,0:T(8,128)(2,1)S(1)} collective-permute-done((bf16[56,896]{1,0:T(8,128)(2,1)S(1)}, bf16[56,896]{1,0:T(8,128)(2,1)S(1)}, u32[]{:S(2)}, u32[]{:S(2)}) %collective-permute-start.8) | collective-permute-done | bytes 100384 | tf_op jit(solution)/shard_map/ppermute | solution.py:270
  174.1 1.6 finish.1
  (53 shorter events, 9.5 us)
Async XLA Ops:
  1.6 1.0 copy-start.3
  2.6 0.9 copy-start.4
  11.5 1.3 copy-start.2
  12.8 7.8 %copy-start.11 = (bf16[896,128]{1,0:T(8,128)(2,1)S(1)}, bf16[896,128]{1,0:T(8,128)(2,1)}, u32[]{:S(2)}) copy-start(bf16[896,128]{1,0:T(8,128)(2,1)} %param.8) | copy-start | bytes 688132
  12.8 7.8 %copy-start.12 = (bf16[896,128]{1,0:T(8,128)(2,1)S(1)}, bf16[896,128]{1,0:T(8,128)(2,1)}, u32[]{:S(2)}) copy-start(bf16[896,128]{1,0:T(8,128)(2,1)} %param.9) | copy-start | bytes 688132
  12.8 20.9 %copy-start.13 = (s32[512,2]{0,1:T(2,128)S(1)}, s32[512,2]{0,1:T(2,128)}, u32[]{:S(2)}) copy-start(s32[512,2]{0,1:T(2,128)} %param.10) | copy-start | bytes 12292
  12.8 43.6 %all-to-all-start = ((bf16[64,2,64,128]{3,2,1,0:T(8,128)(2,1)}), bf16[64,2,64,128]{3,2,1,0:T(8,128)(2,1)S(1)}, u32[]{:S(2)}, u32[]{:S(2)}) async-start(bf16[64,2,64,128]{3,2,1,0:T(8,128)(2,1)} %copy-done.2), calls=%async_computation | async-start | bytes 4194304 | tf_op jit(solution)/shard_map/all_to_all | solution.py:308
  20.7 32.1 %collective-permute-start.2 = (bf16[896,256]{1,0:T(8,128)(2,1)S(1)}, bf16[896,256]{1,0:T(8,128)(2,1)S(1)}, u32[]{:S(2)}, u32[]{:S(2)}) collective-permute-start(bf16[896,256]{1,0:T(8,128)(2,1)S(1)} %constant_dynamic-update-slice_fusion.refs_4_), channel_id=1, source_target_pairs={{0,2},{1,3},{2,4},{3,5},{4,6},{5,7},{6,8},{7,9},{8,10},{9,11},{10,... | collective-permute-start | bytes 1376264 | tf_op jit(solution)/shard_map/ppermute | solution.py:270
  25.9 26.9 %collective-permute-start.1 = (bf16[896,256]{1,0:T(8,128)(2,1)S(1)}, bf16[896,256]{1,0:T(8,128)(2,1)}, u32[]{:S(2)}, u32[]{:S(2)}) collective-permute-start(bf16[896,256]{1,0:T(8,128)(2,1)S(1)} %constant_dynamic-update-slice_fusion.refs_4_), channel_id=1, source_target_pairs={{0,15},{1,0},{2,1},{3,2},{4,3},{5,4},{6,5},{7,6},{8,7},{9,8},{10,9... | collective-permute-start | bytes 1376264 | tf_op jit(solution)/shard_map/ppermute | solution.py:270
  27.9 28.5 %collective-permute-start = (bf16[896,256]{1,0:T(8,128)(2,1)S(1)}, bf16[896,256]{1,0:T(8,128)(2,1)}, u32[]{:S(2)}, u32[]{:S(2)}) collective-permute-start(bf16[896,256]{1,0:T(8,128)(2,1)S(1)} %constant_dynamic-update-slice_fusion.refs_4_), channel_id=1, source_target_pairs={{0,1},{1,2},{2,3},{3,4},{4,5},{5,6},{6,7},{7,8},{8,9},{9,10},{10,1... | collective-permute-start | bytes 1376264 | tf_op jit(solution)/shard_map/ppermute | solution.py:270
  76.6 0.6 copy-start.5
  77.2 11.3 %all-to-all-start.2 = ((f32[64,2,128]{2,1,0:T(2,128)}), f32[64,2,128]{2,1,0:T(2,128)S(1)}, u32[]{:S(2)}, u32[]{:S(2)}) async-start(f32[64,2,128]{2,1,0:T(2,128)} %copy-done.5), calls=%async_computation.2 | async-start | bytes 131072 | tf_op jit(solution)/shard_map/all_to_all | solution.py:348
  88.6 1.5 copy-start
  107.7 1.5 copy-start.1
  109.2 0.6 copy-start.6
  109.9 0.7 copy-start.8
  110.5 0.6 copy-start.9
  111.2 0.6 copy-start.10
  111.8 62.3 %all-to-all-start.3 = ((bf16[32,320,128]{2,1,0:T(8,128)(2,1)}), bf16[32,320,128]{2,1,0:T(8,128)(2,1)S(1)}, u32[]{:S(2)}, u32[]{:S(2)}) async-start(bf16[32,320,128]{2,1,0:T(8,128)(2,1)} %copy-done.1), calls=%async_computation.3 | async-start | bytes 5242880 | tf_op jit(solution)/shard_map/all_to_all | solution.py:373
  117.0 12.8 %collective-permute-start.3 = (bf16[4,56,256]{2,1,0:T(8,128)(2,1)}, bf16[4,56,256]{2,1,0:T(8,128)(2,1)S(1)}, u32[]{:S(2)}, u32[]{:S(2)}) collective-permute-start(bf16[4,56,256]{2,1,0:T(8,128)(2,1)} %copy-done.10), channel_id=1, source_target_pairs={{0,1},{1,2},{2,3},{3,4},{4,5},{5,6},{6,7},{7,8},{8,9},{9,10},{10,1... | collective-permute-start | bytes 344072 | tf_op jit(solution)/shard_map/ppermute | solution.py:270
  121.2 9.0 %collective-permute-start.4 = (bf16[4,56,256]{2,1,0:T(8,128)(2,1)}, bf16[4,56,256]{2,1,0:T(8,128)(2,1)S(1)}, u32[]{:S(2)}, u32[]{:S(2)}) collective-permute-start(bf16[4,56,256]{2,1,0:T(8,128)(2,1)} %copy-done.9), channel_id=1, source_target_pairs={{0,15},{1,0},{2,1},{3,2},{4,3},{5,4},{6,5},{7,6},{8,7},{9,8},{10,9... | collective-permute-start | bytes 344072 | tf_op jit(solution)/shard_map/ppermute | solution.py:270
  127.2 9.2 %collective-permute-start.5 = (bf16[4,56,256]{2,1,0:T(8,128)(2,1)}, bf16[4,56,256]{2,1,0:T(8,128)(2,1)S(1)}, u32[]{:S(2)}, u32[]{:S(2)}) collective-permute-start(bf16[4,56,256]{2,1,0:T(8,128)(2,1)} %copy-done.8), channel_id=1, source_target_pairs={{0,2},{1,3},{2,4},{3,5},{4,6},{5,7},{6,8},{7,9},{8,10},{9,11},{10,... | collective-permute-start | bytes 344072 | tf_op jit(solution)/shard_map/ppermute | solution.py:270
  136.5 0.9 copy-start.7
  139.7 20.2 %collective-permute-start.6 = (bf16[56,896]{1,0:T(8,128)(2,1)S(1)}, bf16[56,896]{1,0:T(8,128)(2,1)S(1)}, u32[]{:S(2)}, u32[]{:S(2)}) collective-permute-start(bf16[56,896]{1,0:T(8,128)(2,1)S(1)} %get-tuple-element.44), channel_id=1, source_target_pairs={{0,4},{1,5},{2,6},{3,7},{4,8},{5,9},{6,10},{7,11},{8,12},{9,13},{1... | collective-permute-start | bytes 301064 | tf_op jit(solution)/shard_map/ppermute | solution.py:270
  147.1 12.9 %collective-permute-start.7 = (bf16[56,896]{1,0:T(8,128)(2,1)S(1)}, bf16[56,896]{1,0:T(8,128)(2,1)S(1)}, u32[]{:S(2)}, u32[]{:S(2)}) collective-permute-start(bf16[56,896]{1,0:T(8,128)(2,1)S(1)} %get-tuple-element.45), channel_id=1, source_target_pairs={{0,12},{1,13},{2,14},{3,15},{4,0},{5,1},{6,2},{7,3},{8,4},{9,5},{1... | collective-permute-start | bytes 301064 | tf_op jit(solution)/shard_map/ppermute | solution.py:270
  149.5 23.9 %collective-permute-start.8 = (bf16[56,896]{1,0:T(8,128)(2,1)S(1)}, bf16[56,896]{1,0:T(8,128)(2,1)S(1)}, u32[]{:S(2)}, u32[]{:S(2)}) collective-permute-start(bf16[56,896]{1,0:T(8,128)(2,1)S(1)} %get-tuple-element.46), channel_id=1, source_target_pairs={{0,8},{1,9},{2,10},{3,11},{4,12},{5,13},{6,14},{7,15},{8,0},{9,1},... | collective-permute-start | bytes 301064 | tf_op jit(solution)/shard_map/ppermute | solution.py:270

commit v3 on v2

v3 whole, which is shorter than its diff:
```python
import math

import jax
import jax.numpy as jnp
from jax import lax
from jax.experimental import pallas as pl
from jax.experimental.pallas import tpu as pltpu
from jax.sharding import PartitionSpec as P

SEGMENT = 64
NEIGH = 2
CAP = 2
NEAR = 4
FAR = (0, 4, -4, 8)
VMEM_LIMIT = 40 * 1024 * 1024
PACK_LIMIT = 60 * 1024 * 1024
VMEM = pltpu.VMEM
SMEM = pltpu.SMEM
HBM = pltpu.HBM


def params(limit=VMEM_LIMIT):
    return pltpu.CompilerParams(vmem_limit_bytes=limit)


def spec(space):
    return pl.BlockSpec(memory_space=space)


def nt_dot(a, b):
    return lax.dot_general(a, b, (((1,), (1,)), ((), ())), preferred_element_type=jnp.float32)


def tn_dot(a, b):
    return lax.dot_general(a, b, (((0,), (0,)), ((), ())), preferred_element_type=jnp.float32)


def nn_dot(a, b):
    return jnp.dot(a, b, preferred_element_type=jnp.float32)


def pack_kernel(block_count, reads_ref, q_ref, g_ref, out_ref, slots_ref, used, stage, sem):
    seq_count = used.shape[0]
    read_count = slots_ref.shape[0]
    first = lax.axis_index("seq") * (read_count // NEIGH)

    def leave(slot):
        pltpu.make_async_copy(stage.at[slot], out_ref.at[slot], sem).start()

    for h in range(seq_count):
        used[h] = 0
    for j in range(read_count):
        holder = lax.div(reads_ref[j % NEIGH, first + j // NEIGH], block_count)
        rank = used[holder]
        used[holder] = rank + 1
        slot = holder * CAP + rank
        slots_ref[j] = slot
        stage[slot, 0] = q_ref[j // NEIGH]
        stage[slot, 1] = g_ref[j // NEIGH]
        leave(slot)

    def blank(h, _):
        for k in range(CAP):
            @pl.when(used[h] <= k)
            def _():
                stage[h * CAP + k] = jnp.zeros(stage.shape[1:], stage.dtype)
                leave(h * CAP + k)

        return 0

    lax.fori_loop(0, seq_count, blank, 0)
    pltpu.make_async_copy(stage, out_ref, sem).wait()


def pair_operands(x_ref, s, kv_a, kv_b):
    head_dim = x_ref.shape[3]

    def diagonal(i):
        one, two = x_ref[CAP * s, i], x_ref[CAP * s + 1, i]
        zero = jnp.zeros_like(one)
        return jnp.concatenate(
            [jnp.concatenate([one, zero], axis=1), jnp.concatenate([zero, two], axis=1)], axis=0
        )

    keys = jnp.concatenate([kv_a[:, :head_dim], kv_b[:, :head_dim]], axis=1)
    values = jnp.concatenate([kv_a[:, head_dim:], kv_b[:, head_dim:]], axis=1)
    return diagonal(0), diagonal(1), keys, values


def stats_kernel(scale, unroll, blocks_ref, x_ref, kv_ref, out_ref):
    def step(s, _):
        kv_a = kv_ref[blocks_ref[CAP * s]]
        kv_b = kv_ref[blocks_ref[CAP * s + 1]]
        q_diag, g_diag, keys, values = pair_operands(x_ref, s, kv_a, kv_b)
        scores = nt_dot(keys, q_diag) * scale
        top = jnp.max(scores, axis=0, keepdims=True)
        weight = jnp.exp(scores - top)
        total = jnp.sum(weight, axis=0, keepdims=True)
        prob_grad = nt_dot(values, g_diag)
        mean = jnp.sum(weight * prob_grad, axis=0, keepdims=True) / total
        both = jnp.concatenate([top + jnp.log(total), mean], axis=0)
        out_ref[CAP * s] = both
        out_ref[CAP * s + 1] = pltpu.roll(both, SEGMENT, 1)
        return 0

    lax.fori_loop(0, x_ref.shape[0] // CAP, step, 0, unroll=unroll)


def merge_kernel(slots_ref, in_ref, out_ref):
    out_ref[...] = jnp.zeros_like(out_ref)
    for c in range(slots_ref.shape[0] // NEIGH):
        slot_a, slot_b = slots_ref[NEIGH * c], slots_ref[NEIGH * c + 1]
        one, two = in_ref[slot_a], in_ref[slot_b]
        lse_a, lse_b = one[0:1], two[0:1]
        top = jnp.maximum(lse_a, lse_b)
        lse = top + jnp.log(jnp.exp(lse_a - top) + jnp.exp(lse_b - top))
        delta = jnp.exp(lse_a - lse) * one[1:2] + jnp.exp(lse_b - lse) * two[1:2]
        both = jnp.concatenate([lse, delta], axis=0)
        out_ref[slot_a] = both
        out_ref[slot_b] = both


def grads_kernel(scale, group, blocks_ref, x_ref, kv_ref, stats_ref, enc_hbm, *refs):
    near = NEAR
    out_ref = refs[0]
    rows_refs = refs[1:1 + near]
    stage, enc_t, rows_all, rows_near, acc_k, acc_v, enc_sem, rows_sems, out_sem = refs[1 + near:]
    head_dim = kv_ref.shape[2] // 2
    seq_count = x_ref.shape[0] // CAP
    pair = CAP * SEGMENT
    parts = 2 * pair
    fetch = pltpu.make_async_copy(enc_hbm, enc_t, enc_sem)
    fetch.start()
    acc_k[...] = jnp.zeros_like(acc_k)
    acc_v[...] = jnp.zeros_like(acc_v)
    left = lax.broadcasted_iota(jnp.int32, (2, pair), 1) < SEGMENT

    def step(i, _):
        sources = [i * group + g for g in range(group)]
        first = [blocks_ref[CAP * s] for s in sources]
        second = [blocks_ref[CAP * s + 1] for s in sources]
        operands = [
            pair_operands(x_ref, s, kv_ref[a], kv_ref[b]) for s, a, b in zip(sources, first, second)
        ]
        stats = [
            jnp.where(left, stats_ref[CAP * s], pltpu.roll(stats_ref[CAP * s + 1], SEGMENT, 1))
            for s in sources
        ]
        scores = [nt_dot(keys, q) * scale for q, _, keys, _ in operands]
        prob_grads = [nt_dot(values, g) for _, g, _, values in operands]
        probs = [jnp.exp(x - stat[0:1]) for x, stat in zip(scores, stats)]
        score_grads = [
            (p * (x - stat[1:2]) * scale).astype(jnp.bfloat16)
            for p, x, stat in zip(probs, prob_grads, stats)
        ]
        probs = [p.astype(jnp.bfloat16) for p in probs]
        attended = [tn_dot(p, ops[3]).astype(jnp.bfloat16) for p, ops in zip(probs, operands)]
        query_grads = [tn_dot(x, ops[2]).astype(jnp.bfloat16) for x, ops in zip(score_grads, operands)]
        value_parts = [nn_dot(p, ops[1]) for p, ops in zip(probs, operands)]
        key_parts = [nn_dot(x, ops[0]) for x, ops in zip(score_grads, operands)]
        for s, att, grad in zip(sources, attended, query_grads):
            stage[s, :SEGMENT] = att[:SEGMENT, :head_dim]
            stage[s, SEGMENT:pair] = grad[:SEGMENT, :head_dim]
            stage[s, pair:pair + SEGMENT] = att[SEGMENT:, head_dim:]
            stage[s, pair + SEGMENT:parts] = grad[SEGMENT:, head_dim:]
        for a, b, key_part, value_part in zip(first, second, key_parts, value_parts):
            acc_k[a] += key_part[:, :head_dim]
            acc_v[a] += value_part[:, :head_dim]
            acc_k[b] += key_part[:, head_dim:]
            acc_v[b] += value_part[:, head_dim:]
        at = pl.ds(i * group, group)
        pltpu.make_async_copy(stage.at[at, :parts], out_ref.at[at, :parts], out_sem).start()
        return 0

    lax.fori_loop(0, seq_count // group, step, 0)
    head_count = near * len(FAR)
    block_count, block_len, _ = acc_k.shape
    row_share = block_len // head_count
    z = lax.axis_index("head")
    rows_copies = []
    for i in range(near):
        partner = lax.bitwise_xor(z, i)
        for j, b in enumerate(FAR):
            dest = lax.rem(partner + (b + head_count), head_count)
            at = pl.ds(pl.multiple_of(dest * row_share, row_share), row_share)
            rows = jnp.concatenate([acc_k[:, at, :], acc_v[:, at, :]], axis=2)
            rows_near[i, j] = rows.reshape(block_count * row_share, 2 * head_dim).astype(jnp.bfloat16)
        rows_copies.append(pltpu.make_async_copy(rows_near.at[i], rows_refs[i], rows_sems.at[i]))
        rows_copies[i].start()
    rows_all[:, :head_dim] = acc_k[...].reshape(-1, head_dim).astype(jnp.bfloat16)
    rows_all[:, head_dim:] = acc_v[...].reshape(-1, head_dim).astype(jnp.bfloat16)
    room = (stage.shape[1] - parts) // 2
    share = enc_t.shape[0] // seq_count
    fetch.wait()
    batch = 8
    for i in range(0, seq_count, batch):
        term = nn_dot(enc_t[i * share:(i + batch) * share], rows_all[...])
        for s in range(batch):
            part = term[s * share:(s + 1) * share]
            if room > share:
                part = jnp.concatenate([part, jnp.zeros((room - share, 2 * head_dim), jnp.float32)], axis=0)
            part = part.astype(jnp.bfloat16)
            stage[i + s, parts:parts + room] = part[:, :head_dim]
            stage[i + s, parts + room:] = part[:, head_dim:]
        pltpu.make_async_copy(
            stage.at[i:i + batch, parts:], out_ref.at[i:i + batch, parts:], out_sem
        ).start()
    for copy in rows_copies:
        copy.wait()
    pltpu.make_async_copy(stage, out_ref, out_sem).wait()


def finish_kernel(slots_ref, in_ref, att_ref, qg_ref, kw_ref, vw_ref):
    share = kw_ref.shape[0]
    parts = 2 * CAP * SEGMENT
    room = (in_ref.shape[1] - parts) // 2

    def step(c, _):
        slot_a, slot_b = slots_ref[NEIGH * c], slots_ref[NEIGH * c + 1]

        def part(slot):
            holder = lax.div(slot, CAP)
            row = pl.multiple_of((slot - holder * CAP) * 2 * SEGMENT, 2 * SEGMENT)
            return in_ref[holder, pl.ds(row, 2 * SEGMENT), :].astype(jnp.float32)

        total = (part(slot_a) + part(slot_b)).astype(jnp.bfloat16)
        att_ref[c] = total[:SEGMENT]
        qg_ref[c] = total[SEGMENT:]
        return 0

    lax.fori_loop(0, att_ref.shape[0], step, 0, unroll=2)
    total = in_ref[0, parts:, :].astype(jnp.float32)
    for s in range(1, in_ref.shape[0]):
        total = total + in_ref[s, parts:, :].astype(jnp.float32)
    kw_ref[...] = total[:share]
    vw_ref[...] = total[room:room + share]


def project_kernel(weights_ref, *refs):
    rows_refs, own_ref, far_refs = refs[:NEAR], refs[NEAR], refs[NEAR + 1:]
    far, rows, width = rows_refs[0].shape
    place = lax.rem(lax.axis_index("head"), NEAR)
    half = far // 2
    for i in range(0, far, half):
        total = jnp.zeros((half * rows, own_ref.shape[1]), jnp.float32)
        for n, rows_ref in enumerate(rows_refs):
            weight = weights_ref[lax.bitwise_xor(place, n)]
            total = total + nt_dot(rows_ref[i:i + half].reshape(half * rows, width), weight)
        for j in range(half):
            part = total[j * rows:(j + 1) * rows]
            if i + j == 0:
                own_ref[...] = part
            else:
                far_refs[i + j - 1][...] = part.astype(jnp.bfloat16)


def moved(x, target):
    return lax.ppermute(x, "head", [(z, target(z)) for z in range(lax.axis_size("head"))])


def on_device(queries, encodings, key_weight, value_weight, reads, out_grad):
    seq_count = lax.axis_size("seq")
    head_count = lax.axis_size("head")
    me = lax.axis_index("seq")
    block_count, block_len, enc_width = encodings.shape
    head_dim = key_weight.shape[1]
    segments = queries.shape[0] // SEGMENT
    read_count = NEIGH * segments
    slot_count = seq_count * CAP
    scale = 1.0 / math.sqrt(head_dim)
    bf16, f32 = jnp.bfloat16, jnp.float32

    packed, slots = pl.pallas_call(
        lambda *refs: pack_kernel(block_count, *refs),
        out_shape=(
            jax.ShapeDtypeStruct((slot_count, 2, SEGMENT, head_dim), bf16),
            jax.ShapeDtypeStruct((read_count,), jnp.int32),
        ),
        in_specs=[spec(SMEM), spec(VMEM), spec(VMEM)],
        out_specs=(spec(HBM), spec(SMEM)),
        scratch_shapes=[
            pltpu.SMEM((seq_count,), jnp.int32),
            pltpu.VMEM((slot_count, 2, SEGMENT, head_dim), bf16),
            pltpu.SemaphoreType.DMA,
        ],
        compiler_params=params(PACK_LIMIT),
        name="pack",
    )(
        reads.T,
        queries.reshape(segments, SEGMENT, head_dim),
        out_grad.reshape(segments, SEGMENT, head_dim),
    )
    arrived = lax.all_to_all(packed, "seq", split_axis=0, concat_axis=0, tiled=True)

    key_weight, value_weight, slots = lax.optimization_barrier((key_weight, value_weight, slots))
    weights = jnp.concatenate([key_weight, value_weight], axis=1)
    groups = [list(range(z, z + NEAR)) for z in range(0, head_count, NEAR)]
    near_weights = lax.all_gather(weights, "head", axis_index_groups=groups)
    flat_enc = encodings.reshape(block_count * block_len, enc_width)
    kv = jnp.dot(flat_enc, weights, preferred_element_type=f32).astype(bf16)
    kv = kv.reshape(block_count, block_len, 2 * head_dim)
    share = enc_width // seq_count
    room = -(-share // 16) * 16
    enc_t = flat_enc.T

    tables = reads.reshape(seq_count, read_count)
    mine = (tables // block_count) == me
    rank = jnp.cumsum(mine.astype(jnp.int32), axis=1)
    blocks = jnp.stack(
        [
            jnp.sum(jnp.where(mine & (rank == k + 1), tables % block_count, 0), axis=1)
            for k in range(CAP)
        ],
        axis=1,
    ).reshape(slot_count)
    kv, enc_t, blocks = lax.optimization_barrier((kv, enc_t, blocks))

    stats = pl.pallas_call(
        lambda *refs: stats_kernel(scale, seq_count, *refs),
        out_shape=jax.ShapeDtypeStruct((slot_count, 2, CAP * SEGMENT), f32),
        in_specs=[spec(SMEM), spec(VMEM), spec(VMEM)],
        out_specs=spec(VMEM),
        compiler_params=params(),
        name="stats",
    )(blocks, arrived, kv)
    stats = lax.all_to_all(stats, "seq", split_axis=0, concat_axis=0, tiled=True)
    merged = pl.pallas_call(
        merge_kernel,
        out_shape=jax.ShapeDtypeStruct(stats.shape, f32),
        in_specs=[spec(SMEM), spec(VMEM)],
        out_specs=spec(VMEM),
        compiler_params=params(),
        name="merge",
    )(slots, stats)
    merged = lax.all_to_all(merged, "seq", split_axis=0, concat_axis=0, tiled=True)

    row_share = block_len // head_count
    rows = block_count * row_share
    near, far = NEAR, len(FAR)
    back_shape = (seq_count, 2 * CAP * SEGMENT + 2 * room, head_dim)
    back, *near_rows = pl.pallas_call(
        lambda *refs: grads_kernel(scale, 8, *refs),
        out_shape=(
            jax.ShapeDtypeStruct(back_shape, bf16),
            *[jax.ShapeDtypeStruct((far, rows, 2 * head_dim), bf16)] * near,
        ),
        in_specs=[spec(SMEM), spec(VMEM), spec(VMEM), spec(VMEM), spec(HBM)],
        out_specs=(spec(HBM), *[spec(HBM)] * near),
        scratch_shapes=[
            pltpu.VMEM(back_shape, bf16),
            pltpu.VMEM((enc_width, block_count * block_len), bf16),
            pltpu.VMEM((block_count * block_len, 2 * head_dim), bf16),
            pltpu.VMEM((near, far, rows, 2 * head_dim), bf16),
            pltpu.VMEM((block_count, block_len, head_dim), f32),
            pltpu.VMEM((block_count, block_len, head_dim), f32),
            pltpu.SemaphoreType.DMA,
            pltpu.SemaphoreType.DMA((near,)),
            pltpu.SemaphoreType.DMA,
        ],
        compiler_params=params(),
        name="grads",
    )(blocks, arrived, kv, merged, enc_t)

    returned = lax.all_to_all(back, "seq", split_axis=0, concat_axis=0, tiled=True)
    near_rows = [r if n == 0 else moved(r, lambda z: z ^ n) for n, r in enumerate(near_rows)]
    own, *far_sums = pl.pallas_call(
        project_kernel,
        out_shape=(
            jax.ShapeDtypeStruct((rows, enc_width), f32),
            *[jax.ShapeDtypeStruct((rows, enc_width), bf16)] * (far - 1),
        ),
        in_specs=[spec(VMEM)] * (1 + near),
        out_specs=(spec(VMEM),) * far,
        compiler_params=params(),
        name="project",
    )(near_weights, *near_rows)
    encoding_grad = own
    for b, part in zip(FAR[1:], far_sums):
        encoding_grad = encoding_grad + moved(part, lambda z: (z + b) % head_count).astype(f32)

    attended, query_grad, key_weight_grad, value_weight_grad = pl.pallas_call(
        finish_kernel,
        out_shape=(
            jax.ShapeDtypeStruct((segments, SEGMENT, head_dim), bf16),
            jax.ShapeDtypeStruct((segments, SEGMENT, head_dim), bf16),
            jax.ShapeDtypeStruct((share, head_dim), f32),
            jax.ShapeDtypeStruct((share, head_dim), f32),
        ),
        in_specs=[spec(SMEM), spec(VMEM)],
        out_specs=(spec(VMEM),) * 4,
        compiler_params=params(),
        name="finish",
    )(slots, returned)
    return (
        attended.reshape(segments * SEGMENT, head_dim),
        query_grad.reshape(segments * SEGMENT, head_dim),
        encoding_grad.reshape(block_count, row_share, enc_width),
        key_weight_grad,
        value_weight_grad,
    )


def solution(mesh):
    in_specs = (
        P("seq", "head"),
        P("seq", None, None),
        P(None, "head"),
        P(None, "head"),
        P(),
        P("seq", "head"),
    )
    out_specs = (
        P("seq", "head"),
        P("seq", "head"),
        P("seq", "head", None),
        P("seq", "head"),
        P("seq", "head"),
    )
    return jax.shard_map(
        on_device, mesh=mesh, in_specs=in_specs, out_specs=out_specs, check_vma=False
    )
```

time: 177 us -> 154 us (0.87)
  the two profiles are of different devices: /device:TPU:34 before, /device:TPU:35 now
where the time goes in v3:
time: 154 us; the launch traced here: 153 us
  starting transfers between devices  45.6 us (30%)
  waiting for transfers between devices  41.3 us (27%)
  blocking collectives  22.9 us (15%)
  Pallas kernels  16.2 us (11%)
  between operations  14.3 us (9%)
  local copies, waits for them, and re-layouts  8.92 us (6%)
  matrix products  2.18 us (1%)
  other arithmetic  1.98 us (1%)
    ppermute x6, starting transfers between devices, moved(): lax.ppermute(x, 'head', [(z, target(z)) for z in range(lax.axis_size('hea...  32.4 us
    ppermute x6, waiting for transfers between devices, moved(): lax.ppermute(x, 'head', [(z, target(z)) for z in range(lax.axis_size('hea...  23.6 us
    all_to_all x1, waiting for transfers between devices, on_device(): lax.all_to_all(packed, 'seq', split_axis=0, concat_axis=0, tiled=True)  17.6 us
    all_to_all x1, blocking collectives, on_device(): lax.all_to_all(stats, 'seq', split_axis=0, concat_axis=0, tiled=True)  12 us
    all_to_all x1, blocking collectives, on_device(): lax.all_to_all(merged, 'seq', split_axis=0, concat_axis=0, tiled=True)  10.9 us
    all_to_all x1, starting transfers between devices, on_device(): lax.all_to_all(packed, 'seq', split_axis=0, concat_axis=0, tiled=True)  8.08 us
    pallas_call x1, Pallas kernels, on_device(): pl.pallas_call(lambda *refs: grads_kernel(scale, 8, *refs), out_shape=(ja...  7.63 us
    all_to_all x1, starting transfers between devices, on_device(): lax.all_to_all(back, 'seq', split_axis=0, concat_axis=0, tiled=True)  5.17 us
  transfers between devices with their start and end apart: 9, of which 5 were waited for; matrix products, arithmetic and copies ran while one was open for 6% of the time, Pallas kernels for 7%

profile of v3, /device:TPU:35, one launch (start us, length us, event | category | flops | bytes accessed | tf_op | source)
XLA Modules:
  0.0 153.4 jit_solution(16472084674198748614)
XLA Ops:
  7.2 3.3 %pack.1 = (bf16[64,2,64,128]{3,2,1,0:T(8,128)(2,1)}, s32[32]{0:T(128)}) custom-call(s32[2,512]{1,0:T(2,128)} %bitcast.25, bf16[16,64,128]{2,1,0:T(8,128)(2,1)} %bitcast.23, bf16[16,64,128]{2,1,0:T(8,128)(2,1)} %bitcast.24), custom_call_target="tpu_custom_call" | custom-call | tf_op jit(solution)/shard_map/pack/pallas_call | solution.py:273
  10.5 8.1 %all-to-all-start = ((bf16[64,2,64,128]{3,2,1,0:T(8,128)(2,1)}), bf16[64,2,64,128]{3,2,1,0:T(8,128)(2,1)S(1)}, u32[]{:S(2)}, u32[]{:S(2)}) async-start(bf16[64,2,64,128]{3,2,1,0:T(8,128)(2,1)} %get-tuple-element.31), calls=%async_computation | async-start | bytes 4194304 | tf_op jit(solution)/shard_map/all_to_all | solution.py:293
  18.8 0.8 copy-done.4
  20.0 0.2 fusion.2
  20.6 0.2 eq.38
  20.8 0.2 eq.41
  21.0 0.5 select_reduce_fusion.1
  22.1 3.6 %copy.17 = bf16[896,896]{0,1:T(8,128)(2,1)} copy(bf16[896,896]{1,0:T(8,128)(2,1)} %bitcast.21) | data formatting | bytes 3211264 | tf_op jit(solution)/shard_map/reshape | solution.py:299
  25.7 2.2 %fusion = bf16[896,256]{0,1:T(8,128)(2,1)S(1)} fusion(bf16[896,256]{1,0:T(8,128)(2,1)S(1)} %copy-done.5, bf16[896,896]{1,0:T(8,128)(2,1)} %bitcast.22), kind=kOutput, calls=%fused_computation.1 | convolution fusion | flops 411271168 | bytes 2523136 | tf_op jit(solution)/shard_map/dot_general | solution.py:300
  27.9 0.2 copy.16
  28.1 17.6 %all-to-all-done.refs_1_ = bf16[64,2,64,128]{3,2,1,0:T(8,128)(2,1)S(1)} async-done(((bf16[64,2,64,128]{3,2,1,0:T(8,128)(2,1)}), bf16[64,2,64,128]{3,2,1,0:T(8,128)(2,1)S(1)}, u32[]{:S(2)}, u32[]{:S(2)}) %all-to-all-start) | async-done | bytes 2097184 | tf_op jit(solution)/shard_map/all_to_all | solution.py:293
  45.8 1.9 %stats.1 = f32[64,2,128]{2,1,0:T(2,128)S(1)} custom-call(s32[64]{0:T(128)S(1)} %reshape.57.refs_0_, bf16[64,2,64,128]{3,2,1,0:T(8,128)(2,1)S(1)} %all-to-all-done.refs_1_, bf16[7,128,256]{2,1,0:T(8,128)(2,1)S(1)} %bitcast.18), custom_call_target="tpu_custom_call" | custom-call | tf_op jit(solution)/shard_map/stats/pallas_call | solution.py:318
  47.7 12.0 %all_to_all.20.in_ref = f32[64,2,128]{2,1,0:T(2,128)S(1)} all-to-all(f32[64,2,128]{2,1,0:T(2,128)S(1)} %stats.1), channel_id=1, replica_groups=mesh['seq'=32,'head'=16] {'seq'}, dimensions={0} | all-to-all | bytes 131072 | tf_op jit(solution)/shard_map/all_to_all | solution.py:326
  59.7 0.6 merge.1
  60.3 10.9 %all_to_all.21.refs_3_ = f32[64,2,128]{2,1,0:T(2,128)S(1)} all-to-all(f32[64,2,128]{2,1,0:T(2,128)S(1)} %merge.1), channel_id=1, replica_groups=mesh['seq'=32,'head'=16] {'seq'}, dimensions={0} | all-to-all | bytes 131072 | tf_op jit(solution)/shard_map/all_to_all | solution.py:335
  71.2 7.6 %grads.1 = (bf16[32,320,128]{2,1,0:T(8,128)(2,1)S(1)}, bf16[4,56,256]{2,1,0:T(8,128)(2,1)S(1)}, bf16[4,56,256]{2,1,0:T(8,128)(2,1)S(1)}, bf16[4,56,256]{2,1,0:T(8,128)(2,1)S(1)}, bf16[4,56,256]{2,1,0:T(8,128)(2,1)S(1)}) custom-call(s32[64]{0:T(128)S(1)} %reshape.57.refs_0_, bf16[64,2,64,128]{3,2,1,0:T(8,128)(2,1)S(1)} %all-to-all-done.refs_1_, ...), custom_call_target="tpu_custom_call" | custom-call | tf_op jit(solution)/shard_map/grads/pallas_call | solution.py:341
  78.9 1.5 copy-done.1
  80.4 5.2 %all-to-all-start.3 = ((bf16[32,320,128]{2,1,0:T(8,128)(2,1)}), bf16[32,320,128]{2,1,0:T(8,128)(2,1)S(1)}, u32[]{:S(2)}, u32[]{:S(2)}) async-start(bf16[32,320,128]{2,1,0:T(8,128)(2,1)} %copy-done.1), calls=%async_computation.3 | async-start | bytes 5242880 | tf_op jit(solution)/shard_map/all_to_all | solution.py:364
  85.6 3.8 %collective-permute-start = (bf16[4,56,256]{2,1,0:T(8,128)(2,1)S(1)}, bf16[4,56,256]{2,1,0:T(8,128)(2,1)S(1)}, u32[]{:S(2)}, u32[]{:S(2)}) collective-permute-start(bf16[4,56,256]{2,1,0:T(8,128)(2,1)S(1)} %get-tuple-element.38), channel_id=1, source_target_pairs={{0,1},{1,0},{2,3},{3,2},{4,5},{5,4},{6,7},{7,6},{8,9},{9,8},{10,11... | collective-permute-start | bytes 344072 | tf_op jit(solution)/shard_map/ppermute | solution.py:258
  89.3 3.1 %collective-permute-start.1 = (bf16[4,56,256]{2,1,0:T(8,128)(2,1)S(1)}, bf16[4,56,256]{2,1,0:T(8,128)(2,1)S(1)}, u32[]{:S(2)}, u32[]{:S(2)}) collective-permute-start(bf16[4,56,256]{2,1,0:T(8,128)(2,1)S(1)} %get-tuple-element.39), channel_id=1, source_target_pairs={{0,2},{1,3},{2,0},{3,1},{4,6},{5,7},{6,4},{7,5},{8,10},{9,11},{10,... | collective-permute-start | bytes 344072 | tf_op jit(solution)/shard_map/ppermute | solution.py:258
  92.4 2.2 %collective-permute-start.2 = (bf16[4,56,256]{2,1,0:T(8,128)(2,1)S(1)}, bf16[4,56,256]{2,1,0:T(8,128)(2,1)S(1)}, u32[]{:S(2)}, u32[]{:S(2)}) collective-permute-start(bf16[4,56,256]{2,1,0:T(8,128)(2,1)S(1)} %get-tuple-element.40), channel_id=1, source_target_pairs={{0,3},{1,2},{2,1},{3,0},{4,7},{5,6},{6,5},{7,4},{8,11},{9,10},{10,... | collective-permute-start | bytes 344072 | tf_op jit(solution)/shard_map/ppermute | solution.py:258
  94.6 1.6 %collective-permute-done.1.refs_2_ = bf16[4,56,256]{2,1,0:T(8,128)(2,1)S(1)} collective-permute-done((bf16[4,56,256]{2,1,0:T(8,128)(2,1)S(1)}, bf16[4,56,256]{2,1,0:T(8,128)(2,1)S(1)}, u32[]{:S(2)}, u32[]{:S(2)}) %collective-permute-start.1) | collective-permute-done | bytes 114720 | tf_op jit(solution)/shard_map/ppermute | solution.py:258
  96.3 6.7 %collective-permute-done.2.refs_3_ = bf16[4,56,256]{2,1,0:T(8,128)(2,1)S(1)} collective-permute-done((bf16[4,56,256]{2,1,0:T(8,128)(2,1)S(1)}, bf16[4,56,256]{2,1,0:T(8,128)(2,1)S(1)}, u32[]{:S(2)}, u32[]{:S(2)}) %collective-permute-start.2) | collective-permute-done | bytes 114720 | tf_op jit(solution)/shard_map/ppermute | solution.py:258
  102.9 1.5 copy-done.2
  104.4 1.2 project.1
  105.6 9.1 %collective-permute-start.3 = (bf16[56,896]{1,0:T(8,128)(2,1)S(1)}, bf16[56,896]{1,0:T(8,128)(2,1)S(1)}, u32[]{:S(2)}, u32[]{:S(2)}) collective-permute-start(bf16[56,896]{1,0:T(8,128)(2,1)S(1)} %get-tuple-element.42), channel_id=1, source_target_pairs={{0,4},{1,5},{2,6},{3,7},{4,8},{5,9},{6,10},{7,11},{8,12},{9,13},{1... | collective-permute-start | bytes 301064 | tf_op jit(solution)/shard_map/ppermute | solution.py:258
  114.7 4.0 %collective-permute-start.4 = (bf16[56,896]{1,0:T(8,128)(2,1)S(1)}, bf16[56,896]{1,0:T(8,128)(2,1)S(1)}, u32[]{:S(2)}, u32[]{:S(2)}) collective-permute-start(bf16[56,896]{1,0:T(8,128)(2,1)S(1)} %get-tuple-element.43), channel_id=1, source_target_pairs={{0,12},{1,13},{2,14},{3,15},{4,0},{5,1},{6,2},{7,3},{8,4},{9,5},{1... | collective-permute-start | bytes 301064 | tf_op jit(solution)/shard_map/ppermute | solution.py:258
  118.7 10.3 %collective-permute-start.5 = (bf16[56,896]{1,0:T(8,128)(2,1)S(1)}, bf16[56,896]{1,0:T(8,128)(2,1)S(1)}, u32[]{:S(2)}, u32[]{:S(2)}) collective-permute-start(bf16[56,896]{1,0:T(8,128)(2,1)S(1)} %get-tuple-element.44), channel_id=1, source_target_pairs={{0,8},{1,9},{2,10},{3,11},{4,12},{5,13},{6,14},{7,15},{8,0},{9,1},... | collective-permute-start | bytes 301064 | tf_op jit(solution)/shard_map/ppermute | solution.py:258
  129.0 1.0 collective-permute-done.4
  130.0 14.3 %collective-permute-done.5 = bf16[56,896]{1,0:T(8,128)(2,1)S(1)} collective-permute-done((bf16[56,896]{1,0:T(8,128)(2,1)S(1)}, bf16[56,896]{1,0:T(8,128)(2,1)S(1)}, u32[]{:S(2)}, u32[]{:S(2)}) %collective-permute-start.5) | collective-permute-done | bytes 100384 | tf_op jit(solution)/shard_map/ppermute | solution.py:258
  144.3 0.7 add_bitcast_fusion
  145.0 1.6 %finish.1 = (bf16[16,64,128]{2,1,0:T(8,128)(2,1)}, bf16[16,64,128]{2,1,0:T(8,128)(2,1)}, f32[28,128]{1,0:T(8,128)}, f32[28,128]{1,0:T(8,128)}) custom-call(s32[32]{0:T(128)S(1)} %copy-done.3, bf16[32,320,128]{2,1,0:T(8,128)(2,1)S(1)} %all-to-all-done.3.in_ref), custom_call_target="tpu_custom_call" | custom-call | tf_op jit(solution)/shard_map/finish/pallas_call | solution.py:381
  (37 shorter events, 1.6 us)
Async XLA Ops:
  10.5 8.2 %copy-start.6 = (bf16[896,128]{1,0:T(8,128)(2,1)S(1)}, bf16[896,128]{1,0:T(8,128)(2,1)}, u32[]{:S(2)}) copy-start(bf16[896,128]{1,0:T(8,128)(2,1)} %param.8) | copy-start | bytes 688132
  10.5 8.2 %copy-start.7 = (bf16[896,128]{1,0:T(8,128)(2,1)S(1)}, bf16[896,128]{1,0:T(8,128)(2,1)}, u32[]{:S(2)}) copy-start(bf16[896,128]{1,0:T(8,128)(2,1)} %param.9) | copy-start | bytes 688132
  10.5 9.1 %copy-start.8 = (s32[512,2]{0,1:T(2,128)S(1)}, s32[512,2]{0,1:T(2,128)}, u32[]{:S(2)}) copy-start(s32[512,2]{0,1:T(2,128)} %param.10) | copy-start | bytes 12292
  10.5 35.3 %all-to-all-start = ((bf16[64,2,64,128]{3,2,1,0:T(8,128)(2,1)}), bf16[64,2,64,128]{3,2,1,0:T(8,128)(2,1)S(1)}, u32[]{:S(2)}, u32[]{:S(2)}) async-start(bf16[64,2,64,128]{3,2,1,0:T(8,128)(2,1)} %get-tuple-element.31), calls=%async_computation | async-start | bytes 4194304 | tf_op jit(solution)/shard_map/all_to_all | solution.py:293
  18.6 84.4 %all-gather.3.cloned.1.call-start = ((), (), s32[]{:S(2)}) async-start(), calls=%async_computation.4 | async-start | bytes 2293760 | tf_op jit(solution)/shard_map/all_gather | solution.py:298
  18.8 0.8 copy-start.4
  21.0 4.7 %copy-start.5 = (bf16[896,256]{1,0:T(8,128)(2,1)S(1)}, bf16[896,256]{1,0:T(8,128)(2,1)}, u32[]{:S(2)}) copy-start(bf16[896,256]{1,0:T(8,128)(2,1)} %copy-done.4) | copy-start | bytes 1376260
  27.9 31.8 %copy-start.3 = (s32[32]{0:T(128)S(1)}, s32[32]{0:T(128)}, u32[]{:S(2)}) copy-start(s32[32]{0:T(128)} %get-tuple-element.27.slots_ref) | copy-start | bytes 388
  45.8 25.4 %copy-start = (bf16[896,896]{0,1:T(8,128)(2,1)S(1)}, bf16[896,896]{0,1:T(8,128)(2,1)}, u32[]{:S(2)}) copy-start(bf16[896,896]{0,1:T(8,128)(2,1)} %copy.17) | copy-start | bytes 4816900
  78.9 1.5 copy-start.1
  80.4 64.6 %all-to-all-start.3 = ((bf16[32,320,128]{2,1,0:T(8,128)(2,1)}), bf16[32,320,128]{2,1,0:T(8,128)(2,1)S(1)}, u32[]{:S(2)}, u32[]{:S(2)}) async-start(bf16[32,320,128]{2,1,0:T(8,128)(2,1)} %copy-done.1), calls=%async_computation.3 | async-start | bytes 5242880 | tf_op jit(solution)/shard_map/all_to_all | solution.py:364
  85.6 9.0 %collective-permute-start = (bf16[4,56,256]{2,1,0:T(8,128)(2,1)S(1)}, bf16[4,56,256]{2,1,0:T(8,128)(2,1)S(1)}, u32[]{:S(2)}, u32[]{:S(2)}) collective-permute-start(bf16[4,56,256]{2,1,0:T(8,128)(2,1)S(1)} %get-tuple-element.38), channel_id=1, source_target_pairs={{0,1},{1,0},{2,3},{3,2},{4,5},{5,4},{6,7},{7,6},{8,9},{9,8},{10,11... | collective-permute-start | bytes 344072 | tf_op jit(solution)/shard_map/ppermute | solution.py:258
  89.3 6.9 %collective-permute-start.1 = (bf16[4,56,256]{2,1,0:T(8,128)(2,1)S(1)}, bf16[4,56,256]{2,1,0:T(8,128)(2,1)S(1)}, u32[]{:S(2)}, u32[]{:S(2)}) collective-permute-start(bf16[4,56,256]{2,1,0:T(8,128)(2,1)S(1)} %get-tuple-element.39), channel_id=1, source_target_pairs={{0,2},{1,3},{2,0},{3,1},{4,6},{5,7},{6,4},{7,5},{8,10},{9,11},{10,... | collective-permute-start | bytes 344072 | tf_op jit(solution)/shard_map/ppermute | solution.py:258
  92.4 10.5 %collective-permute-start.2 = (bf16[4,56,256]{2,1,0:T(8,128)(2,1)S(1)}, bf16[4,56,256]{2,1,0:T(8,128)(2,1)S(1)}, u32[]{:S(2)}, u32[]{:S(2)}) collective-permute-start(bf16[4,56,256]{2,1,0:T(8,128)(2,1)S(1)} %get-tuple-element.40), channel_id=1, source_target_pairs={{0,3},{1,2},{2,1},{3,0},{4,7},{5,6},{6,5},{7,4},{8,11},{9,10},{10,... | collective-permute-start | bytes 344072 | tf_op jit(solution)/shard_map/ppermute | solution.py:258
  102.9 1.5 copy-start.2
  105.6 23.4 %collective-permute-start.3 = (bf16[56,896]{1,0:T(8,128)(2,1)S(1)}, bf16[56,896]{1,0:T(8,128)(2,1)S(1)}, u32[]{:S(2)}, u32[]{:S(2)}) collective-permute-start(bf16[56,896]{1,0:T(8,128)(2,1)S(1)} %get-tuple-element.42), channel_id=1, source_target_pairs={{0,4},{1,5},{2,6},{3,7},{4,8},{5,9},{6,10},{7,11},{8,12},{9,13},{1... | collective-permute-start | bytes 301064 | tf_op jit(solution)/shard_map/ppermute | solution.py:258
  114.7 15.3 %collective-permute-start.4 = (bf16[56,896]{1,0:T(8,128)(2,1)S(1)}, bf16[56,896]{1,0:T(8,128)(2,1)S(1)}, u32[]{:S(2)}, u32[]{:S(2)}) collective-permute-start(bf16[56,896]{1,0:T(8,128)(2,1)S(1)} %get-tuple-element.43), channel_id=1, source_target_pairs={{0,12},{1,13},{2,14},{3,15},{4,0},{5,1},{6,2},{7,3},{8,4},{9,5},{1... | collective-permute-start | bytes 301064 | tf_op jit(solution)/shard_map/ppermute | solution.py:258
  118.7 25.6 %collective-permute-start.5 = (bf16[56,896]{1,0:T(8,128)(2,1)S(1)}, bf16[56,896]{1,0:T(8,128)(2,1)S(1)}, u32[]{:S(2)}, u32[]{:S(2)}) collective-permute-start(bf16[56,896]{1,0:T(8,128)(2,1)S(1)} %get-tuple-element.44), channel_id=1, source_target_pairs={{0,8},{1,9},{2,10},{3,11},{4,12},{5,13},{6,14},{7,15},{8,0},{9,1},... | collective-permute-start | bytes 301064 | tf_op jit(solution)/shard_map/ppermute | solution.py:258
Sparse Core Ops, SparseCore 0:
  21.5 53.6 all-gather.2

commit v4 on v3

--- a/solution.py
+++ b/solution.py
@@ -10,10 +10,11 @@
 SEGMENT = 64
 NEIGH = 2
 CAP = 2
-NEAR = 4
+NEAR = (0, 1, -1, 2)
 FAR = (0, 4, -4, 8)
+LANES = 128
 VMEM_LIMIT = 40 * 1024 * 1024
-PACK_LIMIT = 60 * 1024 * 1024
+LARGE_LIMIT = 60 * 1024 * 1024
 VMEM = pltpu.VMEM
 SMEM = pltpu.SMEM
 HBM = pltpu.HBM
@@ -120,15 +121,22 @@
         out_ref[slot_b] = both
 
 
-def grads_kernel(scale, group, blocks_ref, x_ref, kv_ref, stats_ref, enc_hbm, *refs):
-    near = NEAR
+def grads_kernel(scale, group, blocks_ref, x_hbm, kv_ref, stats_ref, enc_hbm, *refs):
+    near = len(NEAR)
     out_ref = refs[0]
     rows_refs = refs[1:1 + near]
-    stage, enc_t, rows_all, rows_near, acc_k, acc_v, enc_sem, rows_sems, out_sem = refs[1 + near:]
+    x_ref, stage, enc_t, rows_all, rows_near, acc_k, acc_v, x_sems, enc_sem, rows_sems, out_sem = refs[1 + near:]
     head_dim = kv_ref.shape[2] // 2
     seq_count = x_ref.shape[0] // CAP
     pair = CAP * SEGMENT
     parts = 2 * pair
+
+    def arrival(i):
+        at = pl.ds(i * group * CAP, group * CAP)
+        return pltpu.make_async_copy(x_hbm.at[at], x_ref.at[at], x_sems.at[i])
+
+    for i in range(seq_count // group):
+        arrival(i).start()
     fetch = pltpu.make_async_copy(enc_hbm, enc_t, enc_sem)
     fetch.start()
     acc_k[...] = jnp.zeros_like(acc_k)
@@ -136,6 +144,7 @@
     left = lax.broadcasted_iota(jnp.int32, (2, pair), 1) < SEGMENT
 
     def step(i, _):
+        arrival(i).wait()
         sources = [i * group + g for g in range(group)]
         first = [blocks_ref[CAP * s] for s in sources]
         second = [blocks_ref[CAP * s + 1] for s in sources]
@@ -178,10 +187,9 @@
     row_share = block_len // head_count
     z = lax.axis_index("head")
     rows_copies = []
-    for i in range(near):
-        partner = lax.bitwise_xor(z, i)
+    for i, a in enumerate(NEAR):
         for j, b in enumerate(FAR):
-            dest = lax.rem(partner + (b + head_count), head_count)
+            dest = lax.rem(z + (a + b + head_count), head_count)
             at = pl.ds(pl.multiple_of(dest * row_share, row_share), row_share)
             rows = jnp.concatenate([acc_k[:, at, :], acc_v[:, at, :]], axis=2)
             rows_near[i, j] = rows.reshape(block_count * row_share, 2 * head_dim).astype(jnp.bfloat16)
@@ -236,26 +244,35 @@
     vw_ref[...] = total[room:room + share]
 
 
-def project_kernel(weights_ref, *refs):
-    rows_refs, own_ref, far_refs = refs[:NEAR], refs[NEAR], refs[NEAR + 1:]
+def project_kernel(*refs):
+    near = len(NEAR)
+    rows_refs, weight_refs, out_refs = refs[:near], refs[near:2 * near], refs[2 * near:]
+    own_ref, up_ref, down_ref, across_up_ref, across_down_ref = out_refs
     far, rows, width = rows_refs[0].shape
-    place = lax.rem(lax.axis_index("head"), NEAR)
+    cut = across_up_ref.shape[1]
     half = far // 2
+    sums = []
     for i in range(0, far, half):
         total = jnp.zeros((half * rows, own_ref.shape[1]), jnp.float32)
-        for n, rows_ref in enumerate(rows_refs):
-            weight = weights_ref[lax.bitwise_xor(place, n)]
-            total = total + nt_dot(rows_ref[i:i + half].reshape(half * rows, width), weight)
-        for j in range(half):
-            part = total[j * rows:(j + 1) * rows]
-            if i + j == 0:
-                own_ref[...] = part
-            else:
-                far_refs[i + j - 1][...] = part.astype(jnp.bfloat16)
-
-
-def moved(x, target):
-    return lax.ppermute(x, "head", [(z, target(z)) for z in range(lax.axis_size("head"))])
+        for rows_ref, weight_ref in zip(rows_refs, weight_refs):
+            total = total + nt_dot(rows_ref[i:i + half].reshape(half * rows, width), weight_ref[...])
+        sums += [total[j * rows:(j + 1) * rows] for j in range(half)]
+    own_ref[...], up_ref[...], down_ref[...] = sums[:3]
+    across_up_ref[...] = sums[3][:, :cut].astype(jnp.bfloat16)
+    across_down_ref[...] = sums[3][:, cut:].astype(jnp.bfloat16)
+
+
+def fold_kernel(up_ref, down_ref, across_up_ref, across_down_ref, up_out_ref, down_out_ref):
+    cut = across_up_ref.shape[1]
+    up_out_ref[:, :cut] = (up_ref[:, :cut] + across_up_ref[...].astype(jnp.float32)).astype(jnp.bfloat16)
+    up_out_ref[:, cut:] = up_ref[:, cut:].astype(jnp.bfloat16)
+    down_out_ref[:, :cut] = down_ref[:, :cut].astype(jnp.bfloat16)
+    down_out_ref[:, cut:] = (down_ref[:, cut:] + across_down_ref[...].astype(jnp.float32)).astype(jnp.bfloat16)
+
+
+def shifted(x, step):
+    count = lax.axis_size("head")
+    return lax.ppermute(x, "head", [(z, (z + step) % count) for z in range(count)])
 
 
 def on_device(queries, encodings, key_weight, value_weight, reads, out_grad):
@@ -283,7 +300,7 @@
             pltpu.VMEM((slot_count, 2, SEGMENT, head_dim), bf16),
             pltpu.SemaphoreType.DMA,
         ],
-        compiler_params=params(PACK_LIMIT),
+        compiler_params=params(LARGE_LIMIT),
         name="pack",
     )(
         reads.T,
@@ -294,8 +311,7 @@
 
     key_weight, value_weight, slots = lax.optimization_barrier((key_weight, value_weight, slots))
     weights = jnp.concatenate([key_weight, value_weight], axis=1)
-    groups = [list(range(z, z + NEAR)) for z in range(0, head_count, NEAR)]
-    near_weights = lax.all_gather(weights, "head", axis_index_groups=groups)
+    near_weights = [weights if a == 0 else shifted(weights, a) for a in NEAR]
     flat_enc = encodings.reshape(block_count * block_len, enc_width)
     kv = jnp.dot(flat_enc, weights, preferred_element_type=f32).astype(bf16)
     kv = kv.reshape(block_count, block_len, 2 * head_dim)
@@ -332,51 +348,64 @@
         compiler_params=params(),
         name="merge",
     )(slots, stats)
+    merged, *near_weights = lax.optimization_barrier((merged, *near_weights))
     merged = lax.all_to_all(merged, "seq", split_axis=0, concat_axis=0, tiled=True)
 
     row_share = block_len // head_count
     rows = block_count * row_share
-    near, far = NEAR, len(FAR)
+    near, far = len(NEAR), len(FAR)
     back_shape = (seq_count, 2 * CAP * SEGMENT + 2 * room, head_dim)
+    group = 8
     back, *near_rows = pl.pallas_call(
-        lambda *refs: grads_kernel(scale, 8, *refs),
+        lambda *refs: grads_kernel(scale, group, *refs),
         out_shape=(
             jax.ShapeDtypeStruct(back_shape, bf16),
             *[jax.ShapeDtypeStruct((far, rows, 2 * head_dim), bf16)] * near,
         ),
-        in_specs=[spec(SMEM), spec(VMEM), spec(VMEM), spec(VMEM), spec(HBM)],
+        in_specs=[spec(SMEM), spec(HBM), spec(VMEM), spec(VMEM), spec(HBM)],
         out_specs=(spec(HBM), *[spec(HBM)] * near),
         scratch_shapes=[
+            pltpu.VMEM(arrived.shape, bf16),
             pltpu.VMEM(back_shape, bf16),
             pltpu.VMEM((enc_width, block_count * block_len), bf16),
             pltpu.VMEM((block_count * block_len, 2 * head_dim), bf16),
             pltpu.VMEM((near, far, rows, 2 * head_dim), bf16),
             pltpu.VMEM((block_count, block_len, head_dim), f32),
             pltpu.VMEM((block_count, block_len, head_dim), f32),
+            pltpu.SemaphoreType.DMA((seq_count // group,)),
             pltpu.SemaphoreType.DMA,
             pltpu.SemaphoreType.DMA((near,)),
             pltpu.SemaphoreType.DMA,
         ],
-        compiler_params=params(),
+        compiler_params=params(LARGE_LIMIT),
         name="grads",
     )(blocks, arrived, kv, merged, enc_t)
 
     returned = lax.all_to_all(back, "seq", split_axis=0, concat_axis=0, tiled=True)
-    near_rows = [r if n == 0 else moved(r, lambda z: z ^ n) for n, r in enumerate(near_rows)]
-    own, *far_sums = pl.pallas_call(
+    near_rows = [r if a == 0 else shifted(r, a) for a, r in zip(NEAR, near_rows)]
+    cut = -(-enc_width // (2 * LANES)) * LANES
+    step = FAR[1]
+    own, up, down, across_up, across_down = pl.pallas_call(
         project_kernel,
         out_shape=(
-            jax.ShapeDtypeStruct((rows, enc_width), f32),
-            *[jax.ShapeDtypeStruct((rows, enc_width), bf16)] * (far - 1),
+            *[jax.ShapeDtypeStruct((rows, enc_width), f32)] * (far - 1),
+            jax.ShapeDtypeStruct((rows, cut), bf16),
+            jax.ShapeDtypeStruct((rows, enc_width - cut), bf16),
         ),
-        in_specs=[spec(VMEM)] * (1 + near),
-        out_specs=(spec(VMEM),) * far,
+        in_specs=[spec(VMEM)] * (2 * near),
+        out_specs=(spec(VMEM),) * (far + 1),
         compiler_params=params(),
         name="project",
-    )(near_weights, *near_rows)
-    encoding_grad = own
-    for b, part in zip(FAR[1:], far_sums):
-        encoding_grad = encoding_grad + moved(part, lambda z: (z + b) % head_count).astype(f32)
+    )(*near_rows, *near_weights)
+    up, down = pl.pallas_call(
+        fold_kernel,
+        out_shape=(jax.ShapeDtypeStruct((rows, enc_width), bf16),) * 2,
+        in_specs=[spec(VMEM)] * 4,
+        out_specs=(spec(VMEM),) * 2,
+        compiler_params=params(),
+        name="fold",
+    )(up, down, shifted(across_up, step), shifted(across_down, -step))
+    encoding_grad = own + shifted(up, step).astype(f32) + shifted(down, -step).astype(f32)
 
     attended, query_grad, key_weight_grad, value_weight_grad = pl.pallas_call(
         finish_kernel,

time: 154 us -> 143 us (0.929)
  the two profiles are of different devices: /device:TPU:35 before, /device:TPU:2 now
where the time goes in v4:
time: 143 us; the launch traced here: 142 us
  starting transfers between devices  60.2 us (42%)
  waiting for transfers between devices  26.9 us (19%)
  blocking collectives  23.2 us (16%)
  Pallas kernels  17.6 us (12%)
  local copies, waits for them, and re-layouts  7.64 us (5%)
  matrix products  2.94 us (2%)
  other arithmetic  2.66 us (2%)
    ppermute x10, starting transfers between devices, shifted(): lax.ppermute(x, 'head', [(z, (z + step) % count) for z in range(count)])  45.3 us
    ppermute x10, waiting for transfers between devices, shifted(): lax.ppermute(x, 'head', [(z, (z + step) % count) for z in range(count)])  24 us
    all_to_all x1, blocking collectives, on_device(): lax.all_to_all(merged, 'seq', split_axis=0, concat_axis=0, tiled=True)  11.8 us
    all_to_all x1, blocking collectives, on_device(): lax.all_to_all(stats, 'seq', split_axis=0, concat_axis=0, tiled=True)  11.4 us
    all_to_all x1, starting transfers between devices, on_device(): lax.all_to_all(packed, 'seq', split_axis=0, concat_axis=0, tiled=True)  9.69 us
    pallas_call x1, Pallas kernels, on_device(): pl.pallas_call(lambda *refs: grads_kernel(scale, group, *refs), out_shape...  7.83 us
    all_to_all x1, starting transfers between devices, on_device(): lax.all_to_all(back, 'seq', split_axis=0, concat_axis=0, tiled=True)  5.17 us
    reshape x1, local copies, waits for them, and re-layouts, on_device(): flat_enc = encodings.reshape(block_count * block_len, enc_width)  3.59 us
  transfers between devices with their start and end apart: 12, of which 6 were waited for; matrix products, arithmetic and copies ran while one was open for 9% of the time, Pallas kernels for 3%

profile of v4, /device:TPU:2, one launch (start us, length us, event | category | flops | bytes accessed | tf_op | source)
XLA Modules:
  0.0 142.1 jit_solution(7291091278931527129)
XLA Ops:
  0.6 3.3 %pack.1 = (bf16[64,2,64,128]{3,2,1,0:T(8,128)(2,1)}, s32[32]{0:T(128)}) custom-call(s32[2,512]{1,0:T(2,128)} %bitcast.23, bf16[16,64,128]{2,1,0:T(8,128)(2,1)} %bitcast.21, bf16[16,64,128]{2,1,0:T(8,128)(2,1)} %bitcast.22), custom_call_target="tpu_custom_call" | custom-call | tf_op jit(solution)/shard_map/pack/pallas_call | solution.py:290
  4.0 9.7 %all-to-all-start = ((bf16[64,2,64,128]{3,2,1,0:T(8,128)(2,1)}), bf16[64,2,64,128]{3,2,1,0:T(8,128)(2,1)S(1)}, u32[]{:S(2)}, u32[]{:S(2)}) async-start(bf16[64,2,64,128]{3,2,1,0:T(8,128)(2,1)} %get-tuple-element.39), calls=%async_computation | async-start | bytes 4194304 | tf_op jit(solution)/shard_map/all_to_all | solution.py:310
  13.8 3.2 %collective-permute-start.2 = (bf16[896,256]{1,0:T(8,128)(2,1)S(1)}, bf16[896,256]{1,0:T(8,128)(2,1)S(1)}, u32[]{:S(2)}, u32[]{:S(2)}) collective-permute-start(bf16[896,256]{1,0:T(8,128)(2,1)S(1)} %constant_dynamic-update-slice_fusion.refs_4_), channel_id=1, source_target_pairs={{0,2},{1,3},{2,4},{3,5},{4,6},{5,7},{6,8},{7,9},{8,10},{9,11},{10,... | collective-permute-start | bytes 1376264 | tf_op jit(solution)/shard_map/ppermute | solution.py:275
  17.1 8.1 %collective-permute-start.1 = (bf16[896,256]{1,0:T(8,128)(2,1)S(1)}, bf16[896,256]{1,0:T(8,128)(2,1)}, u32[]{:S(2)}, u32[]{:S(2)}) collective-permute-start(bf16[896,256]{1,0:T(8,128)(2,1)S(1)} %constant_dynamic-update-slice_fusion.refs_4_), channel_id=1, source_target_pairs={{0,15},{1,0},{2,1},{3,2},{4,3},{5,4},{6,5},{7,6},{8,7},{9,8},{10,9... | collective-permute-start | bytes 1376264 | tf_op jit(solution)/shard_map/ppermute | solution.py:275
  25.2 1.9 %collective-permute-start = (bf16[896,256]{1,0:T(8,128)(2,1)S(1)}, bf16[896,256]{1,0:T(8,128)(2,1)}, u32[]{:S(2)}, u32[]{:S(2)}) collective-permute-start(bf16[896,256]{1,0:T(8,128)(2,1)S(1)} %constant_dynamic-update-slice_fusion.refs_4_), channel_id=1, source_target_pairs={{0,1},{1,2},{2,3},{3,4},{4,5},{5,6},{6,7},{7,8},{8,9},{9,10},{10,1... | collective-permute-start | bytes 1376264 | tf_op jit(solution)/shard_map/ppermute | solution.py:275
  27.5 0.8 and.26
  28.5 0.7 fusion.4
  31.0 3.6 %copy.17 = bf16[896,896]{0,1:T(8,128)(2,1)} copy(bf16[896,896]{1,0:T(8,128)(2,1)} %bitcast.19) | data formatting | bytes 3211264 | tf_op jit(solution)/shard_map/reshape | solution.py:315
  34.6 2.9 %fusion = bf16[896,256]{0,1:T(8,128)(2,1)} fusion(bf16[896,256]{1,0:T(8,128)(2,1)S(1)} %constant_dynamic-update-slice_fusion.refs_4_, bf16[896,896]{1,0:T(8,128)(2,1)} %bitcast.20), kind=kOutput, calls=%fused_computation.1 | convolution fusion | flops 411271168 | bytes 2523136 | tf_op jit(solution)/shard_map/dot_general | solution.py:316
  37.5 1.2 copy.16
  38.7 2.9 %all-to-all-done.refs_1_ = bf16[64,2,64,128]{3,2,1,0:T(8,128)(2,1)S(1)} async-done(((bf16[64,2,64,128]{3,2,1,0:T(8,128)(2,1)}), bf16[64,2,64,128]{3,2,1,0:T(8,128)(2,1)S(1)}, u32[]{:S(2)}, u32[]{:S(2)}) %all-to-all-start) | async-done | bytes 2097184 | tf_op jit(solution)/shard_map/all_to_all | solution.py:310
  41.7 1.9 %stats.1 = f32[64,2,128]{2,1,0:T(2,128)S(1)} custom-call(s32[64]{0:T(128)S(1)} %reshape.57.refs_0_, bf16[64,2,64,128]{3,2,1,0:T(8,128)(2,1)S(1)} %all-to-all-done.refs_1_, bf16[7,128,256]{2,1,0:T(8,128)(2,1)S(1)} %bitcast.16), custom_call_target="tpu_custom_call" | custom-call | tf_op jit(solution)/shard_map/stats/pallas_call | solution.py:334
  43.6 11.4 %all_to_all.20.in_ref = f32[64,2,128]{2,1,0:T(2,128)S(1)} all-to-all(f32[64,2,128]{2,1,0:T(2,128)S(1)} %stats.1), channel_id=1, replica_groups=mesh['seq'=32,'head'=16] {'seq'}, dimensions={0} | all-to-all | bytes 131072 | tf_op jit(solution)/shard_map/all_to_all | solution.py:342
  55.6 11.8 %all_to_all.21.refs_3_ = f32[64,2,128]{2,1,0:T(2,128)} all-to-all(f32[64,2,128]{2,1,0:T(2,128)S(1)} %merge.1), channel_id=1, replica_groups=mesh['seq'=32,'head'=16] {'seq'}, dimensions={0} | all-to-all | bytes 131072 | tf_op jit(solution)/shard_map/all_to_all | solution.py:352
  67.4 7.8 %grads.1 = (bf16[32,320,128]{2,1,0:T(8,128)(2,1)}, bf16[4,56,256]{2,1,0:T(8,128)(2,1)}, bf16[4,56,256]{2,1,0:T(8,128)(2,1)}, bf16[4,56,256]{2,1,0:T(8,128)(2,1)}, bf16[4,56,256]{2,1,0:T(8,128)(2,1)}) custom-call(s32[64]{0:T(128)} %copy-done.3, bf16[64,2,64,128]{3,2,1,0:T(8,128)(2,1)} %copy-done, bf16[7,128,256]{2,1,0:T(8,128)(2,1)} %bitcast.17, ...), custom_call_target="tpu_custom_call" | custom-call | tf_op jit(solution)/shard_map/grads/pallas_call | solution.py:359
  75.3 5.2 %all-to-all-start.3 = ((bf16[32,320,128]{2,1,0:T(8,128)(2,1)}), bf16[32,320,128]{2,1,0:T(8,128)(2,1)S(1)}, u32[]{:S(2)}, u32[]{:S(2)}) async-start(bf16[32,320,128]{2,1,0:T(8,128)(2,1)} %get-tuple-element.43), calls=%async_computation.3 | async-start | bytes 5242880 | tf_op jit(solution)/shard_map/all_to_all | solution.py:384
  80.5 1.9 %collective-permute-start.3 = (bf16[4,56,256]{2,1,0:T(8,128)(2,1)}, bf16[4,56,256]{2,1,0:T(8,128)(2,1)S(1)}, u32[]{:S(2)}, u32[]{:S(2)}) collective-permute-start(bf16[4,56,256]{2,1,0:T(8,128)(2,1)} %get-tuple-element.47), channel_id=1, source_target_pairs={{0,1},{1,2},{2,3},{3,4},{4,5},{5,6},{6,7},{7,8},{8,9},{9,10},{10,1... | collective-permute-start | bytes 344072 | tf_op jit(solution)/shard_map/ppermute | solution.py:275
  82.4 8.7 %collective-permute-start.4 = (bf16[4,56,256]{2,1,0:T(8,128)(2,1)}, bf16[4,56,256]{2,1,0:T(8,128)(2,1)S(1)}, u32[]{:S(2)}, u32[]{:S(2)}) collective-permute-start(bf16[4,56,256]{2,1,0:T(8,128)(2,1)} %get-tuple-element.48), channel_id=1, source_target_pairs={{0,15},{1,0},{2,1},{3,2},{4,3},{5,4},{6,5},{7,6},{8,7},{9,8},{10,9... | collective-permute-start | bytes 344072 | tf_op jit(solution)/shard_map/ppermute | solution.py:275
  91.1 1.9 %collective-permute-start.5 = (bf16[4,56,256]{2,1,0:T(8,128)(2,1)}, bf16[4,56,256]{2,1,0:T(8,128)(2,1)S(1)}, u32[]{:S(2)}, u32[]{:S(2)}) collective-permute-start(bf16[4,56,256]{2,1,0:T(8,128)(2,1)} %get-tuple-element.49), channel_id=1, source_target_pairs={{0,2},{1,3},{2,4},{3,5},{4,6},{5,7},{6,8},{7,9},{8,10},{9,11},{10,... | collective-permute-start | bytes 344072 | tf_op jit(solution)/shard_map/ppermute | solution.py:275
  93.0 1.1 collective-permute-done.4.refs_2_
  94.1 8.3 %collective-permute-done.5.refs_3_ = bf16[4,56,256]{2,1,0:T(8,128)(2,1)S(1)} collective-permute-done((bf16[4,56,256]{2,1,0:T(8,128)(2,1)}, bf16[4,56,256]{2,1,0:T(8,128)(2,1)S(1)}, u32[]{:S(2)}, u32[]{:S(2)}) %collective-permute-start.5) | collective-permute-done | bytes 114720 | tf_op jit(solution)/shard_map/ppermute | solution.py:275
  102.4 0.9 copy-done.2
  103.3 2.3 %project.1 = (f32[56,896]{1,0:T(8,128)S(1)}, f32[56,896]{1,0:T(8,128)S(1)}, f32[56,896]{1,0:T(8,128)S(1)}, bf16[56,512]{1,0:T(8,128)(2,1)S(1)}, bf16[56,384]{1,0:T(8,128)(2,1)S(1)}) custom-call(bf16[4,56,256]{2,1,0:T(8,128)(2,1)S(1)} %copy-done.2, bf16[4,56,256]{2,1,0:T(8,128)(2,1)S(1)} %collective-permute-done.3.refs_1_, ...), custom_call_target="tpu_custom_call" | custom-call | tf_op jit(solution)/shard_map/project/pallas_call | solution.py:388
  105.6 1.9 %collective-permute-start.6 = (bf16[56,512]{1,0:T(8,128)(2,1)S(1)}, bf16[56,512]{1,0:T(8,128)(2,1)S(1)}, u32[]{:S(2)}, u32[]{:S(2)}) collective-permute-start(bf16[56,512]{1,0:T(8,128)(2,1)S(1)} %get-tuple-element.57), channel_id=1, source_target_pairs={{0,4},{1,5},{2,6},{3,7},{4,8},{5,9},{6,10},{7,11},{8,12},{9,13},{1... | collective-permute-start | bytes 172040 | tf_op jit(solution)/shard_map/ppermute | solution.py:275
  107.5 7.8 %collective-permute-start.7 = (bf16[56,384]{1,0:T(8,128)(2,1)S(1)}, bf16[56,384]{1,0:T(8,128)(2,1)S(1)}, u32[]{:S(2)}, u32[]{:S(2)}) collective-permute-start(bf16[56,384]{1,0:T(8,128)(2,1)S(1)} %get-tuple-element.58), channel_id=1, source_target_pairs={{0,12},{1,13},{2,14},{3,15},{4,0},{5,1},{6,2},{7,3},{8,4},{9,5},{1... | collective-permute-start | bytes 129032 | tf_op jit(solution)/shard_map/ppermute | solution.py:275
  115.4 4.0 %collective-permute-done.7.across_down_ref = bf16[56,384]{1,0:T(8,128)(2,1)S(1)} collective-permute-done((bf16[56,384]{1,0:T(8,128)(2,1)S(1)}, bf16[56,384]{1,0:T(8,128)(2,1)S(1)}, u32[]{:S(2)}, u32[]{:S(2)}) %collective-permute-start.7) | collective-permute-done | bytes 43040 | tf_op jit(solution)/shard_map/ppermute | solution.py:275
  119.4 7.6 %collective-permute-start.8 = (bf16[56,896]{1,0:T(8,128)(2,1)S(1)}, bf16[56,896]{1,0:T(8,128)(2,1)S(1)}, u32[]{:S(2)}, u32[]{:S(2)}) collective-permute-start(bf16[56,896]{1,0:T(8,128)(2,1)S(1)} %get-tuple-element.59), channel_id=1, source_target_pairs={{0,4},{1,5},{2,6},{3,7},{4,8},{5,9},{6,10},{7,11},{8,12},{9,13},{1... | collective-permute-start | bytes 301064 | tf_op jit(solution)/shard_map/ppermute | solution.py:275
  126.9 2.2 %collective-permute-start.9 = (bf16[56,896]{1,0:T(8,128)(2,1)S(1)}, bf16[56,896]{1,0:T(8,128)(2,1)S(1)}, u32[]{:S(2)}, u32[]{:S(2)}) collective-permute-start(bf16[56,896]{1,0:T(8,128)(2,1)S(1)} %get-tuple-element.60), channel_id=1, source_target_pairs={{0,12},{1,13},{2,14},{3,15},{4,0},{5,1},{6,2},{7,3},{8,4},{9,5},{1... | collective-permute-start | bytes 301064 | tf_op jit(solution)/shard_map/ppermute | solution.py:275
  129.1 2.7 %collective-permute-done.8 = bf16[56,896]{1,0:T(8,128)(2,1)S(1)} collective-permute-done((bf16[56,896]{1,0:T(8,128)(2,1)S(1)}, bf16[56,896]{1,0:T(8,128)(2,1)S(1)}, u32[]{:S(2)}, u32[]{:S(2)}) %collective-permute-start.8) | collective-permute-done | bytes 100384 | tf_op jit(solution)/shard_map/ppermute | solution.py:275
  131.8 8.0 %collective-permute-done.9 = bf16[56,896]{1,0:T(8,128)(2,1)S(1)} collective-permute-done((bf16[56,896]{1,0:T(8,128)(2,1)S(1)}, bf16[56,896]{1,0:T(8,128)(2,1)S(1)}, u32[]{:S(2)}, u32[]{:S(2)}) %collective-permute-start.9) | collective-permute-done | bytes 100384 | tf_op jit(solution)/shard_map/ppermute | solution.py:275
  139.8 0.7 add_bitcast_fusion
  140.5 1.6 %finish.1 = (bf16[16,64,128]{2,1,0:T(8,128)(2,1)}, bf16[16,64,128]{2,1,0:T(8,128)(2,1)}, f32[28,128]{1,0:T(8,128)}, f32[28,128]{1,0:T(8,128)}) custom-call(s32[32]{0:T(128)S(1)} %copy-done.4, bf16[32,320,128]{2,1,0:T(8,128)(2,1)S(1)} %all-to-all-done.3.in_ref), custom_call_target="tpu_custom_call" | custom-call | tf_op jit(solution)/shard_map/finish/pallas_call | solution.py:410
  (41 shorter events, 3.1 us)
Async XLA Ops:
  4.0 9.7 %copy-start.5 = (bf16[896,128]{1,0:T(8,128)(2,1)S(1)}, bf16[896,128]{1,0:T(8,128)(2,1)}, u32[]{:S(2)}) copy-start(bf16[896,128]{1,0:T(8,128)(2,1)} %param.8) | copy-start | bytes 688132
  4.0 9.8 %copy-start.6 = (bf16[896,128]{1,0:T(8,128)(2,1)S(1)}, bf16[896,128]{1,0:T(8,128)(2,1)}, u32[]{:S(2)}) copy-start(bf16[896,128]{1,0:T(8,128)(2,1)} %param.9) | copy-start | bytes 688132
  4.0 23.2 %copy-start.7 = (s32[512,2]{0,1:T(2,128)S(1)}, s32[512,2]{0,1:T(2,128)}, u32[]{:S(2)}) copy-start(s32[512,2]{0,1:T(2,128)} %param.10) | copy-start | bytes 12292
  4.0 37.7 %all-to-all-start = ((bf16[64,2,64,128]{3,2,1,0:T(8,128)(2,1)}), bf16[64,2,64,128]{3,2,1,0:T(8,128)(2,1)S(1)}, u32[]{:S(2)}, u32[]{:S(2)}) async-start(bf16[64,2,64,128]{3,2,1,0:T(8,128)(2,1)} %get-tuple-element.39), calls=%async_computation | async-start | bytes 4194304 | tf_op jit(solution)/shard_map/all_to_all | solution.py:310
  13.8 41.8 %collective-permute-start.2 = (bf16[896,256]{1,0:T(8,128)(2,1)S(1)}, bf16[896,256]{1,0:T(8,128)(2,1)S(1)}, u32[]{:S(2)}, u32[]{:S(2)}) collective-permute-start(bf16[896,256]{1,0:T(8,128)(2,1)S(1)} %constant_dynamic-update-slice_fusion.refs_4_), channel_id=1, source_target_pairs={{0,2},{1,3},{2,4},{3,5},{4,6},{5,7},{6,8},{7,9},{8,10},{9,11},{10,... | collective-permute-start | bytes 1376264 | tf_op jit(solution)/shard_map/ppermute | solution.py:275
  17.1 38.5 %collective-permute-start.1 = (bf16[896,256]{1,0:T(8,128)(2,1)S(1)}, bf16[896,256]{1,0:T(8,128)(2,1)}, u32[]{:S(2)}, u32[]{:S(2)}) collective-permute-start(bf16[896,256]{1,0:T(8,128)(2,1)S(1)} %constant_dynamic-update-slice_fusion.refs_4_), channel_id=1, source_target_pairs={{0,15},{1,0},{2,1},{3,2},{4,3},{5,4},{6,5},{7,6},{8,7},{9,8},{10,9... | collective-permute-start | bytes 1376264 | tf_op jit(solution)/shard_map/ppermute | solution.py:275
  25.2 30.4 %collective-permute-start = (bf16[896,256]{1,0:T(8,128)(2,1)S(1)}, bf16[896,256]{1,0:T(8,128)(2,1)}, u32[]{:S(2)}, u32[]{:S(2)}) collective-permute-start(bf16[896,256]{1,0:T(8,128)(2,1)S(1)} %constant_dynamic-update-slice_fusion.refs_4_), channel_id=1, source_target_pairs={{0,1},{1,2},{2,3},{3,4},{4,5},{5,6},{6,7},{7,8},{8,9},{9,10},{10,1... | collective-permute-start | bytes 1376264 | tf_op jit(solution)/shard_map/ppermute | solution.py:275
  31.0 10.7 %copy-start.3 = (s32[64]{0:T(128)}, s32[64]{0:T(128)S(1)}, u32[]{:S(2)}) copy-start(s32[64]{0:T(128)S(1)} %reshape.57.refs_0_) | copy-start | bytes 772
  38.7 28.7 %copy-start.1 = (bf16[896,256]{1,0:T(8,128)(2,1)}, bf16[896,256]{1,0:T(8,128)(2,1)S(1)}, u32[]{:S(2)}) copy-start(bf16[896,256]{1,0:T(8,128)(2,1)S(1)} %copy.16) | copy-start | bytes 1376260
  38.7 16.2 %copy-start.4 = (s32[32]{0:T(128)S(1)}, s32[32]{0:T(128)}, u32[]{:S(2)}) copy-start(s32[32]{0:T(128)} %get-tuple-element.35.slots_ref) | copy-start | bytes 388
  41.7 25.8 %copy-start = (bf16[64,2,64,128]{3,2,1,0:T(8,128)(2,1)}, bf16[64,2,64,128]{3,2,1,0:T(8,128)(2,1)S(1)}, u32[]{:S(2)}) copy-start(bf16[64,2,64,128]{3,2,1,0:T(8,128)(2,1)S(1)} %all-to-all-done.refs_1_) | copy-start | bytes 6291460
  75.3 65.2 %all-to-all-start.3 = ((bf16[32,320,128]{2,1,0:T(8,128)(2,1)}), bf16[32,320,128]{2,1,0:T(8,128)(2,1)S(1)}, u32[]{:S(2)}, u32[]{:S(2)}) async-start(bf16[32,320,128]{2,1,0:T(8,128)(2,1)} %get-tuple-element.43), calls=%async_computation.3 | async-start | bytes 5242880 | tf_op jit(solution)/shard_map/all_to_all | solution.py:384
  80.5 12.5 %collective-permute-start.3 = (bf16[4,56,256]{2,1,0:T(8,128)(2,1)}, bf16[4,56,256]{2,1,0:T(8,128)(2,1)S(1)}, u32[]{:S(2)}, u32[]{:S(2)}) collective-permute-start(bf16[4,56,256]{2,1,0:T(8,128)(2,1)} %get-tuple-element.47), channel_id=1, source_target_pairs={{0,1},{1,2},{2,3},{3,4},{4,5},{5,6},{6,7},{7,8},{8,9},{9,10},{10,1... | collective-permute-start | bytes 344072 | tf_op jit(solution)/shard_map/ppermute | solution.py:275
  82.4 11.7 %collective-permute-start.4 = (bf16[4,56,256]{2,1,0:T(8,128)(2,1)}, bf16[4,56,256]{2,1,0:T(8,128)(2,1)S(1)}, u32[]{:S(2)}, u32[]{:S(2)}) collective-permute-start(bf16[4,56,256]{2,1,0:T(8,128)(2,1)} %get-tuple-element.48), channel_id=1, source_target_pairs={{0,15},{1,0},{2,1},{3,2},{4,3},{5,4},{6,5},{7,6},{8,7},{9,8},{10,9... | collective-permute-start | bytes 344072 | tf_op jit(solution)/shard_map/ppermute | solution.py:275
  91.1 11.3 %collective-permute-start.5 = (bf16[4,56,256]{2,1,0:T(8,128)(2,1)}, bf16[4,56,256]{2,1,0:T(8,128)(2,1)S(1)}, u32[]{:S(2)}, u32[]{:S(2)}) collective-permute-start(bf16[4,56,256]{2,1,0:T(8,128)(2,1)} %get-tuple-element.49), channel_id=1, source_target_pairs={{0,2},{1,3},{2,4},{3,5},{4,6},{5,7},{6,8},{7,9},{8,10},{9,11},{10,... | collective-permute-start | bytes 344072 | tf_op jit(solution)/shard_map/ppermute | solution.py:275
  102.4 0.9 copy-start.2
  105.6 13.7 %collective-permute-start.6 = (bf16[56,512]{1,0:T(8,128)(2,1)S(1)}, bf16[56,512]{1,0:T(8,128)(2,1)S(1)}, u32[]{:S(2)}, u32[]{:S(2)}) collective-permute-start(bf16[56,512]{1,0:T(8,128)(2,1)S(1)} %get-tuple-element.57), channel_id=1, source_target_pairs={{0,4},{1,5},{2,6},{3,7},{4,8},{5,9},{6,10},{7,11},{8,12},{9,13},{1... | collective-permute-start | bytes 172040 | tf_op jit(solution)/shard_map/ppermute | solution.py:275
  107.5 11.8 %collective-permute-start.7 = (bf16[56,384]{1,0:T(8,128)(2,1)S(1)}, bf16[56,384]{1,0:T(8,128)(2,1)S(1)}, u32[]{:S(2)}, u32[]{:S(2)}) collective-permute-start(bf16[56,384]{1,0:T(8,128)(2,1)S(1)} %get-tuple-element.58), channel_id=1, source_target_pairs={{0,12},{1,13},{2,14},{3,15},{4,0},{5,1},{6,2},{7,3},{8,4},{9,5},{1... | collective-permute-start | bytes 129032 | tf_op jit(solution)/shard_map/ppermute | solution.py:275
  119.4 12.4 %collective-permute-start.8 = (bf16[56,896]{1,0:T(8,128)(2,1)S(1)}, bf16[56,896]{1,0:T(8,128)(2,1)S(1)}, u32[]{:S(2)}, u32[]{:S(2)}) collective-permute-start(bf16[56,896]{1,0:T(8,128)(2,1)S(1)} %get-tuple-element.59), channel_id=1, source_target_pairs={{0,4},{1,5},{2,6},{3,7},{4,8},{5,9},{6,10},{7,11},{8,12},{9,13},{1... | collective-permute-start | bytes 301064 | tf_op jit(solution)/shard_map/ppermute | solution.py:275
  126.9 12.9 %collective-permute-start.9 = (bf16[56,896]{1,0:T(8,128)(2,1)S(1)}, bf16[56,896]{1,0:T(8,128)(2,1)S(1)}, u32[]{:S(2)}, u32[]{:S(2)}) collective-permute-start(bf16[56,896]{1,0:T(8,128)(2,1)S(1)} %get-tuple-element.60), channel_id=1, source_target_pairs={{0,12},{1,13},{2,14},{3,15},{4,0},{5,1},{6,2},{7,3},{8,4},{9,5},{1... | collective-permute-start | bytes 301064 | tf_op jit(solution)/shard_map/ppermute | solution.py:275

commit v5 on v4

--- a/solution.py
+++ b/solution.py
@@ -12,7 +12,6 @@
 CAP = 2
 NEAR = (0, 1, -1, 2)
 FAR = (0, 4, -4, 8)
-LANES = 128
 VMEM_LIMIT = 40 * 1024 * 1024
 LARGE_LIMIT = 60 * 1024 * 1024
 VMEM = pltpu.VMEM
@@ -246,28 +245,19 @@
 
 def project_kernel(*refs):
     near = len(NEAR)
-    rows_refs, weight_refs, out_refs = refs[:near], refs[near:2 * near], refs[2 * near:]
-    own_ref, up_ref, down_ref, across_up_ref, across_down_ref = out_refs
+    rows_refs, weight_refs, own_ref, far_refs = refs[:near], refs[near:2 * near], refs[2 * near + 1], refs[2 * near + 2:-1]
     far, rows, width = rows_refs[0].shape
-    cut = across_up_ref.shape[1]
     half = far // 2
-    sums = []
     for i in range(0, far, half):
         total = jnp.zeros((half * rows, own_ref.shape[1]), jnp.float32)
         for rows_ref, weight_ref in zip(rows_refs, weight_refs):
             total = total + nt_dot(rows_ref[i:i + half].reshape(half * rows, width), weight_ref[...])
-        sums += [total[j * rows:(j + 1) * rows] for j in range(half)]
-    own_ref[...], up_ref[...], down_ref[...] = sums[:3]
-    across_up_ref[...] = sums[3][:, :cut].astype(jnp.bfloat16)
-    across_down_ref[...] = sums[3][:, cut:].astype(jnp.bfloat16)
-
-
-def fold_kernel(up_ref, down_ref, across_up_ref, across_down_ref, up_out_ref, down_out_ref):
-    cut = across_up_ref.shape[1]
-    up_out_ref[:, :cut] = (up_ref[:, :cut] + across_up_ref[...].astype(jnp.float32)).astype(jnp.bfloat16)
-    up_out_ref[:, cut:] = up_ref[:, cut:].astype(jnp.bfloat16)
-    down_out_ref[:, :cut] = down_ref[:, :cut].astype(jnp.bfloat16)
-    down_out_ref[:, cut:] = (down_ref[:, cut:] + across_down_ref[...].astype(jnp.float32)).astype(jnp.bfloat16)
+        for j in range(half):
+            part = total[j * rows:(j + 1) * rows]
+            if i + j == 0:
+                own_ref[...] = part
+            else:
+                far_refs[i + j - 1][...] = part.astype(jnp.bfloat16)
 
 
 def shifted(x, step):
@@ -381,31 +371,24 @@
         name="grads",
     )(blocks, arrived, kv, merged, enc_t)
 
-    returned = lax.all_to_all(back, "seq", split_axis=0, concat_axis=0, tiled=True)
     near_rows = [r if a == 0 else shifted(r, a) for a, r in zip(NEAR, near_rows)]
-    cut = -(-enc_width // (2 * LANES)) * LANES
-    step = FAR[1]
-    own, up, down, across_up, across_down = pl.pallas_call(
+    own, *far_sums, back = pl.pallas_call(
         project_kernel,
         out_shape=(
-            *[jax.ShapeDtypeStruct((rows, enc_width), f32)] * (far - 1),
-            jax.ShapeDtypeStruct((rows, cut), bf16),
-            jax.ShapeDtypeStruct((rows, enc_width - cut), bf16),
+            jax.ShapeDtypeStruct((rows, enc_width), f32),
+            *[jax.ShapeDtypeStruct((rows, enc_width), bf16)] * (far - 1),
+            jax.ShapeDtypeStruct(back_shape, bf16),
         ),
-        in_specs=[spec(VMEM)] * (2 * near),
-        out_specs=(spec(VMEM),) * (far + 1),
-        compiler_params=params(),
+        in_specs=[*[spec(VMEM)] * (2 * near), spec(HBM)],
+        out_specs=(*[spec(VMEM)] * far, spec(HBM)),
+        input_output_aliases={2 * near: far},
+        compiler_params=params(LARGE_LIMIT),
         name="project",
-    )(*near_rows, *near_weights)
-    up, down = pl.pallas_call(
-        fold_kernel,
-        out_shape=(jax.ShapeDtypeStruct((rows, enc_width), bf16),) * 2,
-        in_specs=[spec(VMEM)] * 4,
-        out_specs=(spec(VMEM),) * 2,
-        compiler_params=params(),
-        name="fold",
-    )(up, down, shifted(across_up, step), shifted(across_down, -step))
-    encoding_grad = own + shifted(up, step).astype(f32) + shifted(down, -step).astype(f32)
+    )(*near_rows, *near_weights, back)
+    returned = lax.all_to_all(back, "seq", split_axis=0, concat_axis=0, tiled=True)
+    encoding_grad = own
+    for b, part in zip(FAR[1:], far_sums):
+        encoding_grad = encoding_grad + shifted(part, b).astype(f32)
 
     attended, query_grad, key_weight_grad, value_weight_grad = pl.pallas_call(
         finish_kernel,

time: 143 us -> 143 us (level)
  the two profiles are of different devices: /device:TPU:2 before, /device:TPU:1 now
where the time goes in v5:
time: 143 us
  starting transfers between devices  58.4 us (41%)
  waiting for transfers between devices  27.4 us (19%)
  blocking collectives  24.1 us (17%)
  Pallas kernels  18.7 us (13%)
  local copies, waits for them, and re-layouts  7.41 us (5%)
  matrix products  2.96 us (2%)
  other arithmetic  2.67 us (2%)
    ppermute x9, starting transfers between devices, shifted(): lax.ppermute(x, 'head', [(z, (z + step) % count) for z in range(count)])  42.8 us
    ppermute x9, waiting for transfers between devices, shifted(): lax.ppermute(x, 'head', [(z, (z + step) % count) for z in range(count)])  22.2 us
    all_to_all x1, blocking collectives, on_device(): lax.all_to_all(stats, 'seq', split_axis=0, concat_axis=0, tiled=True)  12.4 us
    all_to_all x1, blocking collectives, on_device(): lax.all_to_all(merged, 'seq', split_axis=0, concat_axis=0, tiled=True)  11.7 us
    all_to_all x1, starting transfers between devices, on_device(): lax.all_to_all(packed, 'seq', split_axis=0, concat_axis=0, tiled=True)  10.7 us
    pallas_call x1, Pallas kernels, on_device(): pl.pallas_call(lambda *refs: grads_kernel(scale, group, *refs), out_shape...  7.81 us
    all_to_all x1, starting transfers between devices, on_device(): lax.all_to_all(back, 'seq', split_axis=0, concat_axis=0, tiled=True)  4.86 us
    reshape x1, local copies, waits for them, and re-layouts, on_device(): flat_enc = encodings.reshape(block_count * block_len, enc_width)  3.57 us
  transfers between devices with their start and end apart: 11, of which 6 were waited for; matrix products, arithmetic and copies ran while one was open for 9% of the time, Pallas kernels for 2%

profile of v5, /device:TPU:1, one launch (start us, length us, event | category | flops | bytes accessed | tf_op | source)
XLA Modules:
  0.0 142.7 jit_solution(14713100949125378947)
XLA Ops:
  0.6 3.3 %pack.1 = (bf16[64,2,64,128]{3,2,1,0:T(8,128)(2,1)}, s32[32]{0:T(128)}) custom-call(s32[2,512]{1,0:T(2,128)} %bitcast.23, bf16[16,64,128]{2,1,0:T(8,128)(2,1)} %bitcast.21, bf16[16,64,128]{2,1,0:T(8,128)(2,1)} %bitcast.22), custom_call_target="tpu_custom_call" | custom-call | tf_op jit(solution)/shard_map/pack/pallas_call | solution.py:280
  3.9 10.7 %all-to-all-start = ((bf16[64,2,64,128]{3,2,1,0:T(8,128)(2,1)}), bf16[64,2,64,128]{3,2,1,0:T(8,128)(2,1)S(1)}, u32[]{:S(2)}, u32[]{:S(2)}) async-start(bf16[64,2,64,128]{3,2,1,0:T(8,128)(2,1)} %get-tuple-element.37), calls=%async_computation | async-start | bytes 4194304 | tf_op jit(solution)/shard_map/all_to_all | solution.py:300
  14.8 2.9 %collective-permute-start.2 = (bf16[896,256]{1,0:T(8,128)(2,1)S(1)}, bf16[896,256]{1,0:T(8,128)(2,1)S(1)}, u32[]{:S(2)}, u32[]{:S(2)}) collective-permute-start(bf16[896,256]{1,0:T(8,128)(2,1)S(1)} %constant_dynamic-update-slice_fusion.refs_4_), channel_id=1, source_target_pairs={{0,2},{1,3},{2,4},{3,5},{4,6},{5,7},{6,8},{7,9},{8,10},{9,11},{10,... | collective-permute-start | bytes 1376264 | tf_op jit(solution)/shard_map/ppermute | solution.py:265
  17.7 8.1 %collective-permute-start.1 = (bf16[896,256]{1,0:T(8,128)(2,1)S(1)}, bf16[896,256]{1,0:T(8,128)(2,1)}, u32[]{:S(2)}, u32[]{:S(2)}) collective-permute-start(bf16[896,256]{1,0:T(8,128)(2,1)S(1)} %constant_dynamic-update-slice_fusion.refs_4_), channel_id=1, source_target_pairs={{0,15},{1,0},{2,1},{3,2},{4,3},{5,4},{6,5},{7,6},{8,7},{9,8},{10,9... | collective-permute-start | bytes 1376264 | tf_op jit(solution)/shard_map/ppermute | solution.py:265
  25.9 1.9 %collective-permute-start = (bf16[896,256]{1,0:T(8,128)(2,1)S(1)}, bf16[896,256]{1,0:T(8,128)(2,1)}, u32[]{:S(2)}, u32[]{:S(2)}) collective-permute-start(bf16[896,256]{1,0:T(8,128)(2,1)S(1)} %constant_dynamic-update-slice_fusion.refs_4_), channel_id=1, source_target_pairs={{0,1},{1,2},{2,3},{3,4},{4,5},{5,6},{6,7},{7,8},{8,9},{9,10},{10,1... | collective-permute-start | bytes 1376264 | tf_op jit(solution)/shard_map/ppermute | solution.py:265
  28.2 0.8 and.26
  29.2 0.7 fusion.4
  30.5 0.5 select_reduce_fusion.1
  31.6 3.6 %copy.18 = bf16[896,896]{0,1:T(8,128)(2,1)} copy(bf16[896,896]{1,0:T(8,128)(2,1)} %bitcast.19) | data formatting | bytes 3211264 | tf_op jit(solution)/shard_map/reshape | solution.py:305
  35.2 3.0 %fusion = bf16[896,256]{0,1:T(8,128)(2,1)} fusion(bf16[896,256]{1,0:T(8,128)(2,1)S(1)} %constant_dynamic-update-slice_fusion.refs_4_, bf16[896,896]{1,0:T(8,128)(2,1)} %bitcast.20), kind=kOutput, calls=%fused_computation.1 | convolution fusion | flops 411271168 | bytes 2523136 | tf_op jit(solution)/shard_map/dot_general | solution.py:306
  38.2 1.2 copy.17
  39.4 3.2 %all-to-all-done.refs_1_ = bf16[64,2,64,128]{3,2,1,0:T(8,128)(2,1)S(1)} async-done(((bf16[64,2,64,128]{3,2,1,0:T(8,128)(2,1)}), bf16[64,2,64,128]{3,2,1,0:T(8,128)(2,1)S(1)}, u32[]{:S(2)}, u32[]{:S(2)}) %all-to-all-start) | async-done | bytes 2097184 | tf_op jit(solution)/shard_map/all_to_all | solution.py:300
  42.6 1.9 %stats.1 = f32[64,2,128]{2,1,0:T(2,128)S(1)} custom-call(s32[64]{0:T(128)S(1)} %reshape.57.refs_0_, bf16[64,2,64,128]{3,2,1,0:T(8,128)(2,1)S(1)} %all-to-all-done.refs_1_, bf16[7,128,256]{2,1,0:T(8,128)(2,1)S(1)} %bitcast.16), custom_call_target="tpu_custom_call" | custom-call | tf_op jit(solution)/shard_map/stats/pallas_call | solution.py:324
  44.6 12.4 %all_to_all.20.in_ref = f32[64,2,128]{2,1,0:T(2,128)S(1)} all-to-all(f32[64,2,128]{2,1,0:T(2,128)S(1)} %stats.1), channel_id=1, replica_groups=mesh['seq'=32,'head'=16] {'seq'}, dimensions={0} | all-to-all | bytes 131072 | tf_op jit(solution)/shard_map/all_to_all | solution.py:332
  57.0 0.6 merge.1
  57.7 11.7 %all_to_all.21.refs_3_ = f32[64,2,128]{2,1,0:T(2,128)} all-to-all(f32[64,2,128]{2,1,0:T(2,128)S(1)} %merge.1), channel_id=1, replica_groups=mesh['seq'=32,'head'=16] {'seq'}, dimensions={0} | all-to-all | bytes 131072 | tf_op jit(solution)/shard_map/all_to_all | solution.py:342
  69.4 7.8 %grads.1 = (bf16[32,320,128]{2,1,0:T(8,128)(2,1)}, bf16[4,56,256]{2,1,0:T(8,128)(2,1)}, bf16[4,56,256]{2,1,0:T(8,128)(2,1)}, bf16[4,56,256]{2,1,0:T(8,128)(2,1)}, bf16[4,56,256]{2,1,0:T(8,128)(2,1)}) custom-call(s32[64]{0:T(128)} %copy-done.2, bf16[64,2,64,128]{3,2,1,0:T(8,128)(2,1)} %copy-done, bf16[7,128,256]{2,1,0:T(8,128)(2,1)} %bitcast.17, ...), custom_call_target="tpu_custom_call" | custom-call | tf_op jit(solution)/shard_map/grads/pallas_call | solution.py:349
  77.2 1.9 %collective-permute-start.3 = (bf16[4,56,256]{2,1,0:T(8,128)(2,1)}, bf16[4,56,256]{2,1,0:T(8,128)(2,1)S(1)}, u32[]{:S(2)}, u32[]{:S(2)}) collective-permute-start(bf16[4,56,256]{2,1,0:T(8,128)(2,1)} %get-tuple-element.42), channel_id=1, source_target_pairs={{0,1},{1,2},{2,3},{3,4},{4,5},{5,6},{6,7},{7,8},{8,9},{9,10},{10,1... | collective-permute-start | bytes 344072 | tf_op jit(solution)/shard_map/ppermute | solution.py:265
  79.1 8.4 %collective-permute-start.4 = (bf16[4,56,256]{2,1,0:T(8,128)(2,1)}, bf16[4,56,256]{2,1,0:T(8,128)(2,1)S(1)}, u32[]{:S(2)}, u32[]{:S(2)}) collective-permute-start(bf16[4,56,256]{2,1,0:T(8,128)(2,1)} %get-tuple-element.43), channel_id=1, source_target_pairs={{0,15},{1,0},{2,1},{3,2},{4,3},{5,4},{6,5},{7,6},{8,7},{9,8},{10,9... | collective-permute-start | bytes 344072 | tf_op jit(solution)/shard_map/ppermute | solution.py:265
  87.6 1.9 %collective-permute-start.5 = (bf16[4,56,256]{2,1,0:T(8,128)(2,1)}, bf16[4,56,256]{2,1,0:T(8,128)(2,1)S(1)}, u32[]{:S(2)}, u32[]{:S(2)}) collective-permute-start(bf16[4,56,256]{2,1,0:T(8,128)(2,1)} %get-tuple-element.44), channel_id=1, source_target_pairs={{0,2},{1,3},{2,4},{3,5},{4,6},{5,7},{6,8},{7,9},{8,10},{9,11},{10,... | collective-permute-start | bytes 344072 | tf_op jit(solution)/shard_map/ppermute | solution.py:265
  90.0 8.5 %collective-permute-done.5.refs_3_ = bf16[4,56,256]{2,1,0:T(8,128)(2,1)S(1)} collective-permute-done((bf16[4,56,256]{2,1,0:T(8,128)(2,1)}, bf16[4,56,256]{2,1,0:T(8,128)(2,1)S(1)}, u32[]{:S(2)}, u32[]{:S(2)}) %collective-permute-start.5) | collective-permute-done | bytes 114720 | tf_op jit(solution)/shard_map/ppermute | solution.py:265
  98.5 0.6 copy-done.11
  99.1 3.5 %project.1 = (f32[56,896]{1,0:T(8,128)}, bf16[56,896]{1,0:T(8,128)(2,1)}, bf16[56,896]{1,0:T(8,128)(2,1)}, bf16[56,896]{1,0:T(8,128)(2,1)}, bf16[32,320,128]{2,1,0:T(8,128)(2,1)}) custom-call(bf16[4,56,256]{2,1,0:T(8,128)(2,1)} %get-tuple-element.41.refs_0_, bf16[4,56,256]{2,1,0:T(8,128)(2,1)} %copy-done.9, ...), custom_call_target="tpu_custom_call", output_to_operand_aliasing={{4}: (8, {})} | custom-call | tf_op jit(solution)/shard_map/project/pallas_call | solution.py:375
  102.6 4.9 %all-to-all-start.3 = ((bf16[32,320,128]{2,1,0:T(8,128)(2,1)}), bf16[32,320,128]{2,1,0:T(8,128)(2,1)S(1)}, u32[]{:S(2)}, u32[]{:S(2)}) async-start(bf16[32,320,128]{2,1,0:T(8,128)(2,1)} %get-tuple-element.50), calls=%async_computation.3 | async-start | bytes 5242880 | tf_op jit(solution)/shard_map/all_to_all | solution.py:388
  107.5 1.9 %collective-permute-start.6 = (bf16[56,896]{1,0:T(8,128)(2,1)S(1)}, bf16[56,896]{1,0:T(8,128)(2,1)S(1)}, u32[]{:S(2)}, u32[]{:S(2)}) collective-permute-start(bf16[56,896]{1,0:T(8,128)(2,1)S(1)} %copy-done.15), channel_id=1, source_target_pairs={{0,4},{1,5},{2,6},{3,7},{4,8},{5,9},{6,10},{7,11},{8,12},{9,13},{1... | collective-permute-start | bytes 301064 | tf_op jit(solution)/shard_map/ppermute | solution.py:265
  109.4 7.3 %collective-permute-start.7 = (bf16[56,896]{1,0:T(8,128)(2,1)S(1)}, bf16[56,896]{1,0:T(8,128)(2,1)S(1)}, u32[]{:S(2)}, u32[]{:S(2)}) collective-permute-start(bf16[56,896]{1,0:T(8,128)(2,1)S(1)} %copy-done.14), channel_id=1, source_target_pairs={{0,12},{1,13},{2,14},{3,15},{4,0},{5,1},{6,2},{7,3},{8,4},{9,5},{1... | collective-permute-start | bytes 301064 | tf_op jit(solution)/shard_map/ppermute | solution.py:265
  116.7 8.4 %collective-permute-start.8 = (bf16[56,896]{1,0:T(8,128)(2,1)S(1)}, bf16[56,896]{1,0:T(8,128)(2,1)S(1)}, u32[]{:S(2)}, u32[]{:S(2)}) collective-permute-start(bf16[56,896]{1,0:T(8,128)(2,1)S(1)} %copy-done.13), channel_id=1, source_target_pairs={{0,8},{1,9},{2,10},{3,11},{4,12},{5,13},{6,14},{7,15},{8,0},{9,1},... | collective-permute-start | bytes 301064 | tf_op jit(solution)/shard_map/ppermute | solution.py:265
  125.1 2.3 %collective-permute-done.7 = bf16[56,896]{1,0:T(8,128)(2,1)S(1)} collective-permute-done((bf16[56,896]{1,0:T(8,128)(2,1)S(1)}, bf16[56,896]{1,0:T(8,128)(2,1)S(1)}, u32[]{:S(2)}, u32[]{:S(2)}) %collective-permute-start.7) | collective-permute-done | bytes 100384 | tf_op jit(solution)/shard_map/ppermute | solution.py:265
  127.5 10.9 %collective-permute-done.8 = bf16[56,896]{1,0:T(8,128)(2,1)S(1)} collective-permute-done((bf16[56,896]{1,0:T(8,128)(2,1)S(1)}, bf16[56,896]{1,0:T(8,128)(2,1)S(1)}, u32[]{:S(2)}, u32[]{:S(2)}) %collective-permute-start.8) | collective-permute-done | bytes 100384 | tf_op jit(solution)/shard_map/ppermute | solution.py:265
  138.4 0.7 add_bitcast_fusion
  139.1 2.0 %all-to-all-done.3.in_ref = bf16[32,320,128]{2,1,0:T(8,128)(2,1)S(1)} async-done(((bf16[32,320,128]{2,1,0:T(8,128)(2,1)}), bf16[32,320,128]{2,1,0:T(8,128)(2,1)S(1)}, u32[]{:S(2)}, u32[]{:S(2)}) %all-to-all-start.3) | async-done | bytes 2621472 | tf_op jit(solution)/shard_map/all_to_all | solution.py:388
  141.1 1.6 %finish.1 = (bf16[16,64,128]{2,1,0:T(8,128)(2,1)}, bf16[16,64,128]{2,1,0:T(8,128)(2,1)}, f32[28,128]{1,0:T(8,128)}, f32[28,128]{1,0:T(8,128)}) custom-call(s32[32]{0:T(128)S(1)} %copy-done.3, bf16[32,320,128]{2,1,0:T(8,128)(2,1)S(1)} %all-to-all-done.3.in_ref), custom_call_target="tpu_custom_call" | custom-call | tf_op jit(solution)/shard_map/finish/pallas_call | solution.py:393
  (54 shorter events, 2.4 us)
Async XLA Ops:
  3.9 10.8 %copy-start.6 = (bf16[896,128]{1,0:T(8,128)(2,1)S(1)}, bf16[896,128]{1,0:T(8,128)(2,1)}, u32[]{:S(2)}) copy-start(bf16[896,128]{1,0:T(8,128)(2,1)} %param.8) | copy-start | bytes 688132
  3.9 10.8 %copy-start.7 = (bf16[896,128]{1,0:T(8,128)(2,1)S(1)}, bf16[896,128]{1,0:T(8,128)(2,1)}, u32[]{:S(2)}) copy-start(bf16[896,128]{1,0:T(8,128)(2,1)} %param.9) | copy-start | bytes 688132
  3.9 23.9 %copy-start.12 = (s32[512,2]{0,1:T(2,128)S(1)}, s32[512,2]{0,1:T(2,128)}, u32[]{:S(2)}) copy-start(s32[512,2]{0,1:T(2,128)} %param.10) | copy-start | bytes 12292
  3.9 38.7 %all-to-all-start = ((bf16[64,2,64,128]{3,2,1,0:T(8,128)(2,1)}), bf16[64,2,64,128]{3,2,1,0:T(8,128)(2,1)S(1)}, u32[]{:S(2)}, u32[]{:S(2)}) async-start(bf16[64,2,64,128]{3,2,1,0:T(8,128)(2,1)} %get-tuple-element.37), calls=%async_computation | async-start | bytes 4194304 | tf_op jit(solution)/shard_map/all_to_all | solution.py:300
  14.8 20.4 %copy-start.4 = (bf16[896,256]{1,0:T(8,128)(2,1)}, bf16[896,256]{1,0:T(8,128)(2,1)S(1)}, u32[]{:S(2)}) copy-start(bf16[896,256]{1,0:T(8,128)(2,1)S(1)} %constant_dynamic-update-slice_fusion.refs_4_) | copy-start | bytes 1376260
  14.8 42.8 %collective-permute-start.2 = (bf16[896,256]{1,0:T(8,128)(2,1)S(1)}, bf16[896,256]{1,0:T(8,128)(2,1)S(1)}, u32[]{:S(2)}, u32[]{:S(2)}) collective-permute-start(bf16[896,256]{1,0:T(8,128)(2,1)S(1)} %constant_dynamic-update-slice_fusion.refs_4_), channel_id=1, source_target_pairs={{0,2},{1,3},{2,4},{3,5},{4,6},{5,7},{6,8},{7,9},{8,10},{9,11},{10,... | collective-permute-start | bytes 1376264 | tf_op jit(solution)/shard_map/ppermute | solution.py:265
  17.7 39.9 %collective-permute-start.1 = (bf16[896,256]{1,0:T(8,128)(2,1)S(1)}, bf16[896,256]{1,0:T(8,128)(2,1)}, u32[]{:S(2)}, u32[]{:S(2)}) collective-permute-start(bf16[896,256]{1,0:T(8,128)(2,1)S(1)} %constant_dynamic-update-slice_fusion.refs_4_), channel_id=1, source_target_pairs={{0,15},{1,0},{2,1},{3,2},{4,3},{5,4},{6,5},{7,6},{8,7},{9,8},{10,9... | collective-permute-start | bytes 1376264 | tf_op jit(solution)/shard_map/ppermute | solution.py:265
  25.9 31.8 %collective-permute-start = (bf16[896,256]{1,0:T(8,128)(2,1)S(1)}, bf16[896,256]{1,0:T(8,128)(2,1)}, u32[]{:S(2)}, u32[]{:S(2)}) collective-permute-start(bf16[896,256]{1,0:T(8,128)(2,1)S(1)} %constant_dynamic-update-slice_fusion.refs_4_), channel_id=1, source_target_pairs={{0,1},{1,2},{2,3},{3,4},{4,5},{5,6},{6,7},{7,8},{8,9},{9,10},{10,1... | collective-permute-start | bytes 1376264 | tf_op jit(solution)/shard_map/ppermute | solution.py:265
  31.6 11.0 %copy-start.2 = (s32[64]{0:T(128)}, s32[64]{0:T(128)S(1)}, u32[]{:S(2)}) copy-start(s32[64]{0:T(128)S(1)} %reshape.57.refs_0_) | copy-start | bytes 772
  38.2 18.8 %copy-start.3 = (s32[32]{0:T(128)S(1)}, s32[32]{0:T(128)}, u32[]{:S(2)}) copy-start(s32[32]{0:T(128)} %get-tuple-element.33.slots_ref) | copy-start | bytes 388
  39.4 30.0 %copy-start.1 = (bf16[896,256]{1,0:T(8,128)(2,1)}, bf16[896,256]{1,0:T(8,128)(2,1)S(1)}, u32[]{:S(2)}) copy-start(bf16[896,256]{1,0:T(8,128)(2,1)S(1)} %copy.17) | copy-start | bytes 1376260
  42.6 26.8 %copy-start = (bf16[64,2,64,128]{3,2,1,0:T(8,128)(2,1)}, bf16[64,2,64,128]{3,2,1,0:T(8,128)(2,1)S(1)}, u32[]{:S(2)}) copy-start(bf16[64,2,64,128]{3,2,1,0:T(8,128)(2,1)S(1)} %all-to-all-done.refs_1_) | copy-start | bytes 6291460
  57.6 19.6 %copy-start.5 = (bf16[896,256]{1,0:T(8,128)(2,1)}, bf16[896,256]{1,0:T(8,128)(2,1)S(1)}, u32[]{:S(2)}) copy-start(bf16[896,256]{1,0:T(8,128)(2,1)S(1)} %collective-permute-done.2.refs_7_) | copy-start | bytes 1376260
  77.2 12.3 %collective-permute-start.3 = (bf16[4,56,256]{2,1,0:T(8,128)(2,1)}, bf16[4,56,256]{2,1,0:T(8,128)(2,1)S(1)}, u32[]{:S(2)}, u32[]{:S(2)}) collective-permute-start(bf16[4,56,256]{2,1,0:T(8,128)(2,1)} %get-tuple-element.42), channel_id=1, source_target_pairs={{0,1},{1,2},{2,3},{3,4},{4,5},{5,6},{6,7},{7,8},{8,9},{9,10},{10,1... | collective-permute-start | bytes 344072 | tf_op jit(solution)/shard_map/ppermute | solution.py:265
  79.1 10.9 %collective-permute-start.4 = (bf16[4,56,256]{2,1,0:T(8,128)(2,1)}, bf16[4,56,256]{2,1,0:T(8,128)(2,1)S(1)}, u32[]{:S(2)}, u32[]{:S(2)}) collective-permute-start(bf16[4,56,256]{2,1,0:T(8,128)(2,1)} %get-tuple-element.43), channel_id=1, source_target_pairs={{0,15},{1,0},{2,1},{3,2},{4,3},{5,4},{6,5},{7,6},{8,7},{9,8},{10,9... | collective-permute-start | bytes 344072 | tf_op jit(solution)/shard_map/ppermute | solution.py:265
  87.6 10.9 %collective-permute-start.5 = (bf16[4,56,256]{2,1,0:T(8,128)(2,1)}, bf16[4,56,256]{2,1,0:T(8,128)(2,1)S(1)}, u32[]{:S(2)}, u32[]{:S(2)}) collective-permute-start(bf16[4,56,256]{2,1,0:T(8,128)(2,1)} %get-tuple-element.44), channel_id=1, source_target_pairs={{0,2},{1,3},{2,4},{3,5},{4,6},{5,7},{6,8},{7,9},{8,10},{9,11},{10,... | collective-permute-start | bytes 344072 | tf_op jit(solution)/shard_map/ppermute | solution.py:265
  89.5 9.0 %copy-start.9 = (bf16[4,56,256]{2,1,0:T(8,128)(2,1)}, bf16[4,56,256]{2,1,0:T(8,128)(2,1)S(1)}, u32[]{:S(2)}) copy-start(bf16[4,56,256]{2,1,0:T(8,128)(2,1)S(1)} %collective-permute-done.3.refs_1_) | copy-start | bytes 344068
  90.0 8.5 %copy-start.10 = (bf16[4,56,256]{2,1,0:T(8,128)(2,1)}, bf16[4,56,256]{2,1,0:T(8,128)(2,1)S(1)}, u32[]{:S(2)}) copy-start(bf16[4,56,256]{2,1,0:T(8,128)(2,1)S(1)} %collective-permute-done.4.refs_2_) | copy-start | bytes 344068
  98.5 0.6 copy-start.11
  102.6 4.9 %copy-start.15 = (bf16[56,896]{1,0:T(8,128)(2,1)S(1)}, bf16[56,896]{1,0:T(8,128)(2,1)}, u32[]{:S(2)}) copy-start(bf16[56,896]{1,0:T(8,128)(2,1)} %get-tuple-element.54) | copy-start | bytes 301060
  102.6 6.8 %copy-start.14 = (bf16[56,896]{1,0:T(8,128)(2,1)S(1)}, bf16[56,896]{1,0:T(8,128)(2,1)}, u32[]{:S(2)}) copy-start(bf16[56,896]{1,0:T(8,128)(2,1)} %get-tuple-element.55) | copy-start | bytes 301060
  102.6 14.1 %copy-start.13 = (bf16[56,896]{1,0:T(8,128)(2,1)S(1)}, bf16[56,896]{1,0:T(8,128)(2,1)}, u32[]{:S(2)}) copy-start(bf16[56,896]{1,0:T(8,128)(2,1)} %get-tuple-element.56) | copy-start | bytes 301060
  102.6 35.7 %copy-start.8 = (f32[56,896]{1,0:T(8,128)S(1)}, f32[56,896]{1,0:T(8,128)}, u32[]{:S(2)}) copy-start(f32[56,896]{1,0:T(8,128)} %get-tuple-element.53) | copy-start | bytes 602116
  102.6 38.5 %all-to-all-start.3 = ((bf16[32,320,128]{2,1,0:T(8,128)(2,1)}), bf16[32,320,128]{2,1,0:T(8,128)(2,1)S(1)}, u32[]{:S(2)}, u32[]{:S(2)}) async-start(bf16[32,320,128]{2,1,0:T(8,128)(2,1)} %get-tuple-element.50), calls=%async_computation.3 | async-start | bytes 5242880 | tf_op jit(solution)/shard_map/all_to_all | solution.py:388
  107.5 17.6 %collective-permute-start.6 = (bf16[56,896]{1,0:T(8,128)(2,1)S(1)}, bf16[56,896]{1,0:T(8,128)(2,1)S(1)}, u32[]{:S(2)}, u32[]{:S(2)}) collective-permute-start(bf16[56,896]{1,0:T(8,128)(2,1)S(1)} %copy-done.15), channel_id=1, source_target_pairs={{0,4},{1,5},{2,6},{3,7},{4,8},{5,9},{6,10},{7,11},{8,12},{9,13},{1... | collective-permute-start | bytes 301064 | tf_op jit(solution)/shard_map/ppermute | solution.py:265
  109.4 18.0 %collective-permute-start.7 = (bf16[56,896]{1,0:T(8,128)(2,1)S(1)}, bf16[56,896]{1,0:T(8,128)(2,1)S(1)}, u32[]{:S(2)}, u32[]{:S(2)}) collective-permute-start(bf16[56,896]{1,0:T(8,128)(2,1)S(1)} %copy-done.14), channel_id=1, source_target_pairs={{0,12},{1,13},{2,14},{3,15},{4,0},{5,1},{6,2},{7,3},{8,4},{9,5},{1... | collective-permute-start | bytes 301064 | tf_op jit(solution)/shard_map/ppermute | solution.py:265
  116.7 21.6 %collective-permute-start.8 = (bf16[56,896]{1,0:T(8,128)(2,1)S(1)}, bf16[56,896]{1,0:T(8,128)(2,1)S(1)}, u32[]{:S(2)}, u32[]{:S(2)}) collective-permute-start(bf16[56,896]{1,0:T(8,128)(2,1)S(1)} %copy-done.13), channel_id=1, source_target_pairs={{0,8},{1,9},{2,10},{3,11},{4,12},{5,13},{6,14},{7,15},{8,0},{9,1},... | collective-permute-start | bytes 301064 | tf_op jit(solution)/shard_map/ppermute | solution.py:265

commit v6 on v5

--- a/solution.py
+++ b/solution.py
@@ -10,8 +10,9 @@
 SEGMENT = 64
 NEIGH = 2
 CAP = 2
+PLACES = 8
 NEAR = (0, 1, -1, 2)
-FAR = (0, 4, -4, 8)
+FAR = (0, 4, 8, -4)
 VMEM_LIMIT = 40 * 1024 * 1024
 LARGE_LIMIT = 60 * 1024 * 1024
 VMEM = pltpu.VMEM
@@ -87,8 +88,10 @@
     return diagonal(0), diagonal(1), keys, values
 
 
-def stats_kernel(scale, unroll, blocks_ref, x_ref, kv_ref, out_ref):
-    def step(s, _):
+def stats_kernel(scale, blocks_ref, to_ref, x_ref, kv_ref, pair_ref, slot_ref, send_ref, places):
+    places[...] = jnp.zeros_like(places)
+    left = lax.broadcasted_iota(jnp.int32, (1, CAP * SEGMENT), 1) < SEGMENT
+    for s in range(x_ref.shape[0] // CAP):
         kv_a = kv_ref[blocks_ref[CAP * s]]
         kv_b = kv_ref[blocks_ref[CAP * s + 1]]
         q_diag, g_diag, keys, values = pair_operands(x_ref, s, kv_a, kv_b)
@@ -98,29 +101,36 @@
         total = jnp.sum(weight, axis=0, keepdims=True)
         prob_grad = nt_dot(values, g_diag)
         mean = jnp.sum(weight * prob_grad, axis=0, keepdims=True) / total
-        both = jnp.concatenate([top + jnp.log(total), mean], axis=0)
-        out_ref[CAP * s] = both
-        out_ref[CAP * s + 1] = pltpu.roll(both, SEGMENT, 1)
-        return 0
-
-    lax.fori_loop(0, x_ref.shape[0] // CAP, step, 0, unroll=unroll)
-
-
-def merge_kernel(slots_ref, in_ref, out_ref):
+        lse = top + jnp.log(total)
+        pair_ref[s] = jnp.concatenate([lse, mean], axis=0)
+        row_a = jnp.where(left, lse, pltpu.roll(mean, SEGMENT, 1))
+        row_b = jnp.where(left, pltpu.roll(lse, SEGMENT, 1), mean)
+        slot_ref[CAP * s:CAP * s + 1, :] = row_a
+        slot_ref[CAP * s + 1:CAP * s + 2, :] = row_b
+        places[pl.ds(to_ref[CAP * s], 1), :] = row_a
+        places[pl.ds(to_ref[CAP * s + 1], 1), :] = row_b
+    send_ref[...] = places[:send_ref.shape[0]]
+
+
+def swap_kernel(slots_ref, in_ref, out_ref):
     out_ref[...] = jnp.zeros_like(out_ref)
     for c in range(slots_ref.shape[0] // NEIGH):
         slot_a, slot_b = slots_ref[NEIGH * c], slots_ref[NEIGH * c + 1]
-        one, two = in_ref[slot_a], in_ref[slot_b]
-        lse_a, lse_b = one[0:1], two[0:1]
-        top = jnp.maximum(lse_a, lse_b)
-        lse = top + jnp.log(jnp.exp(lse_a - top) + jnp.exp(lse_b - top))
-        delta = jnp.exp(lse_a - lse) * one[1:2] + jnp.exp(lse_b - lse) * two[1:2]
-        both = jnp.concatenate([lse, delta], axis=0)
-        out_ref[slot_a] = both
-        out_ref[slot_b] = both
-
-
-def grads_kernel(scale, group, blocks_ref, x_hbm, kv_ref, stats_ref, enc_hbm, *refs):
+        out_ref[pl.ds(slot_a, 1), :] = in_ref[pl.ds(slot_b, 1), :]
+        out_ref[pl.ds(slot_b, 1), :] = in_ref[pl.ds(slot_a, 1), :]
+
+
+def merge_stats(own, row_a, row_b, left):
+    other_lse = jnp.where(left, row_a, pltpu.roll(row_b, SEGMENT, 1))
+    other_mean = jnp.where(left, pltpu.roll(row_a, SEGMENT, 1), row_b)
+    lse, mean = own[0:1], own[1:2]
+    top = jnp.maximum(lse, other_lse)
+    merged = top + jnp.log(jnp.exp(lse - top) + jnp.exp(other_lse - top))
+    delta = jnp.exp(lse - merged) * mean + jnp.exp(other_lse - merged) * other_mean
+    return merged, delta
+
+
+def grads_kernel(scale, group, blocks_ref, from_ref, x_hbm, kv_ref, own_ref, other_ref, enc_hbm, *refs):
     near = len(NEAR)
     out_ref = refs[0]
     rows_refs = refs[1:1 + near]
@@ -140,7 +150,7 @@
     fetch.start()
     acc_k[...] = jnp.zeros_like(acc_k)
     acc_v[...] = jnp.zeros_like(acc_v)
-    left = lax.broadcasted_iota(jnp.int32, (2, pair), 1) < SEGMENT
+    left = lax.broadcasted_iota(jnp.int32, (1, pair), 1) < SEGMENT
 
     def step(i, _):
         arrival(i).wait()
@@ -151,14 +161,19 @@
             pair_operands(x_ref, s, kv_ref[a], kv_ref[b]) for s, a, b in zip(sources, first, second)
         ]
         stats = [
-            jnp.where(left, stats_ref[CAP * s], pltpu.roll(stats_ref[CAP * s + 1], SEGMENT, 1))
+            merge_stats(
+                own_ref[s],
+                other_ref[pl.ds(from_ref[CAP * s], 1), :],
+                other_ref[pl.ds(from_ref[CAP * s + 1], 1), :],
+                left,
+            )
             for s in sources
         ]
         scores = [nt_dot(keys, q) * scale for q, _, keys, _ in operands]
         prob_grads = [nt_dot(values, g) for _, g, _, values in operands]
-        probs = [jnp.exp(x - stat[0:1]) for x, stat in zip(scores, stats)]
+        probs = [jnp.exp(x - stat[0]) for x, stat in zip(scores, stats)]
         score_grads = [
-            (p * (x - stat[1:2]) * scale).astype(jnp.bfloat16)
+            (p * (x - stat[1]) * scale).astype(jnp.bfloat16)
             for p, x, stat in zip(probs, prob_grads, stats)
         ]
         probs = [p.astype(jnp.bfloat16) for p in probs]
@@ -245,7 +260,7 @@
 
 def project_kernel(*refs):
     near = len(NEAR)
-    rows_refs, weight_refs, own_ref, far_refs = refs[:near], refs[near:2 * near], refs[2 * near + 1], refs[2 * near + 2:-1]
+    rows_refs, weight_refs, own_ref, far_refs = refs[:near], refs[near:2 * near], refs[2 * near], refs[2 * near + 1:]
     far, rows, width = rows_refs[0].shape
     half = far // 2
     for i in range(0, far, half):
@@ -301,7 +316,6 @@
 
     key_weight, value_weight, slots = lax.optimization_barrier((key_weight, value_weight, slots))
     weights = jnp.concatenate([key_weight, value_weight], axis=1)
-    near_weights = [weights if a == 0 else shifted(weights, a) for a in NEAR]
     flat_enc = encodings.reshape(block_count * block_len, enc_width)
     kv = jnp.dot(flat_enc, weights, preferred_element_type=f32).astype(bf16)
     kv = kv.reshape(block_count, block_len, 2 * head_dim)
@@ -310,36 +324,67 @@
     enc_t = flat_enc.T
 
     tables = reads.reshape(seq_count, read_count)
-    mine = (tables // block_count) == me
+    holders = tables // block_count
+    partners = holders.reshape(-1, NEIGH)[:, ::-1].reshape(seq_count, read_count)
+    mine = holders == me
     rank = jnp.cumsum(mine.astype(jnp.int32), axis=1)
-    blocks = jnp.stack(
-        [
-            jnp.sum(jnp.where(mine & (rank == k + 1), tables % block_count, 0), axis=1)
-            for k in range(CAP)
-        ],
-        axis=1,
+    code = (tables % block_count) + (partners + 1) * block_count
+    code = jnp.stack(
+        [jnp.sum(jnp.where(mine & (rank == k + 1), code, 0), axis=1) for k in range(CAP)], axis=1
     ).reshape(slot_count)
-    kv, enc_t, blocks = lax.optimization_barrier((kv, enc_t, blocks))
-
-    stats = pl.pallas_call(
-        lambda *refs: stats_kernel(scale, seq_count, *refs),
-        out_shape=jax.ShapeDtypeStruct((slot_count, 2, CAP * SEGMENT), f32),
-        in_specs=[spec(SMEM), spec(VMEM), spec(VMEM)],
-        out_specs=spec(VMEM),
+    blocks = code % block_count
+    partner = code // block_count - 1
+    taken = partner >= 0
+    order = jnp.arange(slot_count)
+    same = (partner[:, None] == partner[None, :]) & (order[None, :] < order[:, None])
+    place = jnp.sum(same.astype(jnp.int32), axis=1)
+    twin = place.reshape(-1, CAP)[:, ::-1].reshape(slot_count)
+    send_to = jnp.where(taken, partner * PLACES + jnp.minimum(place, PLACES - 1), seq_count * PLACES)
+    taken_from = jnp.minimum(jnp.where(partner == me, twin, place), PLACES - 1)
+    taken_from = jnp.where(taken, partner * PLACES + taken_from, 0)
+    pairs = jax.nn.one_hot(holders.reshape(-1, NEIGH), seq_count, dtype=bf16)
+    shared = lax.dot_general(
+        pairs[:, 0], pairs[:, 1], (((0,), (0,)), ((), ())), preferred_element_type=f32
+    )
+    fits = jnp.max(shared + shared.T) <= PLACES
+    taken_from = jnp.where(fits, taken_from, order)
+    kv, enc_t, blocks, send_to, taken_from, fits, weights = lax.optimization_barrier(
+        (kv, enc_t, blocks, send_to, taken_from, fits, weights)
+    )
+    near_weights = [weights if a == 0 else shifted(weights, a) for a in NEAR]
+
+    place_count = seq_count * PLACES
+    own_stats, slot_stats, sent = pl.pallas_call(
+        lambda *refs: stats_kernel(scale, *refs),
+        out_shape=(
+            jax.ShapeDtypeStruct((seq_count, 2, CAP * SEGMENT), f32),
+            jax.ShapeDtypeStruct((slot_count, CAP * SEGMENT), f32),
+            jax.ShapeDtypeStruct((place_count, CAP * SEGMENT), f32),
+        ),
+        in_specs=[spec(SMEM), spec(SMEM), spec(VMEM), spec(VMEM)],
+        out_specs=(spec(VMEM),) * 3,
+        scratch_shapes=[pltpu.VMEM((place_count + 8, CAP * SEGMENT), f32)],
         compiler_params=params(),
         name="stats",
-    )(blocks, arrived, kv)
-    stats = lax.all_to_all(stats, "seq", split_axis=0, concat_axis=0, tiled=True)
-    merged = pl.pallas_call(
-        merge_kernel,
-        out_shape=jax.ShapeDtypeStruct(stats.shape, f32),
-        in_specs=[spec(SMEM), spec(VMEM)],
-        out_specs=spec(VMEM),
-        compiler_params=params(),
-        name="merge",
-    )(slots, stats)
-    merged, *near_weights = lax.optimization_barrier((merged, *near_weights))
-    merged = lax.all_to_all(merged, "seq", split_axis=0, concat_axis=0, tiled=True)
+    )(blocks, send_to, arrived, kv)
+
+    def one_hop(sent, slot_stats, slots):
+        return lax.all_to_all(sent, "seq", split_axis=0, concat_axis=0, tiled=True)
+
+    def two_hops(sent, slot_stats, slots):
+        at_reader = lax.all_to_all(slot_stats, "seq", split_axis=0, concat_axis=0, tiled=True)
+        swapped = pl.pallas_call(
+            swap_kernel,
+            out_shape=jax.ShapeDtypeStruct(slot_stats.shape, f32),
+            in_specs=[spec(SMEM), spec(VMEM)],
+            out_specs=spec(VMEM),
+            compiler_params=params(),
+            name="swap",
+        )(slots, at_reader)
+        swapped = lax.all_to_all(swapped, "seq", split_axis=0, concat_axis=0, tiled=True)
+        return jnp.pad(swapped, ((0, place_count - slot_count), (0, 0)))
+
+    other_stats = lax.cond(fits, one_hop, two_hops, sent, slot_stats, slots)
 
     row_share = block_len // head_count
     rows = block_count * row_share
@@ -352,7 +397,7 @@
             jax.ShapeDtypeStruct(back_shape, bf16),
             *[jax.ShapeDtypeStruct((far, rows, 2 * head_dim), bf16)] * near,
         ),
-        in_specs=[spec(SMEM), spec(HBM), spec(VMEM), spec(VMEM), spec(HBM)],
+        in_specs=[spec(SMEM), spec(SMEM), spec(HBM), spec(VMEM), spec(VMEM), spec(VMEM), spec(HBM)],
         out_specs=(spec(HBM), *[spec(HBM)] * near),
         scratch_shapes=[
             pltpu.VMEM(arrived.shape, bf16),
@@ -369,23 +414,22 @@
         ],
         compiler_params=params(LARGE_LIMIT),
         name="grads",
-    )(blocks, arrived, kv, merged, enc_t)
-
+    )(blocks, taken_from, arrived, kv, own_stats, other_stats, enc_t)
+
+    back, *near_weights = lax.optimization_barrier((back, *near_weights))
+    returned = lax.all_to_all(back, "seq", split_axis=0, concat_axis=0, tiled=True)
     near_rows = [r if a == 0 else shifted(r, a) for a, r in zip(NEAR, near_rows)]
-    own, *far_sums, back = pl.pallas_call(
+    own, *far_sums = pl.pallas_call(
         project_kernel,
         out_shape=(
             jax.ShapeDtypeStruct((rows, enc_width), f32),
             *[jax.ShapeDtypeStruct((rows, enc_width), bf16)] * (far - 1),
-            jax.ShapeDtypeStruct(back_shape, bf16),
         ),
-        in_specs=[*[spec(VMEM)] * (2 * near), spec(HBM)],
-        out_specs=(*[spec(VMEM)] * far, spec(HBM)),
-        input_output_aliases={2 * near: far},
-        compiler_params=params(LARGE_LIMIT),
+        in_specs=[spec(VMEM)] * (2 * near),
+        out_specs=(spec(VMEM),) * far,
+        compiler_params=params(),
         name="project",
-    )(*near_rows, *near_weights, back)
-    returned = lax.all_to_all(back, "seq", split_axis=0, concat_axis=0, tiled=True)
+    )(*near_rows, *near_weights)
     encoding_grad = own
     for b, part in zip(FAR[1:], far_sums):
         encoding_grad = encoding_grad + shifted(part, b).astype(f32)

time: 143 us -> 129 us (0.902)
  blocking collectives: 24.1 us -> 14.3 us
  waiting for transfers between devices: 27.4 us -> 23.8 us
    all_to_all x2 -> x1, blocking collectives: 24.1 us -> 14.3 us  [one_hop(): return lax.all_to_all(sent, 'seq', split_axis=0, concat_axis=0, tiled=True)]
    all_to_all x1, waiting for transfers between devices: 2.02 us -> 0.01 us  [on_device(): lax.all_to_all(back, 'seq', split_axis=0, concat_axis=0, tiled=True)]
    ppermute x9, starting transfers between devices: 42.8 us -> 40.8 us  [shifted(): lax.ppermute(x, 'head', [(z, (z + step) % count) for z in range(count)])]
  transfers between devices with their start and end apart: 11 -> 11, of which waited for: 6 -> 5; matrix products, arithmetic and copies ran while one was open for 9% -> 9% of each run, Pallas kernels for 2% -> 10%
where the time goes in v6:
time: 129 us
  starting transfers between devices  57.5 us (45%)
  waiting for transfers between devices  23.8 us (18%)
  Pallas kernels  17.7 us (14%)
  blocking collectives  14.3 us (11%)
  local copies, waits for them, and re-layouts  7.94 us (6%)
  other arithmetic  3.33 us (3%)
  matrix products  2.31 us (2%)
  between operations  1.63 us (1%)
    ppermute x9, starting transfers between devices, shifted(): lax.ppermute(x, 'head', [(z, (z + step) % count) for z in range(count)])  40.8 us
    ppermute x9, waiting for transfers between devices, shifted(): lax.ppermute(x, 'head', [(z, (z + step) % count) for z in range(count)])  21 us
    all_to_all x1, blocking collectives, one_hop(): return lax.all_to_all(sent, 'seq', split_axis=0, concat_axis=0, tiled=True)  14.3 us
    all_to_all x1, starting transfers between devices, on_device(): lax.all_to_all(packed, 'seq', split_axis=0, concat_axis=0, tiled=True)  10.5 us
    pallas_call x1, Pallas kernels, on_device(): pl.pallas_call(lambda *refs: grads_kernel(scale, group, *refs), out_shape...  7.86 us
    all_to_all x1, starting transfers between devices, on_device(): lax.all_to_all(back, 'seq', split_axis=0, concat_axis=0, tiled=True)  6.19 us
    reshape x1, local copies, waits for them, and re-layouts, on_device(): flat_enc = encodings.reshape(block_count * block_len, enc_width)  3.64 us
    pallas_call x1, Pallas kernels, on_device(): pl.pallas_call(lambda *refs: pack_kernel(block_count, *refs), out_shape=(...  3.38 us
  transfers between devices with their start and end apart: 11, of which 5 were waited for; matrix products, arithmetic and copies ran while one was open for 9% of the time, Pallas kernels for 10%

profile of v6, /device:TPU:1, one launch (start us, length us, event | category | flops | bytes accessed | tf_op | source)
XLA Modules:
  0.0 128.6 jit_solution(4634462152710958582)
XLA Ops:
  0.6 3.4 %pack.1 = (bf16[64,2,64,128]{3,2,1,0:T(8,128)(2,1)}, s32[32]{0:T(128)S(1)}) custom-call(s32[2,512]{1,0:T(2,128)} %bitcast.45, bf16[16,64,128]{2,1,0:T(8,128)(2,1)} %bitcast.40, bf16[16,64,128]{2,1,0:T(8,128)(2,1)} %bitcast.41), custom_call_target="tpu_custom_call" | custom-call | tf_op jit(solution)/shard_map/pack/pallas_call | solution.py:295
  4.0 10.5 %all-to-all-start.3 = ((bf16[64,2,64,128]{3,2,1,0:T(8,128)(2,1)}), bf16[64,2,64,128]{3,2,1,0:T(8,128)(2,1)S(1)}, u32[]{:S(2)}, u32[]{:S(2)}) async-start(bf16[64,2,64,128]{3,2,1,0:T(8,128)(2,1)} %get-tuple-element.54), calls=%async_computation.3 | async-start | bytes 4194304 | tf_op jit(solution)/shard_map/all_to_all | solution.py:315
  15.2 0.4 rev.6
  16.8 0.4 select_reduce_fusion.1
  18.8 3.6 %copy.31 = bf16[896,896]{0,1:T(8,128)(2,1)} copy(bf16[896,896]{1,0:T(8,128)(2,1)} %bitcast.37) | data formatting | bytes 3211264 | tf_op jit(solution)/shard_map/reshape | solution.py:319
  22.5 2.2 %fusion = bf16[896,256]{0,1:T(8,128)(2,1)S(1)} fusion(bf16[896,256]{1,0:T(8,128)(2,1)S(1)} %constant_dynamic-update-slice_fusion.refs_4_, bf16[896,896]{1,0:T(8,128)(2,1)} %bitcast.38), kind=kOutput, calls=%fused_computation.1 | convolution fusion | flops 411271168 | bytes 2523136 | tf_op jit(solution)/shard_map/dot_general | solution.py:320
  24.9 0.7 fusion.6
  26.2 0.5 broadcast_select_fusion
  26.8 2.9 %collective-permute-start.2 = (bf16[896,256]{1,0:T(8,128)(2,1)S(1)}, bf16[896,256]{1,0:T(8,128)(2,1)S(1)}, u32[]{:S(2)}, u32[]{:S(2)}) collective-permute-start(bf16[896,256]{1,0:T(8,128)(2,1)S(1)} %constant_dynamic-update-slice_fusion.refs_4_), channel_id=1, source_target_pairs={{0,2},{1,3},{2,4},{3,5},{4,6},{5,7},{6,8},{7,9},{8,10},{9,11},{10,... | collective-permute-start | bytes 1376264 | tf_op jit(solution)/shard_map/ppermute | solution.py:280
  29.7 8.1 %collective-permute-start.1 = (bf16[896,256]{1,0:T(8,128)(2,1)S(1)}, bf16[896,256]{1,0:T(8,128)(2,1)}, u32[]{:S(2)}, u32[]{:S(2)}) collective-permute-start(bf16[896,256]{1,0:T(8,128)(2,1)S(1)} %constant_dynamic-update-slice_fusion.refs_4_), channel_id=1, source_target_pairs={{0,15},{1,0},{2,1},{3,2},{4,3},{5,4},{6,5},{7,6},{8,7},{9,8},{10,9... | collective-permute-start | bytes 1376264 | tf_op jit(solution)/shard_map/ppermute | solution.py:280
  37.8 1.9 %collective-permute-start = (bf16[896,256]{1,0:T(8,128)(2,1)S(1)}, bf16[896,256]{1,0:T(8,128)(2,1)}, u32[]{:S(2)}, u32[]{:S(2)}) collective-permute-start(bf16[896,256]{1,0:T(8,128)(2,1)S(1)} %constant_dynamic-update-slice_fusion.refs_4_), channel_id=1, source_target_pairs={{0,1},{1,2},{2,3},{3,4},{4,5},{5,6},{6,7},{7,8},{8,9},{9,10},{10,1... | collective-permute-start | bytes 1376264 | tf_op jit(solution)/shard_map/ppermute | solution.py:280
  39.8 2.8 %all-to-all-done.3.refs_2_ = bf16[64,2,64,128]{3,2,1,0:T(8,128)(2,1)S(1)} async-done(((bf16[64,2,64,128]{3,2,1,0:T(8,128)(2,1)}), bf16[64,2,64,128]{3,2,1,0:T(8,128)(2,1)S(1)}, u32[]{:S(2)}, u32[]{:S(2)}) %all-to-all-start.3) | async-done | bytes 2097184 | tf_op jit(solution)/shard_map/all_to_all | solution.py:315
  42.5 2.6 %stats.1 = (f32[32,2,128]{2,1,0:T(2,128)S(1)}, f32[64,128]{1,0:T(8,128)S(1)}, f32[256,128]{1,0:T(8,128)}) custom-call(s32[64]{0:T(128)S(1)} %get-tuple-element.52.refs_0_, s32[64]{0:T(128)S(1)} %get-tuple-element.56.refs_1_, bf16[64,2,64,128]{3,2,1,0:T(8,128)(2,1)S(1)} %all-to-all-done.3.refs_2_, bf16[7,128,256]{2,1,0:T(8,128)(2,1)S(1)} %bitcast.32), custom_call_target="tpu_custom_call" | custom-call | tf_op jit(solution)/shard_map/stats/pallas_call | solution.py:357
  45.1 0.6 copy-done.3
  45.7 14.3 %conditional.1 = (f32[256,128]{1,0:T(8,128)}) conditional(s32[]{:T(128)} %convert_element_type.32, (f32[64,128]{1,0:T(8,128)S(1)}, s32[32]{0:T(128)S(1)}) %tuple.19, f32[256,128]{1,0:T(8,128)} %get-tuple-element.60), branch_computations={%region_7.8_spmd, %region_8.9_spmd} | conditional | bytes 294924 | solution.py:387
  45.7 14.3 %all_to_all.38 = f32[32,8,128]{2,1,0:T(8,128)} all-to-all(f32[32,8,128]{2,1,0:T(8,128)} %bitcast.43), channel_id=1, replica_groups=mesh['seq'=32,'head'=16] {'seq'}, dimensions={0} | all-to-all | bytes 262144 | tf_op jit(solution)/shard_map/cond/branch_1_fun/all_to_all | solution.py:372
  60.0 7.9 %grads.1 = (bf16[32,320,128]{2,1,0:T(8,128)(2,1)}, bf16[4,56,256]{2,1,0:T(8,128)(2,1)}, bf16[4,56,256]{2,1,0:T(8,128)(2,1)}, bf16[4,56,256]{2,1,0:T(8,128)(2,1)}, bf16[4,56,256]{2,1,0:T(8,128)(2,1)}) custom-call(s32[64]{0:T(128)} %copy-done.4, s32[64]{0:T(128)} %get-tuple-element.53.refs_1_, bf16[64,2,64,128]{3,2,1,0:T(8,128)(2,1)} %copy-done, ...), custom_call_target="tpu_custom_call" | custom-call | tf_op jit(solution)/shard_map/grads/pallas_call | solution.py:394
  67.9 6.2 %all-to-all-start.4 = ((bf16[32,320,128]{2,1,0:T(8,128)(2,1)}), bf16[32,320,128]{2,1,0:T(8,128)(2,1)S(1)}, u32[]{:S(2)}, u32[]{:S(2)}) async-start(bf16[32,320,128]{2,1,0:T(8,128)(2,1)} %get-tuple-element.64), calls=%async_computation.4 | async-start | bytes 5242880 | tf_op jit(solution)/shard_map/all_to_all | solution.py:420
  74.2 1.9 %collective-permute-start.3 = (bf16[4,56,256]{2,1,0:T(8,128)(2,1)}, bf16[4,56,256]{2,1,0:T(8,128)(2,1)S(1)}, u32[]{:S(2)}, u32[]{:S(2)}) collective-permute-start(bf16[4,56,256]{2,1,0:T(8,128)(2,1)} %get-tuple-element.68), channel_id=1, source_target_pairs={{0,1},{1,2},{2,3},{3,4},{4,5},{5,6},{6,7},{7,8},{8,9},{9,10},{10,1... | collective-permute-start | bytes 344072 | tf_op jit(solution)/shard_map/ppermute | solution.py:280
  76.1 7.0 %collective-permute-start.4 = (bf16[4,56,256]{2,1,0:T(8,128)(2,1)}, bf16[4,56,256]{2,1,0:T(8,128)(2,1)S(1)}, u32[]{:S(2)}, u32[]{:S(2)}) collective-permute-start(bf16[4,56,256]{2,1,0:T(8,128)(2,1)} %get-tuple-element.69), channel_id=1, source_target_pairs={{0,15},{1,0},{2,1},{3,2},{4,3},{5,4},{6,5},{7,6},{8,7},{9,8},{10,9... | collective-permute-start | bytes 344072 | tf_op jit(solution)/shard_map/ppermute | solution.py:280
  83.1 1.9 %collective-permute-start.5 = (bf16[4,56,256]{2,1,0:T(8,128)(2,1)}, bf16[4,56,256]{2,1,0:T(8,128)(2,1)S(1)}, u32[]{:S(2)}, u32[]{:S(2)}) collective-permute-start(bf16[4,56,256]{2,1,0:T(8,128)(2,1)} %get-tuple-element.70), channel_id=1, source_target_pairs={{0,2},{1,3},{2,4},{3,5},{4,6},{5,7},{6,8},{7,9},{8,10},{9,11},{10,... | collective-permute-start | bytes 344072 | tf_op jit(solution)/shard_map/ppermute | solution.py:280
  85.0 0.5 collective-permute-done.4.refs_2_
  85.5 8.5 %collective-permute-done.5.refs_3_ = bf16[4,56,256]{2,1,0:T(8,128)(2,1)S(1)} collective-permute-done((bf16[4,56,256]{2,1,0:T(8,128)(2,1)}, bf16[4,56,256]{2,1,0:T(8,128)(2,1)S(1)}, u32[]{:S(2)}, u32[]{:S(2)}) %collective-permute-start.5) | collective-permute-done | bytes 114720 | tf_op jit(solution)/shard_map/ppermute | solution.py:280
  94.0 0.9 copy-done.2
  94.9 2.3 %project.1 = (f32[56,896]{1,0:T(8,128)S(1)}, bf16[56,896]{1,0:T(8,128)(2,1)S(1)}, bf16[56,896]{1,0:T(8,128)(2,1)S(1)}, bf16[56,896]{1,0:T(8,128)(2,1)S(1)}) custom-call(bf16[4,56,256]{2,1,0:T(8,128)(2,1)S(1)} %copy-done.2, bf16[4,56,256]{2,1,0:T(8,128)(2,1)S(1)} %collective-permute-done.3.refs_1_, bf16[4,56,256]{2,1,0:T(8,128)(2,1)S(1)} %collective-permute-done.4.refs_2_, ...), custom_call_target="tpu_custom_call" | custom-call | tf_op jit(solution)/shard_map/project/pallas_call | solution.py:422
  97.2 1.9 %collective-permute-start.6 = (bf16[56,896]{1,0:T(8,128)(2,1)S(1)}, bf16[56,896]{1,0:T(8,128)(2,1)S(1)}, u32[]{:S(2)}, u32[]{:S(2)}) collective-permute-start(bf16[56,896]{1,0:T(8,128)(2,1)S(1)} %get-tuple-element.76), channel_id=1, source_target_pairs={{0,4},{1,5},{2,6},{3,7},{4,8},{5,9},{6,10},{7,11},{8,12},{9,13},{1... | collective-permute-start | bytes 301064 | tf_op jit(solution)/shard_map/ppermute | solution.py:280
  99.2 8.2 %collective-permute-start.7 = (bf16[56,896]{1,0:T(8,128)(2,1)S(1)}, bf16[56,896]{1,0:T(8,128)(2,1)S(1)}, u32[]{:S(2)}, u32[]{:S(2)}) collective-permute-start(bf16[56,896]{1,0:T(8,128)(2,1)S(1)} %get-tuple-element.77), channel_id=1, source_target_pairs={{0,8},{1,9},{2,10},{3,11},{4,12},{5,13},{6,14},{7,15},{8,0},{9,1},... | collective-permute-start | bytes 301064 | tf_op jit(solution)/shard_map/ppermute | solution.py:280
  107.4 6.9 %collective-permute-start.8 = (bf16[56,896]{1,0:T(8,128)(2,1)S(1)}, bf16[56,896]{1,0:T(8,128)(2,1)S(1)}, u32[]{:S(2)}, u32[]{:S(2)}) collective-permute-start(bf16[56,896]{1,0:T(8,128)(2,1)S(1)} %get-tuple-element.78), channel_id=1, source_target_pairs={{0,12},{1,13},{2,14},{3,15},{4,0},{5,1},{6,2},{7,3},{8,4},{9,5},{1... | collective-permute-start | bytes 301064 | tf_op jit(solution)/shard_map/ppermute | solution.py:280
  114.3 2.7 %collective-permute-done.7 = bf16[56,896]{1,0:T(8,128)(2,1)S(1)} collective-permute-done((bf16[56,896]{1,0:T(8,128)(2,1)S(1)}, bf16[56,896]{1,0:T(8,128)(2,1)S(1)}, u32[]{:S(2)}, u32[]{:S(2)}) %collective-permute-start.7) | collective-permute-done | bytes 100384 | tf_op jit(solution)/shard_map/ppermute | solution.py:280
  117.0 9.3 %collective-permute-done.8 = bf16[56,896]{1,0:T(8,128)(2,1)S(1)} collective-permute-done((bf16[56,896]{1,0:T(8,128)(2,1)S(1)}, bf16[56,896]{1,0:T(8,128)(2,1)S(1)}, u32[]{:S(2)}, u32[]{:S(2)}) %collective-permute-start.8) | collective-permute-done | bytes 100384 | tf_op jit(solution)/shard_map/ppermute | solution.py:280
  126.3 0.7 add_bitcast_fusion
  127.1 1.6 %finish.1 = (bf16[16,64,128]{2,1,0:T(8,128)(2,1)}, bf16[16,64,128]{2,1,0:T(8,128)(2,1)}, f32[28,128]{1,0:T(8,128)}, f32[28,128]{1,0:T(8,128)}) custom-call(s32[32]{0:T(128)S(1)} %get-tuple-element.49.slots_ref, bf16[32,320,128]{2,1,0:T(8,128)(2,1)S(1)} %all-to-all-done.4.in_ref), custom_call_target="tpu_custom_call" | custom-call | tf_op jit(solution)/shard_map/finish/pallas_call | solution.py:437
  (54 shorter events, 3.6 us)
Async XLA Ops:
  4.0 10.6 %copy-start.7 = (s32[512,2]{0,1:T(2,128)S(1)}, s32[512,2]{0,1:T(2,128)}, u32[]{:S(2)}) copy-start(s32[512,2]{0,1:T(2,128)} %param.12) | copy-start | bytes 12292
  4.0 38.5 %all-to-all-start.3 = ((bf16[64,2,64,128]{3,2,1,0:T(8,128)(2,1)}), bf16[64,2,64,128]{3,2,1,0:T(8,128)(2,1)S(1)}, u32[]{:S(2)}, u32[]{:S(2)}) async-start(bf16[64,2,64,128]{3,2,1,0:T(8,128)(2,1)} %get-tuple-element.54), calls=%async_computation.3 | async-start | bytes 4194304 | tf_op jit(solution)/shard_map/all_to_all | solution.py:315
  18.3 24.3 %copy-start.4 = (s32[64]{0:T(128)}, s32[64]{0:T(128)S(1)}, u32[]{:S(2)}) copy-start(s32[64]{0:T(128)S(1)} %get-tuple-element.52.refs_0_) | copy-start | bytes 772
  18.8 3.7 %copy-start.5 = (bf16[896,128]{1,0:T(8,128)(2,1)S(1)}, bf16[896,128]{1,0:T(8,128)(2,1)}, u32[]{:S(2)}) copy-start(bf16[896,128]{1,0:T(8,128)(2,1)} %param.10) | copy-start | bytes 688132
  18.8 3.7 %copy-start.6 = (bf16[896,128]{1,0:T(8,128)(2,1)S(1)}, bf16[896,128]{1,0:T(8,128)(2,1)}, u32[]{:S(2)}) copy-start(bf16[896,128]{1,0:T(8,128)(2,1)} %param.11) | copy-start | bytes 688132
  24.9 20.8 %copy-start.1 = (bf16[896,256]{1,0:T(8,128)(2,1)}, bf16[896,256]{1,0:T(8,128)(2,1)S(1)}, u32[]{:S(2)}) copy-start(bf16[896,256]{1,0:T(8,128)(2,1)S(1)} %copy.30) | copy-start | bytes 1376260
  26.8 41.2 %collective-permute-start.2 = (bf16[896,256]{1,0:T(8,128)(2,1)S(1)}, bf16[896,256]{1,0:T(8,128)(2,1)S(1)}, u32[]{:S(2)}, u32[]{:S(2)}) collective-permute-start(bf16[896,256]{1,0:T(8,128)(2,1)S(1)} %constant_dynamic-update-slice_fusion.refs_4_), channel_id=1, source_target_pairs={{0,2},{1,3},{2,4},{3,5},{4,6},{5,7},{6,8},{7,9},{8,10},{9,11},{10,... | collective-permute-start | bytes 1376264 | tf_op jit(solution)/shard_map/ppermute | solution.py:280
  29.7 38.3 %collective-permute-start.1 = (bf16[896,256]{1,0:T(8,128)(2,1)S(1)}, bf16[896,256]{1,0:T(8,128)(2,1)}, u32[]{:S(2)}, u32[]{:S(2)}) collective-permute-start(bf16[896,256]{1,0:T(8,128)(2,1)S(1)} %constant_dynamic-update-slice_fusion.refs_4_), channel_id=1, source_target_pairs={{0,15},{1,0},{2,1},{3,2},{4,3},{5,4},{6,5},{7,6},{8,7},{9,8},{10,9... | collective-permute-start | bytes 1376264 | tf_op jit(solution)/shard_map/ppermute | solution.py:280
  37.8 30.1 %collective-permute-start = (bf16[896,256]{1,0:T(8,128)(2,1)S(1)}, bf16[896,256]{1,0:T(8,128)(2,1)}, u32[]{:S(2)}, u32[]{:S(2)}) collective-permute-start(bf16[896,256]{1,0:T(8,128)(2,1)S(1)} %constant_dynamic-update-slice_fusion.refs_4_), channel_id=1, source_target_pairs={{0,1},{1,2},{2,3},{3,4},{4,5},{5,6},{6,7},{7,8},{8,9},{9,10},{10,1... | collective-permute-start | bytes 1376264 | tf_op jit(solution)/shard_map/ppermute | solution.py:280
  42.5 17.5 %copy-start = (bf16[64,2,64,128]{3,2,1,0:T(8,128)(2,1)}, bf16[64,2,64,128]{3,2,1,0:T(8,128)(2,1)S(1)}, u32[]{:S(2)}) copy-start(bf16[64,2,64,128]{3,2,1,0:T(8,128)(2,1)S(1)} %all-to-all-done.3.refs_2_) | copy-start | bytes 6291460
  45.1 0.6 copy-start.3
  67.9 59.1 %all-to-all-start.4 = ((bf16[32,320,128]{2,1,0:T(8,128)(2,1)}), bf16[32,320,128]{2,1,0:T(8,128)(2,1)S(1)}, u32[]{:S(2)}, u32[]{:S(2)}) async-start(bf16[32,320,128]{2,1,0:T(8,128)(2,1)} %get-tuple-element.64), calls=%async_computation.4 | async-start | bytes 5242880 | tf_op jit(solution)/shard_map/all_to_all | solution.py:420
  74.2 10.8 %collective-permute-start.3 = (bf16[4,56,256]{2,1,0:T(8,128)(2,1)}, bf16[4,56,256]{2,1,0:T(8,128)(2,1)S(1)}, u32[]{:S(2)}, u32[]{:S(2)}) collective-permute-start(bf16[4,56,256]{2,1,0:T(8,128)(2,1)} %get-tuple-element.68), channel_id=1, source_target_pairs={{0,1},{1,2},{2,3},{3,4},{4,5},{5,6},{6,7},{7,8},{8,9},{9,10},{10,1... | collective-permute-start | bytes 344072 | tf_op jit(solution)/shard_map/ppermute | solution.py:280
  76.1 9.5 %collective-permute-start.4 = (bf16[4,56,256]{2,1,0:T(8,128)(2,1)}, bf16[4,56,256]{2,1,0:T(8,128)(2,1)S(1)}, u32[]{:S(2)}, u32[]{:S(2)}) collective-permute-start(bf16[4,56,256]{2,1,0:T(8,128)(2,1)} %get-tuple-element.69), channel_id=1, source_target_pairs={{0,15},{1,0},{2,1},{3,2},{4,3},{5,4},{6,5},{7,6},{8,7},{9,8},{10,9... | collective-permute-start | bytes 344072 | tf_op jit(solution)/shard_map/ppermute | solution.py:280
  83.1 10.9 %collective-permute-start.5 = (bf16[4,56,256]{2,1,0:T(8,128)(2,1)}, bf16[4,56,256]{2,1,0:T(8,128)(2,1)S(1)}, u32[]{:S(2)}, u32[]{:S(2)}) collective-permute-start(bf16[4,56,256]{2,1,0:T(8,128)(2,1)} %get-tuple-element.70), channel_id=1, source_target_pairs={{0,2},{1,3},{2,4},{3,5},{4,6},{5,7},{6,8},{7,9},{8,10},{9,11},{10,... | collective-permute-start | bytes 344072 | tf_op jit(solution)/shard_map/ppermute | solution.py:280
  94.0 0.9 copy-start.2
  97.2 17.0 %collective-permute-start.6 = (bf16[56,896]{1,0:T(8,128)(2,1)S(1)}, bf16[56,896]{1,0:T(8,128)(2,1)S(1)}, u32[]{:S(2)}, u32[]{:S(2)}) collective-permute-start(bf16[56,896]{1,0:T(8,128)(2,1)S(1)} %get-tuple-element.76), channel_id=1, source_target_pairs={{0,4},{1,5},{2,6},{3,7},{4,8},{5,9},{6,10},{7,11},{8,12},{9,13},{1... | collective-permute-start | bytes 301064 | tf_op jit(solution)/shard_map/ppermute | solution.py:280
  99.2 17.8 %collective-permute-start.7 = (bf16[56,896]{1,0:T(8,128)(2,1)S(1)}, bf16[56,896]{1,0:T(8,128)(2,1)S(1)}, u32[]{:S(2)}, u32[]{:S(2)}) collective-permute-start(bf16[56,896]{1,0:T(8,128)(2,1)S(1)} %get-tuple-element.77), channel_id=1, source_target_pairs={{0,8},{1,9},{2,10},{3,11},{4,12},{5,13},{6,14},{7,15},{8,0},{9,1},... | collective-permute-start | bytes 301064 | tf_op jit(solution)/shard_map/ppermute | solution.py:280
  107.4 18.9 %collective-permute-start.8 = (bf16[56,896]{1,0:T(8,128)(2,1)S(1)}, bf16[56,896]{1,0:T(8,128)(2,1)S(1)}, u32[]{:S(2)}, u32[]{:S(2)}) collective-permute-start(bf16[56,896]{1,0:T(8,128)(2,1)S(1)} %get-tuple-element.78), channel_id=1, source_target_pairs={{0,12},{1,13},{2,14},{3,15},{4,0},{5,1},{6,2},{7,3},{8,4},{9,5},{1... | collective-permute-start | bytes 301064 | tf_op jit(solution)/shard_map/ppermute | solution.py:280

commit v7 on v6

--- a/solution.py
+++ b/solution.py
@@ -130,11 +130,11 @@
     return merged, delta
 
 
-def grads_kernel(scale, group, blocks_ref, from_ref, x_hbm, kv_ref, own_ref, other_ref, enc_hbm, *refs):
+def grads_kernel(scale, group, blocks_ref, from_ref, x_hbm, kv_ref, own_ref, other_ref, *refs):
     near = len(NEAR)
     out_ref = refs[0]
     rows_refs = refs[1:1 + near]
-    x_ref, stage, enc_t, rows_all, rows_near, acc_k, acc_v, x_sems, enc_sem, rows_sems, out_sem = refs[1 + near:]
+    all_ref, x_ref, stage, rows_all, rows_near, acc_k, acc_v, x_sems, rows_sems, out_sem = refs[1 + near:]
     head_dim = kv_ref.shape[2] // 2
     seq_count = x_ref.shape[0] // CAP
     pair = CAP * SEGMENT
@@ -146,8 +146,6 @@
 
     for i in range(seq_count // group):
         arrival(i).start()
-    fetch = pltpu.make_async_copy(enc_hbm, enc_t, enc_sem)
-    fetch.start()
     acc_k[...] = jnp.zeros_like(acc_k)
     acc_v[...] = jnp.zeros_like(acc_v)
     left = lax.broadcasted_iota(jnp.int32, (1, pair), 1) < SEGMENT
@@ -192,7 +190,7 @@
             acc_k[b] += key_part[:, head_dim:]
             acc_v[b] += value_part[:, head_dim:]
         at = pl.ds(i * group, group)
-        pltpu.make_async_copy(stage.at[at, :parts], out_ref.at[at, :parts], out_sem).start()
+        pltpu.make_async_copy(stage.at[at], out_ref.at[at, :parts], out_sem).start()
         return 0
 
     lax.fori_loop(0, seq_count // group, step, 0)
@@ -211,25 +209,30 @@
         rows_copies[i].start()
     rows_all[:, :head_dim] = acc_k[...].reshape(-1, head_dim).astype(jnp.bfloat16)
     rows_all[:, head_dim:] = acc_v[...].reshape(-1, head_dim).astype(jnp.bfloat16)
-    room = (stage.shape[1] - parts) // 2
-    share = enc_t.shape[0] // seq_count
-    fetch.wait()
+    rows_copies.append(pltpu.make_async_copy(rows_all, all_ref, rows_sems.at[near]))
+    rows_copies[near].start()
+    for copy in rows_copies:
+        copy.wait()
+    pltpu.make_async_copy(stage, out_ref.at[:, :parts], out_sem).wait()
+
+
+def weigh_kernel(parts, rows_ref, enc_t_ref, back_ref, out_ref, stage, sem):
+    head_dim = rows_ref.shape[1] // 2
+    seq_count, room = stage.shape[0], stage.shape[1] // 2
+    share = enc_t_ref.shape[0] // seq_count
     batch = 8
     for i in range(0, seq_count, batch):
-        term = nn_dot(enc_t[i * share:(i + batch) * share], rows_all[...])
+        term = nn_dot(enc_t_ref[i * share:(i + batch) * share], rows_ref[...])
         for s in range(batch):
             part = term[s * share:(s + 1) * share]
             if room > share:
                 part = jnp.concatenate([part, jnp.zeros((room - share, 2 * head_dim), jnp.float32)], axis=0)
             part = part.astype(jnp.bfloat16)
-            stage[i + s, parts:parts + room] = part[:, :head_dim]
-            stage[i + s, parts + room:] = part[:, head_dim:]
-        pltpu.make_async_copy(
-            stage.at[i:i + batch, parts:], out_ref.at[i:i + batch, parts:], out_sem
-        ).start()
-    for copy in rows_copies:
-        copy.wait()
-    pltpu.make_async_copy(stage, out_ref, out_sem).wait()
+            stage[i + s, :room] = part[:, :head_dim]
+            stage[i + s, room:] = part[:, head_dim:]
+        at = pl.ds(i, batch)
+        pltpu.make_async_copy(stage.at[at], out_ref.at[at, parts:], sem).start()
+    pltpu.make_async_copy(stage, out_ref.at[:, parts:], sem).wait()
 
 
 def finish_kernel(slots_ref, in_ref, att_ref, qg_ref, kw_ref, vw_ref):
@@ -273,6 +276,11 @@
                 own_ref[...] = part
             else:
                 far_refs[i + j - 1][...] = part.astype(jnp.bfloat16)
+
+
+def total_kernel(own_ref, one_ref, two_ref, three_ref, done_ref, out_ref):
+    total = own_ref[...] + one_ref[...].astype(jnp.float32)
+    out_ref[...] = total + two_ref[...].astype(jnp.float32) + three_ref[...].astype(jnp.float32)
 
 
 def shifted(x, step):
@@ -389,36 +397,46 @@
     row_share = block_len // head_count
     rows = block_count * row_share
     near, far = len(NEAR), len(FAR)
-    back_shape = (seq_count, 2 * CAP * SEGMENT + 2 * room, head_dim)
+    parts = 2 * CAP * SEGMENT
+    back_shape = (seq_count, parts + 2 * room, head_dim)
     group = 8
-    back, *near_rows = pl.pallas_call(
+    back, *near_rows, grad_rows = pl.pallas_call(
         lambda *refs: grads_kernel(scale, group, *refs),
         out_shape=(
             jax.ShapeDtypeStruct(back_shape, bf16),
             *[jax.ShapeDtypeStruct((far, rows, 2 * head_dim), bf16)] * near,
+            jax.ShapeDtypeStruct((block_count * block_len, 2 * head_dim), bf16),
         ),
-        in_specs=[spec(SMEM), spec(SMEM), spec(HBM), spec(VMEM), spec(VMEM), spec(VMEM), spec(HBM)],
-        out_specs=(spec(HBM), *[spec(HBM)] * near),
+        in_specs=[spec(SMEM), spec(SMEM), spec(HBM), spec(VMEM), spec(VMEM), spec(VMEM)],
+        out_specs=(spec(HBM),) * (near + 2),
         scratch_shapes=[
             pltpu.VMEM(arrived.shape, bf16),
-            pltpu.VMEM(back_shape, bf16),
-            pltpu.VMEM((enc_width, block_count * block_len), bf16),
+            pltpu.VMEM((seq_count, parts, head_dim), bf16),
             pltpu.VMEM((block_count * block_len, 2 * head_dim), bf16),
             pltpu.VMEM((near, far, rows, 2 * head_dim), bf16),
             pltpu.VMEM((block_count, block_len, head_dim), f32),
             pltpu.VMEM((block_count, block_len, head_dim), f32),
             pltpu.SemaphoreType.DMA((seq_count // group,)),
-            pltpu.SemaphoreType.DMA,
-            pltpu.SemaphoreType.DMA((near,)),
+            pltpu.SemaphoreType.DMA((near + 1,)),
             pltpu.SemaphoreType.DMA,
         ],
         compiler_params=params(LARGE_LIMIT),
         name="grads",
-    )(blocks, taken_from, arrived, kv, own_stats, other_stats, enc_t)
+    )(blocks, taken_from, arrived, kv, own_stats, other_stats)
 
     back, *near_weights = lax.optimization_barrier((back, *near_weights))
+    near_rows = [r if a == 0 else shifted(r, a) for a, r in zip(NEAR, near_rows)]
+    back = pl.pallas_call(
+        lambda *refs: weigh_kernel(parts, *refs),
+        out_shape=jax.ShapeDtypeStruct(back_shape, bf16),
+        in_specs=[spec(VMEM), spec(VMEM), spec(HBM)],
+        out_specs=spec(HBM),
+        scratch_shapes=[pltpu.VMEM((seq_count, 2 * room, head_dim), bf16), pltpu.SemaphoreType.DMA],
+        input_output_aliases={2: 0},
+        compiler_params=params(LARGE_LIMIT),
+        name="weigh",
+    )(grad_rows, enc_t, back)
     returned = lax.all_to_all(back, "seq", split_axis=0, concat_axis=0, tiled=True)
-    near_rows = [r if a == 0 else shifted(r, a) for a, r in zip(NEAR, near_rows)]
     own, *far_sums = pl.pallas_call(
         project_kernel,
         out_shape=(
@@ -428,12 +446,9 @@
         in_specs=[spec(VMEM)] * (2 * near),
         out_specs=(spec(VMEM),) * far,
         compiler_params=params(),
+        cost_estimate=pl.CostEstimate(flops=6 * 10**10, bytes_accessed=2 * 10**6, transcendentals=0),
         name="project",
     )(*near_rows, *near_weights)
-    encoding_grad = own
-    for b, part in zip(FAR[1:], far_sums):
-        encoding_grad = encoding_grad + shifted(part, b).astype(f32)
-
     attended, query_grad, key_weight_grad, value_weight_grad = pl.pallas_call(
         finish_kernel,
         out_shape=(
@@ -447,6 +462,14 @@
         compiler_params=params(),
         name="finish",
     )(slots, returned)
+    encoding_grad = pl.pallas_call(
+        total_kernel,
+        out_shape=jax.ShapeDtypeStruct((rows, enc_width), f32),
+        in_specs=[*[spec(VMEM)] * far, spec(HBM)],
+        out_specs=spec(VMEM),
+        compiler_params=params(),
+        name="total",
+    )(own, *[shifted(part, b) for b, part in zip(FAR[1:], far_sums)], key_weight_grad)
     return (
         attended.reshape(segments * SEGMENT, head_dim),
         query_grad.reshape(segments * SEGMENT, head_dim),

time: 129 us -> 124 us (0.961)
  waiting for transfers between devices: 23.8 us -> 13.8 us
  Pallas kernels: 17.7 us -> 21.1 us
  local copies, waits for them, and re-layouts: 7.94 us -> 9.66 us
    ppermute x9, waiting for transfers between devices: 21 us -> 2.26 us  [shifted(): lax.ppermute(x, 'head', [(z, (z + step) % count) for z in range(count)])]
    all_to_all x1, waiting for transfers between devices: 0.01 us -> 10.5 us  [on_device(): lax.all_to_all(back, 'seq', split_axis=0, concat_axis=0, tiled=True)]
    pallas_call x0 -> x2, Pallas kernels: none -> 3.67 us  [the longest x1 2.93 us: on_device(): pl.pallas_call(lambda *refs: weigh_kernel(parts, *refs), out_shape=jax.Sh...]
    all_to_all x1, waiting for transfers between devices: 2.78 us -> 1 us  [on_device(): lax.all_to_all(packed, 'seq', split_axis=0, concat_axis=0, tiled=True)]
    all_to_all x1, starting transfers between devices: 6.19 us -> 4.55 us  [on_device(): lax.all_to_all(back, 'seq', split_axis=0, concat_axis=0, tiled=True)]
    ppermute x9, starting transfers between devices: 40.8 us -> 42.2 us  [shifted(): lax.ppermute(x, 'head', [(z, (z + step) % count) for z in range(count)])]
  transfers between devices with their start and end apart: 11 -> 11, of which waited for: 5 -> 4; matrix products, arithmetic and copies ran while one was open for 9% -> 11% of each run, Pallas kernels for 10% -> 14%
where the time goes in v7:
time: 124 us; the launch traced here: 123 us
  starting transfers between devices  57.3 us (46%)
  Pallas kernels  21.1 us (17%)
  blocking collectives  14.1 us (11%)
  waiting for transfers between devices  13.8 us (11%)
  local copies, waits for them, and re-layouts  9.66 us (8%)
  matrix products  3.11 us (3%)
  other arithmetic  2.61 us (2%)
  between operations  1.67 us (1%)
    ppermute x9, starting transfers between devices, shifted(): lax.ppermute(x, 'head', [(z, (z + step) % count) for z in range(count)])  42.2 us
    all_to_all x1, blocking collectives, one_hop(): return lax.all_to_all(sent, 'seq', split_axis=0, concat_axis=0, tiled=True)  14.1 us
    all_to_all x1, starting transfers between devices, on_device(): lax.all_to_all(packed, 'seq', split_axis=0, concat_axis=0, tiled=True)  10.6 us
    all_to_all x1, waiting for transfers between devices, on_device(): lax.all_to_all(back, 'seq', split_axis=0, concat_axis=0, tiled=True)  10.5 us
    pallas_call x1, Pallas kernels, on_device(): pl.pallas_call(lambda *refs: grads_kernel(scale, group, *refs), out_shape...  7.32 us
    all_to_all x1, starting transfers between devices, on_device(): lax.all_to_all(back, 'seq', split_axis=0, concat_axis=0, tiled=True)  4.55 us
    reshape x1, local copies, waits for them, and re-layouts, on_device(): flat_enc = encodings.reshape(block_count * block_len, enc_width)  3.59 us
    pallas_call x1, Pallas kernels, on_device(): pl.pallas_call(lambda *refs: pack_kernel(block_count, *refs), out_shape=(...  3.39 us
  transfers between devices with their start and end apart: 11, of which 4 were waited for; matrix products, arithmetic and copies ran while one was open for 11% of the time, Pallas kernels for 14%

profile of v7, /device:TPU:1, one launch (start us, length us, event | category | flops | bytes accessed | tf_op | source)
XLA Modules:
  0.0 123.4 jit_solution(8986719067247554297)
XLA Ops:
  0.6 3.4 %pack.1 = (bf16[64,2,64,128]{3,2,1,0:T(8,128)(2,1)}, s32[32]{0:T(128)S(1)}) custom-call(s32[2,512]{1,0:T(2,128)} %bitcast.45, bf16[16,64,128]{2,1,0:T(8,128)(2,1)} %bitcast.39, bf16[16,64,128]{2,1,0:T(8,128)(2,1)} %bitcast.40), custom_call_target="tpu_custom_call" | custom-call | tf_op jit(solution)/shard_map/pack/pallas_call | solution.py:303
  4.0 10.6 %all-to-all-start.3 = ((bf16[64,2,64,128]{3,2,1,0:T(8,128)(2,1)}), bf16[64,2,64,128]{3,2,1,0:T(8,128)(2,1)S(1)}, u32[]{:S(2)}, u32[]{:S(2)}) async-start(bf16[64,2,64,128]{3,2,1,0:T(8,128)(2,1)} %get-tuple-element.55), calls=%async_computation.3 | async-start | bytes 4194304 | tf_op jit(solution)/shard_map/all_to_all | solution.py:323
  18.8 3.6 %copy.32 = bf16[896,896]{0,1:T(8,128)(2,1)} copy(bf16[896,896]{1,0:T(8,128)(2,1)} %bitcast.36) | data formatting | bytes 3211264 | tf_op jit(solution)/shard_map/reshape | solution.py:327
  22.5 3.0 %fusion = bf16[896,256]{0,1:T(8,128)(2,1)} fusion(bf16[896,256]{1,0:T(8,128)(2,1)S(1)} %constant_dynamic-update-slice_fusion.refs_4_, bf16[896,896]{1,0:T(8,128)(2,1)} %bitcast.37), kind=kOutput, calls=%fused_computation.1 | convolution fusion | flops 411271168 | bytes 2523136 | tf_op jit(solution)/shard_map/dot_general | solution.py:328
  25.5 1.2 copy.31
  26.7 0.7 fusion.6
  28.0 0.5 broadcast_select_fusion
  28.5 1.9 %collective-permute-start = (bf16[896,256]{1,0:T(8,128)(2,1)S(1)}, bf16[896,256]{1,0:T(8,128)(2,1)}, u32[]{:S(2)}, u32[]{:S(2)}) collective-permute-start(bf16[896,256]{1,0:T(8,128)(2,1)S(1)} %constant_dynamic-update-slice_fusion.refs_4_), channel_id=1, source_target_pairs={{0,1},{1,2},{2,3},{3,4},{4,5},{5,6},{6,7},{7,8},{8,9},{9,10},{10,1... | collective-permute-start | bytes 1376264 | tf_op jit(solution)/shard_map/ppermute | solution.py:288
  30.4 9.2 %collective-permute-start.1 = (bf16[896,256]{1,0:T(8,128)(2,1)S(1)}, bf16[896,256]{1,0:T(8,128)(2,1)}, u32[]{:S(2)}, u32[]{:S(2)}) collective-permute-start(bf16[896,256]{1,0:T(8,128)(2,1)S(1)} %constant_dynamic-update-slice_fusion.refs_4_), channel_id=1, source_target_pairs={{0,15},{1,0},{2,1},{3,2},{4,3},{5,4},{6,5},{7,6},{8,7},{9,8},{10,9... | collective-permute-start | bytes 1376264 | tf_op jit(solution)/shard_map/ppermute | solution.py:288
  39.6 1.9 %collective-permute-start.2 = (bf16[896,256]{1,0:T(8,128)(2,1)S(1)}, bf16[896,256]{1,0:T(8,128)(2,1)}, u32[]{:S(2)}, u32[]{:S(2)}) collective-permute-start(bf16[896,256]{1,0:T(8,128)(2,1)S(1)} %constant_dynamic-update-slice_fusion.refs_4_), channel_id=1, source_target_pairs={{0,2},{1,3},{2,4},{3,5},{4,6},{5,7},{6,8},{7,9},{8,10},{9,11},{10,... | collective-permute-start | bytes 1376264 | tf_op jit(solution)/shard_map/ppermute | solution.py:288
  41.5 1.0 all-to-all-done.3.refs_2_
  42.6 1.9 %stats.1 = (f32[32,2,128]{2,1,0:T(2,128)S(1)}, f32[64,128]{1,0:T(8,128)S(1)}, f32[256,128]{1,0:T(8,128)S(1)}) custom-call(s32[64]{0:T(128)S(1)} %get-tuple-element.53.refs_0_, s32[64]{0:T(128)S(1)} %get-tuple-element.57.refs_1_, bf16[64,2,64,128]{3,2,1,0:T(8,128)(2,1)S(1)} %all-to-all-done.3.refs_2_, bf16[7,128,256]{2,1,0:T(8,128)(2,1)S(1)} %bitcast.31), custom_call_target="tpu_custom_call" | custom-call | tf_op jit(solution)/shard_map/stats/pallas_call | solution.py:365
  44.5 14.1 %conditional.1 = (f32[256,128]{1,0:T(8,128)S(1)}) conditional(s32[]{:T(128)} %convert_element_type.23, (f32[64,128]{1,0:T(8,128)S(1)}, s32[32]{0:T(128)S(1)}) %tuple.19, f32[256,128]{1,0:T(8,128)S(1)} %get-tuple-element.61), branch_computations={%region_7.8_spmd, %region_8.9_spmd} | conditional | bytes 294924 | solution.py:395
  44.5 14.1 %all_to_all.38 = f32[32,8,128]{2,1,0:T(8,128)S(1)} all-to-all(f32[32,8,128]{2,1,0:T(8,128)S(1)} %bitcast.43), channel_id=1, replica_groups=mesh['seq'=32,'head'=16] {'seq'}, dimensions={0} | all-to-all | bytes 262144 | tf_op jit(solution)/shard_map/cond/branch_1_fun/all_to_all | solution.py:380
  58.6 7.3 %grads.1 = (bf16[32,320,128]{2,1,0:T(8,128)(2,1)}, bf16[4,56,256]{2,1,0:T(8,128)(2,1)}, bf16[4,56,256]{2,1,0:T(8,128)(2,1)}, bf16[4,56,256]{2,1,0:T(8,128)(2,1)}...) custom-call(s32[64]{0:T(128)} %copy-done.4, s32[64]{0:T(128)} %get-tuple-element.54.refs_1_, ...), custom_call_target="tpu_custom_call" | custom-call | tf_op jit(solution)/shard_map/grads/pallas_call | solution.py:403
  66.0 1.9 %collective-permute-start.3 = (bf16[4,56,256]{2,1,0:T(8,128)(2,1)}, bf16[4,56,256]{2,1,0:T(8,128)(2,1)S(1)}, u32[]{:S(2)}, u32[]{:S(2)}) collective-permute-start(bf16[4,56,256]{2,1,0:T(8,128)(2,1)} %get-tuple-element.70), channel_id=1, source_target_pairs={{0,1},{1,2},{2,3},{3,4},{4,5},{5,6},{6,7},{7,8},{8,9},{9,10},{10,1... | collective-permute-start | bytes 344072 | tf_op jit(solution)/shard_map/ppermute | solution.py:288
  67.9 7.7 %collective-permute-start.4 = (bf16[4,56,256]{2,1,0:T(8,128)(2,1)}, bf16[4,56,256]{2,1,0:T(8,128)(2,1)S(1)}, u32[]{:S(2)}, u32[]{:S(2)}) collective-permute-start(bf16[4,56,256]{2,1,0:T(8,128)(2,1)} %get-tuple-element.71), channel_id=1, source_target_pairs={{0,15},{1,0},{2,1},{3,2},{4,3},{5,4},{6,5},{7,6},{8,7},{9,8},{10,9... | collective-permute-start | bytes 344072 | tf_op jit(solution)/shard_map/ppermute | solution.py:288
  75.6 1.9 %collective-permute-start.5 = (bf16[4,56,256]{2,1,0:T(8,128)(2,1)}, bf16[4,56,256]{2,1,0:T(8,128)(2,1)}, u32[]{:S(2)}, u32[]{:S(2)}) collective-permute-start(bf16[4,56,256]{2,1,0:T(8,128)(2,1)} %get-tuple-element.72), channel_id=1, source_target_pairs={{0,2},{1,3},{2,4},{3,5},{4,6},{5,7},{6,8},{7,9},{8,10},{9,11},{10,... | collective-permute-start | bytes 344072 | tf_op jit(solution)/shard_map/ppermute | solution.py:288
  77.6 2.9 %weigh.1 = bf16[32,320,128]{2,1,0:T(8,128)(2,1)} custom-call(bf16[896,256]{1,0:T(8,128)(2,1)} %get-tuple-element.62.refs_0_, bf16[896,896]{1,0:T(8,128)(2,1)} %bitcast.35, bf16[32,320,128]{2,1,0:T(8,128)(2,1)} %get-tuple-element.66.refs_2_), custom_call_target="tpu_custom_call", output_to_operand_aliasing={{}: (2, {})} | custom-call | tf_op jit(solution)/shard_map/weigh/pallas_call | solution.py:429
  80.5 4.5 %all-to-all-start.4 = ((bf16[32,320,128]{2,1,0:T(8,128)(2,1)}), bf16[32,320,128]{2,1,0:T(8,128)(2,1)S(1)}, u32[]{:S(2)}, u32[]{:S(2)}) async-start(bf16[32,320,128]{2,1,0:T(8,128)(2,1)} %weigh.1), calls=%async_computation.4 | async-start | bytes 5242880 | tf_op jit(solution)/shard_map/all_to_all | solution.py:439
  85.1 0.6 copy-done.6
  85.7 0.9 collective-permute-done.5.refs_3_
  86.6 0.9 copy-done.7
  87.5 3.2 %project.1 = (f32[56,896]{1,0:T(8,128)S(1)}, bf16[56,896]{1,0:T(8,128)(2,1)}, bf16[56,896]{1,0:T(8,128)(2,1)}, bf16[56,896]{1,0:T(8,128)(2,1)}) custom-call(bf16[4,56,256]{2,1,0:T(8,128)(2,1)S(1)} %copy-done.5, bf16[4,56,256]{2,1,0:T(8,128)(2,1)S(1)} %collective-permute-done.3.refs_1_, bf16[4,56,256]{2,1,0:T(8,128)(2,1)S(1)} %copy-done.7, ...), custom_call_target="tpu_custom_call" | custom-call | flops 60000002048 | bytes 2000000 | tf_op jit(solution)/shard_map/project/pallas_call | solution.py:440
  90.7 5.3 %collective-permute-start.6 = (bf16[56,896]{1,0:T(8,128)(2,1)}, bf16[56,896]{1,0:T(8,128)(2,1)S(1)}, u32[]{:S(2)}, u32[]{:S(2)}) collective-permute-start(bf16[56,896]{1,0:T(8,128)(2,1)} %get-tuple-element.78), channel_id=1, source_target_pairs={{0,4},{1,5},{2,6},{3,7},{4,8},{5,9},{6,10},{7,11},{8,12},{9,13},{1... | collective-permute-start | bytes 301064 | tf_op jit(solution)/shard_map/ppermute | solution.py:288
  96.1 7.2 %collective-permute-start.7 = (bf16[56,896]{1,0:T(8,128)(2,1)}, bf16[56,896]{1,0:T(8,128)(2,1)S(1)}, u32[]{:S(2)}, u32[]{:S(2)}) collective-permute-start(bf16[56,896]{1,0:T(8,128)(2,1)} %get-tuple-element.79), channel_id=1, source_target_pairs={{0,8},{1,9},{2,10},{3,11},{4,12},{5,13},{6,14},{7,15},{8,0},{9,1},... | collective-permute-start | bytes 301064 | tf_op jit(solution)/shard_map/ppermute | solution.py:288
  103.3 5.2 %collective-permute-start.8 = (bf16[56,896]{1,0:T(8,128)(2,1)}, bf16[56,896]{1,0:T(8,128)(2,1)S(1)}, u32[]{:S(2)}, u32[]{:S(2)}) collective-permute-start(bf16[56,896]{1,0:T(8,128)(2,1)} %get-tuple-element.80), channel_id=1, source_target_pairs={{0,12},{1,13},{2,14},{3,15},{4,0},{5,1},{6,2},{7,3},{8,4},{9,5},{1... | collective-permute-start | bytes 301064 | tf_op jit(solution)/shard_map/ppermute | solution.py:288
  108.5 10.5 %all-to-all-done.4.in_ref = bf16[32,320,128]{2,1,0:T(8,128)(2,1)S(1)} async-done(((bf16[32,320,128]{2,1,0:T(8,128)(2,1)}), bf16[32,320,128]{2,1,0:T(8,128)(2,1)S(1)}, u32[]{:S(2)}, u32[]{:S(2)}) %all-to-all-start.4) | async-done | bytes 2621472 | tf_op jit(solution)/shard_map/all_to_all | solution.py:439
  119.0 1.6 %finish.1 = (bf16[16,64,128]{2,1,0:T(8,128)(2,1)}, bf16[16,64,128]{2,1,0:T(8,128)(2,1)}, f32[28,128]{1,0:T(8,128)}, f32[28,128]{1,0:T(8,128)}) custom-call(s32[32]{0:T(128)S(1)} %get-tuple-element.50.slots_ref, bf16[32,320,128]{2,1,0:T(8,128)(2,1)S(1)} %all-to-all-done.4.in_ref), custom_call_target="tpu_custom_call" | custom-call | tf_op jit(solution)/shard_map/finish/pallas_call | solution.py:452
  120.6 1.4 %collective-permute-done.8.three_ref = bf16[56,896]{1,0:T(8,128)(2,1)S(1)} collective-permute-done((bf16[56,896]{1,0:T(8,128)(2,1)}, bf16[56,896]{1,0:T(8,128)(2,1)S(1)}, u32[]{:S(2)}, u32[]{:S(2)}) %collective-permute-start.8) | collective-permute-done | bytes 100384 | tf_op jit(solution)/shard_map/ppermute | solution.py:288
  121.9 0.7 copy-done.3
  122.6 0.7 total.1
  (61 shorter events, 4.2 us)
Async XLA Ops:
  4.0 10.6 %copy-start.10 = (s32[512,2]{0,1:T(2,128)S(1)}, s32[512,2]{0,1:T(2,128)}, u32[]{:S(2)}) copy-start(s32[512,2]{0,1:T(2,128)} %param.12) | copy-start | bytes 12292
  4.0 38.5 %all-to-all-start.3 = ((bf16[64,2,64,128]{3,2,1,0:T(8,128)(2,1)}), bf16[64,2,64,128]{3,2,1,0:T(8,128)(2,1)S(1)}, u32[]{:S(2)}, u32[]{:S(2)}) async-start(bf16[64,2,64,128]{3,2,1,0:T(8,128)(2,1)} %get-tuple-element.55), calls=%async_computation.3 | async-start | bytes 4194304 | tf_op jit(solution)/shard_map/all_to_all | solution.py:323
  16.8 5.6 %copy-start.8 = (bf16[896,128]{1,0:T(8,128)(2,1)S(1)}, bf16[896,128]{1,0:T(8,128)(2,1)}, u32[]{:S(2)}) copy-start(bf16[896,128]{1,0:T(8,128)(2,1)} %param.10) | copy-start | bytes 688132
  17.3 5.1 %copy-start.9 = (bf16[896,128]{1,0:T(8,128)(2,1)S(1)}, bf16[896,128]{1,0:T(8,128)(2,1)}, u32[]{:S(2)}) copy-start(bf16[896,128]{1,0:T(8,128)(2,1)} %param.11) | copy-start | bytes 688132
  18.1 24.5 %copy-start.4 = (s32[64]{0:T(128)}, s32[64]{0:T(128)S(1)}, u32[]{:S(2)}) copy-start(s32[64]{0:T(128)S(1)} %get-tuple-element.53.refs_0_) | copy-start | bytes 772
  26.7 31.9 %copy-start.1 = (bf16[896,256]{1,0:T(8,128)(2,1)}, bf16[896,256]{1,0:T(8,128)(2,1)S(1)}, u32[]{:S(2)}) copy-start(bf16[896,256]{1,0:T(8,128)(2,1)S(1)} %copy.31) | copy-start | bytes 1376260
  28.5 47.1 %collective-permute-start = (bf16[896,256]{1,0:T(8,128)(2,1)S(1)}, bf16[896,256]{1,0:T(8,128)(2,1)}, u32[]{:S(2)}, u32[]{:S(2)}) collective-permute-start(bf16[896,256]{1,0:T(8,128)(2,1)S(1)} %constant_dynamic-update-slice_fusion.refs_4_), channel_id=1, source_target_pairs={{0,1},{1,2},{2,3},{3,4},{4,5},{5,6},{6,7},{7,8},{8,9},{9,10},{10,1... | collective-permute-start | bytes 1376264 | tf_op jit(solution)/shard_map/ppermute | solution.py:288
  30.4 47.1 %collective-permute-start.1 = (bf16[896,256]{1,0:T(8,128)(2,1)S(1)}, bf16[896,256]{1,0:T(8,128)(2,1)}, u32[]{:S(2)}, u32[]{:S(2)}) collective-permute-start(bf16[896,256]{1,0:T(8,128)(2,1)S(1)} %constant_dynamic-update-slice_fusion.refs_4_), channel_id=1, source_target_pairs={{0,15},{1,0},{2,1},{3,2},{4,3},{5,4},{6,5},{7,6},{8,7},{9,8},{10,9... | collective-permute-start | bytes 1376264 | tf_op jit(solution)/shard_map/ppermute | solution.py:288
  39.6 37.9 %collective-permute-start.2 = (bf16[896,256]{1,0:T(8,128)(2,1)S(1)}, bf16[896,256]{1,0:T(8,128)(2,1)}, u32[]{:S(2)}, u32[]{:S(2)}) collective-permute-start(bf16[896,256]{1,0:T(8,128)(2,1)S(1)} %constant_dynamic-update-slice_fusion.refs_4_), channel_id=1, source_target_pairs={{0,2},{1,3},{2,4},{3,5},{4,6},{5,7},{6,8},{7,9},{8,10},{9,11},{10,... | collective-permute-start | bytes 1376264 | tf_op jit(solution)/shard_map/ppermute | solution.py:288
  42.6 16.1 %copy-start = (bf16[64,2,64,128]{3,2,1,0:T(8,128)(2,1)}, bf16[64,2,64,128]{3,2,1,0:T(8,128)(2,1)S(1)}, u32[]{:S(2)}) copy-start(bf16[64,2,64,128]{3,2,1,0:T(8,128)(2,1)S(1)} %all-to-all-done.3.refs_2_) | copy-start | bytes 6291460
  44.5 14.2 %copy-start.2 = (f32[32,2,128]{2,1,0:T(2,128)}, f32[32,2,128]{2,1,0:T(2,128)S(1)}, u32[]{:S(2)}) copy-start(f32[32,2,128]{2,1,0:T(2,128)S(1)} %get-tuple-element.58.refs_4_) | copy-start | bytes 98308
  66.0 19.1 %collective-permute-start.3 = (bf16[4,56,256]{2,1,0:T(8,128)(2,1)}, bf16[4,56,256]{2,1,0:T(8,128)(2,1)S(1)}, u32[]{:S(2)}, u32[]{:S(2)}) collective-permute-start(bf16[4,56,256]{2,1,0:T(8,128)(2,1)} %get-tuple-element.70), channel_id=1, source_target_pairs={{0,1},{1,2},{2,3},{3,4},{4,5},{5,6},{6,7},{7,8},{8,9},{9,10},{10,1... | collective-permute-start | bytes 344072 | tf_op jit(solution)/shard_map/ppermute | solution.py:288
  67.9 17.2 %collective-permute-start.4 = (bf16[4,56,256]{2,1,0:T(8,128)(2,1)}, bf16[4,56,256]{2,1,0:T(8,128)(2,1)S(1)}, u32[]{:S(2)}, u32[]{:S(2)}) collective-permute-start(bf16[4,56,256]{2,1,0:T(8,128)(2,1)} %get-tuple-element.71), channel_id=1, source_target_pairs={{0,15},{1,0},{2,1},{3,2},{4,3},{5,4},{6,5},{7,6},{8,7},{9,8},{10,9... | collective-permute-start | bytes 344072 | tf_op jit(solution)/shard_map/ppermute | solution.py:288
  75.6 11.0 %collective-permute-start.5 = (bf16[4,56,256]{2,1,0:T(8,128)(2,1)}, bf16[4,56,256]{2,1,0:T(8,128)(2,1)}, u32[]{:S(2)}, u32[]{:S(2)}) collective-permute-start(bf16[4,56,256]{2,1,0:T(8,128)(2,1)} %get-tuple-element.72), channel_id=1, source_target_pairs={{0,2},{1,3},{2,4},{3,5},{4,6},{5,7},{6,8},{7,9},{8,10},{9,11},{10,... | collective-permute-start | bytes 344072 | tf_op jit(solution)/shard_map/ppermute | solution.py:288
  80.5 6.1 %copy-start.5 = (bf16[4,56,256]{2,1,0:T(8,128)(2,1)S(1)}, bf16[4,56,256]{2,1,0:T(8,128)(2,1)}, u32[]{:S(2)}) copy-start(bf16[4,56,256]{2,1,0:T(8,128)(2,1)} %get-tuple-element.69.refs_0_) | copy-start | bytes 344068
  80.5 38.5 %all-to-all-start.4 = ((bf16[32,320,128]{2,1,0:T(8,128)(2,1)}), bf16[32,320,128]{2,1,0:T(8,128)(2,1)S(1)}, u32[]{:S(2)}, u32[]{:S(2)}) async-start(bf16[32,320,128]{2,1,0:T(8,128)(2,1)} %weigh.1), calls=%async_computation.4 | async-start | bytes 5242880 | tf_op jit(solution)/shard_map/all_to_all | solution.py:439
  85.1 0.6 copy-start.6
  86.6 0.9 copy-start.7
  90.7 29.8 %collective-permute-start.6 = (bf16[56,896]{1,0:T(8,128)(2,1)}, bf16[56,896]{1,0:T(8,128)(2,1)S(1)}, u32[]{:S(2)}, u32[]{:S(2)}) collective-permute-start(bf16[56,896]{1,0:T(8,128)(2,1)} %get-tuple-element.78), channel_id=1, source_target_pairs={{0,4},{1,5},{2,6},{3,7},{4,8},{5,9},{6,10},{7,11},{8,12},{9,13},{1... | collective-permute-start | bytes 301064 | tf_op jit(solution)/shard_map/ppermute | solution.py:288
  96.1 24.5 %collective-permute-start.7 = (bf16[56,896]{1,0:T(8,128)(2,1)}, bf16[56,896]{1,0:T(8,128)(2,1)S(1)}, u32[]{:S(2)}, u32[]{:S(2)}) collective-permute-start(bf16[56,896]{1,0:T(8,128)(2,1)} %get-tuple-element.79), channel_id=1, source_target_pairs={{0,8},{1,9},{2,10},{3,11},{4,12},{5,13},{6,14},{7,15},{8,0},{9,1},... | collective-permute-start | bytes 301064 | tf_op jit(solution)/shard_map/ppermute | solution.py:288
  103.3 18.6 %collective-permute-start.8 = (bf16[56,896]{1,0:T(8,128)(2,1)}, bf16[56,896]{1,0:T(8,128)(2,1)S(1)}, u32[]{:S(2)}, u32[]{:S(2)}) collective-permute-start(bf16[56,896]{1,0:T(8,128)(2,1)} %get-tuple-element.80), channel_id=1, source_target_pairs={{0,12},{1,13},{2,14},{3,15},{4,0},{5,1},{6,2},{7,3},{8,4},{9,5},{1... | collective-permute-start | bytes 301064 | tf_op jit(solution)/shard_map/ppermute | solution.py:288
  121.9 0.7 copy-start.3

commit v8 on v7

--- a/solution.py
+++ b/solution.py
@@ -15,6 +15,7 @@
 FAR = (0, 4, 8, -4)
 VMEM_LIMIT = 40 * 1024 * 1024
 LARGE_LIMIT = 60 * 1024 * 1024
+SMALL_LIMIT = 16 * 1024 * 1024
 VMEM = pltpu.VMEM
 SMEM = pltpu.SMEM
 HBM = pltpu.HBM
@@ -216,26 +217,34 @@
     pltpu.make_async_copy(stage, out_ref.at[:, :parts], out_sem).wait()
 
 
-def weigh_kernel(parts, rows_ref, enc_t_ref, back_ref, out_ref, stage, sem):
+def weigh_kernel(parts, rows_ref, enc_hbm, back_ref, out_ref, enc_t, stage, enc_sems, sem):
     head_dim = rows_ref.shape[1] // 2
     seq_count, room = stage.shape[0], stage.shape[1] // 2
-    share = enc_t_ref.shape[0] // seq_count
-    batch = 8
-    for i in range(0, seq_count, batch):
-        term = nn_dot(enc_t_ref[i * share:(i + batch) * share], rows_ref[...])
+    share = enc_t.shape[0] // seq_count
+    batch = seq_count // enc_sems.shape[0]
+
+    def fetch(i):
+        at = pl.ds(i * batch * share, batch * share)
+        return pltpu.make_async_copy(enc_hbm.at[at], enc_t.at[at], enc_sems.at[i])
+
+    for i in range(enc_sems.shape[0]):
+        fetch(i).start()
+    for i in range(enc_sems.shape[0]):
+        fetch(i).wait()
+        term = nn_dot(enc_t[i * batch * share:(i + 1) * batch * share], rows_ref[...])
         for s in range(batch):
             part = term[s * share:(s + 1) * share]
             if room > share:
                 part = jnp.concatenate([part, jnp.zeros((room - share, 2 * head_dim), jnp.float32)], axis=0)
             part = part.astype(jnp.bfloat16)
-            stage[i + s, :room] = part[:, :head_dim]
-            stage[i + s, room:] = part[:, head_dim:]
-        at = pl.ds(i, batch)
+            stage[i * batch + s, :room] = part[:, :head_dim]
+            stage[i * batch + s, room:] = part[:, head_dim:]
+        at = pl.ds(i * batch, batch)
         pltpu.make_async_copy(stage.at[at], out_ref.at[at, parts:], sem).start()
     pltpu.make_async_copy(stage, out_ref.at[:, parts:], sem).wait()
 
 
-def finish_kernel(slots_ref, in_ref, att_ref, qg_ref, kw_ref, vw_ref):
+def finish_kernel(slots_ref, in_ref, own_ref, one_ref, two_ref, three_ref, att_ref, qg_ref, enc_ref, kw_ref, vw_ref):
     share = kw_ref.shape[0]
     parts = 2 * CAP * SEGMENT
     room = (in_ref.shape[1] - parts) // 2
@@ -253,34 +262,40 @@
         qg_ref[c] = total[SEGMENT:]
         return 0
 
-    lax.fori_loop(0, att_ref.shape[0], step, 0, unroll=2)
+    lax.fori_loop(0, att_ref.shape[0], step, 0, unroll=4)
     total = in_ref[0, parts:, :].astype(jnp.float32)
     for s in range(1, in_ref.shape[0]):
         total = total + in_ref[s, parts:, :].astype(jnp.float32)
     kw_ref[...] = total[:share]
     vw_ref[...] = total[room:room + share]
+    total = own_ref[...] + one_ref[...].astype(jnp.float32)
+    enc_ref[...] = total + two_ref[...].astype(jnp.float32) + three_ref[...].astype(jnp.float32)
 
 
 def project_kernel(*refs):
     near = len(NEAR)
-    rows_refs, weight_refs, own_ref, far_refs = refs[:near], refs[near:2 * near], refs[2 * near], refs[2 * near + 1:]
-    far, rows, width = rows_refs[0].shape
+    rows_hbm, weights_hbm, own_ref, far_refs = refs[:near], refs[near:2 * near], refs[2 * near], refs[2 * near + 1:-3]
+    rows_ref, weights_ref, sems = refs[-3:]
+    _, far, rows, width = rows_ref.shape
+    copies = []
+    for n in range(near):
+        copies.append(pltpu.make_async_copy(weights_hbm[n], weights_ref.at[n], sems.at[n]))
+        copies.append(pltpu.make_async_copy(rows_hbm[n], rows_ref.at[n], sems.at[near + n]))
+    for copy in copies:
+        copy.start()
+    for copy in copies:
+        copy.wait()
     half = far // 2
     for i in range(0, far, half):
         total = jnp.zeros((half * rows, own_ref.shape[1]), jnp.float32)
-        for rows_ref, weight_ref in zip(rows_refs, weight_refs):
-            total = total + nt_dot(rows_ref[i:i + half].reshape(half * rows, width), weight_ref[...])
+        for n in range(near):
+            total = total + nt_dot(rows_ref[n, i:i + half].reshape(half * rows, width), weights_ref[n])
         for j in range(half):
             part = total[j * rows:(j + 1) * rows]
             if i + j == 0:
                 own_ref[...] = part
             else:
                 far_refs[i + j - 1][...] = part.astype(jnp.bfloat16)
-
-
-def total_kernel(own_ref, one_ref, two_ref, three_ref, done_ref, out_ref):
-    total = own_ref[...] + one_ref[...].astype(jnp.float32)
-    out_ref[...] = total + two_ref[...].astype(jnp.float32) + three_ref[...].astype(jnp.float32)
 
 
 def shifted(x, step):
@@ -429,9 +444,14 @@
     back = pl.pallas_call(
         lambda *refs: weigh_kernel(parts, *refs),
         out_shape=jax.ShapeDtypeStruct(back_shape, bf16),
-        in_specs=[spec(VMEM), spec(VMEM), spec(HBM)],
+        in_specs=[spec(VMEM), spec(HBM), spec(HBM)],
         out_specs=spec(HBM),
-        scratch_shapes=[pltpu.VMEM((seq_count, 2 * room, head_dim), bf16), pltpu.SemaphoreType.DMA],
+        scratch_shapes=[
+            pltpu.VMEM(enc_t.shape, bf16),
+            pltpu.VMEM((seq_count, 2 * room, head_dim), bf16),
+            pltpu.SemaphoreType.DMA((4,)),
+            pltpu.SemaphoreType.DMA,
+        ],
         input_output_aliases={2: 0},
         compiler_params=params(LARGE_LIMIT),
         name="weigh",
@@ -443,33 +463,32 @@
             jax.ShapeDtypeStruct((rows, enc_width), f32),
             *[jax.ShapeDtypeStruct((rows, enc_width), bf16)] * (far - 1),
         ),
-        in_specs=[spec(VMEM)] * (2 * near),
+        in_specs=[spec(HBM)] * (2 * near),
         out_specs=(spec(VMEM),) * far,
-        compiler_params=params(),
+        scratch_shapes=[
+            pltpu.VMEM((near, far, rows, 2 * head_dim), bf16),
+            pltpu.VMEM((near, enc_width, 2 * head_dim), bf16),
+            pltpu.SemaphoreType.DMA((2 * near,)),
+        ],
+        compiler_params=params(SMALL_LIMIT),
         cost_estimate=pl.CostEstimate(flops=6 * 10**10, bytes_accessed=2 * 10**6, transcendentals=0),
         name="project",
     )(*near_rows, *near_weights)
-    attended, query_grad, key_weight_grad, value_weight_grad = pl.pallas_call(
+    far_sums = [shifted(part, b) for b, part in zip(FAR[1:], far_sums)]
+    attended, query_grad, encoding_grad, key_weight_grad, value_weight_grad = pl.pallas_call(
         finish_kernel,
         out_shape=(
             jax.ShapeDtypeStruct((segments, SEGMENT, head_dim), bf16),
             jax.ShapeDtypeStruct((segments, SEGMENT, head_dim), bf16),
+            jax.ShapeDtypeStruct((rows, enc_width), f32),
             jax.ShapeDtypeStruct((share, head_dim), f32),
             jax.ShapeDtypeStruct((share, head_dim), f32),
         ),
-        in_specs=[spec(SMEM), spec(VMEM)],
-        out_specs=(spec(VMEM),) * 4,
+        in_specs=[spec(SMEM), *[spec(VMEM)] * (1 + far)],
+        out_specs=(spec(VMEM),) * 5,
         compiler_params=params(),
         name="finish",
-    )(slots, returned)
-    encoding_grad = pl.pallas_call(
-        total_kernel,
-        out_shape=jax.ShapeDtypeStruct((rows, enc_width), f32),
-        in_specs=[*[spec(VMEM)] * far, spec(HBM)],
-        out_specs=spec(VMEM),
-        compiler_params=params(),
-        name="total",
-    )(own, *[shifted(part, b) for b, part in zip(FAR[1:], far_sums)], key_weight_grad)
+    )(slots, returned, own, *far_sums)
     return (
         attended.reshape(segments * SEGMENT, head_dim),
         query_grad.reshape(segments * SEGMENT, head_dim),

time: 124 us -> 125 us (level)
    ppermute x9, waiting for transfers between devices: 2.26 us -> 13.1 us  [shifted(): lax.ppermute(x, 'head', [(z, (z + step) % count) for z in range(count)])]
    all_to_all x1, waiting for transfers between devices: 10.5 us -> 0.01 us  [on_device(): lax.all_to_all(back, 'seq', split_axis=0, concat_axis=0, tiled=True)]
    pallas_call x1, Pallas kernels: 2.93 us -> 4.3 us  [on_device(): pl.pallas_call(lambda *refs: weigh_kernel(parts, *refs), out_shape=jax.Sh...]
  transfers between devices with their start and end apart: 11 -> 11, of which waited for: 4 -> 3; matrix products, arithmetic and copies ran while one was open for 11% -> 11% of each run, Pallas kernels for 14% -> 13%
where the time goes in v8:
time: 125 us; the launch traced here: 124 us
  starting transfers between devices  58.3 us (47%)
  Pallas kernels  21.6 us (17%)
  waiting for transfers between devices  14.2 us (11%)
  blocking collectives  14.1 us (11%)
  local copies, waits for them, and re-layouts  8.95 us (7%)
  matrix products  3.09 us (2%)
  other arithmetic  2.61 us (2%)
  between operations  1.68 us (1%)
    ppermute x9, starting transfers between devices, shifted(): lax.ppermute(x, 'head', [(z, (z + step) % count) for z in range(count)])  43.1 us
    all_to_all x1, blocking collectives, one_hop(): return lax.all_to_all(sent, 'seq', split_axis=0, concat_axis=0, tiled=True)  14.1 us
    ppermute x9, waiting for transfers between devices, shifted(): lax.ppermute(x, 'head', [(z, (z + step) % count) for z in range(count)])  13.1 us
    all_to_all x1, starting transfers between devices, on_device(): lax.all_to_all(packed, 'seq', split_axis=0, concat_axis=0, tiled=True)  10.6 us
    pallas_call x1, Pallas kernels, on_device(): pl.pallas_call(lambda *refs: grads_kernel(scale, group, *refs), out_shape...  7.33 us
    all_to_all x1, starting transfers between devices, on_device(): lax.all_to_all(back, 'seq', split_axis=0, concat_axis=0, tiled=True)  4.54 us
    pallas_call x1, Pallas kernels, on_device(): pl.pallas_call(lambda *refs: weigh_kernel(parts, *refs), out_shape=jax.Sh...  4.3 us
    reshape x1, local copies, waits for them, and re-layouts, on_device(): flat_enc = encodings.reshape(block_count * block_len, enc_width)  3.59 us
  transfers between devices with their start and end apart: 11, of which 3 were waited for; matrix products, arithmetic and copies ran while one was open for 11% of the time, Pallas kernels for 13%

profile of v8, /device:TPU:1, one launch (start us, length us, event | category | flops | bytes accessed | tf_op | source)
XLA Modules:
  0.0 124.4 jit_solution(17025260232651495275)
XLA Ops:
  0.6 3.4 %pack.1 = (bf16[64,2,64,128]{3,2,1,0:T(8,128)(2,1)}, s32[32]{0:T(128)S(1)}) custom-call(s32[2,512]{1,0:T(2,128)} %bitcast.44, bf16[16,64,128]{2,1,0:T(8,128)(2,1)} %bitcast.39, bf16[16,64,128]{2,1,0:T(8,128)(2,1)} %bitcast.40), custom_call_target="tpu_custom_call" | custom-call | tf_op jit(solution)/shard_map/pack/pallas_call | solution.py:318
  4.0 10.6 %all-to-all-start.3 = ((bf16[64,2,64,128]{3,2,1,0:T(8,128)(2,1)}), bf16[64,2,64,128]{3,2,1,0:T(8,128)(2,1)S(1)}, u32[]{:S(2)}, u32[]{:S(2)}) async-start(bf16[64,2,64,128]{3,2,1,0:T(8,128)(2,1)} %get-tuple-element.56), calls=%async_computation.3 | async-start | bytes 4194304 | tf_op jit(solution)/shard_map/all_to_all | solution.py:338
  14.9 0.3 broadcast_compare_fusion
  16.1 0.4 rev.6
  16.4 0.4 select_reduce_fusion.1
  18.8 3.6 %copy.32 = bf16[896,896]{0,1:T(8,128)(2,1)} copy(bf16[896,896]{1,0:T(8,128)(2,1)} %bitcast.36) | data formatting | bytes 3211264 | tf_op jit(solution)/shard_map/reshape | solution.py:342
  22.5 2.9 %fusion = bf16[896,256]{0,1:T(8,128)(2,1)} fusion(bf16[896,256]{1,0:T(8,128)(2,1)S(1)} %constant_dynamic-update-slice_fusion.refs_4_, bf16[896,896]{1,0:T(8,128)(2,1)} %bitcast.37), kind=kOutput, calls=%fused_computation.1 | convolution fusion | flops 411271168 | bytes 2523136 | tf_op jit(solution)/shard_map/dot_general | solution.py:343
  25.5 1.2 copy.31
  26.7 0.7 fusion.6
  28.0 0.5 broadcast_select_fusion
  28.5 1.9 %collective-permute-start = (bf16[896,256]{1,0:T(8,128)(2,1)S(1)}, bf16[896,256]{1,0:T(8,128)(2,1)}, u32[]{:S(2)}, u32[]{:S(2)}) collective-permute-start(bf16[896,256]{1,0:T(8,128)(2,1)S(1)} %constant_dynamic-update-slice_fusion.refs_4_), channel_id=1, source_target_pairs={{0,1},{1,2},{2,3},{3,4},{4,5},{5,6},{6,7},{7,8},{8,9},{9,10},{10,1... | collective-permute-start | bytes 1376264 | tf_op jit(solution)/shard_map/ppermute | solution.py:303
  30.5 9.1 %collective-permute-start.1 = (bf16[896,256]{1,0:T(8,128)(2,1)S(1)}, bf16[896,256]{1,0:T(8,128)(2,1)}, u32[]{:S(2)}, u32[]{:S(2)}) collective-permute-start(bf16[896,256]{1,0:T(8,128)(2,1)S(1)} %constant_dynamic-update-slice_fusion.refs_4_), channel_id=1, source_target_pairs={{0,15},{1,0},{2,1},{3,2},{4,3},{5,4},{6,5},{7,6},{8,7},{9,8},{10,9... | collective-permute-start | bytes 1376264 | tf_op jit(solution)/shard_map/ppermute | solution.py:303
  39.6 1.9 %collective-permute-start.2 = (bf16[896,256]{1,0:T(8,128)(2,1)S(1)}, bf16[896,256]{1,0:T(8,128)(2,1)}, u32[]{:S(2)}, u32[]{:S(2)}) collective-permute-start(bf16[896,256]{1,0:T(8,128)(2,1)S(1)} %constant_dynamic-update-slice_fusion.refs_4_), channel_id=1, source_target_pairs={{0,2},{1,3},{2,4},{3,5},{4,6},{5,7},{6,8},{7,9},{8,10},{9,11},{10,... | collective-permute-start | bytes 1376264 | tf_op jit(solution)/shard_map/ppermute | solution.py:303
  41.5 1.0 all-to-all-done.3.refs_2_
  42.6 1.9 %stats.1 = (f32[32,2,128]{2,1,0:T(2,128)S(1)}, f32[64,128]{1,0:T(8,128)S(1)}, f32[256,128]{1,0:T(8,128)S(1)}) custom-call(s32[64]{0:T(128)S(1)} %get-tuple-element.54.refs_0_, s32[64]{0:T(128)S(1)} %get-tuple-element.58.refs_1_, bf16[64,2,64,128]{3,2,1,0:T(8,128)(2,1)S(1)} %all-to-all-done.3.refs_2_, bf16[7,128,256]{2,1,0:T(8,128)(2,1)S(1)} %bitcast.31), custom_call_target="tpu_custom_call" | custom-call | tf_op jit(solution)/shard_map/stats/pallas_call | solution.py:380
  44.5 14.1 %conditional.1 = (f32[256,128]{1,0:T(8,128)S(1)}) conditional(s32[]{:T(128)} %convert_element_type.23, (f32[64,128]{1,0:T(8,128)S(1)}, s32[32]{0:T(128)S(1)}) %tuple.19, f32[256,128]{1,0:T(8,128)S(1)} %get-tuple-element.62), branch_computations={%region_7.8_spmd, %region_8.9_spmd} | conditional | bytes 294924 | solution.py:410
  44.5 14.1 %all_to_all.38 = f32[32,8,128]{2,1,0:T(8,128)S(1)} all-to-all(f32[32,8,128]{2,1,0:T(8,128)S(1)} %bitcast.42), channel_id=1, replica_groups=mesh['seq'=32,'head'=16] {'seq'}, dimensions={0} | all-to-all | bytes 262144 | tf_op jit(solution)/shard_map/cond/branch_1_fun/all_to_all | solution.py:395
  58.6 7.3 %grads.1 = (bf16[32,320,128]{2,1,0:T(8,128)(2,1)}, bf16[4,56,256]{2,1,0:T(8,128)(2,1)}, bf16[4,56,256]{2,1,0:T(8,128)(2,1)}, bf16[4,56,256]{2,1,0:T(8,128)(2,1)}...) custom-call(s32[64]{0:T(128)} %copy-done.3, s32[64]{0:T(128)} %get-tuple-element.55.refs_1_, ...), custom_call_target="tpu_custom_call" | custom-call | tf_op jit(solution)/shard_map/grads/pallas_call | solution.py:418
  66.0 1.9 %collective-permute-start.3 = (bf16[4,56,256]{2,1,0:T(8,128)(2,1)}, bf16[4,56,256]{2,1,0:T(8,128)(2,1)S(1)}, u32[]{:S(2)}, u32[]{:S(2)}) collective-permute-start(bf16[4,56,256]{2,1,0:T(8,128)(2,1)} %get-tuple-element.69), channel_id=1, source_target_pairs={{0,1},{1,2},{2,3},{3,4},{4,5},{5,6},{6,7},{7,8},{8,9},{9,10},{10,1... | collective-permute-start | bytes 344072 | tf_op jit(solution)/shard_map/ppermute | solution.py:303
  67.9 7.7 %collective-permute-start.4 = (bf16[4,56,256]{2,1,0:T(8,128)(2,1)}, bf16[4,56,256]{2,1,0:T(8,128)(2,1)S(1)}, u32[]{:S(2)}, u32[]{:S(2)}) collective-permute-start(bf16[4,56,256]{2,1,0:T(8,128)(2,1)} %get-tuple-element.70), channel_id=1, source_target_pairs={{0,15},{1,0},{2,1},{3,2},{4,3},{5,4},{6,5},{7,6},{8,7},{9,8},{10,9... | collective-permute-start | bytes 344072 | tf_op jit(solution)/shard_map/ppermute | solution.py:303
  75.6 1.9 %collective-permute-start.5 = (bf16[4,56,256]{2,1,0:T(8,128)(2,1)}, bf16[4,56,256]{2,1,0:T(8,128)(2,1)}, u32[]{:S(2)}, u32[]{:S(2)}) collective-permute-start(bf16[4,56,256]{2,1,0:T(8,128)(2,1)} %get-tuple-element.71), channel_id=1, source_target_pairs={{0,2},{1,3},{2,4},{3,5},{4,6},{5,7},{6,8},{7,9},{8,10},{9,11},{10,... | collective-permute-start | bytes 344072 | tf_op jit(solution)/shard_map/ppermute | solution.py:303
  77.6 4.3 %weigh.1 = bf16[32,320,128]{2,1,0:T(8,128)(2,1)} custom-call(bf16[896,256]{1,0:T(8,128)(2,1)} %get-tuple-element.63.refs_0_, bf16[896,896]{1,0:T(8,128)(2,1)} %bitcast.35, bf16[32,320,128]{2,1,0:T(8,128)(2,1)} %get-tuple-element.67.refs_2_), custom_call_target="tpu_custom_call", output_to_operand_aliasing={{}: (2, {})} | custom-call | tf_op jit(solution)/shard_map/weigh/pallas_call | solution.py:444
  81.9 4.5 %all-to-all-start.4 = ((bf16[32,320,128]{2,1,0:T(8,128)(2,1)}), bf16[32,320,128]{2,1,0:T(8,128)(2,1)S(1)}, u32[]{:S(2)}, u32[]{:S(2)}) async-start(bf16[32,320,128]{2,1,0:T(8,128)(2,1)} %weigh.1), calls=%async_computation.4 | async-start | bytes 5242880 | tf_op jit(solution)/shard_map/all_to_all | solution.py:459
  86.5 0.6 copy-done.5
  87.1 0.9 copy-done.6
  88.0 3.1 %project.1 = (f32[56,896]{1,0:T(8,128)S(1)}, bf16[56,896]{1,0:T(8,128)(2,1)S(1)}, bf16[56,896]{1,0:T(8,128)(2,1)S(1)}, bf16[56,896]{1,0:T(8,128)(2,1)S(1)}) custom-call(bf16[4,56,256]{2,1,0:T(8,128)(2,1)S(1)} %copy-done.4, bf16[4,56,256]{2,1,0:T(8,128)(2,1)S(1)} %collective-permute-done.3.refs_1_, bf16[4,56,256]{2,1,0:T(8,128)(2,1)S(1)} %copy-done.6, ...), custom_call_target="tpu_custom_call" | custom-call | flops 60000002048 | bytes 2000000 | tf_op jit(solution)/shard_map/project/pallas_call | solution.py:460
  91.1 6.2 %collective-permute-start.6 = (bf16[56,896]{1,0:T(8,128)(2,1)S(1)}, bf16[56,896]{1,0:T(8,128)(2,1)S(1)}, u32[]{:S(2)}, u32[]{:S(2)}) collective-permute-start(bf16[56,896]{1,0:T(8,128)(2,1)S(1)} %get-tuple-element.77), channel_id=1, source_target_pairs={{0,4},{1,5},{2,6},{3,7},{4,8},{5,9},{6,10},{7,11},{8,12},{9,13},{1... | collective-permute-start | bytes 301064 | tf_op jit(solution)/shard_map/ppermute | solution.py:303
  97.3 7.2 %collective-permute-start.7 = (bf16[56,896]{1,0:T(8,128)(2,1)S(1)}, bf16[56,896]{1,0:T(8,128)(2,1)S(1)}, u32[]{:S(2)}, u32[]{:S(2)}) collective-permute-start(bf16[56,896]{1,0:T(8,128)(2,1)S(1)} %get-tuple-element.78), channel_id=1, source_target_pairs={{0,8},{1,9},{2,10},{3,11},{4,12},{5,13},{6,14},{7,15},{8,0},{9,1},... | collective-permute-start | bytes 301064 | tf_op jit(solution)/shard_map/ppermute | solution.py:303
  104.5 5.2 %collective-permute-start.8 = (bf16[56,896]{1,0:T(8,128)(2,1)S(1)}, bf16[56,896]{1,0:T(8,128)(2,1)S(1)}, u32[]{:S(2)}, u32[]{:S(2)}) collective-permute-start(bf16[56,896]{1,0:T(8,128)(2,1)S(1)} %get-tuple-element.79), channel_id=1, source_target_pairs={{0,12},{1,13},{2,14},{3,15},{4,0},{5,1},{6,2},{7,3},{8,4},{9,5},{1... | collective-permute-start | bytes 301064 | tf_op jit(solution)/shard_map/ppermute | solution.py:303
  109.7 8.2 %collective-permute-done.7.two_ref = bf16[56,896]{1,0:T(8,128)(2,1)S(1)} collective-permute-done((bf16[56,896]{1,0:T(8,128)(2,1)S(1)}, bf16[56,896]{1,0:T(8,128)(2,1)S(1)}, u32[]{:S(2)}, u32[]{:S(2)}) %collective-permute-start.7) | collective-permute-done | bytes 100384 | tf_op jit(solution)/shard_map/ppermute | solution.py:303
  117.9 4.9 %collective-permute-done.8.three_ref = bf16[56,896]{1,0:T(8,128)(2,1)S(1)} collective-permute-done((bf16[56,896]{1,0:T(8,128)(2,1)S(1)}, bf16[56,896]{1,0:T(8,128)(2,1)S(1)}, u32[]{:S(2)}, u32[]{:S(2)}) %collective-permute-start.8) | collective-permute-done | bytes 100384 | tf_op jit(solution)/shard_map/ppermute | solution.py:303
  122.8 1.6 %finish.1 = (bf16[16,64,128]{2,1,0:T(8,128)(2,1)}, bf16[16,64,128]{2,1,0:T(8,128)(2,1)}, f32[56,896]{1,0:T(8,128)}, f32[28,128]{1,0:T(8,128)}, f32[28,128]{1,0:T(8,128)}) custom-call(s32[32]{0:T(128)S(1)} %get-tuple-element.51.slots_ref, bf16[32,320,128]{2,1,0:T(8,128)(2,1)S(1)} %all-to-all-done.4.in_ref, f32[56,896]{1,0:T(8,128)S(1)} %get-tuple-element.76.own_ref, ...), custom_call_target="tpu_custom_call" | custom-call | tf_op jit(solution)/shard_map/finish/pallas_call | solution.py:478
  (58 shorter events, 3.2 us)
Async XLA Ops:
  4.0 10.6 %copy-start.9 = (s32[512,2]{0,1:T(2,128)S(1)}, s32[512,2]{0,1:T(2,128)}, u32[]{:S(2)}) copy-start(s32[512,2]{0,1:T(2,128)} %param.12) | copy-start | bytes 12292
  4.0 38.6 %all-to-all-start.3 = ((bf16[64,2,64,128]{3,2,1,0:T(8,128)(2,1)}), bf16[64,2,64,128]{3,2,1,0:T(8,128)(2,1)S(1)}, u32[]{:S(2)}, u32[]{:S(2)}) async-start(bf16[64,2,64,128]{3,2,1,0:T(8,128)(2,1)} %get-tuple-element.56), calls=%async_computation.3 | async-start | bytes 4194304 | tf_op jit(solution)/shard_map/all_to_all | solution.py:338
  16.9 5.6 %copy-start.7 = (bf16[896,128]{1,0:T(8,128)(2,1)S(1)}, bf16[896,128]{1,0:T(8,128)(2,1)}, u32[]{:S(2)}) copy-start(bf16[896,128]{1,0:T(8,128)(2,1)} %param.10) | copy-start | bytes 688132
  17.3 5.1 %copy-start.8 = (bf16[896,128]{1,0:T(8,128)(2,1)S(1)}, bf16[896,128]{1,0:T(8,128)(2,1)}, u32[]{:S(2)}) copy-start(bf16[896,128]{1,0:T(8,128)(2,1)} %param.11) | copy-start | bytes 688132
  18.1 24.5 %copy-start.3 = (s32[64]{0:T(128)}, s32[64]{0:T(128)S(1)}, u32[]{:S(2)}) copy-start(s32[64]{0:T(128)S(1)} %get-tuple-element.54.refs_0_) | copy-start | bytes 772
  26.7 31.9 %copy-start.1 = (bf16[896,256]{1,0:T(8,128)(2,1)}, bf16[896,256]{1,0:T(8,128)(2,1)S(1)}, u32[]{:S(2)}) copy-start(bf16[896,256]{1,0:T(8,128)(2,1)S(1)} %copy.31) | copy-start | bytes 1376260
  28.5 47.1 %collective-permute-start = (bf16[896,256]{1,0:T(8,128)(2,1)S(1)}, bf16[896,256]{1,0:T(8,128)(2,1)}, u32[]{:S(2)}, u32[]{:S(2)}) collective-permute-start(bf16[896,256]{1,0:T(8,128)(2,1)S(1)} %constant_dynamic-update-slice_fusion.refs_4_), channel_id=1, source_target_pairs={{0,1},{1,2},{2,3},{3,4},{4,5},{5,6},{6,7},{7,8},{8,9},{9,10},{10,1... | collective-permute-start | bytes 1376264 | tf_op jit(solution)/shard_map/ppermute | solution.py:303
  30.5 47.1 %collective-permute-start.1 = (bf16[896,256]{1,0:T(8,128)(2,1)S(1)}, bf16[896,256]{1,0:T(8,128)(2,1)}, u32[]{:S(2)}, u32[]{:S(2)}) collective-permute-start(bf16[896,256]{1,0:T(8,128)(2,1)S(1)} %constant_dynamic-update-slice_fusion.refs_4_), channel_id=1, source_target_pairs={{0,15},{1,0},{2,1},{3,2},{4,3},{5,4},{6,5},{7,6},{8,7},{9,8},{10,9... | collective-permute-start | bytes 1376264 | tf_op jit(solution)/shard_map/ppermute | solution.py:303
  39.6 37.9 %collective-permute-start.2 = (bf16[896,256]{1,0:T(8,128)(2,1)S(1)}, bf16[896,256]{1,0:T(8,128)(2,1)}, u32[]{:S(2)}, u32[]{:S(2)}) collective-permute-start(bf16[896,256]{1,0:T(8,128)(2,1)S(1)} %constant_dynamic-update-slice_fusion.refs_4_), channel_id=1, source_target_pairs={{0,2},{1,3},{2,4},{3,5},{4,6},{5,7},{6,8},{7,9},{8,10},{9,11},{10,... | collective-permute-start | bytes 1376264 | tf_op jit(solution)/shard_map/ppermute | solution.py:303
  42.6 16.0 %copy-start = (bf16[64,2,64,128]{3,2,1,0:T(8,128)(2,1)}, bf16[64,2,64,128]{3,2,1,0:T(8,128)(2,1)S(1)}, u32[]{:S(2)}) copy-start(bf16[64,2,64,128]{3,2,1,0:T(8,128)(2,1)S(1)} %all-to-all-done.3.refs_2_) | copy-start | bytes 6291460
  44.5 14.1 %copy-start.2 = (f32[32,2,128]{2,1,0:T(2,128)}, f32[32,2,128]{2,1,0:T(2,128)S(1)}, u32[]{:S(2)}) copy-start(f32[32,2,128]{2,1,0:T(2,128)S(1)} %get-tuple-element.59.refs_4_) | copy-start | bytes 98308
  66.0 20.5 %collective-permute-start.3 = (bf16[4,56,256]{2,1,0:T(8,128)(2,1)}, bf16[4,56,256]{2,1,0:T(8,128)(2,1)S(1)}, u32[]{:S(2)}, u32[]{:S(2)}) collective-permute-start(bf16[4,56,256]{2,1,0:T(8,128)(2,1)} %get-tuple-element.69), channel_id=1, source_target_pairs={{0,1},{1,2},{2,3},{3,4},{4,5},{5,6},{6,7},{7,8},{8,9},{9,10},{10,1... | collective-permute-start | bytes 344072 | tf_op jit(solution)/shard_map/ppermute | solution.py:303
  67.9 18.6 %collective-permute-start.4 = (bf16[4,56,256]{2,1,0:T(8,128)(2,1)}, bf16[4,56,256]{2,1,0:T(8,128)(2,1)S(1)}, u32[]{:S(2)}, u32[]{:S(2)}) collective-permute-start(bf16[4,56,256]{2,1,0:T(8,128)(2,1)} %get-tuple-element.70), channel_id=1, source_target_pairs={{0,15},{1,0},{2,1},{3,2},{4,3},{5,4},{6,5},{7,6},{8,7},{9,8},{10,9... | collective-permute-start | bytes 344072 | tf_op jit(solution)/shard_map/ppermute | solution.py:303
  75.6 11.5 %collective-permute-start.5 = (bf16[4,56,256]{2,1,0:T(8,128)(2,1)}, bf16[4,56,256]{2,1,0:T(8,128)(2,1)}, u32[]{:S(2)}, u32[]{:S(2)}) collective-permute-start(bf16[4,56,256]{2,1,0:T(8,128)(2,1)} %get-tuple-element.71), channel_id=1, source_target_pairs={{0,2},{1,3},{2,4},{3,5},{4,6},{5,7},{6,8},{7,9},{8,10},{9,11},{10,... | collective-permute-start | bytes 344072 | tf_op jit(solution)/shard_map/ppermute | solution.py:303
  81.9 5.2 %copy-start.4 = (bf16[4,56,256]{2,1,0:T(8,128)(2,1)S(1)}, bf16[4,56,256]{2,1,0:T(8,128)(2,1)}, u32[]{:S(2)}) copy-start(bf16[4,56,256]{2,1,0:T(8,128)(2,1)} %get-tuple-element.68.refs_0_) | copy-start | bytes 344068
  81.9 40.9 %all-to-all-start.4 = ((bf16[32,320,128]{2,1,0:T(8,128)(2,1)}), bf16[32,320,128]{2,1,0:T(8,128)(2,1)S(1)}, u32[]{:S(2)}, u32[]{:S(2)}) async-start(bf16[32,320,128]{2,1,0:T(8,128)(2,1)} %weigh.1), calls=%async_computation.4 | async-start | bytes 5242880 | tf_op jit(solution)/shard_map/all_to_all | solution.py:459
  86.5 0.6 copy-start.5
  87.1 0.9 copy-start.6
  91.1 18.6 %collective-permute-start.6 = (bf16[56,896]{1,0:T(8,128)(2,1)S(1)}, bf16[56,896]{1,0:T(8,128)(2,1)S(1)}, u32[]{:S(2)}, u32[]{:S(2)}) collective-permute-start(bf16[56,896]{1,0:T(8,128)(2,1)S(1)} %get-tuple-element.77), channel_id=1, source_target_pairs={{0,4},{1,5},{2,6},{3,7},{4,8},{5,9},{6,10},{7,11},{8,12},{9,13},{1... | collective-permute-start | bytes 301064 | tf_op jit(solution)/shard_map/ppermute | solution.py:303
  97.3 20.6 %collective-permute-start.7 = (bf16[56,896]{1,0:T(8,128)(2,1)S(1)}, bf16[56,896]{1,0:T(8,128)(2,1)S(1)}, u32[]{:S(2)}, u32[]{:S(2)}) collective-permute-start(bf16[56,896]{1,0:T(8,128)(2,1)S(1)} %get-tuple-element.78), channel_id=1, source_target_pairs={{0,8},{1,9},{2,10},{3,11},{4,12},{5,13},{6,14},{7,15},{8,0},{9,1},... | collective-permute-start | bytes 301064 | tf_op jit(solution)/shard_map/ppermute | solution.py:303
  104.5 18.3 %collective-permute-start.8 = (bf16[56,896]{1,0:T(8,128)(2,1)S(1)}, bf16[56,896]{1,0:T(8,128)(2,1)S(1)}, u32[]{:S(2)}, u32[]{:S(2)}) collective-permute-start(bf16[56,896]{1,0:T(8,128)(2,1)S(1)} %get-tuple-element.79), channel_id=1, source_target_pairs={{0,12},{1,13},{2,14},{3,15},{4,0},{5,1},{6,2},{7,3},{8,4},{9,5},{1... | collective-permute-start | bytes 301064 | tf_op jit(solution)/shard_map/ppermute | solution.py:303

commit v9 on v6

--- a/solution.py
+++ b/solution.py
@@ -15,6 +15,7 @@
 FAR = (0, 4, 8, -4)
 VMEM_LIMIT = 40 * 1024 * 1024
 LARGE_LIMIT = 60 * 1024 * 1024
+SMALL_LIMIT = 16 * 1024 * 1024
 VMEM = pltpu.VMEM
 SMEM = pltpu.SMEM
 HBM = pltpu.HBM
@@ -232,7 +233,7 @@
     pltpu.make_async_copy(stage, out_ref, out_sem).wait()
 
 
-def finish_kernel(slots_ref, in_ref, att_ref, qg_ref, kw_ref, vw_ref):
+def finish_kernel(slots_ref, in_ref, own_ref, one_ref, two_ref, three_ref, att_ref, qg_ref, enc_ref, kw_ref, vw_ref):
     share = kw_ref.shape[0]
     parts = 2 * CAP * SEGMENT
     room = (in_ref.shape[1] - parts) // 2
@@ -250,23 +251,34 @@
         qg_ref[c] = total[SEGMENT:]
         return 0
 
-    lax.fori_loop(0, att_ref.shape[0], step, 0, unroll=2)
+    lax.fori_loop(0, att_ref.shape[0], step, 0, unroll=4)
     total = in_ref[0, parts:, :].astype(jnp.float32)
     for s in range(1, in_ref.shape[0]):
         total = total + in_ref[s, parts:, :].astype(jnp.float32)
     kw_ref[...] = total[:share]
     vw_ref[...] = total[room:room + share]
+    total = own_ref[...] + one_ref[...].astype(jnp.float32)
+    enc_ref[...] = total + two_ref[...].astype(jnp.float32) + three_ref[...].astype(jnp.float32)
 
 
 def project_kernel(*refs):
     near = len(NEAR)
-    rows_refs, weight_refs, own_ref, far_refs = refs[:near], refs[near:2 * near], refs[2 * near], refs[2 * near + 1:]
-    far, rows, width = rows_refs[0].shape
+    rows_hbm, weights_hbm, own_ref, far_refs = refs[:near], refs[near:2 * near], refs[2 * near], refs[2 * near + 1:-3]
+    rows_ref, weights_ref, sems = refs[-3:]
+    _, far, rows, width = rows_ref.shape
+    copies = []
+    for n in range(near):
+        copies.append(pltpu.make_async_copy(weights_hbm[n], weights_ref.at[n], sems.at[n]))
+        copies.append(pltpu.make_async_copy(rows_hbm[n], rows_ref.at[n], sems.at[near + n]))
+    for copy in copies:
+        copy.start()
+    for copy in copies:
+        copy.wait()
     half = far // 2
     for i in range(0, far, half):
         total = jnp.zeros((half * rows, own_ref.shape[1]), jnp.float32)
-        for rows_ref, weight_ref in zip(rows_refs, weight_refs):
-            total = total + nt_dot(rows_ref[i:i + half].reshape(half * rows, width), weight_ref[...])
+        for n in range(near):
+            total = total + nt_dot(rows_ref[n, i:i + half].reshape(half * rows, width), weights_ref[n])
         for j in range(half):
             part = total[j * rows:(j + 1) * rows]
             if i + j == 0:
@@ -417,36 +429,40 @@
     )(blocks, taken_from, arrived, kv, own_stats, other_stats, enc_t)
 
     back, *near_weights = lax.optimization_barrier((back, *near_weights))
+    near_rows = [r if a == 0 else shifted(r, a) for a, r in zip(NEAR, near_rows)]
     returned = lax.all_to_all(back, "seq", split_axis=0, concat_axis=0, tiled=True)
-    near_rows = [r if a == 0 else shifted(r, a) for a, r in zip(NEAR, near_rows)]
     own, *far_sums = pl.pallas_call(
         project_kernel,
         out_shape=(
             jax.ShapeDtypeStruct((rows, enc_width), f32),
             *[jax.ShapeDtypeStruct((rows, enc_width), bf16)] * (far - 1),
         ),
-        in_specs=[spec(VMEM)] * (2 * near),
+        in_specs=[spec(HBM)] * (2 * near),
         out_specs=(spec(VMEM),) * far,
-        compiler_params=params(),
+        scratch_shapes=[
+            pltpu.VMEM((near, far, rows, 2 * head_dim), bf16),
+            pltpu.VMEM((near, enc_width, 2 * head_dim), bf16),
+            pltpu.SemaphoreType.DMA((2 * near,)),
+        ],
+        compiler_params=params(SMALL_LIMIT),
+        cost_estimate=pl.CostEstimate(flops=6 * 10**10, bytes_accessed=2 * 10**6, transcendentals=0),
         name="project",
     )(*near_rows, *near_weights)
-    encoding_grad = own
-    for b, part in zip(FAR[1:], far_sums):
-        encoding_grad = encoding_grad + shifted(part, b).astype(f32)
-
-    attended, query_grad, key_weight_grad, value_weight_grad = pl.pallas_call(
+    far_sums = [shifted(part, b) for b, part in zip(FAR[1:], far_sums)]
+    attended, query_grad, encoding_grad, key_weight_grad, value_weight_grad = pl.pallas_call(
         finish_kernel,
         out_shape=(
             jax.ShapeDtypeStruct((segments, SEGMENT, head_dim), bf16),
             jax.ShapeDtypeStruct((segments, SEGMENT, head_dim), bf16),
+            jax.ShapeDtypeStruct((rows, enc_width), f32),
             jax.ShapeDtypeStruct((share, head_dim), f32),
             jax.ShapeDtypeStruct((share, head_dim), f32),
         ),
-        in_specs=[spec(SMEM), spec(VMEM)],
-        out_specs=(spec(VMEM),) * 4,
+        in_specs=[spec(SMEM), *[spec(VMEM)] * (1 + far)],
+        out_specs=(spec(VMEM),) * 5,
         compiler_params=params(),
         name="finish",
-    )(slots, returned)
+    )(slots, returned, own, *far_sums)
     return (
         attended.reshape(segments * SEGMENT, head_dim),
         query_grad.reshape(segments * SEGMENT, head_dim),

time: 129 us -> 123 us (0.953)
  waiting for transfers between devices: 23.8 us -> 19.4 us
  starting transfers between devices: 57.5 us -> 54.7 us
    ppermute x9, waiting for transfers between devices: 21 us -> 18.4 us  [shifted(): lax.ppermute(x, 'head', [(z, (z + step) % count) for z in range(count)])]
    all_to_all x1, waiting for transfers between devices: 2.78 us -> 0.96 us  [on_device(): lax.all_to_all(packed, 'seq', split_axis=0, concat_axis=0, tiled=True)]
    all_to_all x1, starting transfers between devices: 6.19 us -> 4.55 us  [on_device(): lax.all_to_all(back, 'seq', split_axis=0, concat_axis=0, tiled=True)]
  transfers between devices with their start and end apart: 11 -> 11, of which waited for: 5 -> 5; matrix products, arithmetic and copies ran while one was open for 9% -> 11% of each run, Pallas kernels for 10% -> 10%
where the time goes in v9:
time: 123 us; the launch traced here: 122 us
  starting transfers between devices  54.7 us (44%)
  waiting for transfers between devices  19.4 us (16%)
  Pallas kernels  17.8 us (14%)
  blocking collectives  14.2 us (12%)
  local copies, waits for them, and re-layouts  9 us (7%)
  matrix products  3.09 us (3%)
  other arithmetic  2.6 us (2%)
  between operations  1.67 us (1%)
    ppermute x9, starting transfers between devices, shifted(): lax.ppermute(x, 'head', [(z, (z + step) % count) for z in range(count)])  39.6 us
    ppermute x9, waiting for transfers between devices, shifted(): lax.ppermute(x, 'head', [(z, (z + step) % count) for z in range(count)])  18.4 us
    all_to_all x1, blocking collectives, one_hop(): return lax.all_to_all(sent, 'seq', split_axis=0, concat_axis=0, tiled=True)  14.2 us
    all_to_all x1, starting transfers between devices, on_device(): lax.all_to_all(packed, 'seq', split_axis=0, concat_axis=0, tiled=True)  10.6 us
    pallas_call x1, Pallas kernels, on_device(): pl.pallas_call(lambda *refs: grads_kernel(scale, group, *refs), out_shape...  7.84 us
    all_to_all x1, starting transfers between devices, on_device(): lax.all_to_all(back, 'seq', split_axis=0, concat_axis=0, tiled=True)  4.55 us
    reshape x1, local copies, waits for them, and re-layouts, on_device(): flat_enc = encodings.reshape(block_count * block_len, enc_width)  3.65 us
    pallas_call x1, Pallas kernels, on_device(): pl.pallas_call(lambda *refs: pack_kernel(block_count, *refs), out_shape=(...  3.36 us
  transfers between devices with their start and end apart: 11, of which 5 were waited for; matrix products, arithmetic and copies ran while one was open for 11% of the time, Pallas kernels for 10%

profile of v9, /device:TPU:1, one launch (start us, length us, event | category | flops | bytes accessed | tf_op | source)
XLA Modules:
  0.0 122.5 jit_solution(5376167090284082772)
XLA Ops:
  0.6 3.4 %pack.1 = (bf16[64,2,64,128]{3,2,1,0:T(8,128)(2,1)}, s32[32]{0:T(128)S(1)}) custom-call(s32[2,512]{1,0:T(2,128)} %bitcast.44, bf16[16,64,128]{2,1,0:T(8,128)(2,1)} %bitcast.39, bf16[16,64,128]{2,1,0:T(8,128)(2,1)} %bitcast.40), custom_call_target="tpu_custom_call" | custom-call | tf_op jit(solution)/shard_map/pack/pallas_call | solution.py:307
  4.0 10.6 %all-to-all-start.3 = ((bf16[64,2,64,128]{3,2,1,0:T(8,128)(2,1)}), bf16[64,2,64,128]{3,2,1,0:T(8,128)(2,1)S(1)}, u32[]{:S(2)}, u32[]{:S(2)}) async-start(bf16[64,2,64,128]{3,2,1,0:T(8,128)(2,1)} %get-tuple-element.55), calls=%async_computation.3 | async-start | bytes 4194304 | tf_op jit(solution)/shard_map/all_to_all | solution.py:327
  15.2 0.4 rev.6
  16.8 0.4 select_reduce_fusion.1
  18.8 3.6 %copy.31 = bf16[896,896]{0,1:T(8,128)(2,1)} copy(bf16[896,896]{1,0:T(8,128)(2,1)} %bitcast.36) | data formatting | bytes 3211264 | tf_op jit(solution)/shard_map/reshape | solution.py:331
  22.6 2.9 %fusion = bf16[896,256]{0,1:T(8,128)(2,1)} fusion(bf16[896,256]{1,0:T(8,128)(2,1)S(1)} %constant_dynamic-update-slice_fusion.refs_4_, bf16[896,896]{1,0:T(8,128)(2,1)} %bitcast.37), kind=kOutput, calls=%fused_computation.1 | convolution fusion | flops 411271168 | bytes 2523136 | tf_op jit(solution)/shard_map/dot_general | solution.py:332
  25.5 1.2 copy.30
  26.7 0.7 fusion.6
  28.0 0.5 broadcast_select_fusion
  28.6 2.9 %collective-permute-start.2 = (bf16[896,256]{1,0:T(8,128)(2,1)S(1)}, bf16[896,256]{1,0:T(8,128)(2,1)}, u32[]{:S(2)}, u32[]{:S(2)}) collective-permute-start(bf16[896,256]{1,0:T(8,128)(2,1)S(1)} %constant_dynamic-update-slice_fusion.refs_4_), channel_id=1, source_target_pairs={{0,2},{1,3},{2,4},{3,5},{4,6},{5,7},{6,8},{7,9},{8,10},{9,11},{10,... | collective-permute-start | bytes 1376264 | tf_op jit(solution)/shard_map/ppermute | solution.py:292
  31.5 8.1 %collective-permute-start.1 = (bf16[896,256]{1,0:T(8,128)(2,1)S(1)}, bf16[896,256]{1,0:T(8,128)(2,1)}, u32[]{:S(2)}, u32[]{:S(2)}) collective-permute-start(bf16[896,256]{1,0:T(8,128)(2,1)S(1)} %constant_dynamic-update-slice_fusion.refs_4_), channel_id=1, source_target_pairs={{0,15},{1,0},{2,1},{3,2},{4,3},{5,4},{6,5},{7,6},{8,7},{9,8},{10,9... | collective-permute-start | bytes 1376264 | tf_op jit(solution)/shard_map/ppermute | solution.py:292
  39.7 1.9 %collective-permute-start = (bf16[896,256]{1,0:T(8,128)(2,1)S(1)}, bf16[896,256]{1,0:T(8,128)(2,1)}, u32[]{:S(2)}, u32[]{:S(2)}) collective-permute-start(bf16[896,256]{1,0:T(8,128)(2,1)S(1)} %constant_dynamic-update-slice_fusion.refs_4_), channel_id=1, source_target_pairs={{0,1},{1,2},{2,3},{3,4},{4,5},{5,6},{6,7},{7,8},{8,9},{9,10},{10,1... | collective-permute-start | bytes 1376264 | tf_op jit(solution)/shard_map/ppermute | solution.py:292
  41.6 1.0 all-to-all-done.3.refs_2_
  42.5 1.9 %stats.1 = (f32[32,2,128]{2,1,0:T(2,128)S(1)}, f32[64,128]{1,0:T(8,128)S(1)}, f32[256,128]{1,0:T(8,128)S(1)}) custom-call(s32[64]{0:T(128)S(1)} %get-tuple-element.53.refs_0_, s32[64]{0:T(128)S(1)} %get-tuple-element.57.refs_1_, bf16[64,2,64,128]{3,2,1,0:T(8,128)(2,1)S(1)} %all-to-all-done.3.refs_2_, bf16[7,128,256]{2,1,0:T(8,128)(2,1)S(1)} %bitcast.31), custom_call_target="tpu_custom_call" | custom-call | tf_op jit(solution)/shard_map/stats/pallas_call | solution.py:369
  44.5 14.2 %conditional.1 = (f32[256,128]{1,0:T(8,128)S(1)}) conditional(s32[]{:T(128)} %convert_element_type.23, (f32[64,128]{1,0:T(8,128)S(1)}, s32[32]{0:T(128)S(1)}) %tuple.19, f32[256,128]{1,0:T(8,128)S(1)} %get-tuple-element.61), branch_computations={%region_7.8_spmd, %region_8.9_spmd} | conditional | bytes 294924 | solution.py:399
  44.5 14.2 %all_to_all.38 = f32[32,8,128]{2,1,0:T(8,128)S(1)} all-to-all(f32[32,8,128]{2,1,0:T(8,128)S(1)} %bitcast.42), channel_id=1, replica_groups=mesh['seq'=32,'head'=16] {'seq'}, dimensions={0} | all-to-all | bytes 262144 | tf_op jit(solution)/shard_map/cond/branch_1_fun/all_to_all | solution.py:384
  58.7 7.8 %grads.1 = (bf16[32,320,128]{2,1,0:T(8,128)(2,1)}, bf16[4,56,256]{2,1,0:T(8,128)(2,1)}, bf16[4,56,256]{2,1,0:T(8,128)(2,1)}, bf16[4,56,256]{2,1,0:T(8,128)(2,1)}, bf16[4,56,256]{2,1,0:T(8,128)(2,1)}) custom-call(s32[64]{0:T(128)} %copy-done.3, s32[64]{0:T(128)} %get-tuple-element.54.refs_1_, bf16[64,2,64,128]{3,2,1,0:T(8,128)(2,1)} %copy-done, ...), custom_call_target="tpu_custom_call" | custom-call | tf_op jit(solution)/shard_map/grads/pallas_call | solution.py:406
  66.5 1.9 %collective-permute-start.3 = (bf16[4,56,256]{2,1,0:T(8,128)(2,1)}, bf16[4,56,256]{2,1,0:T(8,128)(2,1)S(1)}, u32[]{:S(2)}, u32[]{:S(2)}) collective-permute-start(bf16[4,56,256]{2,1,0:T(8,128)(2,1)} %get-tuple-element.67), channel_id=1, source_target_pairs={{0,1},{1,2},{2,3},{3,4},{4,5},{5,6},{6,7},{7,8},{8,9},{9,10},{10,1... | collective-permute-start | bytes 344072 | tf_op jit(solution)/shard_map/ppermute | solution.py:292
  68.5 7.6 %collective-permute-start.4 = (bf16[4,56,256]{2,1,0:T(8,128)(2,1)}, bf16[4,56,256]{2,1,0:T(8,128)(2,1)S(1)}, u32[]{:S(2)}, u32[]{:S(2)}) collective-permute-start(bf16[4,56,256]{2,1,0:T(8,128)(2,1)} %get-tuple-element.68), channel_id=1, source_target_pairs={{0,15},{1,0},{2,1},{3,2},{4,3},{5,4},{6,5},{7,6},{8,7},{9,8},{10,9... | collective-permute-start | bytes 344072 | tf_op jit(solution)/shard_map/ppermute | solution.py:292
  76.1 1.9 %collective-permute-start.5 = (bf16[4,56,256]{2,1,0:T(8,128)(2,1)}, bf16[4,56,256]{2,1,0:T(8,128)(2,1)}, u32[]{:S(2)}, u32[]{:S(2)}) collective-permute-start(bf16[4,56,256]{2,1,0:T(8,128)(2,1)} %get-tuple-element.69), channel_id=1, source_target_pairs={{0,2},{1,3},{2,4},{3,5},{4,6},{5,7},{6,8},{7,9},{8,10},{9,11},{10,... | collective-permute-start | bytes 344072 | tf_op jit(solution)/shard_map/ppermute | solution.py:292
  78.1 4.5 %all-to-all-start.4 = ((bf16[32,320,128]{2,1,0:T(8,128)(2,1)}), bf16[32,320,128]{2,1,0:T(8,128)(2,1)S(1)}, u32[]{:S(2)}, u32[]{:S(2)}) async-start(bf16[32,320,128]{2,1,0:T(8,128)(2,1)} %get-tuple-element.65), calls=%async_computation.4 | async-start | bytes 5242880 | tf_op jit(solution)/shard_map/all_to_all | solution.py:433
  82.7 0.6 copy-done.5
  83.3 3.8 %collective-permute-done.5.refs_3_ = bf16[4,56,256]{2,1,0:T(8,128)(2,1)} collective-permute-done((bf16[4,56,256]{2,1,0:T(8,128)(2,1)}, bf16[4,56,256]{2,1,0:T(8,128)(2,1)}, u32[]{:S(2)}, u32[]{:S(2)}) %collective-permute-start.5) | collective-permute-done | bytes 114720 | tf_op jit(solution)/shard_map/ppermute | solution.py:292
  87.1 0.9 copy-done.6
  88.0 3.1 %project.1 = (f32[56,896]{1,0:T(8,128)S(1)}, bf16[56,896]{1,0:T(8,128)(2,1)S(1)}, bf16[56,896]{1,0:T(8,128)(2,1)S(1)}, bf16[56,896]{1,0:T(8,128)(2,1)S(1)}) custom-call(bf16[4,56,256]{2,1,0:T(8,128)(2,1)S(1)} %copy-done.4, bf16[4,56,256]{2,1,0:T(8,128)(2,1)S(1)} %collective-permute-done.3.refs_1_, bf16[4,56,256]{2,1,0:T(8,128)(2,1)S(1)} %copy-done.6, ...), custom_call_target="tpu_custom_call" | custom-call | flops 60000002048 | bytes 2000000 | tf_op jit(solution)/shard_map/project/pallas_call | solution.py:434
  91.1 1.9 %collective-permute-start.6 = (bf16[56,896]{1,0:T(8,128)(2,1)S(1)}, bf16[56,896]{1,0:T(8,128)(2,1)S(1)}, u32[]{:S(2)}, u32[]{:S(2)}) collective-permute-start(bf16[56,896]{1,0:T(8,128)(2,1)S(1)} %get-tuple-element.75), channel_id=1, source_target_pairs={{0,4},{1,5},{2,6},{3,7},{4,8},{5,9},{6,10},{7,11},{8,12},{9,13},{1... | collective-permute-start | bytes 301064 | tf_op jit(solution)/shard_map/ppermute | solution.py:292
  93.0 8.0 %collective-permute-start.7 = (bf16[56,896]{1,0:T(8,128)(2,1)S(1)}, bf16[56,896]{1,0:T(8,128)(2,1)S(1)}, u32[]{:S(2)}, u32[]{:S(2)}) collective-permute-start(bf16[56,896]{1,0:T(8,128)(2,1)S(1)} %get-tuple-element.76), channel_id=1, source_target_pairs={{0,8},{1,9},{2,10},{3,11},{4,12},{5,13},{6,14},{7,15},{8,0},{9,1},... | collective-permute-start | bytes 301064 | tf_op jit(solution)/shard_map/ppermute | solution.py:292
  101.1 5.2 %collective-permute-start.8 = (bf16[56,896]{1,0:T(8,128)(2,1)S(1)}, bf16[56,896]{1,0:T(8,128)(2,1)S(1)}, u32[]{:S(2)}, u32[]{:S(2)}) collective-permute-start(bf16[56,896]{1,0:T(8,128)(2,1)S(1)} %get-tuple-element.77), channel_id=1, source_target_pairs={{0,12},{1,13},{2,14},{3,15},{4,0},{5,1},{6,2},{7,3},{8,4},{9,5},{1... | collective-permute-start | bytes 301064 | tf_op jit(solution)/shard_map/ppermute | solution.py:292
  106.3 0.8 collective-permute-done.6.one_ref
  107.1 6.6 %collective-permute-done.7.two_ref = bf16[56,896]{1,0:T(8,128)(2,1)S(1)} collective-permute-done((bf16[56,896]{1,0:T(8,128)(2,1)S(1)}, bf16[56,896]{1,0:T(8,128)(2,1)S(1)}, u32[]{:S(2)}, u32[]{:S(2)}) %collective-permute-start.7) | collective-permute-done | bytes 100384 | tf_op jit(solution)/shard_map/ppermute | solution.py:292
  113.7 7.1 %collective-permute-done.8.three_ref = bf16[56,896]{1,0:T(8,128)(2,1)S(1)} collective-permute-done((bf16[56,896]{1,0:T(8,128)(2,1)S(1)}, bf16[56,896]{1,0:T(8,128)(2,1)S(1)}, u32[]{:S(2)}, u32[]{:S(2)}) %collective-permute-start.8) | collective-permute-done | bytes 100384 | tf_op jit(solution)/shard_map/ppermute | solution.py:292
  120.8 1.6 %finish.1 = (bf16[16,64,128]{2,1,0:T(8,128)(2,1)}, bf16[16,64,128]{2,1,0:T(8,128)(2,1)}, f32[56,896]{1,0:T(8,128)}, f32[28,128]{1,0:T(8,128)}, f32[28,128]{1,0:T(8,128)}) custom-call(s32[32]{0:T(128)S(1)} %get-tuple-element.50.slots_ref, bf16[32,320,128]{2,1,0:T(8,128)(2,1)S(1)} %all-to-all-done.4.in_ref, f32[56,896]{1,0:T(8,128)S(1)} %get-tuple-element.74.own_ref, ...), custom_call_target="tpu_custom_call" | custom-call | tf_op jit(solution)/shard_map/finish/pallas_call | solution.py:452
  (57 shorter events, 3.4 us)
Async XLA Ops:
  4.0 10.6 %copy-start.9 = (s32[512,2]{0,1:T(2,128)S(1)}, s32[512,2]{0,1:T(2,128)}, u32[]{:S(2)}) copy-start(s32[512,2]{0,1:T(2,128)} %param.12) | copy-start | bytes 12292
  4.0 38.5 %all-to-all-start.3 = ((bf16[64,2,64,128]{3,2,1,0:T(8,128)(2,1)}), bf16[64,2,64,128]{3,2,1,0:T(8,128)(2,1)S(1)}, u32[]{:S(2)}, u32[]{:S(2)}) async-start(bf16[64,2,64,128]{3,2,1,0:T(8,128)(2,1)} %get-tuple-element.55), calls=%async_computation.3 | async-start | bytes 4194304 | tf_op jit(solution)/shard_map/all_to_all | solution.py:327
  18.3 24.3 %copy-start.3 = (s32[64]{0:T(128)}, s32[64]{0:T(128)S(1)}, u32[]{:S(2)}) copy-start(s32[64]{0:T(128)S(1)} %get-tuple-element.53.refs_0_) | copy-start | bytes 772
  18.8 3.7 %copy-start.7 = (bf16[896,128]{1,0:T(8,128)(2,1)S(1)}, bf16[896,128]{1,0:T(8,128)(2,1)}, u32[]{:S(2)}) copy-start(bf16[896,128]{1,0:T(8,128)(2,1)} %param.10) | copy-start | bytes 688132
  18.8 3.7 %copy-start.8 = (bf16[896,128]{1,0:T(8,128)(2,1)S(1)}, bf16[896,128]{1,0:T(8,128)(2,1)}, u32[]{:S(2)}) copy-start(bf16[896,128]{1,0:T(8,128)(2,1)} %param.11) | copy-start | bytes 688132
  26.7 17.8 %copy-start.1 = (bf16[896,256]{1,0:T(8,128)(2,1)}, bf16[896,256]{1,0:T(8,128)(2,1)S(1)}, u32[]{:S(2)}) copy-start(bf16[896,256]{1,0:T(8,128)(2,1)S(1)} %copy.30) | copy-start | bytes 1376260
  28.6 47.6 %collective-permute-start.2 = (bf16[896,256]{1,0:T(8,128)(2,1)S(1)}, bf16[896,256]{1,0:T(8,128)(2,1)}, u32[]{:S(2)}, u32[]{:S(2)}) collective-permute-start(bf16[896,256]{1,0:T(8,128)(2,1)S(1)} %constant_dynamic-update-slice_fusion.refs_4_), channel_id=1, source_target_pairs={{0,2},{1,3},{2,4},{3,5},{4,6},{5,7},{6,8},{7,9},{8,10},{9,11},{10,... | collective-permute-start | bytes 1376264 | tf_op jit(solution)/shard_map/ppermute | solution.py:292
  31.5 46.5 %collective-permute-start.1 = (bf16[896,256]{1,0:T(8,128)(2,1)S(1)}, bf16[896,256]{1,0:T(8,128)(2,1)}, u32[]{:S(2)}, u32[]{:S(2)}) collective-permute-start(bf16[896,256]{1,0:T(8,128)(2,1)S(1)} %constant_dynamic-update-slice_fusion.refs_4_), channel_id=1, source_target_pairs={{0,15},{1,0},{2,1},{3,2},{4,3},{5,4},{6,5},{7,6},{8,7},{9,8},{10,9... | collective-permute-start | bytes 1376264 | tf_op jit(solution)/shard_map/ppermute | solution.py:292
  39.7 38.4 %collective-permute-start = (bf16[896,256]{1,0:T(8,128)(2,1)S(1)}, bf16[896,256]{1,0:T(8,128)(2,1)}, u32[]{:S(2)}, u32[]{:S(2)}) collective-permute-start(bf16[896,256]{1,0:T(8,128)(2,1)S(1)} %constant_dynamic-update-slice_fusion.refs_4_), channel_id=1, source_target_pairs={{0,1},{1,2},{2,3},{3,4},{4,5},{5,6},{6,7},{7,8},{8,9},{9,10},{10,1... | collective-permute-start | bytes 1376264 | tf_op jit(solution)/shard_map/ppermute | solution.py:292
  42.5 16.1 %copy-start = (bf16[64,2,64,128]{3,2,1,0:T(8,128)(2,1)}, bf16[64,2,64,128]{3,2,1,0:T(8,128)(2,1)S(1)}, u32[]{:S(2)}) copy-start(bf16[64,2,64,128]{3,2,1,0:T(8,128)(2,1)S(1)} %all-to-all-done.3.refs_2_) | copy-start | bytes 6291460
  44.5 14.2 %copy-start.2 = (f32[32,2,128]{2,1,0:T(2,128)}, f32[32,2,128]{2,1,0:T(2,128)S(1)}, u32[]{:S(2)}) copy-start(f32[32,2,128]{2,1,0:T(2,128)S(1)} %get-tuple-element.58.refs_4_) | copy-start | bytes 98308
  66.5 16.1 %collective-permute-start.3 = (bf16[4,56,256]{2,1,0:T(8,128)(2,1)}, bf16[4,56,256]{2,1,0:T(8,128)(2,1)S(1)}, u32[]{:S(2)}, u32[]{:S(2)}) collective-permute-start(bf16[4,56,256]{2,1,0:T(8,128)(2,1)} %get-tuple-element.67), channel_id=1, source_target_pairs={{0,1},{1,2},{2,3},{3,4},{4,5},{5,6},{6,7},{7,8},{8,9},{9,10},{10,1... | collective-permute-start | bytes 344072 | tf_op jit(solution)/shard_map/ppermute | solution.py:292
  68.5 14.2 %collective-permute-start.4 = (bf16[4,56,256]{2,1,0:T(8,128)(2,1)}, bf16[4,56,256]{2,1,0:T(8,128)(2,1)S(1)}, u32[]{:S(2)}, u32[]{:S(2)}) collective-permute-start(bf16[4,56,256]{2,1,0:T(8,128)(2,1)} %get-tuple-element.68), channel_id=1, source_target_pairs={{0,15},{1,0},{2,1},{3,2},{4,3},{5,4},{6,5},{7,6},{8,7},{9,8},{10,9... | collective-permute-start | bytes 344072 | tf_op jit(solution)/shard_map/ppermute | solution.py:292
  76.1 11.0 %collective-permute-start.5 = (bf16[4,56,256]{2,1,0:T(8,128)(2,1)}, bf16[4,56,256]{2,1,0:T(8,128)(2,1)}, u32[]{:S(2)}, u32[]{:S(2)}) collective-permute-start(bf16[4,56,256]{2,1,0:T(8,128)(2,1)} %get-tuple-element.69), channel_id=1, source_target_pairs={{0,2},{1,3},{2,4},{3,5},{4,6},{5,7},{6,8},{7,9},{8,10},{9,11},{10,... | collective-permute-start | bytes 344072 | tf_op jit(solution)/shard_map/ppermute | solution.py:292
  78.1 9.1 %copy-start.4 = (bf16[4,56,256]{2,1,0:T(8,128)(2,1)S(1)}, bf16[4,56,256]{2,1,0:T(8,128)(2,1)}, u32[]{:S(2)}) copy-start(bf16[4,56,256]{2,1,0:T(8,128)(2,1)} %get-tuple-element.66.refs_0_) | copy-start | bytes 344068
  78.1 42.8 %all-to-all-start.4 = ((bf16[32,320,128]{2,1,0:T(8,128)(2,1)}), bf16[32,320,128]{2,1,0:T(8,128)(2,1)S(1)}, u32[]{:S(2)}, u32[]{:S(2)}) async-start(bf16[32,320,128]{2,1,0:T(8,128)(2,1)} %get-tuple-element.65), calls=%async_computation.4 | async-start | bytes 5242880 | tf_op jit(solution)/shard_map/all_to_all | solution.py:433
  82.7 0.6 copy-start.5
  87.1 0.9 copy-start.6
  91.1 16.0 %collective-permute-start.6 = (bf16[56,896]{1,0:T(8,128)(2,1)S(1)}, bf16[56,896]{1,0:T(8,128)(2,1)S(1)}, u32[]{:S(2)}, u32[]{:S(2)}) collective-permute-start(bf16[56,896]{1,0:T(8,128)(2,1)S(1)} %get-tuple-element.75), channel_id=1, source_target_pairs={{0,4},{1,5},{2,6},{3,7},{4,8},{5,9},{6,10},{7,11},{8,12},{9,13},{1... | collective-permute-start | bytes 301064 | tf_op jit(solution)/shard_map/ppermute | solution.py:292
  93.0 20.7 %collective-permute-start.7 = (bf16[56,896]{1,0:T(8,128)(2,1)S(1)}, bf16[56,896]{1,0:T(8,128)(2,1)S(1)}, u32[]{:S(2)}, u32[]{:S(2)}) collective-permute-start(bf16[56,896]{1,0:T(8,128)(2,1)S(1)} %get-tuple-element.76), channel_id=1, source_target_pairs={{0,8},{1,9},{2,10},{3,11},{4,12},{5,13},{6,14},{7,15},{8,0},{9,1},... | collective-permute-start | bytes 301064 | tf_op jit(solution)/shard_map/ppermute | solution.py:292
  101.1 19.8 %collective-permute-start.8 = (bf16[56,896]{1,0:T(8,128)(2,1)S(1)}, bf16[56,896]{1,0:T(8,128)(2,1)S(1)}, u32[]{:S(2)}, u32[]{:S(2)}) collective-permute-start(bf16[56,896]{1,0:T(8,128)(2,1)S(1)} %get-tuple-element.77), channel_id=1, source_target_pairs={{0,12},{1,13},{2,14},{3,15},{4,0},{5,1},{6,2},{7,3},{8,4},{9,5},{1... | collective-permute-start | bytes 301064 | tf_op jit(solution)/shard_map/ppermute | solution.py:292

commit v10 on v9

--- a/solution.py
+++ b/solution.py
@@ -11,8 +11,8 @@
 NEIGH = 2
 CAP = 2
 PLACES = 8
-NEAR = (0, 1, -1, 2)
-FAR = (0, 4, 8, -4)
+NEAR = (0, -1, 2, 1)
+FAR = (0, -4, 8, 4)
 VMEM_LIMIT = 40 * 1024 * 1024
 LARGE_LIMIT = 60 * 1024 * 1024
 SMALL_LIMIT = 16 * 1024 * 1024
@@ -402,7 +402,7 @@
     rows = block_count * row_share
     near, far = len(NEAR), len(FAR)
     back_shape = (seq_count, 2 * CAP * SEGMENT + 2 * room, head_dim)
-    group = 8
+    group = 16
     back, *near_rows = pl.pallas_call(
         lambda *refs: grads_kernel(scale, group, *refs),
         out_shape=(

time: 123 us -> 123 us (level)
  the two profiles are of different devices: /device:TPU:1 before, /device:TPU:35 now
where the time goes in v10:
time: 123 us
  starting transfers between devices  56 us (46%)
  waiting for transfers between devices  19.9 us (16%)
  Pallas kernels  17.6 us (14%)
  blocking collectives  12.8 us (10%)
  local copies, waits for them, and re-layouts  9 us (7%)
  matrix products  3.09 us (3%)
  other arithmetic  2.6 us (2%)
  between operations  1.68 us (1%)
    ppermute x9, starting transfers between devices, shifted(): lax.ppermute(x, 'head', [(z, (z + step) % count) for z in range(count)])  42.2 us
    ppermute x9, waiting for transfers between devices, shifted(): lax.ppermute(x, 'head', [(z, (z + step) % count) for z in range(count)])  18.2 us
    all_to_all x1, blocking collectives, one_hop(): return lax.all_to_all(sent, 'seq', split_axis=0, concat_axis=0, tiled=True)  12.8 us
    all_to_all x1, starting transfers between devices, on_device(): lax.all_to_all(packed, 'seq', split_axis=0, concat_axis=0, tiled=True)  7.95 us
    pallas_call x1, Pallas kernels, on_device(): pl.pallas_call(lambda *refs: grads_kernel(scale, group, *refs), out_shape...  7.64 us
    all_to_all x1, starting transfers between devices, on_device(): lax.all_to_all(back, 'seq', split_axis=0, concat_axis=0, tiled=True)  5.91 us
    reshape x1, local copies, waits for them, and re-layouts, on_device(): flat_enc = encodings.reshape(block_count * block_len, enc_width)  3.65 us
    pallas_call x1, Pallas kernels, on_device(): pl.pallas_call(lambda *refs: pack_kernel(block_count, *refs), out_shape=(...  3.38 us
  transfers between devices with their start and end apart: 11, of which 4 were waited for; matrix products, arithmetic and copies ran while one was open for 11% of the time, Pallas kernels for 10%

profile of v10, /device:TPU:35, one launch (start us, length us, event | category | flops | bytes accessed | tf_op | source)
XLA Modules:
  0.0 122.7 jit_solution(2660124200606041177)
XLA Ops:
  0.6 3.4 %pack.1 = (bf16[64,2,64,128]{3,2,1,0:T(8,128)(2,1)}, s32[32]{0:T(128)S(1)}) custom-call(s32[2,512]{1,0:T(2,128)} %bitcast.44, bf16[16,64,128]{2,1,0:T(8,128)(2,1)} %bitcast.39, bf16[16,64,128]{2,1,0:T(8,128)(2,1)} %bitcast.40), custom_call_target="tpu_custom_call" | custom-call | tf_op jit(solution)/shard_map/pack/pallas_call | solution.py:307
  4.0 7.9 %all-to-all-start.3 = ((bf16[64,2,64,128]{3,2,1,0:T(8,128)(2,1)}), bf16[64,2,64,128]{3,2,1,0:T(8,128)(2,1)S(1)}, u32[]{:S(2)}, u32[]{:S(2)}) async-start(bf16[64,2,64,128]{3,2,1,0:T(8,128)(2,1)} %get-tuple-element.55), calls=%async_computation.3 | async-start | bytes 4194304 | tf_op jit(solution)/shard_map/all_to_all | solution.py:327
  12.3 0.3 broadcast_compare_fusion
  12.6 0.4 rev.6
  14.2 0.4 select_reduce_fusion.1
  16.2 3.6 %copy.31 = bf16[896,896]{0,1:T(8,128)(2,1)} copy(bf16[896,896]{1,0:T(8,128)(2,1)} %bitcast.36) | data formatting | bytes 3211264 | tf_op jit(solution)/shard_map/reshape | solution.py:331
  19.9 2.9 %fusion = bf16[896,256]{0,1:T(8,128)(2,1)} fusion(bf16[896,256]{1,0:T(8,128)(2,1)S(1)} %constant_dynamic-update-slice_fusion.refs_4_, bf16[896,896]{1,0:T(8,128)(2,1)} %bitcast.37), kind=kOutput, calls=%fused_computation.1 | convolution fusion | flops 411271168 | bytes 2523136 | tf_op jit(solution)/shard_map/dot_general | solution.py:332
  22.9 1.2 copy.30
  24.1 0.7 fusion.6
  25.4 0.5 broadcast_select_fusion
  26.0 3.5 %collective-permute-start.2 = (bf16[896,256]{1,0:T(8,128)(2,1)S(1)}, bf16[896,256]{1,0:T(8,128)(2,1)}, u32[]{:S(2)}, u32[]{:S(2)}) collective-permute-start(bf16[896,256]{1,0:T(8,128)(2,1)S(1)} %constant_dynamic-update-slice_fusion.refs_4_), channel_id=1, source_target_pairs={{0,1},{1,2},{2,3},{3,4},{4,5},{5,6},{6,7},{7,8},{8,9},{9,10},{10,1... | collective-permute-start | bytes 1376264 | tf_op jit(solution)/shard_map/ppermute | solution.py:292
  29.5 6.1 %collective-permute-start.1 = (bf16[896,256]{1,0:T(8,128)(2,1)S(1)}, bf16[896,256]{1,0:T(8,128)(2,1)}, u32[]{:S(2)}, u32[]{:S(2)}) collective-permute-start(bf16[896,256]{1,0:T(8,128)(2,1)S(1)} %constant_dynamic-update-slice_fusion.refs_4_), channel_id=1, source_target_pairs={{0,2},{1,3},{2,4},{3,5},{4,6},{5,7},{6,8},{7,9},{8,10},{9,11},{10,... | collective-permute-start | bytes 1376264 | tf_op jit(solution)/shard_map/ppermute | solution.py:292
  35.6 1.9 %collective-permute-start = (bf16[896,256]{1,0:T(8,128)(2,1)S(1)}, bf16[896,256]{1,0:T(8,128)(2,1)}, u32[]{:S(2)}, u32[]{:S(2)}) collective-permute-start(bf16[896,256]{1,0:T(8,128)(2,1)S(1)} %constant_dynamic-update-slice_fusion.refs_4_), channel_id=1, source_target_pairs={{0,15},{1,0},{2,1},{3,2},{4,3},{5,4},{6,5},{7,6},{8,7},{9,8},{10,9... | collective-permute-start | bytes 1376264 | tf_op jit(solution)/shard_map/ppermute | solution.py:292
  37.5 1.6 %all-to-all-done.3.refs_2_ = bf16[64,2,64,128]{3,2,1,0:T(8,128)(2,1)S(1)} async-done(((bf16[64,2,64,128]{3,2,1,0:T(8,128)(2,1)}), bf16[64,2,64,128]{3,2,1,0:T(8,128)(2,1)S(1)}, u32[]{:S(2)}, u32[]{:S(2)}) %all-to-all-start.3) | async-done | bytes 2097184 | tf_op jit(solution)/shard_map/all_to_all | solution.py:327
  39.2 1.9 %stats.1 = (f32[32,2,128]{2,1,0:T(2,128)S(1)}, f32[64,128]{1,0:T(8,128)S(1)}, f32[256,128]{1,0:T(8,128)S(1)}) custom-call(s32[64]{0:T(128)S(1)} %get-tuple-element.53.refs_0_, s32[64]{0:T(128)S(1)} %get-tuple-element.57.refs_1_, bf16[64,2,64,128]{3,2,1,0:T(8,128)(2,1)S(1)} %all-to-all-done.3.refs_2_, bf16[7,128,256]{2,1,0:T(8,128)(2,1)S(1)} %bitcast.31), custom_call_target="tpu_custom_call" | custom-call | tf_op jit(solution)/shard_map/stats/pallas_call | solution.py:369
  41.1 12.8 %conditional.1 = (f32[256,128]{1,0:T(8,128)S(1)}) conditional(s32[]{:T(128)} %convert_element_type.23, (f32[64,128]{1,0:T(8,128)S(1)}, s32[32]{0:T(128)S(1)}) %tuple.19, f32[256,128]{1,0:T(8,128)S(1)} %get-tuple-element.61), branch_computations={%region_7.8_spmd, %region_8.9_spmd} | conditional | bytes 294924 | solution.py:399
  41.1 12.8 %all_to_all.38 = f32[32,8,128]{2,1,0:T(8,128)S(1)} all-to-all(f32[32,8,128]{2,1,0:T(8,128)S(1)} %bitcast.42), channel_id=1, replica_groups=mesh['seq'=32,'head'=16] {'seq'}, dimensions={0} | all-to-all | bytes 262144 | tf_op jit(solution)/shard_map/cond/branch_1_fun/all_to_all | solution.py:384
  53.9 7.6 %grads.1 = (bf16[32,320,128]{2,1,0:T(8,128)(2,1)}, bf16[4,56,256]{2,1,0:T(8,128)(2,1)}, bf16[4,56,256]{2,1,0:T(8,128)(2,1)}, bf16[4,56,256]{2,1,0:T(8,128)(2,1)}, bf16[4,56,256]{2,1,0:T(8,128)(2,1)}) custom-call(s32[64]{0:T(128)} %copy-done.3, s32[64]{0:T(128)} %get-tuple-element.54.refs_1_, bf16[64,2,64,128]{3,2,1,0:T(8,128)(2,1)} %copy-done, ...), custom_call_target="tpu_custom_call" | custom-call | tf_op jit(solution)/shard_map/grads/pallas_call | solution.py:406
  61.6 4.8 %collective-permute-start.3 = (bf16[4,56,256]{2,1,0:T(8,128)(2,1)}, bf16[4,56,256]{2,1,0:T(8,128)(2,1)S(1)}, u32[]{:S(2)}, u32[]{:S(2)}) collective-permute-start(bf16[4,56,256]{2,1,0:T(8,128)(2,1)} %get-tuple-element.67), channel_id=1, source_target_pairs={{0,15},{1,0},{2,1},{3,2},{4,3},{5,4},{6,5},{7,6},{8,7},{9,8},{10,9... | collective-permute-start | bytes 344072 | tf_op jit(solution)/shard_map/ppermute | solution.py:292
  66.4 2.1 %collective-permute-start.4 = (bf16[4,56,256]{2,1,0:T(8,128)(2,1)}, bf16[4,56,256]{2,1,0:T(8,128)(2,1)S(1)}, u32[]{:S(2)}, u32[]{:S(2)}) collective-permute-start(bf16[4,56,256]{2,1,0:T(8,128)(2,1)} %get-tuple-element.68), channel_id=1, source_target_pairs={{0,2},{1,3},{2,4},{3,5},{4,6},{5,7},{6,8},{7,9},{8,10},{9,11},{10,... | collective-permute-start | bytes 344072 | tf_op jit(solution)/shard_map/ppermute | solution.py:292
  68.5 4.8 %collective-permute-start.5 = (bf16[4,56,256]{2,1,0:T(8,128)(2,1)}, bf16[4,56,256]{2,1,0:T(8,128)(2,1)}, u32[]{:S(2)}, u32[]{:S(2)}) collective-permute-start(bf16[4,56,256]{2,1,0:T(8,128)(2,1)} %get-tuple-element.69), channel_id=1, source_target_pairs={{0,1},{1,2},{2,3},{3,4},{4,5},{5,6},{6,7},{7,8},{8,9},{9,10},{10,1... | collective-permute-start | bytes 344072 | tf_op jit(solution)/shard_map/ppermute | solution.py:292
  73.3 5.9 %all-to-all-start.4 = ((bf16[32,320,128]{2,1,0:T(8,128)(2,1)}), bf16[32,320,128]{2,1,0:T(8,128)(2,1)S(1)}, u32[]{:S(2)}, u32[]{:S(2)}) async-start(bf16[32,320,128]{2,1,0:T(8,128)(2,1)} %get-tuple-element.65), calls=%async_computation.4 | async-start | bytes 5242880 | tf_op jit(solution)/shard_map/all_to_all | solution.py:433
  79.3 0.6 copy-done.5
  79.9 2.5 %collective-permute-done.5.refs_3_ = bf16[4,56,256]{2,1,0:T(8,128)(2,1)} collective-permute-done((bf16[4,56,256]{2,1,0:T(8,128)(2,1)}, bf16[4,56,256]{2,1,0:T(8,128)(2,1)}, u32[]{:S(2)}, u32[]{:S(2)}) %collective-permute-start.5) | collective-permute-done | bytes 114720 | tf_op jit(solution)/shard_map/ppermute | solution.py:292
  82.5 0.9 copy-done.6
  83.4 3.1 %project.1 = (f32[56,896]{1,0:T(8,128)S(1)}, bf16[56,896]{1,0:T(8,128)(2,1)S(1)}, bf16[56,896]{1,0:T(8,128)(2,1)S(1)}, bf16[56,896]{1,0:T(8,128)(2,1)S(1)}) custom-call(bf16[4,56,256]{2,1,0:T(8,128)(2,1)S(1)} %copy-done.4, bf16[4,56,256]{2,1,0:T(8,128)(2,1)S(1)} %collective-permute-done.3.refs_1_, bf16[4,56,256]{2,1,0:T(8,128)(2,1)S(1)} %copy-done.6, ...), custom_call_target="tpu_custom_call" | custom-call | flops 60000002048 | bytes 2000000 | tf_op jit(solution)/shard_map/project/pallas_call | solution.py:434
  86.4 6.8 %collective-permute-start.6 = (bf16[56,896]{1,0:T(8,128)(2,1)S(1)}, bf16[56,896]{1,0:T(8,128)(2,1)S(1)}, u32[]{:S(2)}, u32[]{:S(2)}) collective-permute-start(bf16[56,896]{1,0:T(8,128)(2,1)S(1)} %get-tuple-element.75), channel_id=1, source_target_pairs={{0,12},{1,13},{2,14},{3,15},{4,0},{5,1},{6,2},{7,3},{8,4},{9,5},{1... | collective-permute-start | bytes 301064 | tf_op jit(solution)/shard_map/ppermute | solution.py:292
  93.2 6.1 %collective-permute-start.7 = (bf16[56,896]{1,0:T(8,128)(2,1)S(1)}, bf16[56,896]{1,0:T(8,128)(2,1)S(1)}, u32[]{:S(2)}, u32[]{:S(2)}) collective-permute-start(bf16[56,896]{1,0:T(8,128)(2,1)S(1)} %get-tuple-element.76), channel_id=1, source_target_pairs={{0,8},{1,9},{2,10},{3,11},{4,12},{5,13},{6,14},{7,15},{8,0},{9,1},... | collective-permute-start | bytes 301064 | tf_op jit(solution)/shard_map/ppermute | solution.py:292
  99.2 6.1 %collective-permute-start.8 = (bf16[56,896]{1,0:T(8,128)(2,1)S(1)}, bf16[56,896]{1,0:T(8,128)(2,1)S(1)}, u32[]{:S(2)}, u32[]{:S(2)}) collective-permute-start(bf16[56,896]{1,0:T(8,128)(2,1)S(1)} %get-tuple-element.77), channel_id=1, source_target_pairs={{0,4},{1,5},{2,6},{3,7},{4,8},{5,9},{6,10},{7,11},{8,12},{9,13},{1... | collective-permute-start | bytes 301064 | tf_op jit(solution)/shard_map/ppermute | solution.py:292
  105.4 4.9 %collective-permute-done.7.two_ref = bf16[56,896]{1,0:T(8,128)(2,1)S(1)} collective-permute-done((bf16[56,896]{1,0:T(8,128)(2,1)S(1)}, bf16[56,896]{1,0:T(8,128)(2,1)S(1)}, u32[]{:S(2)}, u32[]{:S(2)}) %collective-permute-start.7) | collective-permute-done | bytes 100384 | tf_op jit(solution)/shard_map/ppermute | solution.py:292
  110.3 10.8 %collective-permute-done.8.three_ref = bf16[56,896]{1,0:T(8,128)(2,1)S(1)} collective-permute-done((bf16[56,896]{1,0:T(8,128)(2,1)S(1)}, bf16[56,896]{1,0:T(8,128)(2,1)S(1)}, u32[]{:S(2)}, u32[]{:S(2)}) %collective-permute-start.8) | collective-permute-done | bytes 100384 | tf_op jit(solution)/shard_map/ppermute | solution.py:292
  121.1 1.6 %finish.1 = (bf16[16,64,128]{2,1,0:T(8,128)(2,1)}, bf16[16,64,128]{2,1,0:T(8,128)(2,1)}, f32[56,896]{1,0:T(8,128)}, f32[28,128]{1,0:T(8,128)}, f32[28,128]{1,0:T(8,128)}) custom-call(s32[32]{0:T(128)S(1)} %get-tuple-element.50.slots_ref, bf16[32,320,128]{2,1,0:T(8,128)(2,1)S(1)} %all-to-all-done.4.in_ref, f32[56,896]{1,0:T(8,128)S(1)} %get-tuple-element.74.own_ref, ...), custom_call_target="tpu_custom_call" | custom-call | tf_op jit(solution)/shard_map/finish/pallas_call | solution.py:452
  (57 shorter events, 3.2 us)
Async XLA Ops:
  4.0 8.0 %copy-start.9 = (s32[512,2]{0,1:T(2,128)S(1)}, s32[512,2]{0,1:T(2,128)}, u32[]{:S(2)}) copy-start(s32[512,2]{0,1:T(2,128)} %param.12) | copy-start | bytes 12292
  4.0 35.1 %all-to-all-start.3 = ((bf16[64,2,64,128]{3,2,1,0:T(8,128)(2,1)}), bf16[64,2,64,128]{3,2,1,0:T(8,128)(2,1)S(1)}, u32[]{:S(2)}, u32[]{:S(2)}) async-start(bf16[64,2,64,128]{3,2,1,0:T(8,128)(2,1)} %get-tuple-element.55), calls=%async_computation.3 | async-start | bytes 4194304 | tf_op jit(solution)/shard_map/all_to_all | solution.py:327
  15.7 23.5 %copy-start.3 = (s32[64]{0:T(128)}, s32[64]{0:T(128)S(1)}, u32[]{:S(2)}) copy-start(s32[64]{0:T(128)S(1)} %get-tuple-element.53.refs_0_) | copy-start | bytes 772
  16.2 3.7 %copy-start.7 = (bf16[896,128]{1,0:T(8,128)(2,1)S(1)}, bf16[896,128]{1,0:T(8,128)(2,1)}, u32[]{:S(2)}) copy-start(bf16[896,128]{1,0:T(8,128)(2,1)} %param.10) | copy-start | bytes 688132
  16.2 3.7 %copy-start.8 = (bf16[896,128]{1,0:T(8,128)(2,1)S(1)}, bf16[896,128]{1,0:T(8,128)(2,1)}, u32[]{:S(2)}) copy-start(bf16[896,128]{1,0:T(8,128)(2,1)} %param.11) | copy-start | bytes 688132
  24.1 17.0 %copy-start.1 = (bf16[896,256]{1,0:T(8,128)(2,1)}, bf16[896,256]{1,0:T(8,128)(2,1)S(1)}, u32[]{:S(2)}) copy-start(bf16[896,256]{1,0:T(8,128)(2,1)S(1)} %copy.30) | copy-start | bytes 1376260
  26.0 42.5 %collective-permute-start.2 = (bf16[896,256]{1,0:T(8,128)(2,1)S(1)}, bf16[896,256]{1,0:T(8,128)(2,1)}, u32[]{:S(2)}, u32[]{:S(2)}) collective-permute-start(bf16[896,256]{1,0:T(8,128)(2,1)S(1)} %constant_dynamic-update-slice_fusion.refs_4_), channel_id=1, source_target_pairs={{0,1},{1,2},{2,3},{3,4},{4,5},{5,6},{6,7},{7,8},{8,9},{9,10},{10,1... | collective-permute-start | bytes 1376264 | tf_op jit(solution)/shard_map/ppermute | solution.py:292
  29.5 43.8 %collective-permute-start.1 = (bf16[896,256]{1,0:T(8,128)(2,1)S(1)}, bf16[896,256]{1,0:T(8,128)(2,1)}, u32[]{:S(2)}, u32[]{:S(2)}) collective-permute-start(bf16[896,256]{1,0:T(8,128)(2,1)S(1)} %constant_dynamic-update-slice_fusion.refs_4_), channel_id=1, source_target_pairs={{0,2},{1,3},{2,4},{3,5},{4,6},{5,7},{6,8},{7,9},{8,10},{9,11},{10,... | collective-permute-start | bytes 1376264 | tf_op jit(solution)/shard_map/ppermute | solution.py:292
  35.6 37.7 %collective-permute-start = (bf16[896,256]{1,0:T(8,128)(2,1)S(1)}, bf16[896,256]{1,0:T(8,128)(2,1)}, u32[]{:S(2)}, u32[]{:S(2)}) collective-permute-start(bf16[896,256]{1,0:T(8,128)(2,1)S(1)} %constant_dynamic-update-slice_fusion.refs_4_), channel_id=1, source_target_pairs={{0,15},{1,0},{2,1},{3,2},{4,3},{5,4},{6,5},{7,6},{8,7},{9,8},{10,9... | collective-permute-start | bytes 1376264 | tf_op jit(solution)/shard_map/ppermute | solution.py:292
  39.2 14.8 %copy-start = (bf16[64,2,64,128]{3,2,1,0:T(8,128)(2,1)}, bf16[64,2,64,128]{3,2,1,0:T(8,128)(2,1)S(1)}, u32[]{:S(2)}) copy-start(bf16[64,2,64,128]{3,2,1,0:T(8,128)(2,1)S(1)} %all-to-all-done.3.refs_2_) | copy-start | bytes 6291460
  41.1 12.8 %copy-start.2 = (f32[32,2,128]{2,1,0:T(2,128)}, f32[32,2,128]{2,1,0:T(2,128)S(1)}, u32[]{:S(2)}) copy-start(f32[32,2,128]{2,1,0:T(2,128)S(1)} %get-tuple-element.58.refs_4_) | copy-start | bytes 98308
  61.6 17.7 %collective-permute-start.3 = (bf16[4,56,256]{2,1,0:T(8,128)(2,1)}, bf16[4,56,256]{2,1,0:T(8,128)(2,1)S(1)}, u32[]{:S(2)}, u32[]{:S(2)}) collective-permute-start(bf16[4,56,256]{2,1,0:T(8,128)(2,1)} %get-tuple-element.67), channel_id=1, source_target_pairs={{0,15},{1,0},{2,1},{3,2},{4,3},{5,4},{6,5},{7,6},{8,7},{9,8},{10,9... | collective-permute-start | bytes 344072 | tf_op jit(solution)/shard_map/ppermute | solution.py:292
  66.4 12.8 %collective-permute-start.4 = (bf16[4,56,256]{2,1,0:T(8,128)(2,1)}, bf16[4,56,256]{2,1,0:T(8,128)(2,1)S(1)}, u32[]{:S(2)}, u32[]{:S(2)}) collective-permute-start(bf16[4,56,256]{2,1,0:T(8,128)(2,1)} %get-tuple-element.68), channel_id=1, source_target_pairs={{0,2},{1,3},{2,4},{3,5},{4,6},{5,7},{6,8},{7,9},{8,10},{9,11},{10,... | collective-permute-start | bytes 344072 | tf_op jit(solution)/shard_map/ppermute | solution.py:292
  68.5 13.9 %collective-permute-start.5 = (bf16[4,56,256]{2,1,0:T(8,128)(2,1)}, bf16[4,56,256]{2,1,0:T(8,128)(2,1)}, u32[]{:S(2)}, u32[]{:S(2)}) collective-permute-start(bf16[4,56,256]{2,1,0:T(8,128)(2,1)} %get-tuple-element.69), channel_id=1, source_target_pairs={{0,1},{1,2},{2,3},{3,4},{4,5},{5,6},{6,7},{7,8},{8,9},{9,10},{10,1... | collective-permute-start | bytes 344072 | tf_op jit(solution)/shard_map/ppermute | solution.py:292
  73.3 9.2 %copy-start.4 = (bf16[4,56,256]{2,1,0:T(8,128)(2,1)S(1)}, bf16[4,56,256]{2,1,0:T(8,128)(2,1)}, u32[]{:S(2)}) copy-start(bf16[4,56,256]{2,1,0:T(8,128)(2,1)} %get-tuple-element.66.refs_0_) | copy-start | bytes 344068
  73.3 47.8 %all-to-all-start.4 = ((bf16[32,320,128]{2,1,0:T(8,128)(2,1)}), bf16[32,320,128]{2,1,0:T(8,128)(2,1)S(1)}, u32[]{:S(2)}, u32[]{:S(2)}) async-start(bf16[32,320,128]{2,1,0:T(8,128)(2,1)} %get-tuple-element.65), calls=%async_computation.4 | async-start | bytes 5242880 | tf_op jit(solution)/shard_map/all_to_all | solution.py:433
  79.3 0.6 copy-start.5
  82.5 0.9 copy-start.6
  86.4 19.0 %collective-permute-start.6 = (bf16[56,896]{1,0:T(8,128)(2,1)S(1)}, bf16[56,896]{1,0:T(8,128)(2,1)S(1)}, u32[]{:S(2)}, u32[]{:S(2)}) collective-permute-start(bf16[56,896]{1,0:T(8,128)(2,1)S(1)} %get-tuple-element.75), channel_id=1, source_target_pairs={{0,12},{1,13},{2,14},{3,15},{4,0},{5,1},{6,2},{7,3},{8,4},{9,5},{1... | collective-permute-start | bytes 301064 | tf_op jit(solution)/shard_map/ppermute | solution.py:292
  93.2 17.1 %collective-permute-start.7 = (bf16[56,896]{1,0:T(8,128)(2,1)S(1)}, bf16[56,896]{1,0:T(8,128)(2,1)S(1)}, u32[]{:S(2)}, u32[]{:S(2)}) collective-permute-start(bf16[56,896]{1,0:T(8,128)(2,1)S(1)} %get-tuple-element.76), channel_id=1, source_target_pairs={{0,8},{1,9},{2,10},{3,11},{4,12},{5,13},{6,14},{7,15},{8,0},{9,1},... | collective-permute-start | bytes 301064 | tf_op jit(solution)/shard_map/ppermute | solution.py:292
  99.2 21.8 %collective-permute-start.8 = (bf16[56,896]{1,0:T(8,128)(2,1)S(1)}, bf16[56,896]{1,0:T(8,128)(2,1)S(1)}, u32[]{:S(2)}, u32[]{:S(2)}) collective-permute-start(bf16[56,896]{1,0:T(8,128)(2,1)S(1)} %get-tuple-element.77), channel_id=1, source_target_pairs={{0,4},{1,5},{2,6},{3,7},{4,8},{5,9},{6,10},{7,11},{8,12},{9,13},{1... | collective-permute-start | bytes 301064 | tf_op jit(solution)/shard_map/ppermute | solution.py:292

commit v11 on v10

--- a/solution.py
+++ b/solution.py
@@ -12,7 +12,7 @@
 CAP = 2
 PLACES = 8
 NEAR = (0, -1, 2, 1)
-FAR = (0, -4, 8, 4)
+FAR = (0, 4, 8, -4)
 VMEM_LIMIT = 40 * 1024 * 1024
 LARGE_LIMIT = 60 * 1024 * 1024
 SMALL_LIMIT = 16 * 1024 * 1024

time: 123 us -> 124 us (level)
  the two profiles are of different devices: /device:TPU:35 before, /device:TPU:1 now
where the time goes in v11:
time: 124 us; the launch traced here: 123 us
  starting transfers between devices  58.8 us (47%)
  Pallas kernels  17.6 us (14%)
  waiting for transfers between devices  15.9 us (13%)
  blocking collectives  14.2 us (11%)
  local copies, waits for them, and re-layouts  9 us (7%)
  matrix products  3.09 us (2%)
  other arithmetic  2.6 us (2%)
  between operations  1.68 us (1%)
    ppermute x9, starting transfers between devices, shifted(): lax.ppermute(x, 'head', [(z, (z + step) % count) for z in range(count)])  43.7 us
    ppermute x9, waiting for transfers between devices, shifted(): lax.ppermute(x, 'head', [(z, (z + step) % count) for z in range(count)])  14.9 us
    all_to_all x1, blocking collectives, one_hop(): return lax.all_to_all(sent, 'seq', split_axis=0, concat_axis=0, tiled=True)  14.2 us
    all_to_all x1, starting transfers between devices, on_device(): lax.all_to_all(packed, 'seq', split_axis=0, concat_axis=0, tiled=True)  10.6 us
    pallas_call x1, Pallas kernels, on_device(): pl.pallas_call(lambda *refs: grads_kernel(scale, group, *refs), out_shape...  7.64 us
    all_to_all x1, starting transfers between devices, on_device(): lax.all_to_all(back, 'seq', split_axis=0, concat_axis=0, tiled=True)  4.54 us
    reshape x1, local copies, waits for them, and re-layouts, on_device(): flat_enc = encodings.reshape(block_count * block_len, enc_width)  3.65 us
    pallas_call x1, Pallas kernels, on_device(): pl.pallas_call(lambda *refs: pack_kernel(block_count, *refs), out_shape=(...  3.35 us
  transfers between devices with their start and end apart: 11, of which 4 were waited for; matrix products, arithmetic and copies ran while one was open for 11% of the time, Pallas kernels for 10%

profile of v11, /device:TPU:1, one launch (start us, length us, event | category | flops | bytes accessed | tf_op | source)
XLA Modules:
  0.0 122.8 jit_solution(7512350143279326458)
XLA Ops:
  0.6 3.4 %pack.1 = (bf16[64,2,64,128]{3,2,1,0:T(8,128)(2,1)}, s32[32]{0:T(128)S(1)}) custom-call(s32[2,512]{1,0:T(2,128)} %bitcast.44, bf16[16,64,128]{2,1,0:T(8,128)(2,1)} %bitcast.39, bf16[16,64,128]{2,1,0:T(8,128)(2,1)} %bitcast.40), custom_call_target="tpu_custom_call" | custom-call | tf_op jit(solution)/shard_map/pack/pallas_call | solution.py:307
  4.0 10.6 %all-to-all-start.3 = ((bf16[64,2,64,128]{3,2,1,0:T(8,128)(2,1)}), bf16[64,2,64,128]{3,2,1,0:T(8,128)(2,1)S(1)}, u32[]{:S(2)}, u32[]{:S(2)}) async-start(bf16[64,2,64,128]{3,2,1,0:T(8,128)(2,1)} %get-tuple-element.55), calls=%async_computation.3 | async-start | bytes 4194304 | tf_op jit(solution)/shard_map/all_to_all | solution.py:327
  14.9 0.3 broadcast_compare_fusion
  15.2 0.4 rev.6
  16.8 0.4 select_reduce_fusion.1
  18.8 3.6 %copy.31 = bf16[896,896]{0,1:T(8,128)(2,1)} copy(bf16[896,896]{1,0:T(8,128)(2,1)} %bitcast.36) | data formatting | bytes 3211264 | tf_op jit(solution)/shard_map/reshape | solution.py:331
  22.6 2.9 %fusion = bf16[896,256]{0,1:T(8,128)(2,1)} fusion(bf16[896,256]{1,0:T(8,128)(2,1)S(1)} %constant_dynamic-update-slice_fusion.refs_4_, bf16[896,896]{1,0:T(8,128)(2,1)} %bitcast.37), kind=kOutput, calls=%fused_computation.1 | convolution fusion | flops 411271168 | bytes 2523136 | tf_op jit(solution)/shard_map/dot_general | solution.py:332
  25.5 1.2 copy.30
  26.7 0.7 fusion.6
  28.0 0.5 broadcast_select_fusion
  28.6 1.9 %collective-permute-start.2 = (bf16[896,256]{1,0:T(8,128)(2,1)S(1)}, bf16[896,256]{1,0:T(8,128)(2,1)}, u32[]{:S(2)}, u32[]{:S(2)}) collective-permute-start(bf16[896,256]{1,0:T(8,128)(2,1)S(1)} %constant_dynamic-update-slice_fusion.refs_4_), channel_id=1, source_target_pairs={{0,1},{1,2},{2,3},{3,4},{4,5},{5,6},{6,7},{7,8},{8,9},{9,10},{10,1... | collective-permute-start | bytes 1376264 | tf_op jit(solution)/shard_map/ppermute | solution.py:292
  30.5 4.6 %collective-permute-start.1 = (bf16[896,256]{1,0:T(8,128)(2,1)S(1)}, bf16[896,256]{1,0:T(8,128)(2,1)}, u32[]{:S(2)}, u32[]{:S(2)}) collective-permute-start(bf16[896,256]{1,0:T(8,128)(2,1)S(1)} %constant_dynamic-update-slice_fusion.refs_4_), channel_id=1, source_target_pairs={{0,2},{1,3},{2,4},{3,5},{4,6},{5,7},{6,8},{7,9},{8,10},{9,11},{10,... | collective-permute-start | bytes 1376264 | tf_op jit(solution)/shard_map/ppermute | solution.py:292
  35.1 6.5 %collective-permute-start = (bf16[896,256]{1,0:T(8,128)(2,1)S(1)}, bf16[896,256]{1,0:T(8,128)(2,1)}, u32[]{:S(2)}, u32[]{:S(2)}) collective-permute-start(bf16[896,256]{1,0:T(8,128)(2,1)S(1)} %constant_dynamic-update-slice_fusion.refs_4_), channel_id=1, source_target_pairs={{0,15},{1,0},{2,1},{3,2},{4,3},{5,4},{6,5},{7,6},{8,7},{9,8},{10,9... | collective-permute-start | bytes 1376264 | tf_op jit(solution)/shard_map/ppermute | solution.py:292
  41.6 1.0 all-to-all-done.3.refs_2_
  42.5 1.9 %stats.1 = (f32[32,2,128]{2,1,0:T(2,128)S(1)}, f32[64,128]{1,0:T(8,128)S(1)}, f32[256,128]{1,0:T(8,128)S(1)}) custom-call(s32[64]{0:T(128)S(1)} %get-tuple-element.53.refs_0_, s32[64]{0:T(128)S(1)} %get-tuple-element.57.refs_1_, bf16[64,2,64,128]{3,2,1,0:T(8,128)(2,1)S(1)} %all-to-all-done.3.refs_2_, bf16[7,128,256]{2,1,0:T(8,128)(2,1)S(1)} %bitcast.31), custom_call_target="tpu_custom_call" | custom-call | tf_op jit(solution)/shard_map/stats/pallas_call | solution.py:369
  44.5 14.2 %conditional.1 = (f32[256,128]{1,0:T(8,128)S(1)}) conditional(s32[]{:T(128)} %convert_element_type.23, (f32[64,128]{1,0:T(8,128)S(1)}, s32[32]{0:T(128)S(1)}) %tuple.19, f32[256,128]{1,0:T(8,128)S(1)} %get-tuple-element.61), branch_computations={%region_7.8_spmd, %region_8.9_spmd} | conditional | bytes 294924 | solution.py:399
  44.5 14.2 %all_to_all.38 = f32[32,8,128]{2,1,0:T(8,128)S(1)} all-to-all(f32[32,8,128]{2,1,0:T(8,128)S(1)} %bitcast.42), channel_id=1, replica_groups=mesh['seq'=32,'head'=16] {'seq'}, dimensions={0} | all-to-all | bytes 262144 | tf_op jit(solution)/shard_map/cond/branch_1_fun/all_to_all | solution.py:384
  58.7 7.6 %grads.1 = (bf16[32,320,128]{2,1,0:T(8,128)(2,1)}, bf16[4,56,256]{2,1,0:T(8,128)(2,1)}, bf16[4,56,256]{2,1,0:T(8,128)(2,1)}, bf16[4,56,256]{2,1,0:T(8,128)(2,1)}, bf16[4,56,256]{2,1,0:T(8,128)(2,1)}) custom-call(s32[64]{0:T(128)} %copy-done.3, s32[64]{0:T(128)} %get-tuple-element.54.refs_1_, bf16[64,2,64,128]{3,2,1,0:T(8,128)(2,1)} %copy-done, ...), custom_call_target="tpu_custom_call" | custom-call | tf_op jit(solution)/shard_map/grads/pallas_call | solution.py:406
  66.3 7.6 %collective-permute-start.3 = (bf16[4,56,256]{2,1,0:T(8,128)(2,1)}, bf16[4,56,256]{2,1,0:T(8,128)(2,1)S(1)}, u32[]{:S(2)}, u32[]{:S(2)}) collective-permute-start(bf16[4,56,256]{2,1,0:T(8,128)(2,1)} %get-tuple-element.67), channel_id=1, source_target_pairs={{0,15},{1,0},{2,1},{3,2},{4,3},{5,4},{6,5},{7,6},{8,7},{9,8},{10,9... | collective-permute-start | bytes 344072 | tf_op jit(solution)/shard_map/ppermute | solution.py:292
  74.0 1.9 %collective-permute-start.4 = (bf16[4,56,256]{2,1,0:T(8,128)(2,1)}, bf16[4,56,256]{2,1,0:T(8,128)(2,1)S(1)}, u32[]{:S(2)}, u32[]{:S(2)}) collective-permute-start(bf16[4,56,256]{2,1,0:T(8,128)(2,1)} %get-tuple-element.68), channel_id=1, source_target_pairs={{0,2},{1,3},{2,4},{3,5},{4,6},{5,7},{6,8},{7,9},{8,10},{9,11},{10,... | collective-permute-start | bytes 344072 | tf_op jit(solution)/shard_map/ppermute | solution.py:292
  75.9 1.9 %collective-permute-start.5 = (bf16[4,56,256]{2,1,0:T(8,128)(2,1)}, bf16[4,56,256]{2,1,0:T(8,128)(2,1)}, u32[]{:S(2)}, u32[]{:S(2)}) collective-permute-start(bf16[4,56,256]{2,1,0:T(8,128)(2,1)} %get-tuple-element.69), channel_id=1, source_target_pairs={{0,1},{1,2},{2,3},{3,4},{4,5},{5,6},{6,7},{7,8},{8,9},{9,10},{10,1... | collective-permute-start | bytes 344072 | tf_op jit(solution)/shard_map/ppermute | solution.py:292
  77.9 4.5 %all-to-all-start.4 = ((bf16[32,320,128]{2,1,0:T(8,128)(2,1)}), bf16[32,320,128]{2,1,0:T(8,128)(2,1)S(1)}, u32[]{:S(2)}, u32[]{:S(2)}) async-start(bf16[32,320,128]{2,1,0:T(8,128)(2,1)} %get-tuple-element.65), calls=%async_computation.4 | async-start | bytes 5242880 | tf_op jit(solution)/shard_map/all_to_all | solution.py:433
  82.5 0.6 copy-done.5
  83.1 1.5 %collective-permute-done.5.refs_3_ = bf16[4,56,256]{2,1,0:T(8,128)(2,1)} collective-permute-done((bf16[4,56,256]{2,1,0:T(8,128)(2,1)}, bf16[4,56,256]{2,1,0:T(8,128)(2,1)}, u32[]{:S(2)}, u32[]{:S(2)}) %collective-permute-start.5) | collective-permute-done | bytes 114720 | tf_op jit(solution)/shard_map/ppermute | solution.py:292
  84.6 0.9 copy-done.6
  85.5 3.1 %project.1 = (f32[56,896]{1,0:T(8,128)S(1)}, bf16[56,896]{1,0:T(8,128)(2,1)S(1)}, bf16[56,896]{1,0:T(8,128)(2,1)S(1)}, bf16[56,896]{1,0:T(8,128)(2,1)S(1)}) custom-call(bf16[4,56,256]{2,1,0:T(8,128)(2,1)S(1)} %copy-done.4, bf16[4,56,256]{2,1,0:T(8,128)(2,1)S(1)} %collective-permute-done.3.refs_1_, bf16[4,56,256]{2,1,0:T(8,128)(2,1)S(1)} %copy-done.6, ...), custom_call_target="tpu_custom_call" | custom-call | flops 60000002048 | bytes 2000000 | tf_op jit(solution)/shard_map/project/pallas_call | solution.py:434
  88.5 3.7 %collective-permute-start.6 = (bf16[56,896]{1,0:T(8,128)(2,1)S(1)}, bf16[56,896]{1,0:T(8,128)(2,1)S(1)}, u32[]{:S(2)}, u32[]{:S(2)}) collective-permute-start(bf16[56,896]{1,0:T(8,128)(2,1)S(1)} %get-tuple-element.75), channel_id=1, source_target_pairs={{0,4},{1,5},{2,6},{3,7},{4,8},{5,9},{6,10},{7,11},{8,12},{9,13},{1... | collective-permute-start | bytes 301064 | tf_op jit(solution)/shard_map/ppermute | solution.py:292
  92.2 10.0 %collective-permute-start.7 = (bf16[56,896]{1,0:T(8,128)(2,1)S(1)}, bf16[56,896]{1,0:T(8,128)(2,1)S(1)}, u32[]{:S(2)}, u32[]{:S(2)}) collective-permute-start(bf16[56,896]{1,0:T(8,128)(2,1)S(1)} %get-tuple-element.76), channel_id=1, source_target_pairs={{0,8},{1,9},{2,10},{3,11},{4,12},{5,13},{6,14},{7,15},{8,0},{9,1},... | collective-permute-start | bytes 301064 | tf_op jit(solution)/shard_map/ppermute | solution.py:292
  102.2 5.5 %collective-permute-start.8 = (bf16[56,896]{1,0:T(8,128)(2,1)S(1)}, bf16[56,896]{1,0:T(8,128)(2,1)S(1)}, u32[]{:S(2)}, u32[]{:S(2)}) collective-permute-start(bf16[56,896]{1,0:T(8,128)(2,1)S(1)} %get-tuple-element.77), channel_id=1, source_target_pairs={{0,12},{1,13},{2,14},{3,15},{4,0},{5,1},{6,2},{7,3},{8,4},{9,5},{1... | collective-permute-start | bytes 301064 | tf_op jit(solution)/shard_map/ppermute | solution.py:292
  107.7 6.7 %collective-permute-done.7.two_ref = bf16[56,896]{1,0:T(8,128)(2,1)S(1)} collective-permute-done((bf16[56,896]{1,0:T(8,128)(2,1)S(1)}, bf16[56,896]{1,0:T(8,128)(2,1)S(1)}, u32[]{:S(2)}, u32[]{:S(2)}) %collective-permute-start.7) | collective-permute-done | bytes 100384 | tf_op jit(solution)/shard_map/ppermute | solution.py:292
  114.4 6.7 %collective-permute-done.8.three_ref = bf16[56,896]{1,0:T(8,128)(2,1)S(1)} collective-permute-done((bf16[56,896]{1,0:T(8,128)(2,1)S(1)}, bf16[56,896]{1,0:T(8,128)(2,1)S(1)}, u32[]{:S(2)}, u32[]{:S(2)}) %collective-permute-start.8) | collective-permute-done | bytes 100384 | tf_op jit(solution)/shard_map/ppermute | solution.py:292
  121.2 1.6 %finish.1 = (bf16[16,64,128]{2,1,0:T(8,128)(2,1)}, bf16[16,64,128]{2,1,0:T(8,128)(2,1)}, f32[56,896]{1,0:T(8,128)}, f32[28,128]{1,0:T(8,128)}, f32[28,128]{1,0:T(8,128)}) custom-call(s32[32]{0:T(128)S(1)} %get-tuple-element.50.slots_ref, bf16[32,320,128]{2,1,0:T(8,128)(2,1)S(1)} %all-to-all-done.4.in_ref, f32[56,896]{1,0:T(8,128)S(1)} %get-tuple-element.74.own_ref, ...), custom_call_target="tpu_custom_call" | custom-call | tf_op jit(solution)/shard_map/finish/pallas_call | solution.py:452
  (57 shorter events, 3.2 us)
Async XLA Ops:
  4.0 10.6 %copy-start.9 = (s32[512,2]{0,1:T(2,128)S(1)}, s32[512,2]{0,1:T(2,128)}, u32[]{:S(2)}) copy-start(s32[512,2]{0,1:T(2,128)} %param.12) | copy-start | bytes 12292
  4.0 38.5 %all-to-all-start.3 = ((bf16[64,2,64,128]{3,2,1,0:T(8,128)(2,1)}), bf16[64,2,64,128]{3,2,1,0:T(8,128)(2,1)S(1)}, u32[]{:S(2)}, u32[]{:S(2)}) async-start(bf16[64,2,64,128]{3,2,1,0:T(8,128)(2,1)} %get-tuple-element.55), calls=%async_computation.3 | async-start | bytes 4194304 | tf_op jit(solution)/shard_map/all_to_all | solution.py:327
  18.3 24.3 %copy-start.3 = (s32[64]{0:T(128)}, s32[64]{0:T(128)S(1)}, u32[]{:S(2)}) copy-start(s32[64]{0:T(128)S(1)} %get-tuple-element.53.refs_0_) | copy-start | bytes 772
  18.8 3.7 %copy-start.7 = (bf16[896,128]{1,0:T(8,128)(2,1)S(1)}, bf16[896,128]{1,0:T(8,128)(2,1)}, u32[]{:S(2)}) copy-start(bf16[896,128]{1,0:T(8,128)(2,1)} %param.10) | copy-start | bytes 688132
  18.8 3.7 %copy-start.8 = (bf16[896,128]{1,0:T(8,128)(2,1)S(1)}, bf16[896,128]{1,0:T(8,128)(2,1)}, u32[]{:S(2)}) copy-start(bf16[896,128]{1,0:T(8,128)(2,1)} %param.11) | copy-start | bytes 688132
  26.7 17.8 %copy-start.1 = (bf16[896,256]{1,0:T(8,128)(2,1)}, bf16[896,256]{1,0:T(8,128)(2,1)S(1)}, u32[]{:S(2)}) copy-start(bf16[896,256]{1,0:T(8,128)(2,1)S(1)} %copy.30) | copy-start | bytes 1376260
  28.6 47.4 %collective-permute-start.2 = (bf16[896,256]{1,0:T(8,128)(2,1)S(1)}, bf16[896,256]{1,0:T(8,128)(2,1)}, u32[]{:S(2)}, u32[]{:S(2)}) collective-permute-start(bf16[896,256]{1,0:T(8,128)(2,1)S(1)} %constant_dynamic-update-slice_fusion.refs_4_), channel_id=1, source_target_pairs={{0,1},{1,2},{2,3},{3,4},{4,5},{5,6},{6,7},{7,8},{8,9},{9,10},{10,1... | collective-permute-start | bytes 1376264 | tf_op jit(solution)/shard_map/ppermute | solution.py:292
  30.5 47.4 %collective-permute-start.1 = (bf16[896,256]{1,0:T(8,128)(2,1)S(1)}, bf16[896,256]{1,0:T(8,128)(2,1)}, u32[]{:S(2)}, u32[]{:S(2)}) collective-permute-start(bf16[896,256]{1,0:T(8,128)(2,1)S(1)} %constant_dynamic-update-slice_fusion.refs_4_), channel_id=1, source_target_pairs={{0,2},{1,3},{2,4},{3,5},{4,6},{5,7},{6,8},{7,9},{8,10},{9,11},{10,... | collective-permute-start | bytes 1376264 | tf_op jit(solution)/shard_map/ppermute | solution.py:292
  35.1 42.8 %collective-permute-start = (bf16[896,256]{1,0:T(8,128)(2,1)S(1)}, bf16[896,256]{1,0:T(8,128)(2,1)}, u32[]{:S(2)}, u32[]{:S(2)}) collective-permute-start(bf16[896,256]{1,0:T(8,128)(2,1)S(1)} %constant_dynamic-update-slice_fusion.refs_4_), channel_id=1, source_target_pairs={{0,15},{1,0},{2,1},{3,2},{4,3},{5,4},{6,5},{7,6},{8,7},{9,8},{10,9... | collective-permute-start | bytes 1376264 | tf_op jit(solution)/shard_map/ppermute | solution.py:292
  42.5 16.1 %copy-start = (bf16[64,2,64,128]{3,2,1,0:T(8,128)(2,1)}, bf16[64,2,64,128]{3,2,1,0:T(8,128)(2,1)S(1)}, u32[]{:S(2)}) copy-start(bf16[64,2,64,128]{3,2,1,0:T(8,128)(2,1)S(1)} %all-to-all-done.3.refs_2_) | copy-start | bytes 6291460
  44.5 14.2 %copy-start.2 = (f32[32,2,128]{2,1,0:T(2,128)}, f32[32,2,128]{2,1,0:T(2,128)S(1)}, u32[]{:S(2)}) copy-start(f32[32,2,128]{2,1,0:T(2,128)S(1)} %get-tuple-element.58.refs_4_) | copy-start | bytes 98308
  66.3 16.1 %collective-permute-start.3 = (bf16[4,56,256]{2,1,0:T(8,128)(2,1)}, bf16[4,56,256]{2,1,0:T(8,128)(2,1)S(1)}, u32[]{:S(2)}, u32[]{:S(2)}) collective-permute-start(bf16[4,56,256]{2,1,0:T(8,128)(2,1)} %get-tuple-element.67), channel_id=1, source_target_pairs={{0,15},{1,0},{2,1},{3,2},{4,3},{5,4},{6,5},{7,6},{8,7},{9,8},{10,9... | collective-permute-start | bytes 344072 | tf_op jit(solution)/shard_map/ppermute | solution.py:292
  74.0 8.5 %collective-permute-start.4 = (bf16[4,56,256]{2,1,0:T(8,128)(2,1)}, bf16[4,56,256]{2,1,0:T(8,128)(2,1)S(1)}, u32[]{:S(2)}, u32[]{:S(2)}) collective-permute-start(bf16[4,56,256]{2,1,0:T(8,128)(2,1)} %get-tuple-element.68), channel_id=1, source_target_pairs={{0,2},{1,3},{2,4},{3,5},{4,6},{5,7},{6,8},{7,9},{8,10},{9,11},{10,... | collective-permute-start | bytes 344072 | tf_op jit(solution)/shard_map/ppermute | solution.py:292
  75.9 8.6 %collective-permute-start.5 = (bf16[4,56,256]{2,1,0:T(8,128)(2,1)}, bf16[4,56,256]{2,1,0:T(8,128)(2,1)}, u32[]{:S(2)}, u32[]{:S(2)}) collective-permute-start(bf16[4,56,256]{2,1,0:T(8,128)(2,1)} %get-tuple-element.69), channel_id=1, source_target_pairs={{0,1},{1,2},{2,3},{3,4},{4,5},{5,6},{6,7},{7,8},{8,9},{9,10},{10,1... | collective-permute-start | bytes 344072 | tf_op jit(solution)/shard_map/ppermute | solution.py:292
  77.9 6.7 %copy-start.4 = (bf16[4,56,256]{2,1,0:T(8,128)(2,1)S(1)}, bf16[4,56,256]{2,1,0:T(8,128)(2,1)}, u32[]{:S(2)}) copy-start(bf16[4,56,256]{2,1,0:T(8,128)(2,1)} %get-tuple-element.66.refs_0_) | copy-start | bytes 344068
  77.9 43.3 %all-to-all-start.4 = ((bf16[32,320,128]{2,1,0:T(8,128)(2,1)}), bf16[32,320,128]{2,1,0:T(8,128)(2,1)S(1)}, u32[]{:S(2)}, u32[]{:S(2)}) async-start(bf16[32,320,128]{2,1,0:T(8,128)(2,1)} %get-tuple-element.65), calls=%async_computation.4 | async-start | bytes 5242880 | tf_op jit(solution)/shard_map/all_to_all | solution.py:433
  82.4 0.6 copy-start.5
  84.6 0.9 copy-start.6
  88.5 19.2 %collective-permute-start.6 = (bf16[56,896]{1,0:T(8,128)(2,1)S(1)}, bf16[56,896]{1,0:T(8,128)(2,1)S(1)}, u32[]{:S(2)}, u32[]{:S(2)}) collective-permute-start(bf16[56,896]{1,0:T(8,128)(2,1)S(1)} %get-tuple-element.75), channel_id=1, source_target_pairs={{0,4},{1,5},{2,6},{3,7},{4,8},{5,9},{6,10},{7,11},{8,12},{9,13},{1... | collective-permute-start | bytes 301064 | tf_op jit(solution)/shard_map/ppermute | solution.py:292
  92.2 22.2 %collective-permute-start.7 = (bf16[56,896]{1,0:T(8,128)(2,1)S(1)}, bf16[56,896]{1,0:T(8,128)(2,1)S(1)}, u32[]{:S(2)}, u32[]{:S(2)}) collective-permute-start(bf16[56,896]{1,0:T(8,128)(2,1)S(1)} %get-tuple-element.76), channel_id=1, source_target_pairs={{0,8},{1,9},{2,10},{3,11},{4,12},{5,13},{6,14},{7,15},{8,0},{9,1},... | collective-permute-start | bytes 301064 | tf_op jit(solution)/shard_map/ppermute | solution.py:292
  102.2 18.9 %collective-permute-start.8 = (bf16[56,896]{1,0:T(8,128)(2,1)S(1)}, bf16[56,896]{1,0:T(8,128)(2,1)S(1)}, u32[]{:S(2)}, u32[]{:S(2)}) collective-permute-start(bf16[56,896]{1,0:T(8,128)(2,1)S(1)} %get-tuple-element.77), channel_id=1, source_target_pairs={{0,12},{1,13},{2,14},{3,15},{4,0},{5,1},{6,2},{7,3},{8,4},{9,5},{1... | collective-permute-start | bytes 301064 | tf_op jit(solution)/shard_map/ppermute | solution.py:292

commit v12 on v11

--- a/solution.py
+++ b/solution.py
@@ -233,7 +233,7 @@
     pltpu.make_async_copy(stage, out_ref, out_sem).wait()
 
 
-def finish_kernel(slots_ref, in_ref, own_ref, one_ref, two_ref, three_ref, att_ref, qg_ref, enc_ref, kw_ref, vw_ref):
+def finish_kernel(slots_ref, in_ref, att_ref, qg_ref, kw_ref, vw_ref, token_ref):
     share = kw_ref.shape[0]
     parts = 2 * CAP * SEGMENT
     room = (in_ref.shape[1] - parts) // 2
@@ -257,14 +257,18 @@
         total = total + in_ref[s, parts:, :].astype(jnp.float32)
     kw_ref[...] = total[:share]
     vw_ref[...] = total[room:room + share]
+    token_ref[0] = slots_ref[0]
+
+
+def total_kernel(token_ref, own_ref, one_ref, two_ref, three_ref, out_ref):
     total = own_ref[...] + one_ref[...].astype(jnp.float32)
-    enc_ref[...] = total + two_ref[...].astype(jnp.float32) + three_ref[...].astype(jnp.float32)
+    out_ref[...] = total + two_ref[...].astype(jnp.float32) + three_ref[...].astype(jnp.float32)
 
 
 def project_kernel(*refs):
     near = len(NEAR)
-    rows_hbm, weights_hbm, own_ref, far_refs = refs[:near], refs[near:2 * near], refs[2 * near], refs[2 * near + 1:-3]
-    rows_ref, weights_ref, sems = refs[-3:]
+    rows_hbm, weights_hbm, own_ref, far_refs = refs[:near], refs[near:2 * near], refs[2 * near], refs[2 * near + 1:-4]
+    rows_ref, weights_ref, acc, sems = refs[-4:]
     _, far, rows, width = rows_ref.shape
     copies = []
     for n in range(near):
@@ -272,19 +276,24 @@
         copies.append(pltpu.make_async_copy(rows_hbm[n], rows_ref.at[n], sems.at[near + n]))
     for copy in copies:
         copy.start()
-    for copy in copies:
-        copy.wait()
     half = far // 2
-    for i in range(0, far, half):
-        total = jnp.zeros((half * rows, own_ref.shape[1]), jnp.float32)
-        for n in range(near):
-            total = total + nt_dot(rows_ref[n, i:i + half].reshape(half * rows, width), weights_ref[n])
-        for j in range(half):
-            part = total[j * rows:(j + 1) * rows]
-            if i + j == 0:
-                own_ref[...] = part
-            else:
-                far_refs[i + j - 1][...] = part.astype(jnp.bfloat16)
+    for n in range(near):
+        copies[2 * n].wait()
+        copies[2 * n + 1].wait()
+        for i in range(0, far, half):
+            at = pl.ds(i * rows, half * rows)
+            total = nt_dot(rows_ref[n, i:i + half].reshape(half * rows, width), weights_ref[n])
+            if n > 0:
+                total = total + acc[at]
+            if n < near - 1:
+                acc[at] = total
+                continue
+            for j in range(half):
+                part = total[j * rows:(j + 1) * rows]
+                if i + j == 0:
+                    own_ref[...] = part
+                else:
+                    far_refs[i + j - 1][...] = part.astype(jnp.bfloat16)
 
 
 def shifted(x, step):
@@ -442,6 +451,7 @@
         scratch_shapes=[
             pltpu.VMEM((near, far, rows, 2 * head_dim), bf16),
             pltpu.VMEM((near, enc_width, 2 * head_dim), bf16),
+            pltpu.VMEM((far * rows, enc_width), f32),
             pltpu.SemaphoreType.DMA((2 * near,)),
         ],
         compiler_params=params(SMALL_LIMIT),
@@ -449,20 +459,28 @@
         name="project",
     )(*near_rows, *near_weights)
     far_sums = [shifted(part, b) for b, part in zip(FAR[1:], far_sums)]
-    attended, query_grad, encoding_grad, key_weight_grad, value_weight_grad = pl.pallas_call(
+    attended, query_grad, key_weight_grad, value_weight_grad, token = pl.pallas_call(
         finish_kernel,
         out_shape=(
             jax.ShapeDtypeStruct((segments, SEGMENT, head_dim), bf16),
             jax.ShapeDtypeStruct((segments, SEGMENT, head_dim), bf16),
-            jax.ShapeDtypeStruct((rows, enc_width), f32),
             jax.ShapeDtypeStruct((share, head_dim), f32),
             jax.ShapeDtypeStruct((share, head_dim), f32),
+            jax.ShapeDtypeStruct((1,), jnp.int32),
         ),
-        in_specs=[spec(SMEM), *[spec(VMEM)] * (1 + far)],
-        out_specs=(spec(VMEM),) * 5,
+        in_specs=[spec(SMEM), spec(VMEM)],
+        out_specs=(*[spec(VMEM)] * 4, spec(SMEM)),
         compiler_params=params(),
         name="finish",
-    )(slots, returned, own, *far_sums)
+    )(slots, returned)
+    encoding_grad = pl.pallas_call(
+        total_kernel,
+        out_shape=jax.ShapeDtypeStruct((rows, enc_width), f32),
+        in_specs=[spec(SMEM), *[spec(VMEM)] * far],
+        out_specs=spec(VMEM),
+        compiler_params=params(),
+        name="total",
+    )(token, own, *far_sums)
     return (
         attended.reshape(segments * SEGMENT, head_dim),
         query_grad.reshape(segments * SEGMENT, head_dim),

time: 124 us -> 124 us (level)
  waiting for transfers between devices: 15.9 us -> 14.6 us
  Pallas kernels: 17.6 us -> 18.9 us
    ppermute x9, waiting for transfers between devices: 14.9 us -> 5.05 us  [shifted(): lax.ppermute(x, 'head', [(z, (z + step) % count) for z in range(count)])]
    all_to_all x1, waiting for transfers between devices: 0.01 us -> 8.54 us  [on_device(): lax.all_to_all(back, 'seq', split_axis=0, concat_axis=0, tiled=True)]
    pallas_call x0 -> x1, Pallas kernels: none -> 1.35 us  [on_device(): pl.pallas_call(total_kernel, out_shape=jax.ShapeDtypeStruct((rows, enc_wi...]
  transfers between devices with their start and end apart: 11 -> 11, of which waited for: 4 -> 4; matrix products, arithmetic and copies ran while one was open for 11% -> 11% of each run, Pallas kernels for 10% -> 12%
where the time goes in v12:
time: 124 us; the launch traced here: 123 us
  starting transfers between devices  58.7 us (47%)
  Pallas kernels  18.9 us (15%)
  waiting for transfers between devices  14.6 us (12%)
  blocking collectives  14.1 us (11%)
  local copies, waits for them, and re-layouts  9 us (7%)
  matrix products  3.09 us (2%)
  other arithmetic  2.6 us (2%)
  between operations  1.69 us (1%)
    ppermute x9, starting transfers between devices, shifted(): lax.ppermute(x, 'head', [(z, (z + step) % count) for z in range(count)])  43.6 us
    all_to_all x1, blocking collectives, one_hop(): return lax.all_to_all(sent, 'seq', split_axis=0, concat_axis=0, tiled=True)  14.1 us
    all_to_all x1, starting transfers between devices, on_device(): lax.all_to_all(packed, 'seq', split_axis=0, concat_axis=0, tiled=True)  10.6 us
    all_to_all x1, waiting for transfers between devices, on_device(): lax.all_to_all(back, 'seq', split_axis=0, concat_axis=0, tiled=True)  8.54 us
    pallas_call x1, Pallas kernels, on_device(): pl.pallas_call(lambda *refs: grads_kernel(scale, group, *refs), out_shape...  7.64 us
    ppermute x9, waiting for transfers between devices, shifted(): lax.ppermute(x, 'head', [(z, (z + step) % count) for z in range(count)])  5.05 us
    all_to_all x1, starting transfers between devices, on_device(): lax.all_to_all(back, 'seq', split_axis=0, concat_axis=0, tiled=True)  4.53 us
    reshape x1, local copies, waits for them, and re-layouts, on_device(): flat_enc = encodings.reshape(block_count * block_len, enc_width)  3.65 us
  transfers between devices with their start and end apart: 11, of which 4 were waited for; matrix products, arithmetic and copies ran while one was open for 11% of the time, Pallas kernels for 12%

profile of v12, /device:TPU:1, one launch (start us, length us, event | category | flops | bytes accessed | tf_op | source)
XLA Modules:
  0.0 122.8 jit_solution(5374116589026571442)
XLA Ops:
  0.6 3.4 %pack.1 = (bf16[64,2,64,128]{3,2,1,0:T(8,128)(2,1)}, s32[32]{0:T(128)S(1)}) custom-call(s32[2,512]{1,0:T(2,128)} %bitcast.45, bf16[16,64,128]{2,1,0:T(8,128)(2,1)} %bitcast.39, bf16[16,64,128]{2,1,0:T(8,128)(2,1)} %bitcast.40), custom_call_target="tpu_custom_call" | custom-call | tf_op jit(solution)/shard_map/pack/pallas_call | solution.py:316
  4.0 10.6 %all-to-all-start.3 = ((bf16[64,2,64,128]{3,2,1,0:T(8,128)(2,1)}), bf16[64,2,64,128]{3,2,1,0:T(8,128)(2,1)S(1)}, u32[]{:S(2)}, u32[]{:S(2)}) async-start(bf16[64,2,64,128]{3,2,1,0:T(8,128)(2,1)} %get-tuple-element.55), calls=%async_computation.3 | async-start | bytes 4194304 | tf_op jit(solution)/shard_map/all_to_all | solution.py:336
  15.2 0.4 rev.6
  16.8 0.4 select_reduce_fusion.1
  18.8 3.6 %copy.31 = bf16[896,896]{0,1:T(8,128)(2,1)} copy(bf16[896,896]{1,0:T(8,128)(2,1)} %bitcast.36) | data formatting | bytes 3211264 | tf_op jit(solution)/shard_map/reshape | solution.py:340
  22.6 2.9 %fusion = bf16[896,256]{0,1:T(8,128)(2,1)} fusion(bf16[896,256]{1,0:T(8,128)(2,1)S(1)} %constant_dynamic-update-slice_fusion.refs_4_, bf16[896,896]{1,0:T(8,128)(2,1)} %bitcast.37), kind=kOutput, calls=%fused_computation.1 | convolution fusion | flops 411271168 | bytes 2523136 | tf_op jit(solution)/shard_map/dot_general | solution.py:341
  25.5 1.2 copy.30
  26.7 0.7 fusion.6
  28.1 0.5 broadcast_select_fusion
  28.6 1.9 %collective-permute-start.2 = (bf16[896,256]{1,0:T(8,128)(2,1)S(1)}, bf16[896,256]{1,0:T(8,128)(2,1)}, u32[]{:S(2)}, u32[]{:S(2)}) collective-permute-start(bf16[896,256]{1,0:T(8,128)(2,1)S(1)} %constant_dynamic-update-slice_fusion.refs_4_), channel_id=1, source_target_pairs={{0,1},{1,2},{2,3},{3,4},{4,5},{5,6},{6,7},{7,8},{8,9},{9,10},{10,1... | collective-permute-start | bytes 1376264 | tf_op jit(solution)/shard_map/ppermute | solution.py:301
  30.5 4.6 %collective-permute-start.1 = (bf16[896,256]{1,0:T(8,128)(2,1)S(1)}, bf16[896,256]{1,0:T(8,128)(2,1)}, u32[]{:S(2)}, u32[]{:S(2)}) collective-permute-start(bf16[896,256]{1,0:T(8,128)(2,1)S(1)} %constant_dynamic-update-slice_fusion.refs_4_), channel_id=1, source_target_pairs={{0,2},{1,3},{2,4},{3,5},{4,6},{5,7},{6,8},{7,9},{8,10},{9,11},{10,... | collective-permute-start | bytes 1376264 | tf_op jit(solution)/shard_map/ppermute | solution.py:301
  35.1 6.5 %collective-permute-start = (bf16[896,256]{1,0:T(8,128)(2,1)S(1)}, bf16[896,256]{1,0:T(8,128)(2,1)}, u32[]{:S(2)}, u32[]{:S(2)}) collective-permute-start(bf16[896,256]{1,0:T(8,128)(2,1)S(1)} %constant_dynamic-update-slice_fusion.refs_4_), channel_id=1, source_target_pairs={{0,15},{1,0},{2,1},{3,2},{4,3},{5,4},{6,5},{7,6},{8,7},{9,8},{10,9... | collective-permute-start | bytes 1376264 | tf_op jit(solution)/shard_map/ppermute | solution.py:301
  41.6 1.0 all-to-all-done.3.refs_2_
  42.6 1.9 %stats.1 = (f32[32,2,128]{2,1,0:T(2,128)S(1)}, f32[64,128]{1,0:T(8,128)S(1)}, f32[256,128]{1,0:T(8,128)S(1)}) custom-call(s32[64]{0:T(128)S(1)} %get-tuple-element.53.refs_0_, s32[64]{0:T(128)S(1)} %get-tuple-element.57.refs_1_, bf16[64,2,64,128]{3,2,1,0:T(8,128)(2,1)S(1)} %all-to-all-done.3.refs_2_, bf16[7,128,256]{2,1,0:T(8,128)(2,1)S(1)} %bitcast.31), custom_call_target="tpu_custom_call" | custom-call | tf_op jit(solution)/shard_map/stats/pallas_call | solution.py:378
  44.5 14.2 %conditional.1 = (f32[256,128]{1,0:T(8,128)S(1)}) conditional(s32[]{:T(128)} %convert_element_type.23, (f32[64,128]{1,0:T(8,128)S(1)}, s32[32]{0:T(128)S(1)}) %tuple.19, f32[256,128]{1,0:T(8,128)S(1)} %get-tuple-element.61), branch_computations={%region_7.8_spmd, %region_8.9_spmd} | conditional | bytes 294924 | solution.py:408
  44.5 14.1 %all_to_all.38 = f32[32,8,128]{2,1,0:T(8,128)S(1)} all-to-all(f32[32,8,128]{2,1,0:T(8,128)S(1)} %bitcast.43), channel_id=1, replica_groups=mesh['seq'=32,'head'=16] {'seq'}, dimensions={0} | all-to-all | bytes 262144 | tf_op jit(solution)/shard_map/cond/branch_1_fun/all_to_all | solution.py:393
  58.7 7.6 %grads.1 = (bf16[32,320,128]{2,1,0:T(8,128)(2,1)}, bf16[4,56,256]{2,1,0:T(8,128)(2,1)}, bf16[4,56,256]{2,1,0:T(8,128)(2,1)}, bf16[4,56,256]{2,1,0:T(8,128)(2,1)}, bf16[4,56,256]{2,1,0:T(8,128)(2,1)}) custom-call(s32[64]{0:T(128)} %copy-done.3, s32[64]{0:T(128)} %get-tuple-element.54.refs_1_, bf16[64,2,64,128]{3,2,1,0:T(8,128)(2,1)} %copy-done, ...), custom_call_target="tpu_custom_call" | custom-call | tf_op jit(solution)/shard_map/grads/pallas_call | solution.py:415
  66.3 7.6 %collective-permute-start.3 = (bf16[4,56,256]{2,1,0:T(8,128)(2,1)}, bf16[4,56,256]{2,1,0:T(8,128)(2,1)S(1)}, u32[]{:S(2)}, u32[]{:S(2)}) collective-permute-start(bf16[4,56,256]{2,1,0:T(8,128)(2,1)} %get-tuple-element.70), channel_id=1, source_target_pairs={{0,15},{1,0},{2,1},{3,2},{4,3},{5,4},{6,5},{7,6},{8,7},{9,8},{10,9... | collective-permute-start | bytes 344072 | tf_op jit(solution)/shard_map/ppermute | solution.py:301
  74.0 1.9 %collective-permute-start.4 = (bf16[4,56,256]{2,1,0:T(8,128)(2,1)}, bf16[4,56,256]{2,1,0:T(8,128)(2,1)S(1)}, u32[]{:S(2)}, u32[]{:S(2)}) collective-permute-start(bf16[4,56,256]{2,1,0:T(8,128)(2,1)} %get-tuple-element.71), channel_id=1, source_target_pairs={{0,2},{1,3},{2,4},{3,5},{4,6},{5,7},{6,8},{7,9},{8,10},{9,11},{10,... | collective-permute-start | bytes 344072 | tf_op jit(solution)/shard_map/ppermute | solution.py:301
  75.9 1.9 %collective-permute-start.5 = (bf16[4,56,256]{2,1,0:T(8,128)(2,1)}, bf16[4,56,256]{2,1,0:T(8,128)(2,1)}, u32[]{:S(2)}, u32[]{:S(2)}) collective-permute-start(bf16[4,56,256]{2,1,0:T(8,128)(2,1)} %get-tuple-element.72), channel_id=1, source_target_pairs={{0,1},{1,2},{2,3},{3,4},{4,5},{5,6},{6,7},{7,8},{8,9},{9,10},{10,1... | collective-permute-start | bytes 344072 | tf_op jit(solution)/shard_map/ppermute | solution.py:301
  77.9 4.5 %all-to-all-start.4 = ((bf16[32,320,128]{2,1,0:T(8,128)(2,1)}), bf16[32,320,128]{2,1,0:T(8,128)(2,1)S(1)}, u32[]{:S(2)}, u32[]{:S(2)}) async-start(bf16[32,320,128]{2,1,0:T(8,128)(2,1)} %get-tuple-element.65), calls=%async_computation.4 | async-start | bytes 5242880 | tf_op jit(solution)/shard_map/all_to_all | solution.py:442
  82.5 0.6 copy-done.5
  83.1 1.5 %collective-permute-done.5.refs_3_ = bf16[4,56,256]{2,1,0:T(8,128)(2,1)} collective-permute-done((bf16[4,56,256]{2,1,0:T(8,128)(2,1)}, bf16[4,56,256]{2,1,0:T(8,128)(2,1)}, u32[]{:S(2)}, u32[]{:S(2)}) %collective-permute-start.5) | collective-permute-done | bytes 114720 | tf_op jit(solution)/shard_map/ppermute | solution.py:301
  84.6 0.9 copy-done.6
  85.5 3.1 %project.1 = (f32[56,896]{1,0:T(8,128)S(1)}, bf16[56,896]{1,0:T(8,128)(2,1)}, bf16[56,896]{1,0:T(8,128)(2,1)}, bf16[56,896]{1,0:T(8,128)(2,1)}) custom-call(bf16[4,56,256]{2,1,0:T(8,128)(2,1)S(1)} %copy-done.4, bf16[4,56,256]{2,1,0:T(8,128)(2,1)S(1)} %collective-permute-done.3.refs_1_, bf16[4,56,256]{2,1,0:T(8,128)(2,1)S(1)} %copy-done.6, ...), custom_call_target="tpu_custom_call" | custom-call | flops 60000002048 | bytes 2000000 | tf_op jit(solution)/shard_map/project/pallas_call | solution.py:443
  88.6 3.7 %collective-permute-start.6 = (bf16[56,896]{1,0:T(8,128)(2,1)}, bf16[56,896]{1,0:T(8,128)(2,1)S(1)}, u32[]{:S(2)}, u32[]{:S(2)}) collective-permute-start(bf16[56,896]{1,0:T(8,128)(2,1)} %get-tuple-element.78), channel_id=1, source_target_pairs={{0,4},{1,5},{2,6},{3,7},{4,8},{5,9},{6,10},{7,11},{8,12},{9,13},{1... | collective-permute-start | bytes 301064 | tf_op jit(solution)/shard_map/ppermute | solution.py:301
  92.3 10.0 %collective-permute-start.7 = (bf16[56,896]{1,0:T(8,128)(2,1)}, bf16[56,896]{1,0:T(8,128)(2,1)S(1)}, u32[]{:S(2)}, u32[]{:S(2)}) collective-permute-start(bf16[56,896]{1,0:T(8,128)(2,1)} %get-tuple-element.79), channel_id=1, source_target_pairs={{0,8},{1,9},{2,10},{3,11},{4,12},{5,13},{6,14},{7,15},{8,0},{9,1},... | collective-permute-start | bytes 301064 | tf_op jit(solution)/shard_map/ppermute | solution.py:301
  102.3 5.5 %collective-permute-start.8 = (bf16[56,896]{1,0:T(8,128)(2,1)}, bf16[56,896]{1,0:T(8,128)(2,1)S(1)}, u32[]{:S(2)}, u32[]{:S(2)}) collective-permute-start(bf16[56,896]{1,0:T(8,128)(2,1)} %get-tuple-element.80), channel_id=1, source_target_pairs={{0,12},{1,13},{2,14},{3,15},{4,0},{5,1},{6,2},{7,3},{8,4},{9,5},{1... | collective-permute-start | bytes 301064 | tf_op jit(solution)/shard_map/ppermute | solution.py:301
  107.8 8.5 %all-to-all-done.4.in_ref = bf16[32,320,128]{2,1,0:T(8,128)(2,1)S(1)} async-done(((bf16[32,320,128]{2,1,0:T(8,128)(2,1)}), bf16[32,320,128]{2,1,0:T(8,128)(2,1)S(1)}, u32[]{:S(2)}, u32[]{:S(2)}) %all-to-all-start.4) | async-done | bytes 2621472 | tf_op jit(solution)/shard_map/all_to_all | solution.py:442
  116.3 1.5 %finish.1 = (bf16[16,64,128]{2,1,0:T(8,128)(2,1)}, bf16[16,64,128]{2,1,0:T(8,128)(2,1)}, f32[28,128]{1,0:T(8,128)}, f32[28,128]{1,0:T(8,128)}, s32[1]{0:T(128)}) custom-call(s32[32]{0:T(128)S(1)} %get-tuple-element.50.slots_ref, bf16[32,320,128]{2,1,0:T(8,128)(2,1)S(1)} %all-to-all-done.4.in_ref), custom_call_target="tpu_custom_call" | custom-call | tf_op jit(solution)/shard_map/finish/pallas_call | solution.py:462
  117.9 3.6 %collective-permute-done.8.three_ref = bf16[56,896]{1,0:T(8,128)(2,1)S(1)} collective-permute-done((bf16[56,896]{1,0:T(8,128)(2,1)}, bf16[56,896]{1,0:T(8,128)(2,1)S(1)}, u32[]{:S(2)}, u32[]{:S(2)}) %collective-permute-start.8) | collective-permute-done | bytes 100384 | tf_op jit(solution)/shard_map/ppermute | solution.py:301
  121.4 1.4 %total.1 = f32[56,896]{1,0:T(8,128)} custom-call(s32[1]{0:T(128)} %get-tuple-element.68.token_ref, f32[56,896]{1,0:T(8,128)S(1)} %get-tuple-element.77.own_ref, bf16[56,896]{1,0:T(8,128)(2,1)S(1)} %collective-permute-done.6.one_ref, bf16[56,896]{1,0:T(8,128)(2,1)S(1)} %collective-permute-done.7.two_ref, bf16[56,896]{1,0:T(8,128)(2,1)S(1)} %collective-permute-done.8.three_ref), custom_call_target="tpu_custom_call" | custom-call | tf_op jit(solution)/shard_map/total/pallas_call | solution.py:476
  (58 shorter events, 3.4 us)
Async XLA Ops:
  4.0 10.6 %copy-start.9 = (s32[512,2]{0,1:T(2,128)S(1)}, s32[512,2]{0,1:T(2,128)}, u32[]{:S(2)}) copy-start(s32[512,2]{0,1:T(2,128)} %param.12) | copy-start | bytes 12292
  4.0 38.5 %all-to-all-start.3 = ((bf16[64,2,64,128]{3,2,1,0:T(8,128)(2,1)}), bf16[64,2,64,128]{3,2,1,0:T(8,128)(2,1)S(1)}, u32[]{:S(2)}, u32[]{:S(2)}) async-start(bf16[64,2,64,128]{3,2,1,0:T(8,128)(2,1)} %get-tuple-element.55), calls=%async_computation.3 | async-start | bytes 4194304 | tf_op jit(solution)/shard_map/all_to_all | solution.py:336
  18.3 24.3 %copy-start.3 = (s32[64]{0:T(128)}, s32[64]{0:T(128)S(1)}, u32[]{:S(2)}) copy-start(s32[64]{0:T(128)S(1)} %get-tuple-element.53.refs_0_) | copy-start | bytes 772
  18.8 3.7 %copy-start.7 = (bf16[896,128]{1,0:T(8,128)(2,1)S(1)}, bf16[896,128]{1,0:T(8,128)(2,1)}, u32[]{:S(2)}) copy-start(bf16[896,128]{1,0:T(8,128)(2,1)} %param.10) | copy-start | bytes 688132
  18.8 3.7 %copy-start.8 = (bf16[896,128]{1,0:T(8,128)(2,1)S(1)}, bf16[896,128]{1,0:T(8,128)(2,1)}, u32[]{:S(2)}) copy-start(bf16[896,128]{1,0:T(8,128)(2,1)} %param.11) | copy-start | bytes 688132
  26.7 17.8 %copy-start.1 = (bf16[896,256]{1,0:T(8,128)(2,1)}, bf16[896,256]{1,0:T(8,128)(2,1)S(1)}, u32[]{:S(2)}) copy-start(bf16[896,256]{1,0:T(8,128)(2,1)S(1)} %copy.30) | copy-start | bytes 1376260
  28.6 47.3 %collective-permute-start.2 = (bf16[896,256]{1,0:T(8,128)(2,1)S(1)}, bf16[896,256]{1,0:T(8,128)(2,1)}, u32[]{:S(2)}, u32[]{:S(2)}) collective-permute-start(bf16[896,256]{1,0:T(8,128)(2,1)S(1)} %constant_dynamic-update-slice_fusion.refs_4_), channel_id=1, source_target_pairs={{0,1},{1,2},{2,3},{3,4},{4,5},{5,6},{6,7},{7,8},{8,9},{9,10},{10,1... | collective-permute-start | bytes 1376264 | tf_op jit(solution)/shard_map/ppermute | solution.py:301
  30.5 47.4 %collective-permute-start.1 = (bf16[896,256]{1,0:T(8,128)(2,1)S(1)}, bf16[896,256]{1,0:T(8,128)(2,1)}, u32[]{:S(2)}, u32[]{:S(2)}) collective-permute-start(bf16[896,256]{1,0:T(8,128)(2,1)S(1)} %constant_dynamic-update-slice_fusion.refs_4_), channel_id=1, source_target_pairs={{0,2},{1,3},{2,4},{3,5},{4,6},{5,7},{6,8},{7,9},{8,10},{9,11},{10,... | collective-permute-start | bytes 1376264 | tf_op jit(solution)/shard_map/ppermute | solution.py:301
  35.1 42.8 %collective-permute-start = (bf16[896,256]{1,0:T(8,128)(2,1)S(1)}, bf16[896,256]{1,0:T(8,128)(2,1)}, u32[]{:S(2)}, u32[]{:S(2)}) collective-permute-start(bf16[896,256]{1,0:T(8,128)(2,1)S(1)} %constant_dynamic-update-slice_fusion.refs_4_), channel_id=1, source_target_pairs={{0,15},{1,0},{2,1},{3,2},{4,3},{5,4},{6,5},{7,6},{8,7},{9,8},{10,9... | collective-permute-start | bytes 1376264 | tf_op jit(solution)/shard_map/ppermute | solution.py:301
  42.6 16.1 %copy-start = (bf16[64,2,64,128]{3,2,1,0:T(8,128)(2,1)}, bf16[64,2,64,128]{3,2,1,0:T(8,128)(2,1)S(1)}, u32[]{:S(2)}) copy-start(bf16[64,2,64,128]{3,2,1,0:T(8,128)(2,1)S(1)} %all-to-all-done.3.refs_2_) | copy-start | bytes 6291460
  44.5 14.2 %copy-start.2 = (f32[32,2,128]{2,1,0:T(2,128)}, f32[32,2,128]{2,1,0:T(2,128)S(1)}, u32[]{:S(2)}) copy-start(f32[32,2,128]{2,1,0:T(2,128)S(1)} %get-tuple-element.58.refs_4_) | copy-start | bytes 98308
  66.3 16.1 %collective-permute-start.3 = (bf16[4,56,256]{2,1,0:T(8,128)(2,1)}, bf16[4,56,256]{2,1,0:T(8,128)(2,1)S(1)}, u32[]{:S(2)}, u32[]{:S(2)}) collective-permute-start(bf16[4,56,256]{2,1,0:T(8,128)(2,1)} %get-tuple-element.70), channel_id=1, source_target_pairs={{0,15},{1,0},{2,1},{3,2},{4,3},{5,4},{6,5},{7,6},{8,7},{9,8},{10,9... | collective-permute-start | bytes 344072 | tf_op jit(solution)/shard_map/ppermute | solution.py:301
  74.0 8.5 %collective-permute-start.4 = (bf16[4,56,256]{2,1,0:T(8,128)(2,1)}, bf16[4,56,256]{2,1,0:T(8,128)(2,1)S(1)}, u32[]{:S(2)}, u32[]{:S(2)}) collective-permute-start(bf16[4,56,256]{2,1,0:T(8,128)(2,1)} %get-tuple-element.71), channel_id=1, source_target_pairs={{0,2},{1,3},{2,4},{3,5},{4,6},{5,7},{6,8},{7,9},{8,10},{9,11},{10,... | collective-permute-start | bytes 344072 | tf_op jit(solution)/shard_map/ppermute | solution.py:301
  75.9 8.6 %collective-permute-start.5 = (bf16[4,56,256]{2,1,0:T(8,128)(2,1)}, bf16[4,56,256]{2,1,0:T(8,128)(2,1)}, u32[]{:S(2)}, u32[]{:S(2)}) collective-permute-start(bf16[4,56,256]{2,1,0:T(8,128)(2,1)} %get-tuple-element.72), channel_id=1, source_target_pairs={{0,1},{1,2},{2,3},{3,4},{4,5},{5,6},{6,7},{7,8},{8,9},{9,10},{10,1... | collective-permute-start | bytes 344072 | tf_op jit(solution)/shard_map/ppermute | solution.py:301
  77.9 6.7 %copy-start.4 = (bf16[4,56,256]{2,1,0:T(8,128)(2,1)S(1)}, bf16[4,56,256]{2,1,0:T(8,128)(2,1)}, u32[]{:S(2)}) copy-start(bf16[4,56,256]{2,1,0:T(8,128)(2,1)} %get-tuple-element.69.refs_0_) | copy-start | bytes 344068
  77.9 38.4 %all-to-all-start.4 = ((bf16[32,320,128]{2,1,0:T(8,128)(2,1)}), bf16[32,320,128]{2,1,0:T(8,128)(2,1)S(1)}, u32[]{:S(2)}, u32[]{:S(2)}) async-start(bf16[32,320,128]{2,1,0:T(8,128)(2,1)} %get-tuple-element.65), calls=%async_computation.4 | async-start | bytes 5242880 | tf_op jit(solution)/shard_map/all_to_all | solution.py:442
  82.4 0.6 copy-start.5
  84.6 0.9 copy-start.6
  88.6 29.3 %collective-permute-start.6 = (bf16[56,896]{1,0:T(8,128)(2,1)}, bf16[56,896]{1,0:T(8,128)(2,1)S(1)}, u32[]{:S(2)}, u32[]{:S(2)}) collective-permute-start(bf16[56,896]{1,0:T(8,128)(2,1)} %get-tuple-element.78), channel_id=1, source_target_pairs={{0,4},{1,5},{2,6},{3,7},{4,8},{5,9},{6,10},{7,11},{8,12},{9,13},{1... | collective-permute-start | bytes 301064 | tf_op jit(solution)/shard_map/ppermute | solution.py:301
  92.3 25.6 %collective-permute-start.7 = (bf16[56,896]{1,0:T(8,128)(2,1)}, bf16[56,896]{1,0:T(8,128)(2,1)S(1)}, u32[]{:S(2)}, u32[]{:S(2)}) collective-permute-start(bf16[56,896]{1,0:T(8,128)(2,1)} %get-tuple-element.79), channel_id=1, source_target_pairs={{0,8},{1,9},{2,10},{3,11},{4,12},{5,13},{6,14},{7,15},{8,0},{9,1},... | collective-permute-start | bytes 301064 | tf_op jit(solution)/shard_map/ppermute | solution.py:301
  102.3 19.1 %collective-permute-start.8 = (bf16[56,896]{1,0:T(8,128)(2,1)}, bf16[56,896]{1,0:T(8,128)(2,1)S(1)}, u32[]{:S(2)}, u32[]{:S(2)}) collective-permute-start(bf16[56,896]{1,0:T(8,128)(2,1)} %get-tuple-element.80), channel_id=1, source_target_pairs={{0,12},{1,13},{2,14},{3,15},{4,0},{5,1},{6,2},{7,3},{8,4},{9,5},{1... | collective-permute-start | bytes 301064 | tf_op jit(solution)/shard_map/ppermute | solution.py:301

commit v13 on v11

--- a/solution.py
+++ b/solution.py
@@ -11,7 +11,7 @@
 NEIGH = 2
 CAP = 2
 PLACES = 8
-NEAR = (0, -1, 2, 1)
+NEAR = (0, 1, -1, 2)
 FAR = (0, 4, 8, -4)
 VMEM_LIMIT = 40 * 1024 * 1024
 LARGE_LIMIT = 60 * 1024 * 1024
@@ -233,32 +233,39 @@
     pltpu.make_async_copy(stage, out_ref, out_sem).wait()
 
 
-def finish_kernel(slots_ref, in_ref, own_ref, one_ref, two_ref, three_ref, att_ref, qg_ref, enc_ref, kw_ref, vw_ref):
+def finish_kernel(
+    slots_ref, in_ref, own_ref, one_ref, two_ref, three_ref,
+    att_hbm, qg_hbm, enc_hbm, kw_ref, vw_ref, att_ref, qg_ref, enc_ref, sems,
+):
     share = kw_ref.shape[0]
     parts = 2 * CAP * SEGMENT
     room = (in_ref.shape[1] - parts) // 2
-
-    def step(c, _):
-        slot_a, slot_b = slots_ref[NEIGH * c], slots_ref[NEIGH * c + 1]
-
-        def part(slot):
-            holder = lax.div(slot, CAP)
-            row = pl.multiple_of((slot - holder * CAP) * 2 * SEGMENT, 2 * SEGMENT)
-            return in_ref[holder, pl.ds(row, 2 * SEGMENT), :].astype(jnp.float32)
-
-        total = (part(slot_a) + part(slot_b)).astype(jnp.bfloat16)
+    leave_att = pltpu.make_async_copy(att_ref, att_hbm, sems.at[0])
+    leave_qg = pltpu.make_async_copy(qg_ref, qg_hbm, sems.at[1])
+    leave_enc = pltpu.make_async_copy(enc_ref, enc_hbm, sems.at[2])
+
+    def part(slot):
+        holder = lax.div(slot, CAP)
+        row = pl.multiple_of((slot - holder * CAP) * 2 * SEGMENT, 2 * SEGMENT)
+        return in_ref[holder, pl.ds(row, 2 * SEGMENT), :].astype(jnp.float32)
+
+    for c in range(att_ref.shape[0]):
+        total = (part(slots_ref[NEIGH * c]) + part(slots_ref[NEIGH * c + 1])).astype(jnp.bfloat16)
         att_ref[c] = total[:SEGMENT]
         qg_ref[c] = total[SEGMENT:]
-        return 0
-
-    lax.fori_loop(0, att_ref.shape[0], step, 0, unroll=4)
+    leave_att.start()
+    leave_qg.start()
+    total = own_ref[...] + one_ref[...].astype(jnp.float32)
+    enc_ref[...] = total + two_ref[...].astype(jnp.float32) + three_ref[...].astype(jnp.float32)
+    leave_enc.start()
     total = in_ref[0, parts:, :].astype(jnp.float32)
     for s in range(1, in_ref.shape[0]):
         total = total + in_ref[s, parts:, :].astype(jnp.float32)
     kw_ref[...] = total[:share]
     vw_ref[...] = total[room:room + share]
-    total = own_ref[...] + one_ref[...].astype(jnp.float32)
-    enc_ref[...] = total + two_ref[...].astype(jnp.float32) + three_ref[...].astype(jnp.float32)
+    leave_att.wait()
+    leave_qg.wait()
+    leave_enc.wait()
 
 
 def project_kernel(*refs):
@@ -459,7 +466,13 @@
             jax.ShapeDtypeStruct((share, head_dim), f32),
         ),
         in_specs=[spec(SMEM), *[spec(VMEM)] * (1 + far)],
-        out_specs=(spec(VMEM),) * 5,
+        out_specs=(*[spec(HBM)] * 3, spec(VMEM), spec(VMEM)),
+        scratch_shapes=[
+            pltpu.VMEM((segments, SEGMENT, head_dim), bf16),
+            pltpu.VMEM((segments, SEGMENT, head_dim), bf16),
+            pltpu.VMEM((rows, enc_width), f32),
+            pltpu.SemaphoreType.DMA((3,)),
+        ],
         compiler_params=params(),
         name="finish",
     )(slots, returned, own, *far_sums)

time: 124 us -> 124 us (level)
  starting transfers between devices: 58.8 us -> 54.8 us
  waiting for transfers between devices: 15.9 us -> 19.3 us
    ppermute x9, starting transfers between devices: 43.7 us -> 39.7 us  [shifted(): lax.ppermute(x, 'head', [(z, (z + step) % count) for z in range(count)])]
    ppermute x9, waiting for transfers between devices: 14.9 us -> 18.3 us  [shifted(): lax.ppermute(x, 'head', [(z, (z + step) % count) for z in range(count)])]
  transfers between devices with their start and end apart: 11 -> 11, of which waited for: 4 -> 5; matrix products, arithmetic and copies ran while one was open for 11% -> 11% of each run, Pallas kernels for 10% -> 10%
where the time goes in v13:
time: 124 us; the launch traced here: 123 us
  starting transfers between devices  54.8 us (44%)
  waiting for transfers between devices  19.3 us (16%)
  Pallas kernels  18.2 us (15%)
  blocking collectives  14.2 us (11%)
  local copies, waits for them, and re-layouts  9 us (7%)
  matrix products  3.09 us (2%)
  other arithmetic  2.6 us (2%)
  between operations  1.67 us (1%)
    ppermute x9, starting transfers between devices, shifted(): lax.ppermute(x, 'head', [(z, (z + step) % count) for z in range(count)])  39.7 us
    ppermute x9, waiting for transfers between devices, shifted(): lax.ppermute(x, 'head', [(z, (z + step) % count) for z in range(count)])  18.3 us
    all_to_all x1, blocking collectives, one_hop(): return lax.all_to_all(sent, 'seq', split_axis=0, concat_axis=0, tiled=True)  14.2 us
    all_to_all x1, starting transfers between devices, on_device(): lax.all_to_all(packed, 'seq', split_axis=0, concat_axis=0, tiled=True)  10.5 us
    pallas_call x1, Pallas kernels, on_device(): pl.pallas_call(lambda *refs: grads_kernel(scale, group, *refs), out_shape...  7.63 us
    all_to_all x1, starting transfers between devices, on_device(): lax.all_to_all(back, 'seq', split_axis=0, concat_axis=0, tiled=True)  4.55 us
    reshape x1, local copies, waits for them, and re-layouts, on_device(): flat_enc = encodings.reshape(block_count * block_len, enc_width)  3.65 us
    pallas_call x1, Pallas kernels, on_device(): pl.pallas_call(lambda *refs: pack_kernel(block_count, *refs), out_shape=(...  3.38 us
  transfers between devices with their start and end apart: 11, of which 5 were waited for; matrix products, arithmetic and copies ran while one was open for 11% of the time, Pallas kernels for 10%

profile of v13, /device:TPU:1, one launch (start us, length us, event | category | flops | bytes accessed | tf_op | source)
XLA Modules:
  0.0 122.8 jit_solution(7212002274669969581)
XLA Ops:
  0.6 3.4 %pack.1 = (bf16[64,2,64,128]{3,2,1,0:T(8,128)(2,1)}, s32[32]{0:T(128)S(1)}) custom-call(s32[2,512]{1,0:T(2,128)} %bitcast.44, bf16[16,64,128]{2,1,0:T(8,128)(2,1)} %bitcast.39, bf16[16,64,128]{2,1,0:T(8,128)(2,1)} %bitcast.40), custom_call_target="tpu_custom_call" | custom-call | tf_op jit(solution)/shard_map/pack/pallas_call | solution.py:314
  4.0 10.5 %all-to-all-start.3 = ((bf16[64,2,64,128]{3,2,1,0:T(8,128)(2,1)}), bf16[64,2,64,128]{3,2,1,0:T(8,128)(2,1)S(1)}, u32[]{:S(2)}, u32[]{:S(2)}) async-start(bf16[64,2,64,128]{3,2,1,0:T(8,128)(2,1)} %get-tuple-element.55), calls=%async_computation.3 | async-start | bytes 4194304 | tf_op jit(solution)/shard_map/all_to_all | solution.py:334
  15.2 0.4 rev.6
  16.8 0.4 select_reduce_fusion.1
  18.8 3.6 %copy.31 = bf16[896,896]{0,1:T(8,128)(2,1)} copy(bf16[896,896]{1,0:T(8,128)(2,1)} %bitcast.36) | data formatting | bytes 3211264 | tf_op jit(solution)/shard_map/reshape | solution.py:338
  22.5 2.9 %fusion = bf16[896,256]{0,1:T(8,128)(2,1)} fusion(bf16[896,256]{1,0:T(8,128)(2,1)S(1)} %constant_dynamic-update-slice_fusion.refs_4_, bf16[896,896]{1,0:T(8,128)(2,1)} %bitcast.37), kind=kOutput, calls=%fused_computation.1 | convolution fusion | flops 411271168 | bytes 2523136 | tf_op jit(solution)/shard_map/dot_general | solution.py:339
  25.5 1.2 copy.30
  26.7 0.7 fusion.6
  28.0 0.5 broadcast_select_fusion
  28.5 3.0 %collective-permute-start.2 = (bf16[896,256]{1,0:T(8,128)(2,1)S(1)}, bf16[896,256]{1,0:T(8,128)(2,1)}, u32[]{:S(2)}, u32[]{:S(2)}) collective-permute-start(bf16[896,256]{1,0:T(8,128)(2,1)S(1)} %constant_dynamic-update-slice_fusion.refs_4_), channel_id=1, source_target_pairs={{0,2},{1,3},{2,4},{3,5},{4,6},{5,7},{6,8},{7,9},{8,10},{9,11},{10,... | collective-permute-start | bytes 1376264 | tf_op jit(solution)/shard_map/ppermute | solution.py:299
  31.5 8.1 %collective-permute-start.1 = (bf16[896,256]{1,0:T(8,128)(2,1)S(1)}, bf16[896,256]{1,0:T(8,128)(2,1)}, u32[]{:S(2)}, u32[]{:S(2)}) collective-permute-start(bf16[896,256]{1,0:T(8,128)(2,1)S(1)} %constant_dynamic-update-slice_fusion.refs_4_), channel_id=1, source_target_pairs={{0,15},{1,0},{2,1},{3,2},{4,3},{5,4},{6,5},{7,6},{8,7},{9,8},{10,9... | collective-permute-start | bytes 1376264 | tf_op jit(solution)/shard_map/ppermute | solution.py:299
  39.7 1.9 %collective-permute-start = (bf16[896,256]{1,0:T(8,128)(2,1)S(1)}, bf16[896,256]{1,0:T(8,128)(2,1)}, u32[]{:S(2)}, u32[]{:S(2)}) collective-permute-start(bf16[896,256]{1,0:T(8,128)(2,1)S(1)} %constant_dynamic-update-slice_fusion.refs_4_), channel_id=1, source_target_pairs={{0,1},{1,2},{2,3},{3,4},{4,5},{5,6},{6,7},{7,8},{8,9},{9,10},{10,1... | collective-permute-start | bytes 1376264 | tf_op jit(solution)/shard_map/ppermute | solution.py:299
  41.6 0.9 all-to-all-done.3.refs_2_
  42.5 1.9 %stats.1 = (f32[32,2,128]{2,1,0:T(2,128)S(1)}, f32[64,128]{1,0:T(8,128)S(1)}, f32[256,128]{1,0:T(8,128)S(1)}) custom-call(s32[64]{0:T(128)S(1)} %get-tuple-element.53.refs_0_, s32[64]{0:T(128)S(1)} %get-tuple-element.57.refs_1_, bf16[64,2,64,128]{3,2,1,0:T(8,128)(2,1)S(1)} %all-to-all-done.3.refs_2_, bf16[7,128,256]{2,1,0:T(8,128)(2,1)S(1)} %bitcast.31), custom_call_target="tpu_custom_call" | custom-call | tf_op jit(solution)/shard_map/stats/pallas_call | solution.py:376
  44.5 14.2 %conditional.1 = (f32[256,128]{1,0:T(8,128)S(1)}) conditional(s32[]{:T(128)} %convert_element_type.23, (f32[64,128]{1,0:T(8,128)S(1)}, s32[32]{0:T(128)S(1)}) %tuple.19, f32[256,128]{1,0:T(8,128)S(1)} %get-tuple-element.61), branch_computations={%region_7.8_spmd, %region_8.9_spmd} | conditional | bytes 294924 | solution.py:406
  44.5 14.2 %all_to_all.38 = f32[32,8,128]{2,1,0:T(8,128)S(1)} all-to-all(f32[32,8,128]{2,1,0:T(8,128)S(1)} %bitcast.42), channel_id=1, replica_groups=mesh['seq'=32,'head'=16] {'seq'}, dimensions={0} | all-to-all | bytes 262144 | tf_op jit(solution)/shard_map/cond/branch_1_fun/all_to_all | solution.py:391
  58.7 7.6 %grads.1 = (bf16[32,320,128]{2,1,0:T(8,128)(2,1)}, bf16[4,56,256]{2,1,0:T(8,128)(2,1)}, bf16[4,56,256]{2,1,0:T(8,128)(2,1)}, bf16[4,56,256]{2,1,0:T(8,128)(2,1)}, bf16[4,56,256]{2,1,0:T(8,128)(2,1)}) custom-call(s32[64]{0:T(128)} %copy-done.3, s32[64]{0:T(128)} %get-tuple-element.54.refs_1_, bf16[64,2,64,128]{3,2,1,0:T(8,128)(2,1)} %copy-done, ...), custom_call_target="tpu_custom_call" | custom-call | tf_op jit(solution)/shard_map/grads/pallas_call | solution.py:413
  66.3 1.9 %collective-permute-start.3 = (bf16[4,56,256]{2,1,0:T(8,128)(2,1)}, bf16[4,56,256]{2,1,0:T(8,128)(2,1)S(1)}, u32[]{:S(2)}, u32[]{:S(2)}) collective-permute-start(bf16[4,56,256]{2,1,0:T(8,128)(2,1)} %get-tuple-element.67), channel_id=1, source_target_pairs={{0,1},{1,2},{2,3},{3,4},{4,5},{5,6},{6,7},{7,8},{8,9},{9,10},{10,1... | collective-permute-start | bytes 344072 | tf_op jit(solution)/shard_map/ppermute | solution.py:299
  68.3 7.7 %collective-permute-start.4 = (bf16[4,56,256]{2,1,0:T(8,128)(2,1)}, bf16[4,56,256]{2,1,0:T(8,128)(2,1)S(1)}, u32[]{:S(2)}, u32[]{:S(2)}) collective-permute-start(bf16[4,56,256]{2,1,0:T(8,128)(2,1)} %get-tuple-element.68), channel_id=1, source_target_pairs={{0,15},{1,0},{2,1},{3,2},{4,3},{5,4},{6,5},{7,6},{8,7},{9,8},{10,9... | collective-permute-start | bytes 344072 | tf_op jit(solution)/shard_map/ppermute | solution.py:299
  75.9 1.9 %collective-permute-start.5 = (bf16[4,56,256]{2,1,0:T(8,128)(2,1)}, bf16[4,56,256]{2,1,0:T(8,128)(2,1)}, u32[]{:S(2)}, u32[]{:S(2)}) collective-permute-start(bf16[4,56,256]{2,1,0:T(8,128)(2,1)} %get-tuple-element.69), channel_id=1, source_target_pairs={{0,2},{1,3},{2,4},{3,5},{4,6},{5,7},{6,8},{7,9},{8,10},{9,11},{10,... | collective-permute-start | bytes 344072 | tf_op jit(solution)/shard_map/ppermute | solution.py:299
  77.9 4.5 %all-to-all-start.4 = ((bf16[32,320,128]{2,1,0:T(8,128)(2,1)}), bf16[32,320,128]{2,1,0:T(8,128)(2,1)S(1)}, u32[]{:S(2)}, u32[]{:S(2)}) async-start(bf16[32,320,128]{2,1,0:T(8,128)(2,1)} %get-tuple-element.65), calls=%async_computation.4 | async-start | bytes 5242880 | tf_op jit(solution)/shard_map/all_to_all | solution.py:440
  82.5 0.6 copy-done.5
  83.1 3.8 %collective-permute-done.5.refs_3_ = bf16[4,56,256]{2,1,0:T(8,128)(2,1)} collective-permute-done((bf16[4,56,256]{2,1,0:T(8,128)(2,1)}, bf16[4,56,256]{2,1,0:T(8,128)(2,1)}, u32[]{:S(2)}, u32[]{:S(2)}) %collective-permute-start.5) | collective-permute-done | bytes 114720 | tf_op jit(solution)/shard_map/ppermute | solution.py:299
  86.9 0.9 copy-done.6
  87.8 3.1 %project.1 = (f32[56,896]{1,0:T(8,128)S(1)}, bf16[56,896]{1,0:T(8,128)(2,1)S(1)}, bf16[56,896]{1,0:T(8,128)(2,1)S(1)}, bf16[56,896]{1,0:T(8,128)(2,1)S(1)}) custom-call(bf16[4,56,256]{2,1,0:T(8,128)(2,1)S(1)} %copy-done.4, bf16[4,56,256]{2,1,0:T(8,128)(2,1)S(1)} %collective-permute-done.3.refs_1_, bf16[4,56,256]{2,1,0:T(8,128)(2,1)S(1)} %copy-done.6, ...), custom_call_target="tpu_custom_call" | custom-call | flops 60000002048 | bytes 2000000 | tf_op jit(solution)/shard_map/project/pallas_call | solution.py:441
  90.9 1.9 %collective-permute-start.6 = (bf16[56,896]{1,0:T(8,128)(2,1)S(1)}, bf16[56,896]{1,0:T(8,128)(2,1)S(1)}, u32[]{:S(2)}, u32[]{:S(2)}) collective-permute-start(bf16[56,896]{1,0:T(8,128)(2,1)S(1)} %get-tuple-element.75), channel_id=1, source_target_pairs={{0,4},{1,5},{2,6},{3,7},{4,8},{5,9},{6,10},{7,11},{8,12},{9,13},{1... | collective-permute-start | bytes 301064 | tf_op jit(solution)/shard_map/ppermute | solution.py:299
  92.8 8.1 %collective-permute-start.7 = (bf16[56,896]{1,0:T(8,128)(2,1)S(1)}, bf16[56,896]{1,0:T(8,128)(2,1)S(1)}, u32[]{:S(2)}, u32[]{:S(2)}) collective-permute-start(bf16[56,896]{1,0:T(8,128)(2,1)S(1)} %get-tuple-element.76), channel_id=1, source_target_pairs={{0,8},{1,9},{2,10},{3,11},{4,12},{5,13},{6,14},{7,15},{8,0},{9,1},... | collective-permute-start | bytes 301064 | tf_op jit(solution)/shard_map/ppermute | solution.py:299
  100.9 5.1 %collective-permute-start.8 = (bf16[56,896]{1,0:T(8,128)(2,1)S(1)}, bf16[56,896]{1,0:T(8,128)(2,1)S(1)}, u32[]{:S(2)}, u32[]{:S(2)}) collective-permute-start(bf16[56,896]{1,0:T(8,128)(2,1)S(1)} %get-tuple-element.77), channel_id=1, source_target_pairs={{0,12},{1,13},{2,14},{3,15},{4,0},{5,1},{6,2},{7,3},{8,4},{9,5},{1... | collective-permute-start | bytes 301064 | tf_op jit(solution)/shard_map/ppermute | solution.py:299
  106.1 0.9 collective-permute-done.6.one_ref
  107.0 6.6 %collective-permute-done.7.two_ref = bf16[56,896]{1,0:T(8,128)(2,1)S(1)} collective-permute-done((bf16[56,896]{1,0:T(8,128)(2,1)S(1)}, bf16[56,896]{1,0:T(8,128)(2,1)S(1)}, u32[]{:S(2)}, u32[]{:S(2)}) %collective-permute-start.7) | collective-permute-done | bytes 100384 | tf_op jit(solution)/shard_map/ppermute | solution.py:299
  113.6 7.0 %collective-permute-done.8.three_ref = bf16[56,896]{1,0:T(8,128)(2,1)S(1)} collective-permute-done((bf16[56,896]{1,0:T(8,128)(2,1)S(1)}, bf16[56,896]{1,0:T(8,128)(2,1)S(1)}, u32[]{:S(2)}, u32[]{:S(2)}) %collective-permute-start.8) | collective-permute-done | bytes 100384 | tf_op jit(solution)/shard_map/ppermute | solution.py:299
  120.6 2.2 %finish.1 = (bf16[16,64,128]{2,1,0:T(8,128)(2,1)}, bf16[16,64,128]{2,1,0:T(8,128)(2,1)}, f32[56,896]{1,0:T(8,128)}, f32[28,128]{1,0:T(8,128)}, f32[28,128]{1,0:T(8,128)}) custom-call(s32[32]{0:T(128)S(1)} %get-tuple-element.50.slots_ref, bf16[32,320,128]{2,1,0:T(8,128)(2,1)S(1)} %all-to-all-done.4.in_ref, f32[56,896]{1,0:T(8,128)S(1)} %get-tuple-element.74.own_ref, ...), custom_call_target="tpu_custom_call" | custom-call | tf_op jit(solution)/shard_map/finish/pallas_call | solution.py:459
  (57 shorter events, 3.4 us)
Async XLA Ops:
  4.0 10.6 %copy-start.9 = (s32[512,2]{0,1:T(2,128)S(1)}, s32[512,2]{0,1:T(2,128)}, u32[]{:S(2)}) copy-start(s32[512,2]{0,1:T(2,128)} %param.12) | copy-start | bytes 12292
  4.0 38.5 %all-to-all-start.3 = ((bf16[64,2,64,128]{3,2,1,0:T(8,128)(2,1)}), bf16[64,2,64,128]{3,2,1,0:T(8,128)(2,1)S(1)}, u32[]{:S(2)}, u32[]{:S(2)}) async-start(bf16[64,2,64,128]{3,2,1,0:T(8,128)(2,1)} %get-tuple-element.55), calls=%async_computation.3 | async-start | bytes 4194304 | tf_op jit(solution)/shard_map/all_to_all | solution.py:334
  18.2 24.3 %copy-start.3 = (s32[64]{0:T(128)}, s32[64]{0:T(128)S(1)}, u32[]{:S(2)}) copy-start(s32[64]{0:T(128)S(1)} %get-tuple-element.53.refs_0_) | copy-start | bytes 772
  18.7 3.7 %copy-start.7 = (bf16[896,128]{1,0:T(8,128)(2,1)S(1)}, bf16[896,128]{1,0:T(8,128)(2,1)}, u32[]{:S(2)}) copy-start(bf16[896,128]{1,0:T(8,128)(2,1)} %param.10) | copy-start | bytes 688132
  18.7 3.7 %copy-start.8 = (bf16[896,128]{1,0:T(8,128)(2,1)S(1)}, bf16[896,128]{1,0:T(8,128)(2,1)}, u32[]{:S(2)}) copy-start(bf16[896,128]{1,0:T(8,128)(2,1)} %param.11) | copy-start | bytes 688132
  26.7 17.8 %copy-start.1 = (bf16[896,256]{1,0:T(8,128)(2,1)}, bf16[896,256]{1,0:T(8,128)(2,1)S(1)}, u32[]{:S(2)}) copy-start(bf16[896,256]{1,0:T(8,128)(2,1)S(1)} %copy.30) | copy-start | bytes 1376260
  28.5 47.4 %collective-permute-start.2 = (bf16[896,256]{1,0:T(8,128)(2,1)S(1)}, bf16[896,256]{1,0:T(8,128)(2,1)}, u32[]{:S(2)}, u32[]{:S(2)}) collective-permute-start(bf16[896,256]{1,0:T(8,128)(2,1)S(1)} %constant_dynamic-update-slice_fusion.refs_4_), channel_id=1, source_target_pairs={{0,2},{1,3},{2,4},{3,5},{4,6},{5,7},{6,8},{7,9},{8,10},{9,11},{10,... | collective-permute-start | bytes 1376264 | tf_op jit(solution)/shard_map/ppermute | solution.py:299
  31.5 46.4 %collective-permute-start.1 = (bf16[896,256]{1,0:T(8,128)(2,1)S(1)}, bf16[896,256]{1,0:T(8,128)(2,1)}, u32[]{:S(2)}, u32[]{:S(2)}) collective-permute-start(bf16[896,256]{1,0:T(8,128)(2,1)S(1)} %constant_dynamic-update-slice_fusion.refs_4_), channel_id=1, source_target_pairs={{0,15},{1,0},{2,1},{3,2},{4,3},{5,4},{6,5},{7,6},{8,7},{9,8},{10,9... | collective-permute-start | bytes 1376264 | tf_op jit(solution)/shard_map/ppermute | solution.py:299
  39.7 38.2 %collective-permute-start = (bf16[896,256]{1,0:T(8,128)(2,1)S(1)}, bf16[896,256]{1,0:T(8,128)(2,1)}, u32[]{:S(2)}, u32[]{:S(2)}) collective-permute-start(bf16[896,256]{1,0:T(8,128)(2,1)S(1)} %constant_dynamic-update-slice_fusion.refs_4_), channel_id=1, source_target_pairs={{0,1},{1,2},{2,3},{3,4},{4,5},{5,6},{6,7},{7,8},{8,9},{9,10},{10,1... | collective-permute-start | bytes 1376264 | tf_op jit(solution)/shard_map/ppermute | solution.py:299
  42.5 16.2 %copy-start = (bf16[64,2,64,128]{3,2,1,0:T(8,128)(2,1)}, bf16[64,2,64,128]{3,2,1,0:T(8,128)(2,1)S(1)}, u32[]{:S(2)}) copy-start(bf16[64,2,64,128]{3,2,1,0:T(8,128)(2,1)S(1)} %all-to-all-done.3.refs_2_) | copy-start | bytes 6291460
  44.5 14.2 %copy-start.2 = (f32[32,2,128]{2,1,0:T(2,128)}, f32[32,2,128]{2,1,0:T(2,128)S(1)}, u32[]{:S(2)}) copy-start(f32[32,2,128]{2,1,0:T(2,128)S(1)} %get-tuple-element.58.refs_4_) | copy-start | bytes 98308
  66.3 16.1 %collective-permute-start.3 = (bf16[4,56,256]{2,1,0:T(8,128)(2,1)}, bf16[4,56,256]{2,1,0:T(8,128)(2,1)S(1)}, u32[]{:S(2)}, u32[]{:S(2)}) collective-permute-start(bf16[4,56,256]{2,1,0:T(8,128)(2,1)} %get-tuple-element.67), channel_id=1, source_target_pairs={{0,1},{1,2},{2,3},{3,4},{4,5},{5,6},{6,7},{7,8},{8,9},{9,10},{10,1... | collective-permute-start | bytes 344072 | tf_op jit(solution)/shard_map/ppermute | solution.py:299
  68.3 14.2 %collective-permute-start.4 = (bf16[4,56,256]{2,1,0:T(8,128)(2,1)}, bf16[4,56,256]{2,1,0:T(8,128)(2,1)S(1)}, u32[]{:S(2)}, u32[]{:S(2)}) collective-permute-start(bf16[4,56,256]{2,1,0:T(8,128)(2,1)} %get-tuple-element.68), channel_id=1, source_target_pairs={{0,15},{1,0},{2,1},{3,2},{4,3},{5,4},{6,5},{7,6},{8,7},{9,8},{10,9... | collective-permute-start | bytes 344072 | tf_op jit(solution)/shard_map/ppermute | solution.py:299
  75.9 11.0 %collective-permute-start.5 = (bf16[4,56,256]{2,1,0:T(8,128)(2,1)}, bf16[4,56,256]{2,1,0:T(8,128)(2,1)}, u32[]{:S(2)}, u32[]{:S(2)}) collective-permute-start(bf16[4,56,256]{2,1,0:T(8,128)(2,1)} %get-tuple-element.69), channel_id=1, source_target_pairs={{0,2},{1,3},{2,4},{3,5},{4,6},{5,7},{6,8},{7,9},{8,10},{9,11},{10,... | collective-permute-start | bytes 344072 | tf_op jit(solution)/shard_map/ppermute | solution.py:299
  77.9 9.0 %copy-start.4 = (bf16[4,56,256]{2,1,0:T(8,128)(2,1)S(1)}, bf16[4,56,256]{2,1,0:T(8,128)(2,1)}, u32[]{:S(2)}) copy-start(bf16[4,56,256]{2,1,0:T(8,128)(2,1)} %get-tuple-element.66.refs_0_) | copy-start | bytes 344068
  77.9 42.7 %all-to-all-start.4 = ((bf16[32,320,128]{2,1,0:T(8,128)(2,1)}), bf16[32,320,128]{2,1,0:T(8,128)(2,1)S(1)}, u32[]{:S(2)}, u32[]{:S(2)}) async-start(bf16[32,320,128]{2,1,0:T(8,128)(2,1)} %get-tuple-element.65), calls=%async_computation.4 | async-start | bytes 5242880 | tf_op jit(solution)/shard_map/all_to_all | solution.py:440
  82.5 0.6 copy-start.5
  86.9 0.9 copy-start.6
  90.9 16.1 %collective-permute-start.6 = (bf16[56,896]{1,0:T(8,128)(2,1)S(1)}, bf16[56,896]{1,0:T(8,128)(2,1)S(1)}, u32[]{:S(2)}, u32[]{:S(2)}) collective-permute-start(bf16[56,896]{1,0:T(8,128)(2,1)S(1)} %get-tuple-element.75), channel_id=1, source_target_pairs={{0,4},{1,5},{2,6},{3,7},{4,8},{5,9},{6,10},{7,11},{8,12},{9,13},{1... | collective-permute-start | bytes 301064 | tf_op jit(solution)/shard_map/ppermute | solution.py:299
  92.8 20.8 %collective-permute-start.7 = (bf16[56,896]{1,0:T(8,128)(2,1)S(1)}, bf16[56,896]{1,0:T(8,128)(2,1)S(1)}, u32[]{:S(2)}, u32[]{:S(2)}) collective-permute-start(bf16[56,896]{1,0:T(8,128)(2,1)S(1)} %get-tuple-element.76), channel_id=1, source_target_pairs={{0,8},{1,9},{2,10},{3,11},{4,12},{5,13},{6,14},{7,15},{8,0},{9,1},... | collective-permute-start | bytes 301064 | tf_op jit(solution)/shard_map/ppermute | solution.py:299
  100.9 19.7 %collective-permute-start.8 = (bf16[56,896]{1,0:T(8,128)(2,1)S(1)}, bf16[56,896]{1,0:T(8,128)(2,1)S(1)}, u32[]{:S(2)}, u32[]{:S(2)}) collective-permute-start(bf16[56,896]{1,0:T(8,128)(2,1)S(1)} %get-tuple-element.77), channel_id=1, source_target_pairs={{0,12},{1,13},{2,14},{3,15},{4,0},{5,1},{6,2},{7,3},{8,4},{9,5},{1... | collective-permute-start | bytes 301064 | tf_op jit(solution)/shard_map/ppermute | solution.py:299
